TPU v7x, 32 devices: a whole 2x2x4 slice. The times are simulated.
32 devices in a mesh: head: 2 (over x), ctx: 16 (over z, y, core).
Axes of the slice: x: 2, y: 2, z: 4, core: 2. Of those that a mesh axis runs over, the one named last changes fastest.
Arguments:
- queries: bfloat16 [2, 16, 1024, 128], P('head', 'ctx'), may hold values from -72 to 72
- keys: bfloat16 [2, 65536, 128], P('head', 'ctx'), may hold values from -24 to 24
- values: bfloat16 [2, 65536, 128], P('head', 'ctx'), may hold values from -6 to 6
- kept: int32 [2, 512], P('head'), may hold values from 0 to 65535, as said below
- roots: int32 [2], P('head'), may hold values from 0 to 15
Outputs:
- compact: float32 [2, 512, 128], P('head')
- fit_error: float32 [], replicated
Inputs may be any that keep to these rules, and one draw needn't show every extreme that they name: `kept`: per head: 512 distinct increasing positions; at most 128 of them lie within one context device's 4096 positions, and exactly 128 within at least one such device.
All inputs are finite; a program needn't handle non-finite values.
Results may differ from a plain program's by a relative error of at most 0.0003.
Values may be sent and summed in bfloat16 or wider, within the bound.
No kernel may reach another device: no remote copies, remote signals or barrier semaphores. Data moves between devices by JAX's collectives and lax.ppermute only.
A program may use at most 64 MiB of HBM per device.

v0:
```python
import math

import jax
import jax.numpy as jnp
from jax import lax
from jax.sharding import PartitionSpec as P

HD = 128
KBLK = 1024
M = 512


ridge_share = 0.01


def spread(array, axis, root):
    mine = lax.axis_index(axis) == root
    return lax.psum(jnp.where(mine, array, jnp.zeros_like(array)), axis)


def merge_parts(first, second):
    first_max, first_sum, first_out = first
    second_max, second_sum, second_out = second
    joint = jnp.maximum(first_max, second_max)
    first_scale = jnp.exp(first_max - joint)
    second_scale = jnp.exp(second_max - joint)
    return (
        joint,
        first_sum * first_scale + second_sum * second_scale,
        first_out * first_scale[:, None] + second_out * second_scale[:, None],
    )


def block_partials(queries_ref, key_slab, value_slab, score_scale):
    blocks = key_slab.shape[0] // KBLK
    key_blocks = key_slab.reshape(blocks, KBLK, HD)
    value_blocks = value_slab.reshape(blocks, KBLK, HD)
    rows = queries_ref.shape[0]

    def visit(carry, pieces):
        key_block, value_block = pieces
        scores = (
            jnp.einsum("rd,kd->rk", queries_ref, key_block, preferred_element_type=jnp.float32)
            * score_scale
        )
        block_max = jnp.max(scores, axis=1)
        weights = jnp.exp(scores - block_max[:, None]).astype(jnp.bfloat16)
        block_sum = jnp.sum(weights.astype(jnp.float32), axis=1)
        block_out = jnp.dot(weights, value_block, preferred_element_type=jnp.float32)
        return (merge_parts(carry, (block_max, block_sum, block_out)), None)

    start = (
        jnp.full((rows,), -jnp.inf, jnp.float32),
        jnp.zeros((rows,), jnp.float32),
        jnp.zeros((rows, HD), jnp.float32),
    )
    return lax.scan(visit, start, (key_blocks, value_blocks))[0]


def compact_softmax(queries_ref, compact_keys, score_scale):
    scores = (
        jnp.einsum("rd,md->rm", queries_ref, compact_keys, preferred_element_type=jnp.float32)
        * score_scale
    )
    return jax.nn.softmax(scores, axis=1)


def inner_left(left, right):
    return lax.dot_general(
        left,
        right,
        (((0,), (0,)), ((), ())),
        precision=lax.Precision.HIGHEST,
        preferred_element_type=jnp.float32,
    )


def per_device(queries, keys, values, kept, roots):
    score_scale = 1.0 / math.sqrt(HD)
    queries_ref = spread(queries[0, 0], "ctx", roots[0])
    run_max, run_sum, run_out = block_partials(queries_ref, keys[0], values[0], score_scale)
    highest = lax.pmax(run_max, "ctx")
    rescale = jnp.exp(run_max - highest)
    run_sum, run_out = lax.psum((run_sum * rescale, run_out * rescale[:, None]), "ctx")
    target = run_out / run_sum[:, None]
    slab = keys.shape[1]
    shard = lax.axis_index("ctx")
    positions = kept[0]
    owner = positions // slab
    local_rows = positions - shard * slab
    mine = owner == shard
    capacity = 4 * M // lax.axis_size("ctx")
    order = jnp.arange(M, dtype=jnp.int32)
    earlier = (owner[:, None] == owner[None, :]) & (order[None, :] < order[:, None])
    ranking = jnp.sum(earlier.astype(jnp.int32), axis=1)
    slot_index = jnp.arange(capacity, dtype=jnp.int32)
    select = (mine[None, :] & (ranking[None, :] == slot_index[:, None])).astype(jnp.int32)
    slot_rows = jnp.sum(select * local_rows[None, :], axis=1)
    slot_keys = jnp.take(keys[0], slot_rows, axis=0)
    gathered = lax.all_gather(slot_keys, "ctx", axis=0, tiled=True)
    compact_keys = jnp.take(gathered, owner * capacity + ranking, axis=0)
    attend = compact_softmax(queries_ref, compact_keys, score_scale)
    gram = inner_left(attend, attend)
    cross = inner_left(attend, target)
    ridge = ridge_share * jnp.trace(gram) / M
    system = gram + ridge * jnp.eye(M, dtype=jnp.float32)
    factor_low = jnp.linalg.cholesky(system)
    halfway = lax.linalg.triangular_solve(factor_low, cross, left_side=True, lower=True)
    compact = lax.linalg.triangular_solve(
        factor_low, halfway, left_side=True, lower=True, transpose_a=True
    )
    target_square = jnp.sum(target * target)
    fitted_square = jnp.sum(
        compact
        * jnp.dot(
            gram, compact, precision=lax.Precision.HIGHEST, preferred_element_type=jnp.float32
        )
    )
    head_error = (target_square - 2.0 * jnp.sum(compact * cross) + fitted_square) / target_square
    fit_error = lax.psum(head_error, "head") / lax.axis_size("head")
    return (compact[None], fit_error)


def solution(mesh):
    placed = (
        P("head", "ctx", None, None),
        P("head", "ctx", None),
        P("head", "ctx", None),
        P("head", None),
        P("head"),
    )
    return jax.shard_map(
        per_device,
        mesh=mesh,
        in_specs=placed,
        out_specs=(P("head", None, None), P()),
        check_vma=False,
    )
```

profile of v0, /device:TPU:0, one launch (start us, length us, event | category | flops | bytes accessed | tf_op | source)
XLA Modules:
  0.0 373.9 jit_solution(874434419411065564)
XLA Ops:
  7.9 0.7 select_bitcast_fusion
  12.6 2.0 gather_fusion
  14.7 24.9 %all_gather.3 = bf16[2048,128]{1,0:T(8,128)(2,1)S(1)} all-gather(bf16[128,128]{1,0:T(8,128)(2,1)S(1)} %broadcast_select_fusion), channel_id=1, replica_groups=mesh['head'=2,'ctx'=16] {'ctx'}, dimensions={0}, use_global_device_ids=true | all-gather | bytes 557056 | tf_op jit(solution)/shard_map/all_gather | solution.py:100
  39.6 1.3 gather_fusion.1
  41.0 62.8 %all-reduce.4.cloned.1.call-done = bf16[1024,128]{1,0:T(8,128)(2,1)} async-done(((bf16[1024,128]{1,0:T(8,128)(2,1)}), bf16[1024,128]{1,0:T(8,128)(2,1)}) %all-reduce.4.cloned.1.call-update) | async-done | bytes 262160 | tf_op jit(solution)/shard_map/psum | solution.py:18
  103.8 18.7 %while.17 = (s32[]{:T(128)}, f32[1024]{0:T(1024)S(1)}, f32[1024]{0:T(1024)S(1)}, f32[1024,128]{1,0:T(8,128)S(1)}, bf16[4,1024,128]{2,1,0:T(8,128)(2,1)}, /*index...) while((s32[]{:T(128)}, f32[1024]{0:T(1024)S(1)}, ...), condition=%wide.region_17.18_spmd.clone, body=%wide.region_14.17_spmd.clone.sunk | while | flops 547887104 | bytes 14475384 | solution.py:57
  103.8 1.7 multiply_reduce_fusion.5
  106.3 2.2 fusion.103
  108.5 1.7 multiply_reduce_fusion.5
  111.0 2.2 fusion.103
  113.2 1.7 multiply_reduce_fusion.5
  115.7 2.2 fusion.103
  117.8 1.7 multiply_reduce_fusion.5
  120.3 2.2 fusion.103
  122.5 32.5 %pmax.7 = f32[1024]{0:T(1024)S(1)} all-reduce(f32[1024]{0:T(1024)S(1)} %get-tuple-element.42), channel_id=1, replica_groups=mesh['head'=2,'ctx'=16] {'ctx'}, use_global_device_ids=true, to_apply=%region_18.19 | all-reduce | flops 1024 | bytes 8192 | tf_op jit(solution)/shard_map/pmax | solution.py:82
  155.0 1.0 broadcast_multiply_fusion
  156.0 1.4 multiply_reduce_fusion.1
  157.9 4.7 %select_reduce_fusion = (f32[]{:T(128)}, f32[512,512]{1,0:T(8,128)S(1)}) fusion(f32[1024,512]{0,1:T(8,128)S(1)} %get-tuple-element.123, f32[1024]{0:T(1024)S(1)} %fusion.11, f32[1024]{0:T(1024)S(1)} %get-tuple-element.122), kind=kOutput, calls=%fused_computation.44 | convolution fusion | flops 3223584768 | bytes 3153924 | tf_op jit(solution)/shard_map/dot_general | solution.py:69
  162.6 1.3 copy.9
  164.6 1.4 fusion.13
  166.0 1.0 copy-done.1
  167.0 11.7 %cholesky.107 = f32[128,128]{1,0:T(8,128)S(1)} custom-call(f32[128,128]{1,0:T(8,128)S(1)} %cholesky.269), custom_call_target="Cholesky" | custom-call | tf_op jit(solution)/shard_map/jit(cholesky)/cholesky | solution.py:107
  178.8 9.8 %custom-call.32 = f32[1,128,128]{1,2,0:T(8,128)S(1)} custom-call(f32[1,128,128]{2,1,0:T(8,128)S(1)} %get-tuple-element.121), custom_call_target="InvertDiagBlocksLowerTriangular" | custom-call | tf_op jit(solution)/shard_map/jit(cholesky)/cholesky | solution.py:107
  188.6 1.2 cholesky.228
  189.8 2.0 constant_dynamic-update-slice_fusion.3
  191.7 1.2 convolution_subtract_fusion
  193.0 11.9 %cholesky.221 = f32[128,128]{1,0:T(8,128)S(1)} custom-call(f32[128,128]{1,0:T(8,128)S(1)} %cholesky.273), custom_call_target="Cholesky" | custom-call | tf_op jit(solution)/shard_map/jit(cholesky)/cholesky | solution.py:107
  205.5 9.8 %custom-call.33 = f32[1,128,128]{1,2,0:T(8,128)S(1)} custom-call(f32[1,128,128]{2,1,0:T(8,128)S(1)} %get-tuple-element.118), custom_call_target="InvertDiagBlocksLowerTriangular" | custom-call | tf_op jit(solution)/shard_map/jit(cholesky)/cholesky | solution.py:107
  215.3 0.9 convolution_dynamic-update-slice_fusion
  216.3 1.4 convolution_subtract_fusion.1
  217.7 11.7 %cholesky.242 = f32[128,128]{1,0:T(8,128)S(1)} custom-call(f32[128,128]{1,0:T(8,128)S(1)} %cholesky.278), custom_call_target="Cholesky" | custom-call | tf_op jit(solution)/shard_map/jit(cholesky)/cholesky | solution.py:107
  230.7 10.0 %custom-call.34 = f32[1,128,128]{1,2,0:T(8,128)S(1)} custom-call(f32[1,128,128]{2,1,0:T(8,128)S(1)} %get-tuple-element.115), custom_call_target="InvertDiagBlocksLowerTriangular" | custom-call | tf_op jit(solution)/shard_map/jit(cholesky)/cholesky | solution.py:107
  240.7 0.8 convolution_dynamic-update-slice_fusion.1
  241.6 1.4 convolution_subtract_fusion.8
  243.0 11.7 %cholesky.259 = f32[128,128]{1,0:T(8,128)S(1)} custom-call(f32[128,128]{1,0:T(8,128)S(1)} %convolution_subtract_fusion.8), custom_call_target="Cholesky" | custom-call | tf_op jit(solution)/shard_map/jit(cholesky)/cholesky | solution.py:107
  259.2 2.4 select_select_fusion
  261.5 14.4 %while.16 = (s32[]{:T(128)}, f32[512,512]{1,0:T(8,128)}, s32[4,2]{0,1:T(2,128)S(1)}, f32[4,128,128]{2,1,0:T(8,128)}, s32[]{:T(128)}) while((s32[]{:T(128)}, f32[512,512]{1,0:T(8,128)}, s32[4,2]{0,1:T(2,128)S(1)}, f32[4,128,128]{2,1,0:T(8,128)}, s32[]{:T(128)}) %tuple.64), condition=%wide.while_cond, body=%wide.while_body.sunk | while | flops 2 | bytes 132205 | solution.py:109
  262.2 3.0 bitcast_dynamic-update-slice_fusion.2
  265.8 3.0 bitcast_dynamic-update-slice_fusion.2
  269.4 3.0 bitcast_dynamic-update-slice_fusion.2
  273.1 2.9 bitcast_dynamic-update-slice_fusion.2
  275.9 40.1 %custom-call.35 = f32[4,128,128]{1,2,0:T(8,128)S(1)} custom-call(f32[4,128,128]{2,1,0:T(8,128)} %get-tuple-element.51), custom_call_target="InvertDiagBlocksLowerTriangular" | custom-call | tf_op jit(solution)/shard_map/triangular_solve | solution.py:109
  316.1 29.7 %psum.30 = f32[1024]{0:T(1024)S(1)} all-reduce(f32[1024]{0:T(1024)S(1)} %get-tuple-element.102), channel_id=1, replica_groups=mesh['head'=2,'ctx'=16] {'ctx'}, use_global_device_ids=true, to_apply=%region_20.21 | all-reduce | flops 1024 | bytes 8192 | tf_op jit(solution)/shard_map/psum | solution.py:84
  345.8 3.2 fusion.16
  353.1 1.7 fusion.15
  354.7 1.3 multiply_reduce_fusion.3
  356.7 0.8 multiply_reduce_fusion.2
  359.5 5.4 %psum.31 = f32[]{:T(128)} all-reduce(f32[]{:T(128)S(6)} %div.80), channel_id=1, replica_groups=mesh['head'=2,'ctx'=16] {'head'}, use_global_device_ids=true, to_apply=%region_24.25 | all-reduce | flops 1 | bytes 8 | tf_op jit(solution)/shard_map/psum | solution.py:120
  (70 shorter events, 18.1 us)
Async XLA Ops:
  7.2 96.7 %all-reduce.4.cloned.1.call-start = ((), (), s32[]{:S(2)}) async-start(), calls=%async_computation | async-start | bytes 524288 | tf_op jit(solution)/shard_map/psum | solution.py:18
  8.6 337.2 %all-reduce.6.cloned.1.call-start = ((), (), s32[]{:S(2)}) async-start(), calls=%async_computation.1 | async-start | bytes 1048576 | tf_op jit(solution)/shard_map/psum | solution.py:84
  166.0 1.0 copy-start.1
  345.8 3.5 copy-start
  350.7 6.0 %copy-start.2 = (f32[1024,128]{1,0:T(8,128)S(1)}, f32[1024,128]{1,0:T(8,128)}, u32[]{:S(2)}) copy-start(f32[1024,128]{1,0:T(8,128)} %all-reduce.6.cloned.1.call-done) | copy-start | bytes 1572868
Sparse Core Ops, SparseCore 0:
  12.0 91.8 all-reduce.3
  156.2 88.2 all-reduce.5
where the time goes:
time: 378 us; the launch traced here: 374 us
  other arithmetic  136 us (36%)
  blocking collectives  92.6 us (24%)
  waiting for transfers between devices  62.9 us (17%)
  matrix products  38.3 us (10%)
  between operations  22.8 us (6%)
  local copies, waits for them, and re-layouts  21.3 us (6%)
    another operation x14, other arithmetic, per_device(): factor_low = jnp.linalg.cholesky(system)  80.6 us
    psum x1, waiting for transfers between devices, spread(): return lax.psum(jnp.where(mine, array, jnp.zeros_like(array)), axis)  62.8 us
    another operation x3, other arithmetic, per_device(): lax.linalg.triangular_solve(factor_low, halfway, left_side=True, lower=Tr...  42.5 us
    pmax x1, blocking collectives, per_device(): highest = lax.pmax(run_max, 'ctx')  32.5 us
    psum x1, blocking collectives, per_device(): lax.psum((run_sum * rescale, run_out * rescale[:, None]), 'ctx')  29.7 us
    all_gather x1, blocking collectives, per_device(): gathered = lax.all_gather(slot_keys, 'ctx', axis=0, tiled=True)  24.9 us
    another operation x12, local copies, waits for them, and re-layouts  14.4 us
    dot_general x4, matrix products, visit(): jnp.dot(weights, value_block, preferred_element_type=jnp.float32)  8.6 us
  transfers between devices with their start and end apart: 2, of which 1 were waited for; matrix products, arithmetic and copies ran while one was open for 44% of the time, Pallas kernels for 0%

commit v1 on v0

v1 whole, which is shorter than its diff:
```python
import functools
import math

import jax
import jax.numpy as jnp
from jax import lax
from jax.experimental import pallas as pl
from jax.experimental.pallas import tpu as pltpu
from jax.sharding import PartitionSpec as P

KBLK = 1024
PANEL = 128
SUB = 8
RIDGE_SHARE = 0.01
F32 = jnp.float32
BF16 = jnp.bfloat16
HIGH = lax.Precision.HIGHEST
VMEM_LIMIT = 48 * 1024 * 1024
VMEM = pl.BlockSpec(memory_space=pltpu.VMEM)
SMEM = pl.BlockSpec(memory_space=pltpu.SMEM)
NT = (((1,), (1,)), ((), ()))
TN = (((0,), (0,)), ((), ()))
NN = (((1,), (0,)), ((), ()))


def params(**extra):
    return pltpu.CompilerParams(vmem_limit_bytes=VMEM_LIMIT, **extra)


def swap(array, axis, step):
    size = lax.axis_size(axis)
    return lax.ppermute(array, axis, [(i, i ^ step) for i in range(size)])


def swaps(arrays, axis, stride):
    return [arrays[0]] + [swap(x, axis, t * stride) for t, x in enumerate(arrays) if t]


def choose(arrays, which):
    result = arrays[0]
    for t, array in enumerate(arrays[1:], 1):
        result = jnp.where(which == t, array, result)
    return result


def attention_kernel(pieces, score_scale, *refs):
    q_refs, (k_ref, v_ref), o_refs = refs[:pieces], refs[pieces : pieces + 2], refs[pieces + 2 : 2 * pieces + 2]
    vt_ref = refs[-1]
    step = pl.program_id(0)
    dims = v_ref.shape[1]
    keys = k_ref.shape[0]
    vt_ref[:dims, :] = v_ref[...].T
    vt_ref[dims:, :] = jnp.ones((vt_ref.shape[0] - dims, keys), BF16)
    factor = score_scale * math.log2(math.e)

    @pl.when(step == 0)
    def _():
        for o_ref in o_refs:
            o_ref[...] = jnp.zeros_like(o_ref)
            o_ref[dims : dims + 1, :] = jnp.full((1, o_ref.shape[1]), -jnp.inf, F32)

    for q_ref, o_ref in zip(q_refs, o_refs):
        s = lax.dot_general(k_ref[...], q_ref[...], NT, preferred_element_type=F32)
        top = jnp.max(s, axis=0, keepdims=True)
        e = jnp.exp2((s - top) * factor).astype(BF16)
        out = lax.dot_general(vt_ref[...], e, NN, preferred_element_type=F32)
        block_sum = out[dims : dims + 1, :]
        top = top * factor
        old_top = o_ref[dims : dims + 1, :]
        joint = jnp.maximum(old_top, top)
        old_scale = jnp.exp2(old_top - joint)
        new_scale = jnp.exp2(top - joint)
        o_ref[:dims, :] = o_ref[:dims, :] * old_scale + out[:dims, :] * new_scale
        o_ref[dims + 1 : dims + 2, :] = o_ref[dims + 1 : dims + 2, :] * old_scale + block_sum * new_scale
        o_ref[dims : dims + 1, :] = joint


def attention(q_pieces, keys, values, score_scale):
    pieces = len(q_pieces)
    rows, dims = q_pieces[0].shape
    slab = keys.shape[0]
    block = min(KBLK, slab)
    full = lambda shape: pl.BlockSpec(shape, lambda b: (0, 0))
    return pl.pallas_call(
        functools.partial(attention_kernel, pieces, score_scale),
        grid=(slab // block,),
        in_specs=[full((rows, dims))] * pieces + [pl.BlockSpec((block, dims), lambda b: (b, 0))] * 2,
        out_specs=[full((dims + SUB, rows))] * pieces,
        out_shape=[jax.ShapeDtypeStruct((dims + SUB, rows), F32)] * pieces,
        scratch_shapes=[pltpu.VMEM((dims + 16, block), BF16)],
        compiler_params=params(),
        cost_estimate=pl.CostEstimate(
            flops=4 * pieces * rows * slab * dims, bytes_accessed=4 * slab * dims, transcendentals=pieces * rows * slab
        ),
        name="attention",
    )(*q_pieces, keys, values)


def joined(refs, dims):
    tops = [ref[dims : dims + 1, :] for ref in refs]
    top = functools.reduce(jnp.maximum, tops)
    scales = [jnp.exp2(t - top) for t in tops]
    total = sum(ref[dims + 1 : dims + 2, :] * w for ref, w in zip(refs, scales))
    return top, total, scales


def merge_kernel(ways, place_ref, *refs):
    ins, outs = refs[:ways], refs[ways:-1]
    acc = refs[-1]
    dims = ins[0].shape[0] - SUB
    top, total, scales = joined(ins, dims)
    acc[...] = sum(ref[:dims, :] * w for ref, w in zip(ins, scales))
    rows = dims // len(outs)
    for t, out in enumerate(outs):
        start = pl.multiple_of((place_ref[0] ^ t) * rows, SUB)
        out[:rows, :] = acc[pl.ds(start, rows), :]
        out[rows:, :] = jnp.zeros((SUB, out.shape[1]), F32)
        out[rows : rows + 1, :] = top
        out[rows + 1 : rows + 2, :] = total


def merge(parts, place, groups):
    dims, rows = parts[0].shape[0] - SUB, parts[0].shape[1]
    return pl.pallas_call(
        functools.partial(merge_kernel, len(parts)),
        in_specs=[SMEM] + [VMEM] * len(parts),
        out_specs=[VMEM] * groups,
        out_shape=[jax.ShapeDtypeStruct((dims // groups + SUB, rows), F32)] * groups,
        scratch_shapes=[pltpu.VMEM((dims, rows), F32)],
        compiler_params=params(),
        cost_estimate=pl.CostEstimate(flops=10**6, bytes_accessed=10**6, transcendentals=0),
        name="merge",
    )(place, *parts)


def finish_kernel(*refs):
    ins, out = refs[:-1], refs[-1]
    dims = out.shape[0]
    _, total, scales = joined(ins, dims)
    out[...] = sum(ref[:dims, :] * (w / total) for ref, w in zip(ins, scales))


def finish(parts):
    dims, rows = parts[0].shape[0] - SUB, parts[0].shape[1]
    return pl.pallas_call(
        finish_kernel,
        in_specs=[VMEM] * len(parts),
        out_specs=VMEM,
        out_shape=jax.ShapeDtypeStruct((dims, rows), F32),
        compiler_params=params(),
        cost_estimate=pl.CostEstimate(flops=10**6, bytes_accessed=10**6, transcendentals=0),
        name="finish",
    )(*parts)


def stack_kernel(place_ref, *refs):
    ins, out = refs[:-1], refs[-1]
    rows = ins[0].shape[0]
    for t, ref in enumerate(ins):
        start = pl.multiple_of((place_ref[0] ^ t) * rows, SUB)
        out[pl.ds(start, rows), :] = ref[...]


def stack(parts, place):
    rows, cols = parts[0].shape
    return pl.pallas_call(
        stack_kernel,
        in_specs=[SMEM] + [VMEM] * len(parts),
        out_specs=VMEM,
        out_shape=jax.ShapeDtypeStruct((rows * len(parts), cols), parts[0].dtype),
        compiler_params=params(),
        cost_estimate=pl.CostEstimate(flops=10**6, bytes_accessed=10**6, transcendentals=0),
        name="stack",
    )(place, *parts)


def gram_kernel(lo, score_scale, place_ref, *refs):
    q_refs, c_refs = refs[:lo], refs[lo : 2 * lo]
    at_ref, h_ref = refs[2 * lo :  2 * lo + 2]
    c_all = refs[-1]
    part = c_refs[0].shape[0]
    for s, c_ref in enumerate(c_refs):
        c_all[pl.ds(pl.multiple_of((place_ref[0] ^ s) * part, 16), part), :] = c_ref[...]
    rows = q_refs[0].shape[0]
    for s, q_ref in enumerate(q_refs):
        scores = lax.dot_general(c_all[...], q_ref[...], NT, preferred_element_type=F32) * score_scale
        weights = jnp.exp(scores - jnp.max(scores, axis=0, keepdims=True))
        weights = weights / jnp.sum(weights, axis=0, keepdims=True)
        at_ref[:, pl.ds(pl.multiple_of((place_ref[0] ^ s) * rows, rows), rows)] = weights
    gram = lax.dot_general(at_ref[...], at_ref[...], NT, precision=HIGH, preferred_element_type=F32)
    kept = gram.shape[0]
    diagonal = lax.broadcasted_iota(jnp.int32, gram.shape, 0) == lax.broadcasted_iota(jnp.int32, gram.shape, 1)
    trace = jnp.sum(jnp.where(diagonal, gram, 0.0))
    h_ref[...] = gram + jnp.where(diagonal, RIDGE_SHARE * trace / kept, 0.0)


def gram_system(q_pieces, c_pieces, place, score_scale):
    lo = len(q_pieces)
    rows = sum(q.shape[0] for q in q_pieces)
    kept = sum(c.shape[0] for c in c_pieces)
    dims = q_pieces[0].shape[1]
    return pl.pallas_call(
        functools.partial(gram_kernel, lo, score_scale),
        in_specs=[SMEM] + [VMEM] * (2 * lo),
        out_specs=[VMEM] * 2,
        out_shape=[jax.ShapeDtypeStruct((kept, rows), F32), jax.ShapeDtypeStruct((kept, kept), F32)],
        scratch_shapes=[pltpu.VMEM((kept, dims), BF16)],
        compiler_params=params(),
        cost_estimate=pl.CostEstimate(flops=12 * rows * kept * kept, bytes_accessed=10**6, transcendentals=rows * kept),
        name="gram",
    )(place, *q_pieces, *c_pieces)


def invert_block(rows):
    count = len(rows)
    size = count * SUB
    lane = lax.broadcasted_iota(jnp.int32, (SUB, size), 1)
    sub = lax.broadcasted_iota(jnp.int32, (SUB, size), 0)
    spread = lambda array, column: jnp.broadcast_to(array[:, column : column + 1], (SUB, size))
    line = lambda array, row: jnp.broadcast_to(array[row : row + 1, :], (SUB, size))
    for k in range(count):
        base = k * SUB
        inside = (lane >= base) & (lane < base + SUB)
        columns = [spread(rows[k], base + j) for j in range(SUB)]
        work = jnp.where(inside, jnp.where(lane - base == sub, 1.0, 0.0), rows[k])
        for j in range(SUB):
            here = sub == j
            inverse = 1.0 / line(columns[j], j)
            step = lambda v: (lambda t: jnp.where(here, t, v - columns[j] * t))(line(v, j) * inverse)
            for i in range(j + 1, SUB):
                columns[i] = step(columns[i])
            work = step(work)
        lines = [line(work, j) for j in range(SUB)]
        updated = []
        for i in range(count):
            if i == k:
                updated.append(work)
                continue
            fresh = jnp.where(inside, 0.0, rows[i])
            for j in range(SUB):
                fresh = fresh - spread(rows[i], base + j) * lines[j]
            updated.append(fresh)
        rows = updated
    return rows


def sweep_kernel(panel, h_ref, out_ref):
    size = h_ref.shape[0]
    at = pl.ds(panel * PANEL, PANEL)
    across = h_ref[at, :]
    block = across[:, panel * PANEL : (panel + 1) * PANEL]
    inverse = jnp.concatenate(
        invert_block([block[i * SUB : (i + 1) * SUB, :] for i in range(PANEL // SUB)]), axis=0
    )
    turned = lax.dot_general(inverse, across, NN, precision=HIGH, preferred_element_type=F32)
    out_ref[...] = h_ref[...] - lax.dot_general(across, turned, TN, precision=HIGH, preferred_element_type=F32)
    out_ref[:, at] = turned.T
    out_ref[at, :] = turned
    out_ref[at, at] = -inverse


def sweep(system, panel):
    size = system.shape[0]
    return pl.pallas_call(
        functools.partial(sweep_kernel, panel),
        in_specs=[VMEM],
        out_specs=VMEM,
        out_shape=jax.ShapeDtypeStruct(system.shape, F32),
        compiler_params=params(),
        cost_estimate=pl.CostEstimate(flops=5 * 10**9, bytes_accessed=4 * size * size, transcendentals=0),
        name="sweep",
    )(system)


def fit_kernel(lo, place_ref, minus_ref, at_ref, *refs):
    y_refs = refs[:lo]
    x_ref, err_ref = refs[lo : lo + 2]
    yt = refs[-1]
    rows = y_refs[0].shape[1]
    for s, y_ref in enumerate(y_refs):
        yt[:, pl.ds(pl.multiple_of((place_ref[0] ^ s) * rows, rows), rows)] = y_ref[...]
    target = yt[...]
    attend = at_ref[...]
    cross = lax.dot_general(target, attend, NT, precision=HIGH, preferred_element_type=F32)
    fitted = -lax.dot_general(cross, minus_ref[...], NN, precision=HIGH, preferred_element_type=F32)
    x_ref[...] = fitted.T
    misfit = lax.dot_general(fitted, attend, NN, precision=HIGH, preferred_element_type=F32) - target
    error = jnp.sum(misfit * misfit) / jnp.sum(target * target)
    err_ref[...] = jnp.full(err_ref.shape, error, F32)


def fit(minus_inverse, attend, y_pieces, place):
    kept, rows = attend.shape
    dims = y_pieces[0].shape[0]
    lo = len(y_pieces)
    return pl.pallas_call(
        functools.partial(fit_kernel, lo),
        in_specs=[SMEM] + [VMEM] * (2 + lo),
        out_specs=[VMEM] * 2,
        out_shape=[jax.ShapeDtypeStruct((kept, dims), F32), jax.ShapeDtypeStruct((SUB, 128), F32)],
        scratch_shapes=[pltpu.VMEM((dims, rows), F32)],
        compiler_params=params(),
        cost_estimate=pl.CostEstimate(flops=24 * rows * kept * dims, bytes_accessed=10**6, transcendentals=0),
        name="fit",
    )(place, minus_inverse, attend, *y_pieces)


def per_device(queries, keys, values, kept, roots):
    dims = queries.shape[3]
    score_scale = 1.0 / math.sqrt(dims)
    count = lax.axis_size("ctx")
    lo = math.gcd(count, 4)
    hi = count // lo
    shard = lax.axis_index("ctx")
    my_lo, my_hi = shard % lo, shard // lo
    root_lo, root_hi = roots[0] % lo, roots[0] // lo
    place_lo = my_lo.reshape(1).astype(jnp.int32)
    place_hi = my_hi.reshape(1).astype(jnp.int32)
    part = lambda array, step: lax.dynamic_index_in_dim(array, my_lo ^ step, 0, keepdims=False)

    own = queries[0, 0].reshape(lo, -1, dims)
    quarter = choose(swaps([part(own, s) for s in range(lo)], "ctx", 1), my_lo ^ root_lo)
    quarter = choose(swaps([quarter] * hi, "ctx", lo), my_hi ^ root_hi)
    q_pieces = swaps([quarter] * lo, "ctx", 1)

    slab = keys.shape[1]
    local = kept[0] - shard * slab
    held = (local >= 0) & (local < slab)
    mine = jnp.where(held[:, None], jnp.take(keys[0], jnp.clip(local, 0, slab - 1), axis=0), jnp.zeros((), keys.dtype))
    mine = mine.reshape(lo, -1, dims)
    chunk = sum(swaps([part(mine, s) for s in range(lo)], "ctx", 1))
    chunk = sum(swaps([chunk] * hi, "ctx", lo))
    c_pieces = swaps([chunk] * lo, "ctx", 1)

    parts = attention(q_pieces[:1], keys[0], values[0], score_scale)
    parts += attention(q_pieces[1:], keys[0], values[0], score_scale)
    parts = swaps(parts, "ctx", 1)

    attend, system = gram_system(q_pieces, c_pieces, place_lo, score_scale)
    panels = system.shape[0] // PANEL
    work = [lambda x, p=p: sweep(x, p) for p in range(panels)]

    def run(x):
        return work.pop(0)(x) if work else x

    def after(x, y):
        return lax.optimization_barrier((x, y))

    system = run(system)
    parts, system = after(parts, system)
    parts = swaps(merge(parts, place_hi, hi), "ctx", lo)
    system = run(system)
    parts, system = after(parts, system)
    done = finish(parts)
    blocks = swaps([done] * hi, "ctx", lo)
    system = run(system)
    blocks, system = after(blocks, system)
    y_pieces = swaps([stack(blocks, place_hi)] * lo, "ctx", 1)
    while work:
        system = run(system)

    compact, error = fit(system, attend, y_pieces, place_lo)
    error = error[0, 0]
    heads = lax.axis_size("head")
    step = 1
    while step < heads:
        error = error + swap(error, "head", step)
        step *= 2
    return (compact[None], error / heads)


def solution(mesh):
    placed = (
        P("head", "ctx", None, None),
        P("head", "ctx", None),
        P("head", "ctx", None),
        P("head", None),
        P("head"),
    )
    return jax.shard_map(
        per_device,
        mesh=mesh,
        in_specs=placed,
        out_specs=(P("head", None, None), P()),
        check_vma=False,
    )
```

time: 378 us -> 95 us (0.25); the launches traced: 374 us -> 94.7 us
  other arithmetic: 136 us -> 2.51 us
  blocking collectives: 92.6 us -> 0 us
  waiting for transfers between devices: 62.9 us -> 5.81 us
  Pallas kernels: 0 us -> 45.6 us
  matrix products: 38.3 us -> 0 us
  starting transfers between devices: 0.08 us -> 32.6 us
  between operations: 22.8 us -> 4.1 us
  local copies, waits for them, and re-layouts: 21.3 us -> 4.02 us
    another operation x17 -> x0, other arithmetic: 123 us -> none  [the longest x14 80.6 us: per_device(): factor_low = jnp.linalg.cholesky(system)]
    psum x2 -> x0, waiting for transfers between devices: 62.8 us -> none  [the longest x1 62.8 us: spread(): return lax.psum(jnp.where(mine, array, jnp.zeros_like(array)), axis)]
    pallas_call x0 -> x11, Pallas kernels: none -> 45.6 us  [the longest x4 22.9 us: sweep(): pl.pallas_call(functools.partial(sweep_kernel, panel), in_specs=[VMEM], o...]
    psum x2 -> x0, blocking collectives: 35.2 us -> none  [the longest x1 29.7 us: per_device(): lax.psum((run_sum * rescale, run_out * rescale[:, None]), 'ctx')]
    ppermute x0 -> x31, starting transfers between devices: none -> 32.6 us  [swap(): return lax.ppermute(array, axis, [(i, i ^ step) for i in range(size)])]
    pmax x1 -> x0, blocking collectives: 32.5 us -> none  [per_device(): highest = lax.pmax(run_max, 'ctx')]
    dot_general x12 -> x0, matrix products: 26.6 us -> none  [the longest x4 8.6 us: visit(): jnp.dot(weights, value_block, preferred_element_type=jnp.float32)]
    all_gather x1 -> x0, blocking collectives: 24.9 us -> none  [per_device(): gathered = lax.all_gather(slot_keys, 'ctx', axis=0, tiled=True)]
  transfers between devices with their start and end apart: 2 -> 31, of which waited for: 1 -> 4; matrix products, arithmetic and copies ran while one was open for 44% -> 5% of each run, Pallas kernels for 0% -> 43%
where the time goes in v1:
time: 95 us; the launch traced here: 94.7 us
  Pallas kernels  45.6 us (48%)
  starting transfers between devices  32.6 us (34%)
  waiting for transfers between devices  5.81 us (6%)
  between operations  4.1 us (4%)
  local copies, waits for them, and re-layouts  4.02 us (4%)
  other arithmetic  2.51 us (3%)
    ppermute x31, starting transfers between devices, swap(): return lax.ppermute(array, axis, [(i, i ^ step) for i in range(size)])  32.6 us
    pallas_call x4, Pallas kernels, sweep(): pl.pallas_call(functools.partial(sweep_kernel, panel), in_specs=[VMEM], o...  22.9 us
    pallas_call x2, Pallas kernels, attention(): pl.pallas_call(functools.partial(attention_kernel, pieces, score_scale),...  12.9 us
    ppermute x31, waiting for transfers between devices, swap(): return lax.ppermute(array, axis, [(i, i ^ step) for i in range(size)])  5.81 us
    pallas_call x1, Pallas kernels, fit(): pl.pallas_call(functools.partial(fit_kernel, lo), in_specs=[SMEM] + [VMEM...  5.03 us
    pallas_call x1, Pallas kernels, gram_system(): pl.pallas_call(functools.partial(gram_kernel, lo, score_scale), in_specs=...  4.71 us
    gather x1, local copies, waits for them, and re-layouts, per_device(): jnp.take(keys[0], jnp.clip(local, 0, slab - 1), axis=0)  2.42 us
  transfers between devices with their start and end apart: 31, of which 4 were waited for; matrix products, arithmetic and copies ran while one was open for 5% of the time, Pallas kernels for 43%

profile of v1, /device:TPU:0, one launch (start us, length us, event | category | flops | bytes accessed | tf_op | source)
XLA Modules:
  0.0 94.7 jit_solution(7214969510834530748)
XLA Ops:
  0.7 1.1 %dynamic-slice_bitcast_fusion = (bf16[256,128]{1,0:T(8,128)(2,1)S(1)}, bf16[256,128]{1,0:T(8,128)(2,1)S(1)}, bf16[256,128]{1,0:T(8,128)(2,1)S(1)}) fusion(bf16[4,256,128]{2,1,0:T(8,128)(2,1)} %bitcast.48, s32[]{:T(128)S(6)} %select_n.111, s32[]{:T(128)S(6)} %select_n.109, s32[]{:T(128)S(6)} %select_n.107), kind=kLoop, calls=%fused_computation.6 | loop fusion | bytes 393228 | tf_op jit(solution)/shard_map/jit(dynamic_index_in_dim)/squeeze | solution.py:319
  1.7 0.5 collective-permute-start.2
  2.3 2.6 %collective-permute-start.1 = (bf16[256,128]{1,0:T(8,128)(2,1)S(1)}, bf16[256,128]{1,0:T(8,128)(2,1)S(1)}, u32[]{:S(2)}, u32[]{:S(2)}) collective-permute-start(bf16[256,128]{1,0:T(8,128)(2,1)S(1)} %get-tuple-element.57), channel_id=1, source_target_pairs={{0,2},{1,3},{2,0},{3,1},{4,6},{5,7},{6,4},{7,5},{8,10},{9,11},{10,... | collective-permute-start | bytes 196616 | tf_op jit(solution)/shard_map/ppermute | solution.py:32
  4.9 0.1 collective-permute-start
  4.9 0.7 and_reduce_fusion
  5.6 0.7 compare_select_fusion
  6.3 2.4 %gather_fusion = bf16[512,128]{1,0:T(8,128)(2,1)S(1)} fusion(bf16[4096,128]{1,0:T(8,128)(2,1)} %bitcast.42, s32[1024]{0:T(1024)S(1)} %pad_clamp_fusion), kind=kCustom, calls=%fused_computation | custom fusion | bytes 264192 | tf_op jit(solution)/shard_map/jit(_take)/gather | solution.py:329
  8.8 0.2 select_select_fusion
  9.0 0.2 collective-permute-start.12
  9.2 1.7 %collective-permute-start.14 = (bf16[128,128]{1,0:T(8,128)(2,1)S(1)}, bf16[128,128]{1,0:T(8,128)(2,1)S(1)}, u32[]{:S(2)}, u32[]{:S(2)}) collective-permute-start(bf16[128,128]{1,0:T(8,128)(2,1)S(1)} %get-tuple-element.60), channel_id=1, source_target_pairs={{0,3},{1,2},{2,1},{3,0},{4,7},{5,6},{6,5},{7,4},{8,11},{9,10},{10,... | collective-permute-start | bytes 98312 | tf_op jit(solution)/shard_map/ppermute | solution.py:32
  11.6 0.4 collective-permute-start.13
  12.0 0.9 fusion.1
  12.9 1.8 %collective-permute-start.5 = (bf16[256,128]{1,0:T(8,128)(2,1)S(1)}, bf16[256,128]{1,0:T(8,128)(2,1)S(1)}, u32[]{:S(2)}, u32[]{:S(2)}) collective-permute-start(bf16[256,128]{1,0:T(8,128)(2,1)S(1)} %fusion.1), channel_id=1, source_target_pairs={{0,4},{1,5},{2,6},{3,7},{4,0},{5,1},{6,2},{7,3},{8,12},{9,13},{10,... | collective-permute-start | bytes 196616 | tf_op jit(solution)/shard_map/ppermute | solution.py:32
  14.7 2.6 %collective-permute-start.4 = (bf16[256,128]{1,0:T(8,128)(2,1)S(1)}, bf16[256,128]{1,0:T(8,128)(2,1)S(1)}, u32[]{:S(2)}, u32[]{:S(2)}) collective-permute-start(bf16[256,128]{1,0:T(8,128)(2,1)S(1)} %fusion.1), channel_id=1, source_target_pairs={{0,8},{1,9},{2,10},{3,11},{4,12},{5,13},{6,14},{7,15},{8,0},{9,1},... | collective-permute-start | bytes 196616 | tf_op jit(solution)/shard_map/ppermute | solution.py:32
  17.3 3.9 %collective-permute-start.17 = (bf16[128,128]{1,0:T(8,128)(2,1)S(1)}, bf16[128,128]{1,0:T(8,128)(2,1)S(1)}, u32[]{:S(2)}, u32[]{:S(2)}) collective-permute-start(bf16[128,128]{1,0:T(8,128)(2,1)S(1)} %fusion.3), channel_id=1, source_target_pairs={{0,12},{1,13},{2,14},{3,15},{4,8},{5,9},{6,10},{7,11},{8,4},{9,5},... | collective-permute-start | bytes 98312 | tf_op jit(solution)/shard_map/ppermute | solution.py:32
  21.2 0.6 collective-permute-start.15
  21.9 2.5 %collective-permute-done.4 = bf16[256,128]{1,0:T(8,128)(2,1)S(1)} collective-permute-done((bf16[256,128]{1,0:T(8,128)(2,1)S(1)}, bf16[256,128]{1,0:T(8,128)(2,1)S(1)}, u32[]{:S(2)}, u32[]{:S(2)}) %collective-permute-start.4) | collective-permute-done | bytes 65568 | tf_op jit(solution)/shard_map/ppermute | solution.py:32
  24.3 0.1 collective-permute-start.8
  24.4 1.6 %collective-permute-start.7 = (bf16[256,128]{1,0:T(8,128)(2,1)S(1)}, bf16[256,128]{1,0:T(8,128)(2,1)S(1)}, u32[]{:S(2)}, u32[]{:S(2)}) collective-permute-start(bf16[256,128]{1,0:T(8,128)(2,1)S(1)} %select_select_fusion.1.refs_0_), channel_id=1, source_target_pairs={{0,2},{1,3},{2,0},{3,1},{4,6},{5,7},{6,4},{7,5},{8,10},{9,11},{10,... | collective-permute-start | bytes 196616 | tf_op jit(solution)/shard_map/ppermute | solution.py:32
  26.0 0.3 collective-permute-start.6
  26.3 0.2 collective-permute-done.16
  26.5 1.0 %collective-permute-start.20 = (bf16[128,128]{1,0:T(8,128)(2,1)S(1)}, bf16[128,128]{1,0:T(8,128)(2,1)S(1)}, u32[]{:S(2)}, u32[]{:S(2)}) collective-permute-start(bf16[128,128]{1,0:T(8,128)(2,1)S(1)} %add_add_fusion.refs_4_), channel_id=1, source_target_pairs={{0,3},{1,2},{2,1},{3,0},{4,7},{5,6},{6,5},{7,4},{8,11},{9,10},{10,... | collective-permute-start | bytes 98312 | tf_op jit(solution)/shard_map/ppermute | solution.py:32
  27.5 0.7 collective-permute-start.19
  28.2 3.6 %attention.2.refs_0_ = f32[136,256]{1,0:T(8,128)S(1)} custom-call(bf16[256,128]{1,0:T(8,128)(2,1)S(1)} %select_select_fusion.1.refs_0_, bf16[4096,128]{1,0:T(8,128)(2,1)S(1)} %bitcast.43, bf16[4096,128]{1,0:T(8,128)(2,1)S(1)} %bitcast.45), custom_call_target="tpu_custom_call" | custom-call | flops 536870912 | bytes 2097152 | tf_op jit(solution)/shard_map/attention/pallas_call | solution.py:84
  31.9 0.2 collective-permute-start.18
  32.1 9.3 %attention.3 = (f32[136,256]{1,0:T(8,128)S(1)}, f32[136,256]{1,0:T(8,128)S(1)}, f32[136,256]{1,0:T(8,128)S(1)}) custom-call(bf16[256,128]{1,0:T(8,128)(2,1)S(1)} %collective-permute-done.6.refs_0_.refs_1_, bf16[256,128]{1,0:T(8,128)(2,1)S(1)} %collective-permute-done.7.refs_1_.refs_2_, bf16[256,128]{1,0:T(8,128)(2,1)S(1)} %collective-permute-done.8.refs_2_.refs_3_, ...), custom_call_target="tpu_custom_call" | custom-call | flops 1610612736 | bytes 2097152 | tf_op jit(solution)/shard_map/attention/pallas_call | solution.py:84
  41.4 0.4 collective-permute-start.9
  41.8 1.3 %collective-permute-start.10 = (f32[136,256]{1,0:T(8,128)S(1)}, f32[136,256]{1,0:T(8,128)S(1)}, u32[]{:S(2)}, u32[]{:S(2)}) collective-permute-start(f32[136,256]{1,0:T(8,128)S(1)} %get-tuple-element.29), channel_id=1, source_target_pairs={{0,2},{1,3},{2,0},{3,1},{4,6},{5,7},{6,4},{7,5},{8,10},{9,11},{10,... | collective-permute-start | bytes 417800 | tf_op jit(solution)/shard_map/ppermute | solution.py:32
  43.1 0.3 collective-permute-start.11
  43.3 4.7 %gram.1 = (f32[512,1024]{1,0:T(8,128)S(1)}, f32[512,512]{1,0:T(8,128)S(1)}) custom-call(s32[1]{0:T(128)} %bitcast.place_ref, bf16[256,128]{1,0:T(8,128)(2,1)S(1)} %select_select_fusion.1.refs_0_, bf16[256,128]{1,0:T(8,128)(2,1)S(1)} %collective-permute-done.6.refs_0_.refs_1_, bf16[256,128]{1,0:T(8,128)(2,1)S(1)} %collective-permute-done.7.refs_1_.refs_2_, ...), custom_call_target="tpu_custom_call" | custom-call | flops 3221225472 | bytes 1000000 | tf_op jit(solution)/shard_map/gram/pallas_call | solution.py:202
  48.0 5.7 %sweep.4.h_ref = f32[512,512]{1,0:T(8,128)S(1)} custom-call(f32[512,512]{1,0:T(8,128)S(1)} %get-tuple-element.31.h_ref), custom_call_target="tpu_custom_call" | custom-call | flops 5000000000 | bytes 1048576 | tf_op jit(solution)/shard_map/sweep/pallas_call | solution.py:264
  53.7 0.1 merge.1
  53.8 1.9 %collective-permute-start.21 = (f32[40,256]{1,0:T(8,128)S(1)}, f32[40,256]{1,0:T(8,128)S(1)}, u32[]{:S(2)}, u32[]{:S(2)}) collective-permute-start(f32[40,256]{1,0:T(8,128)S(1)} %get-tuple-element.37), channel_id=1, source_target_pairs={{0,4},{1,5},{2,6},{3,7},{4,0},{5,1},{6,2},{7,3},{8,12},{9,13},{10,... | collective-permute-start | bytes 122888 | tf_op jit(solution)/shard_map/ppermute | solution.py:32
  55.7 1.1 %collective-permute-start.22 = (f32[40,256]{1,0:T(8,128)S(1)}, f32[40,256]{1,0:T(8,128)S(1)}, u32[]{:S(2)}, u32[]{:S(2)}) collective-permute-start(f32[40,256]{1,0:T(8,128)S(1)} %get-tuple-element.38), channel_id=1, source_target_pairs={{0,8},{1,9},{2,10},{3,11},{4,12},{5,13},{6,14},{7,15},{8,0},{9,1},... | collective-permute-start | bytes 122888 | tf_op jit(solution)/shard_map/ppermute | solution.py:32
  56.9 1.4 %collective-permute-start.23 = (f32[40,256]{1,0:T(8,128)S(1)}, f32[40,256]{1,0:T(8,128)S(1)}, u32[]{:S(2)}, u32[]{:S(2)}) collective-permute-start(f32[40,256]{1,0:T(8,128)S(1)} %get-tuple-element.39), channel_id=1, source_target_pairs={{0,12},{1,13},{2,14},{3,15},{4,8},{5,9},{6,10},{7,11},{8,4},{9,5},... | collective-permute-start | bytes 122888 | tf_op jit(solution)/shard_map/ppermute | solution.py:32
  58.3 5.8 %sweep.5.h_ref = f32[512,512]{1,0:T(8,128)S(1)} custom-call(f32[512,512]{1,0:T(8,128)S(1)} %sweep.4.h_ref), custom_call_target="tpu_custom_call" | custom-call | flops 5000000000 | bytes 1048576 | tf_op jit(solution)/shard_map/sweep/pallas_call | solution.py:264
  64.2 2.5 %collective-permute-start.26 = (f32[32,256]{1,0:T(8,128)S(1)}, f32[32,256]{1,0:T(8,128)S(1)}, u32[]{:S(2)}, u32[]{:S(2)}) collective-permute-start(f32[32,256]{1,0:T(8,128)S(1)} %finish.1.refs_0_), channel_id=1, source_target_pairs={{0,12},{1,13},{2,14},{3,15},{4,8},{5,9},{6,10},{7,11},{8,4},{9,5},... | collective-permute-start | bytes 98312 | tf_op jit(solution)/shard_map/ppermute | solution.py:32
  66.7 2.0 %collective-permute-start.24 = (f32[32,256]{1,0:T(8,128)S(1)}, f32[32,256]{1,0:T(8,128)S(1)}, u32[]{:S(2)}, u32[]{:S(2)}) collective-permute-start(f32[32,256]{1,0:T(8,128)S(1)} %finish.1.refs_0_), channel_id=1, source_target_pairs={{0,4},{1,5},{2,6},{3,7},{4,0},{5,1},{6,2},{7,3},{8,12},{9,13},{10,... | collective-permute-start | bytes 98312 | tf_op jit(solution)/shard_map/ppermute | solution.py:32
  68.6 5.7 %sweep.6.h_ref = f32[512,512]{1,0:T(8,128)S(1)} custom-call(f32[512,512]{1,0:T(8,128)S(1)} %sweep.5.h_ref), custom_call_target="tpu_custom_call" | custom-call | flops 5000000000 | bytes 1048576 | tf_op jit(solution)/shard_map/sweep/pallas_call | solution.py:264
  74.4 0.2 collective-permute-start.29
  74.5 1.5 %collective-permute-start.28 = (f32[128,256]{1,0:T(8,128)S(1)}, f32[128,256]{1,0:T(8,128)S(1)}, u32[]{:S(2)}, u32[]{:S(2)}) collective-permute-start(f32[128,256]{1,0:T(8,128)S(1)} %stack.1.refs_0_), channel_id=1, source_target_pairs={{0,2},{1,3},{2,0},{3,1},{4,6},{5,7},{6,4},{7,5},{8,10},{9,11},{10,... | collective-permute-start | bytes 393224 | tf_op jit(solution)/shard_map/ppermute | solution.py:32
  76.0 0.2 collective-permute-start.27
  76.3 5.8 %sweep.7.minus_ref = f32[512,512]{1,0:T(8,128)S(1)} custom-call(f32[512,512]{1,0:T(8,128)S(1)} %sweep.6.h_ref), custom_call_target="tpu_custom_call" | custom-call | flops 5000000000 | bytes 1048576 | tf_op jit(solution)/shard_map/sweep/pallas_call | solution.py:264
  82.1 1.0 %collective-permute-done.28.refs_2_ = f32[128,256]{1,0:T(8,128)S(1)} collective-permute-done((f32[128,256]{1,0:T(8,128)S(1)}, f32[128,256]{1,0:T(8,128)S(1)}, u32[]{:S(2)}, u32[]{:S(2)}) %collective-permute-start.28) | collective-permute-done | bytes 131104 | tf_op jit(solution)/shard_map/ppermute | solution.py:32
  83.0 5.0 %fit.1 = (f32[512,128]{1,0:T(8,128)}, f32[8,128]{1,0:T(8,128)S(1)}) custom-call(s32[1]{0:T(128)} %bitcast.place_ref, f32[512,512]{1,0:T(8,128)S(1)} %sweep.7.minus_ref, f32[512,1024]{1,0:T(8,128)S(1)} %get-tuple-element.47.at_ref, f32[128,256]{1,0:T(8,128)S(1)} %stack.1.refs_0_, f32[128,256]{1,0:T(8,128)S(1)} %collective-permute-done.27.refs_1_, ...), custom_call_target="tpu_custom_call" | custom-call | flops 1610612736 | bytes 1000000 | tf_op jit(solution)/shard_map/fit/pallas_call | solution.py:296
  88.1 0.5 slice.3
  88.6 1.5 %collective-permute-start.30 = (f32[]{:T(128)}, f32[]{:T(128)}, u32[]{:S(2)}, u32[]{:S(2)}) collective-permute-start(f32[]{:T(128)} %bitcast.19), channel_id=1, source_target_pairs={{0,16},{16,0},{1,17},{17,1},{2,18},{18,2},{3,19},{19,3},{4,20},{20... | collective-permute-start | bytes 20 | tf_op jit(solution)/shard_map/ppermute | solution.py:32
  90.1 2.1 %collective-permute-done.30 = f32[]{:T(128)} collective-permute-done((f32[]{:T(128)}, f32[]{:T(128)}, u32[]{:S(2)}, u32[]{:S(2)}) %collective-permute-start.30) | collective-permute-done | bytes 36 | tf_op jit(solution)/shard_map/ppermute | solution.py:32
  (42 shorter events, 0.2 us)
Async XLA Ops:
  0.6 27.6 %copy-start = (bf16[1,4096,128]{2,1,0:T(8,128)(2,1)S(1)}, bf16[1,4096,128]{2,1,0:T(8,128)(2,1)}, u32[]{:S(2)}) copy-start(bf16[1,4096,128]{2,1,0:T(8,128)(2,1)} %param.6) | copy-start | bytes 3145732
  0.6 27.6 %copy-start.1 = (bf16[1,4096,128]{2,1,0:T(8,128)(2,1)S(1)}, bf16[1,4096,128]{2,1,0:T(8,128)(2,1)}, u32[]{:S(2)}) copy-start(bf16[1,4096,128]{2,1,0:T(8,128)(2,1)} %param.7) | copy-start | bytes 3145732
  1.7 9.9 %collective-permute-start.2 = (bf16[256,128]{1,0:T(8,128)(2,1)S(1)}, bf16[256,128]{1,0:T(8,128)(2,1)S(1)}, u32[]{:S(2)}, u32[]{:S(2)}) collective-permute-start(bf16[256,128]{1,0:T(8,128)(2,1)S(1)} %get-tuple-element.56), channel_id=1, source_target_pairs={{0,1},{1,0},{2,3},{3,2},{4,5},{5,4},{6,7},{7,6},{8,9},{9,8},{10,11... | collective-permute-start | bytes 196616 | tf_op jit(solution)/shard_map/ppermute | solution.py:32
  2.3 9.7 %collective-permute-start.1 = (bf16[256,128]{1,0:T(8,128)(2,1)S(1)}, bf16[256,128]{1,0:T(8,128)(2,1)S(1)}, u32[]{:S(2)}, u32[]{:S(2)}) collective-permute-start(bf16[256,128]{1,0:T(8,128)(2,1)S(1)} %get-tuple-element.57), channel_id=1, source_target_pairs={{0,2},{1,3},{2,0},{3,1},{4,6},{5,7},{6,4},{7,5},{8,10},{9,11},{10,... | collective-permute-start | bytes 196616 | tf_op jit(solution)/shard_map/ppermute | solution.py:32
  4.9 7.1 %collective-permute-start = (bf16[256,128]{1,0:T(8,128)(2,1)S(1)}, bf16[256,128]{1,0:T(8,128)(2,1)S(1)}, u32[]{:S(2)}, u32[]{:S(2)}) collective-permute-start(bf16[256,128]{1,0:T(8,128)(2,1)S(1)} %get-tuple-element.58), channel_id=1, source_target_pairs={{0,3},{1,2},{2,1},{3,0},{4,7},{5,6},{6,5},{7,4},{8,11},{9,10},{10,... | collective-permute-start | bytes 196616 | tf_op jit(solution)/shard_map/ppermute | solution.py:32
  9.0 8.3 %collective-permute-start.12 = (bf16[128,128]{1,0:T(8,128)(2,1)S(1)}, bf16[128,128]{1,0:T(8,128)(2,1)S(1)}, u32[]{:S(2)}, u32[]{:S(2)}) collective-permute-start(bf16[128,128]{1,0:T(8,128)(2,1)S(1)} %get-tuple-element.59), channel_id=1, source_target_pairs={{0,1},{1,0},{2,3},{3,2},{4,5},{5,4},{6,7},{7,6},{8,9},{9,8},{10,11... | collective-permute-start | bytes 98312 | tf_op jit(solution)/shard_map/ppermute | solution.py:32
  9.2 8.1 %collective-permute-start.14 = (bf16[128,128]{1,0:T(8,128)(2,1)S(1)}, bf16[128,128]{1,0:T(8,128)(2,1)S(1)}, u32[]{:S(2)}, u32[]{:S(2)}) collective-permute-start(bf16[128,128]{1,0:T(8,128)(2,1)S(1)} %get-tuple-element.60), channel_id=1, source_target_pairs={{0,3},{1,2},{2,1},{3,0},{4,7},{5,6},{6,5},{7,4},{8,11},{9,10},{10,... | collective-permute-start | bytes 98312 | tf_op jit(solution)/shard_map/ppermute | solution.py:32
  11.6 5.7 %collective-permute-start.13 = (bf16[128,128]{1,0:T(8,128)(2,1)S(1)}, bf16[128,128]{1,0:T(8,128)(2,1)S(1)}, u32[]{:S(2)}, u32[]{:S(2)}) collective-permute-start(bf16[128,128]{1,0:T(8,128)(2,1)S(1)} %get-tuple-element.61), channel_id=1, source_target_pairs={{0,2},{1,3},{2,0},{3,1},{4,6},{5,7},{6,4},{7,5},{8,10},{9,11},{10,... | collective-permute-start | bytes 98312 | tf_op jit(solution)/shard_map/ppermute | solution.py:32
  12.9 8.4 %collective-permute-start.5 = (bf16[256,128]{1,0:T(8,128)(2,1)S(1)}, bf16[256,128]{1,0:T(8,128)(2,1)S(1)}, u32[]{:S(2)}, u32[]{:S(2)}) collective-permute-start(bf16[256,128]{1,0:T(8,128)(2,1)S(1)} %fusion.1), channel_id=1, source_target_pairs={{0,4},{1,5},{2,6},{3,7},{4,0},{5,1},{6,2},{7,3},{8,12},{9,13},{10,... | collective-permute-start | bytes 196616 | tf_op jit(solution)/shard_map/ppermute | solution.py:32
  14.7 9.6 %collective-permute-start.4 = (bf16[256,128]{1,0:T(8,128)(2,1)S(1)}, bf16[256,128]{1,0:T(8,128)(2,1)S(1)}, u32[]{:S(2)}, u32[]{:S(2)}) collective-permute-start(bf16[256,128]{1,0:T(8,128)(2,1)S(1)} %fusion.1), channel_id=1, source_target_pairs={{0,8},{1,9},{2,10},{3,11},{4,12},{5,13},{6,14},{7,15},{8,0},{9,1},... | collective-permute-start | bytes 196616 | tf_op jit(solution)/shard_map/ppermute | solution.py:32
  17.3 7.0 %collective-permute-start.3 = (bf16[256,128]{1,0:T(8,128)(2,1)S(1)}, bf16[256,128]{1,0:T(8,128)(2,1)S(1)}, u32[]{:S(2)}, u32[]{:S(2)}) collective-permute-start(bf16[256,128]{1,0:T(8,128)(2,1)S(1)} %fusion.1), channel_id=1, source_target_pairs={{0,12},{1,13},{2,14},{3,15},{4,8},{5,9},{6,10},{7,11},{8,4},{9,5},... | collective-permute-start | bytes 196616 | tf_op jit(solution)/shard_map/ppermute | solution.py:32
  17.3 8.7 %collective-permute-start.17 = (bf16[128,128]{1,0:T(8,128)(2,1)S(1)}, bf16[128,128]{1,0:T(8,128)(2,1)S(1)}, u32[]{:S(2)}, u32[]{:S(2)}) collective-permute-start(bf16[128,128]{1,0:T(8,128)(2,1)S(1)} %fusion.3), channel_id=1, source_target_pairs={{0,12},{1,13},{2,14},{3,15},{4,8},{5,9},{6,10},{7,11},{8,4},{9,5},... | collective-permute-start | bytes 98312 | tf_op jit(solution)/shard_map/ppermute | solution.py:32
  21.2 5.3 %collective-permute-start.16 = (bf16[128,128]{1,0:T(8,128)(2,1)S(1)}, bf16[128,128]{1,0:T(8,128)(2,1)S(1)}, u32[]{:S(2)}, u32[]{:S(2)}) collective-permute-start(bf16[128,128]{1,0:T(8,128)(2,1)S(1)} %fusion.3), channel_id=1, source_target_pairs={{0,8},{1,9},{2,10},{3,11},{4,12},{5,13},{6,14},{7,15},{8,0},{9,1},... | collective-permute-start | bytes 98312 | tf_op jit(solution)/shard_map/ppermute | solution.py:32
  21.2 5.3 %collective-permute-start.15 = (bf16[128,128]{1,0:T(8,128)(2,1)S(1)}, bf16[128,128]{1,0:T(8,128)(2,1)S(1)}, u32[]{:S(2)}, u32[]{:S(2)}) collective-permute-start(bf16[128,128]{1,0:T(8,128)(2,1)S(1)} %fusion.3), channel_id=1, source_target_pairs={{0,4},{1,5},{2,6},{3,7},{4,0},{5,1},{6,2},{7,3},{8,12},{9,13},{10,... | collective-permute-start | bytes 98312 | tf_op jit(solution)/shard_map/ppermute | solution.py:32
  24.3 7.5 %collective-permute-start.8 = (bf16[256,128]{1,0:T(8,128)(2,1)S(1)}, bf16[256,128]{1,0:T(8,128)(2,1)S(1)}, u32[]{:S(2)}, u32[]{:S(2)}) collective-permute-start(bf16[256,128]{1,0:T(8,128)(2,1)S(1)} %select_select_fusion.1.refs_0_), channel_id=1, source_target_pairs={{0,3},{1,2},{2,1},{3,0},{4,7},{5,6},{6,5},{7,4},{8,11},{9,10},{10,... | collective-permute-start | bytes 196616 | tf_op jit(solution)/shard_map/ppermute | solution.py:32
  24.4 7.7 %collective-permute-start.7 = (bf16[256,128]{1,0:T(8,128)(2,1)S(1)}, bf16[256,128]{1,0:T(8,128)(2,1)S(1)}, u32[]{:S(2)}, u32[]{:S(2)}) collective-permute-start(bf16[256,128]{1,0:T(8,128)(2,1)S(1)} %select_select_fusion.1.refs_0_), channel_id=1, source_target_pairs={{0,2},{1,3},{2,0},{3,1},{4,6},{5,7},{6,4},{7,5},{8,10},{9,11},{10,... | collective-permute-start | bytes 196616 | tf_op jit(solution)/shard_map/ppermute | solution.py:32
  26.0 6.1 %collective-permute-start.6 = (bf16[256,128]{1,0:T(8,128)(2,1)S(1)}, bf16[256,128]{1,0:T(8,128)(2,1)S(1)}, u32[]{:S(2)}, u32[]{:S(2)}) collective-permute-start(bf16[256,128]{1,0:T(8,128)(2,1)S(1)} %select_select_fusion.1.refs_0_), channel_id=1, source_target_pairs={{0,1},{1,0},{2,3},{3,2},{4,5},{5,4},{6,7},{7,6},{8,9},{9,8},{10,11... | collective-permute-start | bytes 196616 | tf_op jit(solution)/shard_map/ppermute | solution.py:32
  26.5 16.6 %collective-permute-start.20 = (bf16[128,128]{1,0:T(8,128)(2,1)S(1)}, bf16[128,128]{1,0:T(8,128)(2,1)S(1)}, u32[]{:S(2)}, u32[]{:S(2)}) collective-permute-start(bf16[128,128]{1,0:T(8,128)(2,1)S(1)} %add_add_fusion.refs_4_), channel_id=1, source_target_pairs={{0,3},{1,2},{2,1},{3,0},{4,7},{5,6},{6,5},{7,4},{8,11},{9,10},{10,... | collective-permute-start | bytes 98312 | tf_op jit(solution)/shard_map/ppermute | solution.py:32
  27.5 15.8 %collective-permute-start.19 = (bf16[128,128]{1,0:T(8,128)(2,1)S(1)}, bf16[128,128]{1,0:T(8,128)(2,1)S(1)}, u32[]{:S(2)}, u32[]{:S(2)}) collective-permute-start(bf16[128,128]{1,0:T(8,128)(2,1)S(1)} %add_add_fusion.refs_4_), channel_id=1, source_target_pairs={{0,2},{1,3},{2,0},{3,1},{4,6},{5,7},{6,4},{7,5},{8,10},{9,11},{10,... | collective-permute-start | bytes 98312 | tf_op jit(solution)/shard_map/ppermute | solution.py:32
  31.9 11.5 %collective-permute-start.18 = (bf16[128,128]{1,0:T(8,128)(2,1)S(1)}, bf16[128,128]{1,0:T(8,128)(2,1)S(1)}, u32[]{:S(2)}, u32[]{:S(2)}) collective-permute-start(bf16[128,128]{1,0:T(8,128)(2,1)S(1)} %add_add_fusion.refs_4_), channel_id=1, source_target_pairs={{0,1},{1,0},{2,3},{3,2},{4,5},{5,4},{6,7},{7,6},{8,9},{9,8},{10,11... | collective-permute-start | bytes 98312 | tf_op jit(solution)/shard_map/ppermute | solution.py:32
  41.4 12.3 %collective-permute-start.9 = (f32[136,256]{1,0:T(8,128)S(1)}, f32[136,256]{1,0:T(8,128)S(1)}, u32[]{:S(2)}, u32[]{:S(2)}) collective-permute-start(f32[136,256]{1,0:T(8,128)S(1)} %get-tuple-element.28), channel_id=1, source_target_pairs={{0,1},{1,0},{2,3},{3,2},{4,5},{5,4},{6,7},{7,6},{8,9},{9,8},{10,11... | collective-permute-start | bytes 417800 | tf_op jit(solution)/shard_map/ppermute | solution.py:32
  41.8 11.9 %collective-permute-start.10 = (f32[136,256]{1,0:T(8,128)S(1)}, f32[136,256]{1,0:T(8,128)S(1)}, u32[]{:S(2)}, u32[]{:S(2)}) collective-permute-start(f32[136,256]{1,0:T(8,128)S(1)} %get-tuple-element.29), channel_id=1, source_target_pairs={{0,2},{1,3},{2,0},{3,1},{4,6},{5,7},{6,4},{7,5},{8,10},{9,11},{10,... | collective-permute-start | bytes 417800 | tf_op jit(solution)/shard_map/ppermute | solution.py:32
  43.1 10.7 %collective-permute-start.11 = (f32[136,256]{1,0:T(8,128)S(1)}, f32[136,256]{1,0:T(8,128)S(1)}, u32[]{:S(2)}, u32[]{:S(2)}) collective-permute-start(f32[136,256]{1,0:T(8,128)S(1)} %get-tuple-element.30), channel_id=1, source_target_pairs={{0,3},{1,2},{2,1},{3,0},{4,7},{5,6},{6,5},{7,4},{8,11},{9,10},{10,... | collective-permute-start | bytes 417800 | tf_op jit(solution)/shard_map/ppermute | solution.py:32
  53.8 10.3 %collective-permute-start.21 = (f32[40,256]{1,0:T(8,128)S(1)}, f32[40,256]{1,0:T(8,128)S(1)}, u32[]{:S(2)}, u32[]{:S(2)}) collective-permute-start(f32[40,256]{1,0:T(8,128)S(1)} %get-tuple-element.37), channel_id=1, source_target_pairs={{0,4},{1,5},{2,6},{3,7},{4,0},{5,1},{6,2},{7,3},{8,12},{9,13},{10,... | collective-permute-start | bytes 122888 | tf_op jit(solution)/shard_map/ppermute | solution.py:32
  55.7 8.4 %collective-permute-start.22 = (f32[40,256]{1,0:T(8,128)S(1)}, f32[40,256]{1,0:T(8,128)S(1)}, u32[]{:S(2)}, u32[]{:S(2)}) collective-permute-start(f32[40,256]{1,0:T(8,128)S(1)} %get-tuple-element.38), channel_id=1, source_target_pairs={{0,8},{1,9},{2,10},{3,11},{4,12},{5,13},{6,14},{7,15},{8,0},{9,1},... | collective-permute-start | bytes 122888 | tf_op jit(solution)/shard_map/ppermute | solution.py:32
  56.9 7.3 %collective-permute-start.23 = (f32[40,256]{1,0:T(8,128)S(1)}, f32[40,256]{1,0:T(8,128)S(1)}, u32[]{:S(2)}, u32[]{:S(2)}) collective-permute-start(f32[40,256]{1,0:T(8,128)S(1)} %get-tuple-element.39), channel_id=1, source_target_pairs={{0,12},{1,13},{2,14},{3,15},{4,8},{5,9},{6,10},{7,11},{8,4},{9,5},... | collective-permute-start | bytes 122888 | tf_op jit(solution)/shard_map/ppermute | solution.py:32
  64.2 10.1 %collective-permute-start.26 = (f32[32,256]{1,0:T(8,128)S(1)}, f32[32,256]{1,0:T(8,128)S(1)}, u32[]{:S(2)}, u32[]{:S(2)}) collective-permute-start(f32[32,256]{1,0:T(8,128)S(1)} %finish.1.refs_0_), channel_id=1, source_target_pairs={{0,12},{1,13},{2,14},{3,15},{4,8},{5,9},{6,10},{7,11},{8,4},{9,5},... | collective-permute-start | bytes 98312 | tf_op jit(solution)/shard_map/ppermute | solution.py:32
  66.7 7.6 %collective-permute-start.25 = (f32[32,256]{1,0:T(8,128)S(1)}, f32[32,256]{1,0:T(8,128)S(1)}, u32[]{:S(2)}, u32[]{:S(2)}) collective-permute-start(f32[32,256]{1,0:T(8,128)S(1)} %finish.1.refs_0_), channel_id=1, source_target_pairs={{0,8},{1,9},{2,10},{3,11},{4,12},{5,13},{6,14},{7,15},{8,0},{9,1},... | collective-permute-start | bytes 98312 | tf_op jit(solution)/shard_map/ppermute | solution.py:32
  66.7 7.6 %collective-permute-start.24 = (f32[32,256]{1,0:T(8,128)S(1)}, f32[32,256]{1,0:T(8,128)S(1)}, u32[]{:S(2)}, u32[]{:S(2)}) collective-permute-start(f32[32,256]{1,0:T(8,128)S(1)} %finish.1.refs_0_), channel_id=1, source_target_pairs={{0,4},{1,5},{2,6},{3,7},{4,0},{5,1},{6,2},{7,3},{8,12},{9,13},{10,... | collective-permute-start | bytes 98312 | tf_op jit(solution)/shard_map/ppermute | solution.py:32
  74.4 7.7 %collective-permute-start.29 = (f32[128,256]{1,0:T(8,128)S(1)}, f32[128,256]{1,0:T(8,128)S(1)}, u32[]{:S(2)}, u32[]{:S(2)}) collective-permute-start(f32[128,256]{1,0:T(8,128)S(1)} %stack.1.refs_0_), channel_id=1, source_target_pairs={{0,3},{1,2},{2,1},{3,0},{4,7},{5,6},{6,5},{7,4},{8,11},{9,10},{10,... | collective-permute-start | bytes 393224 | tf_op jit(solution)/shard_map/ppermute | solution.py:32
  74.5 8.5 %collective-permute-start.28 = (f32[128,256]{1,0:T(8,128)S(1)}, f32[128,256]{1,0:T(8,128)S(1)}, u32[]{:S(2)}, u32[]{:S(2)}) collective-permute-start(f32[128,256]{1,0:T(8,128)S(1)} %stack.1.refs_0_), channel_id=1, source_target_pairs={{0,2},{1,3},{2,0},{3,1},{4,6},{5,7},{6,4},{7,5},{8,10},{9,11},{10,... | collective-permute-start | bytes 393224 | tf_op jit(solution)/shard_map/ppermute | solution.py:32
  76.0 7.0 %collective-permute-start.27 = (f32[128,256]{1,0:T(8,128)S(1)}, f32[128,256]{1,0:T(8,128)S(1)}, u32[]{:S(2)}, u32[]{:S(2)}) collective-permute-start(f32[128,256]{1,0:T(8,128)S(1)} %stack.1.refs_0_), channel_id=1, source_target_pairs={{0,1},{1,0},{2,3},{3,2},{4,5},{5,4},{6,7},{7,6},{8,9},{9,8},{10,11... | collective-permute-start | bytes 393224 | tf_op jit(solution)/shard_map/ppermute | solution.py:32
  88.6 3.6 %collective-permute-start.30 = (f32[]{:T(128)}, f32[]{:T(128)}, u32[]{:S(2)}, u32[]{:S(2)}) collective-permute-start(f32[]{:T(128)} %bitcast.19), channel_id=1, source_target_pairs={{0,16},{16,0},{1,17},{17,1},{2,18},{18,2},{3,19},{19,3},{4,20},{20... | collective-permute-start | bytes 20 | tf_op jit(solution)/shard_map/ppermute | solution.py:32

commit v2 on v1

v2 whole, which is shorter than its diff:
```python
import functools
import math

import jax
import jax.numpy as jnp
from jax import lax
from jax.experimental import pallas as pl
from jax.experimental.pallas import tpu as pltpu
from jax.sharding import PartitionSpec as P

KBLK = 1024
PANEL = 128
SUB = 8
RIDGE_SHARE = 0.01
F32 = jnp.float32
BF16 = jnp.bfloat16
HIGH = lax.Precision.HIGHEST
VMEM_LIMIT = 48 * 1024 * 1024
VMEM = pl.BlockSpec(memory_space=pltpu.VMEM)
NT = (((1,), (1,)), ((), ()))
TN = (((0,), (0,)), ((), ()))
NN = (((1,), (0,)), ((), ()))


def params(**extra):
    return pltpu.CompilerParams(vmem_limit_bytes=VMEM_LIMIT, **extra)


def swap(array, axis, step):
    size = lax.axis_size(axis)
    return lax.ppermute(array, axis, [(i, i ^ step) for i in range(size)])


def exchange(array):
    return lax.all_to_all(array, "ctx", 0, 0, tiled=True)


def gathered(array):
    return exchange(jnp.broadcast_to(array[None], (lax.axis_size("ctx"),) + array.shape))


def attention_kernel(lanes, blocks, score_scale, q_ref, k_ref, v_ref, out_ref, vt_ref, acc_ref, top_ref, sum_ref):
    step = pl.program_id(0)
    dims = v_ref.shape[1]
    keys = k_ref.shape[0] // blocks
    chunks = q_ref.shape[0] // lanes
    factor = score_scale * math.log2(math.e)
    vt_ref[:dims, :] = v_ref[...].T
    vt_ref[dims:, :] = jnp.ones((vt_ref.shape[0] - dims, v_ref.shape[0]), BF16)

    @pl.when(step == 0)
    def _():
        acc_ref[...] = jnp.zeros_like(acc_ref)
        sum_ref[...] = jnp.zeros_like(sum_ref)
        top_ref[...] = jnp.full(top_ref.shape, -jnp.inf, F32)

    def scores(b, c):
        return lax.dot_general(
            k_ref[b * keys : (b + 1) * keys, :],
            q_ref[c * lanes : (c + 1) * lanes, :],
            NT,
            preferred_element_type=F32,
        )

    stages = [(b, c) for b in range(blocks) for c in range(chunks)]
    ahead = scores(*stages[0])
    for n, (b, c) in enumerate(stages):
        s = ahead
        if n + 1 < len(stages):
            ahead = scores(*stages[n + 1])
        at = slice(c * lanes, (c + 1) * lanes)
        top = jnp.max(s, axis=0, keepdims=True)
        e = jnp.exp2((s - top) * factor).astype(BF16)
        out = lax.dot_general(vt_ref[:, b * keys : (b + 1) * keys], e, NN, preferred_element_type=F32)
        top = top * factor
        old_top = top_ref[:, at]
        joint = jnp.maximum(old_top, top)
        old_scale = jnp.exp2(old_top - joint)
        new_scale = jnp.exp2(top - joint)
        acc_ref[:, at] = acc_ref[:, at] * old_scale + out[:dims, :] * new_scale
        sum_ref[:, at] = sum_ref[:, at] * old_scale + out[dims : dims + 1, :] * new_scale
        top_ref[:, at] = joint

    @pl.when(step == pl.num_programs(0) - 1)
    def _():
        rows = out_ref.shape[1] - SUB
        for j in range(out_ref.shape[0]):
            h, c = divmod(j, chunks)
            at = slice(c * lanes, (c + 1) * lanes)
            out_ref[j, :rows, :] = acc_ref[h * rows : (h + 1) * rows, at]
            out_ref[j, rows:, :] = jnp.concatenate(
                [top_ref[:, at], sum_ref[:, at], jnp.zeros((SUB - 2, lanes), F32)], axis=0
            )


def attention(queries, keys, values, score_scale, groups, chunks):
    rows, dims = queries.shape
    slab = keys.shape[0]
    block = min(KBLK, slab)
    blocks = 2 if slab % (2 * block) == 0 else 1
    lanes = rows // chunks
    shape = (groups * chunks, dims // groups + SUB, lanes)
    return pl.pallas_call(
        functools.partial(attention_kernel, lanes, blocks, score_scale),
        grid=(slab // (block * blocks),),
        in_specs=[pl.BlockSpec((rows, dims), lambda b: (0, 0))]
        + [pl.BlockSpec((block * blocks, dims), lambda b: (b, 0))] * 2,
        out_specs=pl.BlockSpec(shape, lambda b: (0, 0, 0)),
        out_shape=jax.ShapeDtypeStruct(shape, F32),
        scratch_shapes=[
            pltpu.VMEM((dims + 16, block * blocks), BF16),
            pltpu.VMEM((dims, rows), F32),
            pltpu.VMEM((1, rows), F32),
            pltpu.VMEM((1, rows), F32),
        ],
        compiler_params=params(),
        cost_estimate=pl.CostEstimate(
            flops=4 * rows * slab * dims, bytes_accessed=4 * slab * dims, transcendentals=rows * slab
        ),
        name="attention",
    )(queries, keys, values)


def merge_kernel(part_ref, out_ref):
    count, rows = part_ref.shape[0], out_ref.shape[1]
    tops = [part_ref[i, rows : rows + 1, :] for i in range(count)]
    top = functools.reduce(jnp.maximum, tops)
    scales = [jnp.exp2(t - top) for t in tops]
    total = sum(part_ref[i, rows + 1 : rows + 2, :] * scales[i] for i in range(count))
    merged = sum(part_ref[i, :rows, :] * scales[i] for i in range(count)) / total
    for i in range(count):
        out_ref[i] = merged


def merge(parts):
    count, rows, lanes = parts.shape
    return pl.pallas_call(
        merge_kernel,
        in_specs=[VMEM],
        out_specs=VMEM,
        out_shape=jax.ShapeDtypeStruct((count, rows - SUB, lanes), F32),
        compiler_params=params(),
        cost_estimate=pl.CostEstimate(flops=10**6, bytes_accessed=10**6, transcendentals=0),
        name="merge",
    )(parts)


def gram_kernel(score_scale, q_ref, c_ref, at_ref, h_ref):
    scores = lax.dot_general(c_ref[...], q_ref[...], NT, preferred_element_type=F32) * score_scale
    weights = jnp.exp(scores - jnp.max(scores, axis=0, keepdims=True))
    at_ref[...] = weights / jnp.sum(weights, axis=0, keepdims=True)
    gram = lax.dot_general(at_ref[...], at_ref[...], NT, precision=HIGH, preferred_element_type=F32)
    kept = gram.shape[0]
    diagonal = lax.broadcasted_iota(jnp.int32, gram.shape, 0) == lax.broadcasted_iota(jnp.int32, gram.shape, 1)
    trace = jnp.sum(jnp.where(diagonal, gram, 0.0))
    h_ref[...] = gram + jnp.where(diagonal, RIDGE_SHARE * trace / kept, 0.0)


def gram_system(queries, kept_keys, score_scale):
    rows, kept = queries.shape[0], kept_keys.shape[0]
    return pl.pallas_call(
        functools.partial(gram_kernel, score_scale),
        in_specs=[VMEM] * 2,
        out_specs=[VMEM] * 2,
        out_shape=[jax.ShapeDtypeStruct((kept, rows), F32), jax.ShapeDtypeStruct((kept, kept), F32)],
        compiler_params=params(),
        cost_estimate=pl.CostEstimate(flops=12 * rows * kept * kept, bytes_accessed=10**6, transcendentals=rows * kept),
        name="gram",
    )(queries, kept_keys)


def invert_block(rows):
    count = len(rows)
    size = count * SUB
    lane = lax.broadcasted_iota(jnp.int32, (SUB, size), 1)
    sub = lax.broadcasted_iota(jnp.int32, (SUB, size), 0)
    spread = lambda array, column: jnp.broadcast_to(array[:, column : column + 1], (SUB, size))
    line = lambda array, row: jnp.broadcast_to(array[row : row + 1, :], (SUB, size))
    for k in range(count):
        base = k * SUB
        inside = (lane >= base) & (lane < base + SUB)
        columns = [spread(rows[k], base + j) for j in range(SUB)]
        work = jnp.where(inside, jnp.where(lane - base == sub, 1.0, 0.0), rows[k])
        for j in range(SUB):
            here = sub == j
            inverse = 1.0 / line(columns[j], j)
            step = lambda v: (lambda t: jnp.where(here, t, v - columns[j] * t))(line(v, j) * inverse)
            for i in range(j + 1, SUB):
                columns[i] = step(columns[i])
            work = step(work)
        lines = [line(work, j) for j in range(SUB)]
        updated = []
        for i in range(count):
            if i == k:
                updated.append(work)
                continue
            fresh = jnp.where(inside, 0.0, rows[i])
            for j in range(SUB):
                fresh = fresh - spread(rows[i], base + j) * lines[j]
            updated.append(fresh)
        rows = updated
    return rows


def sweep_kernel(panel, h_ref, out_ref):
    size = h_ref.shape[0]
    at = pl.ds(panel * PANEL, PANEL)
    across = h_ref[at, :]
    block = across[:, panel * PANEL : (panel + 1) * PANEL]
    inverse = jnp.concatenate(
        invert_block([block[i * SUB : (i + 1) * SUB, :] for i in range(PANEL // SUB)]), axis=0
    )
    turned = lax.dot_general(inverse, across, NN, precision=HIGH, preferred_element_type=F32)
    out_ref[...] = h_ref[...] - lax.dot_general(across, turned, TN, precision=HIGH, preferred_element_type=F32)
    out_ref[:, at] = turned.T
    out_ref[at, :] = turned
    out_ref[at, at] = -inverse


def sweep(system, panel):
    size = system.shape[0]
    return pl.pallas_call(
        functools.partial(sweep_kernel, panel),
        in_specs=[VMEM],
        out_specs=VMEM,
        out_shape=jax.ShapeDtypeStruct(system.shape, F32),
        compiler_params=params(),
        cost_estimate=pl.CostEstimate(flops=5 * 10**9, bytes_accessed=4 * size * size, transcendentals=0),
        name="sweep",
    )(system)


def fit_kernel(minus_ref, at_ref, y_ref, x_ref, err_ref, yt):
    count, high, wide = y_ref.shape
    chunks = at_ref.shape[1] // wide
    for j in range(count):
        h, c = divmod(j, chunks)
        yt[h * high : (h + 1) * high, c * wide : (c + 1) * wide] = y_ref[j]
    target = yt[...]
    attend = at_ref[...]
    cross = lax.dot_general(target, attend, NT, precision=HIGH, preferred_element_type=F32)
    fitted = -lax.dot_general(cross, minus_ref[...], NN, precision=HIGH, preferred_element_type=F32)
    x_ref[...] = fitted.T
    misfit = lax.dot_general(fitted, attend, NN, precision=HIGH, preferred_element_type=F32) - target
    error = jnp.sum(misfit * misfit) / jnp.sum(target * target)
    err_ref[...] = jnp.full(err_ref.shape, error, F32)


def fit(minus_inverse, attend, blocks):
    kept, rows = attend.shape
    dims = blocks.size // rows
    return pl.pallas_call(
        fit_kernel,
        in_specs=[VMEM] * 3,
        out_specs=[VMEM] * 2,
        out_shape=[jax.ShapeDtypeStruct((kept, dims), F32), jax.ShapeDtypeStruct((SUB, 128), F32)],
        scratch_shapes=[pltpu.VMEM((dims, rows), F32)],
        compiler_params=params(),
        cost_estimate=pl.CostEstimate(flops=24 * rows * kept * dims, bytes_accessed=10**6, transcendentals=0),
        name="fit",
    )(minus_inverse, attend, blocks)


def per_device(queries, keys, values, kept, roots):
    rows, dims = queries.shape[2:]
    score_scale = 1.0 / math.sqrt(dims)
    count = lax.axis_size("ctx")
    chunks = math.gcd(count, 4)
    groups = count // chunks
    shard = lax.axis_index("ctx")

    share = exchange(queries[0, 0].reshape(count, -1, dims))
    share = lax.dynamic_index_in_dim(share, roots[0], 0, keepdims=False)
    reference = gathered(share).reshape(rows, dims)

    slab = keys.shape[1]
    local = kept[0] - shard * slab
    held = (local >= 0) & (local < slab)
    mine = jnp.where(held[:, None], jnp.take(keys[0], jnp.clip(local, 0, slab - 1), axis=0), jnp.zeros((), keys.dtype))
    share = jnp.sum(exchange(mine.reshape(count, -1, dims)), axis=0, dtype=keys.dtype)
    kept_keys = gathered(share).reshape(-1, dims)

    parts = exchange(attention(reference, keys[0], values[0], score_scale, groups, chunks))

    attend, system = gram_system(reference, kept_keys, score_scale)
    panels = system.shape[0] // PANEL
    before = panels // 2
    for panel in range(before):
        system = sweep(system, panel)
    parts, system = lax.optimization_barrier((parts, system))
    blocks = exchange(merge(parts))
    for panel in range(before, panels):
        system = sweep(system, panel)

    compact, error = fit(system, attend, blocks)
    error = error[0, 0]
    heads = lax.axis_size("head")
    step = 1
    while step < heads:
        error = error + swap(error, "head", step)
        step *= 2
    return (compact[None], error / heads)


def solution(mesh):
    placed = (
        P("head", "ctx", None, None),
        P("head", "ctx", None),
        P("head", "ctx", None),
        P("head", None),
        P("head"),
    )
    return jax.shard_map(
        per_device,
        mesh=mesh,
        in_specs=placed,
        out_specs=(P("head", None, None), P()),
        check_vma=False,
    )
```

time: 95 us -> 114 us (1.20)
  waiting for transfers between devices: 5.81 us -> 24.6 us
  local copies, waits for them, and re-layouts: 4.02 us -> 8.92 us
  Pallas kernels: 45.6 us -> 40.9 us
    ppermute x31 -> x1, starting transfers between devices: 32.6 us -> 1.51 us  [swap(): return lax.ppermute(array, axis, [(i, i ^ step) for i in range(size)])]
    all_to_all x0 -> x6, starting transfers between devices: none -> 30.3 us  [exchange(): return lax.all_to_all(array, 'ctx', 0, 0, tiled=True)]
    all_to_all x0 -> x6, waiting for transfers between devices: none -> 22.3 us  [exchange(): return lax.all_to_all(array, 'ctx', 0, 0, tiled=True)]
    pallas_call x7 -> x4, Pallas kernels: 22.8 us -> 18.2 us  [the longest x1 8.06 us: attention(): pl.pallas_call(functools.partial(attention_kernel, lanes, blocks, score_s...]
    unnamed x4 -> x12, local copies, waits for them, and re-layouts: 0.01 us -> 4.39 us
    ppermute x31 -> x1, waiting for transfers between devices: 5.81 us -> 2.27 us  [swap(): return lax.ppermute(array, axis, [(i, i ^ step) for i in range(size)])]
    broadcast_in_dim x0 -> x3, local copies, waits for them, and re-layouts: none -> 1.43 us  [gathered(): jnp.broadcast_to(array[None], (lax.axis_size('ctx'),) + array.shape)]
  transfers between devices with their start and end apart: 31 -> 7, of which waited for: 4 -> 5; matrix products, arithmetic and copies ran while one was open for 5% -> 5% of each run, Pallas kernels for 43% -> 31%
where the time goes in v2:
time: 114 us; the launch traced here: 113 us
  Pallas kernels  40.9 us (36%)
  starting transfers between devices  31.8 us (28%)
  waiting for transfers between devices  24.6 us (22%)
  local copies, waits for them, and re-layouts  8.92 us (8%)
  between operations  3.89 us (3%)
  other arithmetic  3 us (3%)
    all_to_all x6, starting transfers between devices, exchange(): return lax.all_to_all(array, 'ctx', 0, 0, tiled=True)  30.3 us
    pallas_call x4, Pallas kernels, sweep(): pl.pallas_call(functools.partial(sweep_kernel, panel), in_specs=[VMEM], o...  22.6 us
    all_to_all x6, waiting for transfers between devices, exchange(): return lax.all_to_all(array, 'ctx', 0, 0, tiled=True)  22.3 us
    pallas_call x1, Pallas kernels, attention(): pl.pallas_call(functools.partial(attention_kernel, lanes, blocks, score_s...  8.06 us
    pallas_call x1, Pallas kernels, fit(): pl.pallas_call(fit_kernel, in_specs=[VMEM] * 3, out_specs=[VMEM] * 2, out...  4.72 us
    pallas_call x1, Pallas kernels, gram_system(): pl.pallas_call(functools.partial(gram_kernel, score_scale), in_specs=[VME...  4.56 us
    unnamed x12, local copies, waits for them, and re-layouts  4.39 us
    gather x1, local copies, waits for them, and re-layouts, per_device(): jnp.take(keys[0], jnp.clip(local, 0, slab - 1), axis=0)  2.42 us
  transfers between devices with their start and end apart: 7, of which 5 were waited for; matrix products, arithmetic and copies ran while one was open for 5% of the time, Pallas kernels for 31%

profile of v2, /device:TPU:0, one launch (start us, length us, event | category | flops | bytes accessed | tf_op | source)
XLA Modules:
  0.0 113.0 jit_solution(9359039351951427968)
XLA Ops:
  0.6 0.0 copy-start
  0.6 0.0 copy-start.1
  0.7 7.5 %all-to-all-start = ((bf16[16,64,128]{2,1,0:T(8,128)(2,1)}), bf16[16,64,128]{2,1,0:T(8,128)(2,1)S(1)}, u32[]{:S(2)}, u32[]{:S(2)}) async-start(bf16[16,64,128]{2,1,0:T(8,128)(2,1)} %bitcast.24), calls=%async_computation | async-start | bytes 524288 | tf_op jit(solution)/shard_map/all_to_all | solution.py:35
  8.2 0.7 and_reduce_fusion
  8.9 0.7 compare_select_fusion.1
  9.6 0.7 clamp_reduce_fusion
  10.3 0.1 and.20
  10.4 0.1 min.16
  10.5 2.4 %gather_fusion = bf16[512,128]{1,0:T(8,128)(2,1)S(1)} fusion(bf16[4096,128]{1,0:T(8,128)(2,1)} %bitcast.17, s32[1024]{0:T(1024)S(1)} %pad_clamp_fusion), kind=kCustom, calls=%fused_computation | custom fusion | bytes 264192 | tf_op jit(solution)/shard_map/jit(_take)/gather | solution.py:279
  12.9 0.9 select_select_fusion
  13.8 4.5 %all-to-all-done = bf16[16,64,128]{2,1,0:T(8,128)(2,1)S(1)} async-done(((bf16[16,64,128]{2,1,0:T(8,128)(2,1)}), bf16[16,64,128]{2,1,0:T(8,128)(2,1)S(1)}, u32[]{:S(2)}, u32[]{:S(2)}) %all-to-all-start) | async-done | bytes 262176 | tf_op jit(solution)/shard_map/all_to_all | solution.py:35
  18.2 3.5 %all-to-all-start.3 = ((bf16[16,32,128]{2,1,0:T(8,128)(2,1)}), bf16[16,32,128]{2,1,0:T(8,128)(2,1)S(1)}, u32[]{:S(2)}, u32[]{:S(2)}) async-start(bf16[16,32,128]{2,1,0:T(8,128)(2,1)} %select_select_fusion), calls=%async_computation.3 | async-start | bytes 262144 | tf_op jit(solution)/shard_map/all_to_all | solution.py:35
  22.4 7.2 %all-to-all-done.3 = bf16[16,32,128]{2,1,0:T(8,128)(2,1)S(1)} async-done(((bf16[16,32,128]{2,1,0:T(8,128)(2,1)}), bf16[16,32,128]{2,1,0:T(8,128)(2,1)S(1)}, u32[]{:S(2)}, u32[]{:S(2)}) %all-to-all-start.3) | async-done | bytes 131104 | tf_op jit(solution)/shard_map/all_to_all | solution.py:35
  29.7 0.8 broadcast_in_dim.41
  30.4 3.5 %all-to-all-start.1 = ((bf16[16,64,128]{2,1,0:T(8,128)(2,1)}), bf16[16,64,128]{2,1,0:T(8,128)(2,1)S(1)}, u32[]{:S(2)}, u32[]{:S(2)}) async-start(bf16[16,64,128]{2,1,0:T(8,128)(2,1)} %broadcast_in_dim.41), calls=%async_computation.1 | async-start | bytes 524288 | tf_op jit(solution)/shard_map/all_to_all | solution.py:35
  34.0 10.0 %all-to-all-done.1 = bf16[16,64,128]{2,1,0:T(8,128)(2,1)S(1)} async-done(((bf16[16,64,128]{2,1,0:T(8,128)(2,1)}), bf16[16,64,128]{2,1,0:T(8,128)(2,1)S(1)}, u32[]{:S(2)}, u32[]{:S(2)}) %all-to-all-start.1) | async-done | bytes 262176 | tf_op jit(solution)/shard_map/all_to_all | solution.py:35
  44.0 0.7 broadcast_in_dim.46
  44.6 3.5 %all-to-all-start.4 = ((bf16[16,32,128]{2,1,0:T(8,128)(2,1)}), bf16[16,32,128]{2,1,0:T(8,128)(2,1)S(1)}, u32[]{:S(2)}, u32[]{:S(2)}) async-start(bf16[16,32,128]{2,1,0:T(8,128)(2,1)} %broadcast_in_dim.46), calls=%async_computation.4 | async-start | bytes 262144 | tf_op jit(solution)/shard_map/all_to_all | solution.py:35
  48.1 0.0 copy-done
  48.2 0.0 copy-done.1
  48.2 8.1 %attention.1 = f32[16,40,256]{2,1,0:T(8,128)} custom-call(bf16[1024,128]{1,0:T(8,128)(2,1)S(1)} %bitcast.19, bf16[4096,128]{1,0:T(8,128)(2,1)S(1)} %bitcast.18, bf16[4096,128]{1,0:T(8,128)(2,1)S(1)} %bitcast.22), custom_call_target="tpu_custom_call" | custom-call | flops 2147483648 | bytes 2097152 | tf_op jit(solution)/shard_map/attention/pallas_call | solution.py:103
  56.2 0.0 all-to-all-done.4
  56.2 6.1 %all-to-all-start.2 = ((f32[16,40,256]{2,1,0:T(8,128)}), f32[16,40,256]{2,1,0:T(8,128)S(1)}, u32[]{:S(2)}, u32[]{:S(2)}) async-start(f32[16,40,256]{2,1,0:T(8,128)} %attention.1), calls=%async_computation.2 | async-start | bytes 1310720 | tf_op jit(solution)/shard_map/all_to_all | solution.py:35
  62.4 4.6 %gram.1 = (f32[512,1024]{1,0:T(8,128)S(1)}, f32[512,512]{1,0:T(8,128)S(1)}) custom-call(bf16[1024,128]{1,0:T(8,128)(2,1)S(1)} %bitcast.20, bf16[512,128]{1,0:T(8,128)(2,1)S(1)} %bitcast.21), custom_call_target="tpu_custom_call" | custom-call | flops 3221225472 | bytes 1000000 | tf_op jit(solution)/shard_map/gram/pallas_call | solution.py:161
  66.9 5.7 %sweep.4.h_ref = f32[512,512]{1,0:T(8,128)S(1)} custom-call(f32[512,512]{1,0:T(8,128)S(1)} %get-tuple-element.8.h_ref), custom_call_target="tpu_custom_call" | custom-call | flops 5000000000 | bytes 1048576 | tf_op jit(solution)/shard_map/sweep/pallas_call | solution.py:222
  72.6 5.6 %sweep.5.h_ref = f32[512,512]{1,0:T(8,128)S(1)} custom-call(f32[512,512]{1,0:T(8,128)S(1)} %sweep.4.h_ref), custom_call_target="tpu_custom_call" | custom-call | flops 5000000000 | bytes 1048576 | tf_op jit(solution)/shard_map/sweep/pallas_call | solution.py:222
  78.2 0.0 copy-start.4
  78.2 1.0 copy-done.4
  79.2 0.0 all-to-all-done.2.part_ref
  79.2 0.9 merge.1
  80.1 6.0 %all-to-all-start.5 = ((f32[16,32,256]{2,1,0:T(8,128)}), f32[16,32,256]{2,1,0:T(8,128)S(1)}, u32[]{:S(2)}, u32[]{:S(2)}) async-start(f32[16,32,256]{2,1,0:T(8,128)} %merge.1), calls=%async_computation.5 | async-start | bytes 1048576 | tf_op jit(solution)/shard_map/all_to_all | solution.py:35
  86.2 0.0 copy-start.5
  86.2 1.2 %copy-done.5 = f32[512,512]{1,0:T(8,128)S(1)} copy-done((f32[512,512]{1,0:T(8,128)S(1)}, f32[512,512]{1,0:T(8,128)}, u32[]{:S(2)}) %copy-start.5) | copy-done | bytes 1048600
  87.4 5.7 %sweep.6.h_ref = f32[512,512]{1,0:T(8,128)S(1)} custom-call(f32[512,512]{1,0:T(8,128)S(1)} %copy-done.5), custom_call_target="tpu_custom_call" | custom-call | flops 5000000000 | bytes 1048576 | tf_op jit(solution)/shard_map/sweep/pallas_call | solution.py:222
  93.0 5.7 %sweep.7.minus_ref = f32[512,512]{1,0:T(8,128)S(1)} custom-call(f32[512,512]{1,0:T(8,128)S(1)} %sweep.6.h_ref), custom_call_target="tpu_custom_call" | custom-call | flops 5000000000 | bytes 1048576 | tf_op jit(solution)/shard_map/sweep/pallas_call | solution.py:222
  98.8 0.0 copy-start.2
  98.8 1.0 copy-done.2
  99.8 0.6 all-to-all-done.5.y_ref
  100.4 0.0 copy-start.3
  100.4 1.2 %copy-done.3 = f32[512,512]{1,0:T(8,128)S(1)} copy-done((f32[512,512]{1,0:T(8,128)S(1)}, f32[512,512]{1,0:T(8,128)}, u32[]{:S(2)}) %copy-start.3) | copy-done | bytes 1048600
  101.6 4.7 %fit.1 = (f32[512,128]{1,0:T(8,128)}, f32[8,128]{1,0:T(8,128)S(1)}) custom-call(f32[512,512]{1,0:T(8,128)S(1)} %copy-done.3, f32[512,1024]{1,0:T(8,128)S(1)} %get-tuple-element.10.at_ref, f32[16,32,256]{2,1,0:T(8,128)S(1)} %all-to-all-done.5.y_ref), custom_call_target="tpu_custom_call" | custom-call | flops 1610612736 | bytes 1000000 | tf_op jit(solution)/shard_map/fit/pallas_call | solution.py:252
  106.3 0.5 slice.3
  106.9 1.5 %collective-permute-start = (f32[]{:T(128)}, f32[]{:T(128)}, u32[]{:S(2)}, u32[]{:S(2)}) collective-permute-start(f32[]{:T(128)} %bitcast.11), channel_id=1, source_target_pairs={{0,16},{16,0},{1,17},{17,1},{2,18},{18,2},{3,19},{19,3},{4,20},{20... | collective-permute-start | bytes 20 | tf_op jit(solution)/shard_map/ppermute | solution.py:31
  108.4 2.3 %collective-permute-done = f32[]{:T(128)} collective-permute-done((f32[]{:T(128)}, f32[]{:T(128)}, u32[]{:S(2)}, u32[]{:S(2)}) %collective-permute-start) | collective-permute-done | bytes 36 | tf_op jit(solution)/shard_map/ppermute | solution.py:31
  (4 shorter events, 0.0 us)
Async XLA Ops:
  0.6 47.5 %copy-start = (bf16[1,4096,128]{2,1,0:T(8,128)(2,1)S(1)}, bf16[1,4096,128]{2,1,0:T(8,128)(2,1)}, u32[]{:S(2)}) copy-start(bf16[1,4096,128]{2,1,0:T(8,128)(2,1)} %param.6) | copy-start | bytes 3145732
  0.6 47.5 %copy-start.1 = (bf16[1,4096,128]{2,1,0:T(8,128)(2,1)S(1)}, bf16[1,4096,128]{2,1,0:T(8,128)(2,1)}, u32[]{:S(2)}) copy-start(bf16[1,4096,128]{2,1,0:T(8,128)(2,1)} %param.7) | copy-start | bytes 3145732
  0.7 17.6 %all-to-all-start = ((bf16[16,64,128]{2,1,0:T(8,128)(2,1)}), bf16[16,64,128]{2,1,0:T(8,128)(2,1)S(1)}, u32[]{:S(2)}, u32[]{:S(2)}) async-start(bf16[16,64,128]{2,1,0:T(8,128)(2,1)} %bitcast.24), calls=%async_computation | async-start | bytes 524288 | tf_op jit(solution)/shard_map/all_to_all | solution.py:35
  18.2 11.4 %all-to-all-start.3 = ((bf16[16,32,128]{2,1,0:T(8,128)(2,1)}), bf16[16,32,128]{2,1,0:T(8,128)(2,1)S(1)}, u32[]{:S(2)}, u32[]{:S(2)}) async-start(bf16[16,32,128]{2,1,0:T(8,128)(2,1)} %select_select_fusion), calls=%async_computation.3 | async-start | bytes 262144 | tf_op jit(solution)/shard_map/all_to_all | solution.py:35
  30.4 13.5 %all-to-all-start.1 = ((bf16[16,64,128]{2,1,0:T(8,128)(2,1)}), bf16[16,64,128]{2,1,0:T(8,128)(2,1)S(1)}, u32[]{:S(2)}, u32[]{:S(2)}) async-start(bf16[16,64,128]{2,1,0:T(8,128)(2,1)} %broadcast_in_dim.41), calls=%async_computation.1 | async-start | bytes 524288 | tf_op jit(solution)/shard_map/all_to_all | solution.py:35
  44.6 11.6 %all-to-all-start.4 = ((bf16[16,32,128]{2,1,0:T(8,128)(2,1)}), bf16[16,32,128]{2,1,0:T(8,128)(2,1)S(1)}, u32[]{:S(2)}, u32[]{:S(2)}) async-start(bf16[16,32,128]{2,1,0:T(8,128)(2,1)} %broadcast_in_dim.46), calls=%async_computation.4 | async-start | bytes 262144 | tf_op jit(solution)/shard_map/all_to_all | solution.py:35
  56.2 22.9 %all-to-all-start.2 = ((f32[16,40,256]{2,1,0:T(8,128)}), f32[16,40,256]{2,1,0:T(8,128)S(1)}, u32[]{:S(2)}, u32[]{:S(2)}) async-start(f32[16,40,256]{2,1,0:T(8,128)} %attention.1), calls=%async_computation.2 | async-start | bytes 1310720 | tf_op jit(solution)/shard_map/all_to_all | solution.py:35
  78.2 1.0 copy-start.4
  80.1 20.3 %all-to-all-start.5 = ((f32[16,32,256]{2,1,0:T(8,128)}), f32[16,32,256]{2,1,0:T(8,128)S(1)}, u32[]{:S(2)}, u32[]{:S(2)}) async-start(f32[16,32,256]{2,1,0:T(8,128)} %merge.1), calls=%async_computation.5 | async-start | bytes 1048576 | tf_op jit(solution)/shard_map/all_to_all | solution.py:35
  86.2 1.2 %copy-start.5 = (f32[512,512]{1,0:T(8,128)S(1)}, f32[512,512]{1,0:T(8,128)}, u32[]{:S(2)}) copy-start(f32[512,512]{1,0:T(8,128)} %copy-done.4) | copy-start | bytes 3145732
  98.8 1.0 copy-start.2
  100.4 1.2 %copy-start.3 = (f32[512,512]{1,0:T(8,128)S(1)}, f32[512,512]{1,0:T(8,128)}, u32[]{:S(2)}) copy-start(f32[512,512]{1,0:T(8,128)} %copy-done.2) | copy-start | bytes 3145732
  106.9 3.8 %collective-permute-start = (f32[]{:T(128)}, f32[]{:T(128)}, u32[]{:S(2)}, u32[]{:S(2)}) collective-permute-start(f32[]{:T(128)} %bitcast.11), channel_id=1, source_target_pairs={{0,16},{16,0},{1,17},{17,1},{2,18},{18,2},{3,19},{19,3},{4,20},{20... | collective-permute-start | bytes 20 | tf_op jit(solution)/shard_map/ppermute | solution.py:31

commit v3 on v2

v3 whole, which is shorter than its diff:
```python
import functools
import math

import jax
import jax.numpy as jnp
from jax import lax
from jax.experimental import pallas as pl
from jax.experimental.pallas import tpu as pltpu
from jax.sharding import PartitionSpec as P

KBLK = 1024
PANEL = 128
SUB = 8
RIDGE_SHARE = 0.01
F32 = jnp.float32
BF16 = jnp.bfloat16
HIGH = lax.Precision.HIGHEST
VMEM_LIMIT = 48 * 1024 * 1024
VMEM = pl.BlockSpec(memory_space=pltpu.VMEM)
SMEM = pl.BlockSpec(memory_space=pltpu.SMEM)
NT = (((1,), (1,)), ((), ()))
TN = (((0,), (0,)), ((), ()))
NN = (((1,), (0,)), ((), ()))


def swap(array, axis, step):
    size = lax.axis_size(axis)
    return lax.ppermute(array, axis, [(i, i ^ step) for i in range(size)])


def call(kernel, ins, outs, cost=0, scratch=(), name=None):
    shapes = [jax.ShapeDtypeStruct(shape, kind) for shape, kind in outs]
    return pl.pallas_call(
        kernel,
        in_specs=[SMEM] + [VMEM] * (len(ins) - 1),
        out_specs=[VMEM] * len(outs),
        out_shape=shapes,
        scratch_shapes=list(scratch),
        compiler_params=pltpu.CompilerParams(vmem_limit_bytes=VMEM_LIMIT),
        cost_estimate=pl.CostEstimate(flops=cost, bytes_accessed=10**5, transcendentals=0),
        name=name,
    )(*ins)


def aligned(value, unit):
    return pl.ds(pl.multiple_of(value * unit, unit), unit)


def prepare_kernel(window, place_ref, q_ref, kept_ref, k_ref, keep_ref, send_ref, spots, picked):
    slab, dims = k_ref.shape
    kept = kept_ref.shape[1]
    base = place_ref[3]
    positions = kept_ref[...]
    before = jnp.sum((positions < base).astype(jnp.int32))
    start = jnp.minimum(before // 16, (kept - window) // 16)
    local = (positions - base).astype(F32)
    for i in range(0, kept, 128):
        spots[i : i + 128, :] = jnp.broadcast_to(local[:, i : i + 128], (128, 128)).T
    mine = spots[pl.ds(pl.multiple_of(start * 16, 16), window), :]
    column = lax.broadcasted_iota(jnp.int32, (window, 128), 1).astype(F32)
    onehot = jnp.concatenate(
        [jnp.where(mine == column + float(i), 1.0, 0.0).astype(BF16) for i in range(0, slab, 128)], axis=1
    )
    rows = lax.dot_general(onehot, k_ref[...], NN, preferred_element_type=F32)
    picked[...] = jnp.zeros_like(picked)
    picked[pl.ds(pl.multiple_of(start * 16, 16), window), :] = rows.astype(BF16)
    share, part = q_ref.shape[0] // 4, kept // 4
    is_root = place_ref[2] == 1
    for out, core in ((keep_ref, place_ref[0]), (send_ref, 1 - place_ref[0])):
        for y in range(2):
            q = q_ref[aligned(2 * y + core, share), :]
            out[y, :share, :] = jnp.where(is_root, q, jnp.zeros_like(q))
            out[y, share:, :] = picked[aligned(2 * y + core, part), :]


def split_add_kernel(place_ref, a_ref, b_ref, keep_ref, send_ref):
    y = place_ref[1]
    keep_ref[...] = a_ref[y] + b_ref[y]
    send_ref[...] = a_ref[1 - y] + b_ref[1 - y]


def add_kernel(place_ref, a_ref, b_ref, out_ref):
    out_ref[...] = a_ref[...] + b_ref[...]


def pair_kernel(place_ref, a_ref, b_ref, out_ref):
    y = place_ref[1]
    out_ref[y] = a_ref[...]
    out_ref[1 - y] = b_ref[...]


def arrange_kernel(place_ref, a_ref, b_ref, q_ref, c_ref):
    share, part = q_ref.shape[0] // 4, c_ref.shape[0] // 4
    for ref, core in ((a_ref, place_ref[0]), (b_ref, 1 - place_ref[0])):
        for y in range(2):
            q_ref[aligned(2 * y + core, share), :] = ref[y, :share, :]
            c_ref[aligned(2 * y + core, part), :] = ref[y, share:, :]


def spread(place, queries, kept, keys):
    rows, dims = queries.shape
    count = kept.shape[1]
    window = 4 * count // lax.axis_size("ctx") + 16
    tall = (rows + count) // 4
    half, quarter = ((2, tall, dims), BF16), ((tall, dims), BF16)
    keep, send = call(
        functools.partial(prepare_kernel, window),
        (place, queries, kept, keys),
        [half, half],
        scratch=[pltpu.VMEM((count, 128), F32), pltpu.VMEM((count, dims), BF16)],
        name="prepare",
    )
    keep, send = call(split_add_kernel, (place, keep, swap(send, "ctx", 1)), [quarter] * 2, name="split")
    (share,) = call(add_kernel, (place, keep, swap(send, "ctx", 2)), [quarter], name="join")
    step = lax.axis_size("ctx") // 2
    while step >= 4:
        (share,) = call(add_kernel, (place, share, swap(share, "ctx", step)), [quarter], name="join")
        step //= 2
    (share,) = call(pair_kernel, (place, share, swap(share, "ctx", 2)), [half], name="pair")
    return call(
        arrange_kernel,
        (place, share, swap(share, "ctx", 1)),
        [((rows, dims), BF16), ((count, dims), BF16)],
        name="arrange",
    )


def attention_kernel(lanes, blocks, score_scale, place_ref, q_ref, k_ref, v_ref, keep_ref, send_ref, vt_ref, acc_ref, top_ref, sum_ref):
    step = pl.program_id(0)
    dims = v_ref.shape[1]
    keys = k_ref.shape[0] // blocks
    chunks = q_ref.shape[0] // lanes
    factor = score_scale * math.log2(math.e)
    vt_ref[:dims, :] = v_ref[...].T
    vt_ref[dims:, :] = jnp.ones((vt_ref.shape[0] - dims, v_ref.shape[0]), BF16)

    @pl.when(step == 0)
    def _():
        acc_ref[...] = jnp.zeros_like(acc_ref)
        sum_ref[...] = jnp.zeros_like(sum_ref)
        top_ref[...] = jnp.full(top_ref.shape, -jnp.inf, F32)

    def scores(b, c):
        return lax.dot_general(
            k_ref[b * keys : (b + 1) * keys, :],
            q_ref[c * lanes : (c + 1) * lanes, :],
            NT,
            preferred_element_type=F32,
        )

    stages = [(b, c) for b in range(blocks) for c in range(chunks)]
    ahead = scores(*stages[0])
    for n, (b, c) in enumerate(stages):
        s = ahead
        if n + 1 < len(stages):
            ahead = scores(*stages[n + 1])
        at = slice(c * lanes, (c + 1) * lanes)
        top = jnp.max(s, axis=0, keepdims=True)
        e = jnp.exp2((s - top) * factor).astype(BF16)
        out = lax.dot_general(vt_ref[:, b * keys : (b + 1) * keys], e, NN, preferred_element_type=F32)
        top = top * factor
        old_top = top_ref[:, at]
        joint = jnp.maximum(old_top, top)
        old_scale = jnp.exp2(old_top - joint)
        new_scale = jnp.exp2(top - joint)
        acc_ref[:, at] = acc_ref[:, at] * old_scale + out[:dims, :] * new_scale
        sum_ref[:, at] = sum_ref[:, at] * old_scale + out[dims : dims + 1, :] * new_scale
        top_ref[:, at] = joint

    @pl.when(step == pl.num_programs(0) - 1)
    def _():
        for out, core in ((keep_ref, place_ref[0]), (send_ref, 1 - place_ref[0])):
            for y in range(2):
                at, to = aligned(2 * y + core, lanes), slice(y * lanes, (y + 1) * lanes)
                out[:dims, to] = acc_ref[:, at]
                out[dims:, to] = jnp.concatenate(
                    [top_ref[:, at], sum_ref[:, at], jnp.zeros((SUB - 2, lanes), F32)], axis=0
                )


def attention(place, queries, keys, values, score_scale):
    rows, dims = queries.shape
    slab = keys.shape[0]
    block = min(KBLK, slab)
    blocks = 2 if slab % (2 * block) == 0 else 1
    lanes = rows // 4
    shape = (dims + SUB, rows // 2)
    return pl.pallas_call(
        functools.partial(attention_kernel, lanes, blocks, score_scale),
        grid=(slab // (block * blocks),),
        in_specs=[SMEM, pl.BlockSpec((rows, dims), lambda b: (0, 0))]
        + [pl.BlockSpec((block * blocks, dims), lambda b: (b, 0))] * 2,
        out_specs=[pl.BlockSpec(shape, lambda b: (0, 0))] * 2,
        out_shape=[jax.ShapeDtypeStruct(shape, F32)] * 2,
        scratch_shapes=[
            pltpu.VMEM((dims + 16, block * blocks), BF16),
            pltpu.VMEM((dims, rows), F32),
            pltpu.VMEM((1, rows), F32),
            pltpu.VMEM((1, rows), F32),
        ],
        compiler_params=pltpu.CompilerParams(vmem_limit_bytes=VMEM_LIMIT),
        cost_estimate=pl.CostEstimate(
            flops=4 * rows * slab * dims, bytes_accessed=4 * slab * dims, transcendentals=rows * slab
        ),
        name="attention",
    )(place, queries, keys, values)


def merged(a_ref, b_ref):
    dims = a_ref.shape[0] - SUB
    a_top, b_top = a_ref[dims : dims + 1, :], b_ref[dims : dims + 1, :]
    top = jnp.maximum(a_top, b_top)
    a_scale, b_scale = jnp.exp2(a_top - top), jnp.exp2(b_top - top)
    total = a_ref[dims + 1 : dims + 2, :] * a_scale + b_ref[dims + 1 : dims + 2, :] * b_scale
    out = a_ref[:dims, :] * a_scale + b_ref[:dims, :] * b_scale
    return out, top, total


def tail(top, total):
    return jnp.concatenate([top, total, jnp.zeros((SUB - 2, top.shape[1]), F32)], axis=0)


def merge_lanes_kernel(place_ref, a_ref, b_ref, keep_ref, send_ref, work):
    out, top, total = merged(a_ref, b_ref)
    dims, lanes = out.shape[0], keep_ref.shape[1]
    work[:dims, :] = out
    work[dims:, :] = tail(top, total)
    y = place_ref[1]
    keep_ref[...] = work[:, aligned(y, lanes)]
    send_ref[...] = work[:, aligned(1 - y, lanes)]


def merge_rows_kernel(step, place_ref, a_ref, b_ref, keep_ref, send_ref, work):
    out, top, total = merged(a_ref, b_ref)
    rows = keep_ref.shape[0] - SUB
    work[...] = out
    bit = (place_ref[4] // step) % 2
    for ref, which in ((keep_ref, bit), (send_ref, 1 - bit)):
        ref[:rows, :] = work[aligned(which, rows), :]
        ref[rows:, :] = tail(top, total)


def finish_kernel(place_ref, a_ref, b_ref, out_ref):
    out, _, total = merged(a_ref, b_ref)
    out_ref[...] = out / total


def stack_rows_kernel(step, place_ref, a_ref, b_ref, out_ref):
    rows = a_ref.shape[0]
    bit = (place_ref[4] // step) % 2
    out_ref[aligned(bit, rows), :] = a_ref[...]
    out_ref[aligned(1 - bit, rows), :] = b_ref[...]


def stack_lanes_kernel(place_ref, a_ref, b_ref, out_ref):
    lanes = a_ref.shape[1]
    y = place_ref[1]
    out_ref[:, aligned(y, lanes)] = a_ref[...]
    out_ref[:, aligned(1 - y, lanes)] = b_ref[...]


def target_rounds(place, keep, send):
    dims, lanes = keep.shape[0] - SUB, keep.shape[1] // 2
    came = yield swap(send, "ctx", 1)
    shape = ((dims + SUB, lanes), F32)
    keep, send = call(
        merge_lanes_kernel, (place, keep, came), [shape] * 2, scratch=[pltpu.VMEM((dims + SUB, 2 * lanes), F32)], name="merge"
    )
    came = yield swap(send, "ctx", 2)
    step, rows = lax.axis_size("ctx") // 2, dims
    while step >= 4:
        shape = ((rows // 2 + SUB, lanes), F32)
        kernel = functools.partial(merge_rows_kernel, step)
        keep, send = call(kernel, (place, keep, came), [shape] * 2, scratch=[pltpu.VMEM((rows, lanes), F32)], name="merge")
        came = yield swap(send, "ctx", step)
        rows //= 2
        step //= 2
    (block,) = call(finish_kernel, (place, keep, came), [((rows, lanes), F32)], name="finish")
    step = 4
    while step < lax.axis_size("ctx"):
        came = yield swap(block, "ctx", step)
        rows *= 2
        (block,) = call(functools.partial(stack_rows_kernel, step), (place, block, came), [((rows, lanes), F32)], name="stack")
        step *= 2
    came = yield swap(block, "ctx", 2)
    (block,) = call(stack_lanes_kernel, (place, block, came), [((dims, 2 * lanes), F32)], name="stack")
    came = yield swap(block, "ctx", 1)
    return block, came


def attend_kernel(score_scale, place_ref, q_ref, c_ref, at_ref):
    scores = lax.dot_general(c_ref[...], q_ref[...], NT, preferred_element_type=F32) * score_scale
    weights = jnp.exp(scores - jnp.max(scores, axis=0, keepdims=True))
    at_ref[...] = weights / jnp.sum(weights, axis=0, keepdims=True)


def gram_kernel(place_ref, at_ref, h_ref):
    gram = lax.dot_general(at_ref[...], at_ref[...], NT, precision=HIGH, preferred_element_type=F32)
    kept = gram.shape[0]
    diagonal = lax.broadcasted_iota(jnp.int32, gram.shape, 0) == lax.broadcasted_iota(jnp.int32, gram.shape, 1)
    trace = jnp.sum(jnp.where(diagonal, gram, 0.0))
    h_ref[...] = gram + jnp.where(diagonal, RIDGE_SHARE * trace / kept, 0.0)


def invert_block(rows):
    count = len(rows)
    size = count * SUB
    lane = lax.broadcasted_iota(jnp.int32, (SUB, size), 1)
    sub = lax.broadcasted_iota(jnp.int32, (SUB, size), 0)
    spread = lambda array, column: jnp.broadcast_to(array[:, column : column + 1], (SUB, size))
    line = lambda array, row: jnp.broadcast_to(array[row : row + 1, :], (SUB, size))
    for k in range(count):
        base = k * SUB
        inside = (lane >= base) & (lane < base + SUB)
        columns = [spread(rows[k], base + j) for j in range(SUB)]
        work = jnp.where(inside, jnp.where(lane - base == sub, 1.0, 0.0), rows[k])
        for j in range(SUB):
            here = sub == j
            inverse = 1.0 / line(columns[j], j)
            step = lambda v: (lambda t: jnp.where(here, t, v - columns[j] * t))(line(v, j) * inverse)
            for i in range(j + 1, SUB):
                columns[i] = step(columns[i])
            work = step(work)
        lines = [line(work, j) for j in range(SUB)]
        updated = []
        for i in range(count):
            if i == k:
                updated.append(work)
                continue
            fresh = jnp.where(inside, 0.0, rows[i])
            for j in range(SUB):
                fresh = fresh - spread(rows[i], base + j) * lines[j]
            updated.append(fresh)
        rows = updated
    return rows


def invert_kernel(panel, place_ref, h_ref, out_ref):
    at = slice(panel * PANEL, (panel + 1) * PANEL)
    block = h_ref[at, at]
    out_ref[...] = jnp.concatenate(
        invert_block([block[i * SUB : (i + 1) * SUB, :] for i in range(PANEL // SUB)]), axis=0
    )


def update_kernel(panel, place_ref, h_ref, inverse_ref, out_ref):
    at = slice(panel * PANEL, (panel + 1) * PANEL)
    across = h_ref[at, :]
    turned = lax.dot_general(inverse_ref[...], across, NN, precision=HIGH, preferred_element_type=F32)
    out_ref[...] = h_ref[...] - lax.dot_general(across, turned, TN, precision=HIGH, preferred_element_type=F32)
    out_ref[:, at] = turned.T
    out_ref[at, :] = turned
    out_ref[at, at] = -inverse_ref[...]


def fit_kernel(place_ref, minus_ref, at_ref, own_ref, other_ref, x_ref, err_ref, yt):
    lanes = own_ref.shape[1] // 2
    for ref, core in ((own_ref, place_ref[0]), (other_ref, 1 - place_ref[0])):
        for y in range(2):
            yt[:, aligned(2 * y + core, lanes)] = ref[:, y * lanes : (y + 1) * lanes]
    target = yt[...]
    attend = at_ref[...]
    cross = lax.dot_general(target, attend, NT, precision=HIGH, preferred_element_type=F32)
    fitted = -lax.dot_general(cross, minus_ref[...], NN, precision=HIGH, preferred_element_type=F32)
    x_ref[...] = fitted.T
    misfit = lax.dot_general(fitted, attend, NN, precision=HIGH, preferred_element_type=F32) - target
    error = jnp.sum(misfit * misfit) / jnp.sum(target * target)
    err_ref[...] = jnp.full(err_ref.shape, error, F32)


def per_device(queries, keys, values, kept, roots):
    rows, dims = queries.shape[2:]
    count = kept.shape[1]
    score_scale = 1.0 / math.sqrt(dims)
    shard = lax.axis_index("ctx")
    place = jnp.stack(
        [shard % 2, shard // 2 % 2, (shard == roots[0]).astype(shard.dtype), shard * keys.shape[1], shard]
    ).astype(jnp.int32)

    reference, kept_keys = spread(place, queries[0, 0], kept, keys[0])
    rounds = target_rounds(place, *attention(place, reference, keys[0], values[0], score_scale))
    came = next(rounds)
    ends = None

    def beside(arrays):
        nonlocal came, ends
        if ends is None:
            arrays, came = lax.optimization_barrier((arrays, came))
            try:
                came = rounds.send(came)
            except StopIteration as stop:
                ends = stop.value
        return arrays

    system_shape = ((count, count), F32)
    (attend,) = call(
        functools.partial(attend_kernel, score_scale), (place, reference, kept_keys), [((count, rows), F32)], 10**9, name="attend"
    )
    attend = beside(attend)
    (system,) = call(gram_kernel, (place, attend), [system_shape], 4 * 10**9, name="gram")
    system = beside(system)
    for panel in range(count // PANEL):
        (inverse,) = call(
            functools.partial(invert_kernel, panel), (place, system), [((PANEL, PANEL), F32)], 5 * 10**9, name="invert"
        )
        inverse = beside(inverse)
        (system,) = call(
            functools.partial(update_kernel, panel), (place, system, inverse), [system_shape], 2 * 10**9, name="update"
        )
        if panel == 0 or panel == count // PANEL - 1:
            system = beside(system)
    while ends is None:
        system = beside(system)

    compact, error = call(
        fit_kernel,
        (place, system, attend, *ends),
        [((count, dims), F32), ((SUB, 128), F32)],
        10**9,
        scratch=[pltpu.VMEM((dims, rows), F32)],
        name="fit",
    )
    heads = lax.axis_size("head")
    step = 1
    while step < heads:
        error = error + swap(error, "head", step)
        step *= 2
    return (compact[None], error[0, 0] / heads)


def solution(mesh):
    placed = (
        P("head", "ctx", None, None),
        P("head", "ctx", None),
        P("head", "ctx", None),
        P("head", None),
        P("head"),
    )
    return jax.shard_map(
        per_device,
        mesh=mesh,
        in_specs=placed,
        out_specs=(P("head", None, None), P()),
        check_vma=False,
    )
```

time: 114 us -> 102 us (0.89)
  Pallas kernels: 40.9 us -> 54.1 us
  starting transfers between devices: 31.8 us -> 20.6 us
  local copies, waits for them, and re-layouts: 8.92 us -> 3.46 us
  waiting for transfers between devices: 24.6 us -> 19.9 us
  other arithmetic: 3 us -> 0.01 us
    all_to_all x6 -> x0, starting transfers between devices: 30.3 us -> none  [exchange(): return lax.all_to_all(array, 'ctx', 0, 0, tiled=True)]
    all_to_all x6 -> x0, waiting for transfers between devices: 22.3 us -> none  [exchange(): return lax.all_to_all(array, 'ctx', 0, 0, tiled=True)]
    ppermute x1 -> x15, starting transfers between devices: 1.51 us -> 20.6 us  [swap(): return lax.ppermute(array, axis, [(i, i ^ step) for i in range(size)])]
    ppermute x1 -> x15, waiting for transfers between devices: 2.27 us -> 19.9 us  [swap(): return lax.ppermute(array, axis, [(i, i ^ step) for i in range(size)])]
    pallas_call x7 -> x25, Pallas kernels: 32.8 us -> 46.1 us  [call(): pl.pallas_call(kernel, in_specs=[SMEM] + [VMEM] * (len(ins) - 1), out_spe...]
    gather x1 -> x0, local copies, waits for them, and re-layouts: 2.42 us -> none  [per_device(): jnp.take(keys[0], jnp.clip(local, 0, slab - 1), axis=0)]
    select_n x2 -> x0, other arithmetic: 1.55 us -> none  [the longest x1 0.86 us: per_device(): jnp.where(held[:, None], jnp.take(keys[0], jnp.clip(local, 0, slab - 1),...]
    unnamed x12 -> x10, local copies, waits for them, and re-layouts: 4.39 us -> 2.86 us
  transfers between devices with their start and end apart: 7 -> 15, of which waited for: 5 -> 9; matrix products, arithmetic and copies ran while one was open for 5% -> 0% of each run, Pallas kernels for 31% -> 28%
where the time goes in v3:
time: 102 us; the launch traced here: 101 us
  Pallas kernels  54.1 us (53%)
  starting transfers between devices  20.6 us (20%)
  waiting for transfers between devices  19.9 us (20%)
  local copies, waits for them, and re-layouts  3.46 us (3%)
  between operations  3.35 us (3%)
    pallas_call x25, Pallas kernels, call(): pl.pallas_call(kernel, in_specs=[SMEM] + [VMEM] * (len(ins) - 1), out_spe...  46.1 us
    ppermute x15, starting transfers between devices, swap(): return lax.ppermute(array, axis, [(i, i ^ step) for i in range(size)])  20.6 us
    ppermute x15, waiting for transfers between devices, swap(): return lax.ppermute(array, axis, [(i, i ^ step) for i in range(size)])  19.9 us
    pallas_call x1, Pallas kernels, attention(): pl.pallas_call(functools.partial(attention_kernel, lanes, blocks, score_s...  8 us
    unnamed x10, local copies, waits for them, and re-layouts  2.86 us
  transfers between devices with their start and end apart: 15, of which 9 were waited for; matrix products, arithmetic and copies ran while one was open for 0% of the time, Pallas kernels for 28%

profile of v3, /device:TPU:0, one launch (start us, length us, event | category | flops | bytes accessed | tf_op | source)
XLA Modules:
  0.0 101.5 jit_solution(4860724105672989688)
XLA Ops:
  1.4 1.2 %copy-done = bf16[1,4096,128]{2,1,0:T(8,128)(2,1)S(1)} copy-done((bf16[1,4096,128]{2,1,0:T(8,128)(2,1)S(1)}, bf16[1,4096,128]{2,1,0:T(8,128)(2,1)}, u32[]{:S(2)}) %copy-start) | copy-done | bytes 1048600
  2.6 0.9 copy-done.2
  3.6 0.7 copy-done.3
  4.3 1.2 %prepare.1 = (bf16[2,384,128]{2,1,0:T(8,128)(2,1)S(1)}, bf16[2,384,128]{2,1,0:T(8,128)(2,1)S(1)}) custom-call(s32[5]{0:T(128)S(1)} %stack.30.place_ref, bf16[1024,128]{1,0:T(8,128)(2,1)S(1)} %bitcast.14, s32[1,512]{1,0:T(1,128)S(1)} %copy-done.3, bf16[4096,128]{1,0:T(8,128)(2,1)S(1)} %bitcast.12), custom_call_target="tpu_custom_call" | custom-call | bytes 100000 | tf_op jit(solution)/shard_map/prepare/pallas_call | solution.py:33
  5.4 0.5 collective-permute-start
  6.0 1.1 %collective-permute-done.b_ref = bf16[2,384,128]{2,1,0:T(8,128)(2,1)S(1)} collective-permute-done((bf16[2,384,128]{2,1,0:T(8,128)(2,1)S(1)}, bf16[2,384,128]{2,1,0:T(8,128)(2,1)S(1)}, u32[]{:S(2)}, u32[]{:S(2)}) %collective-permute-start) | collective-permute-done | bytes 196640 | tf_op jit(solution)/shard_map/ppermute | solution.py:28
  7.0 0.6 split.1
  7.6 2.9 %collective-permute-start.1 = (bf16[384,128]{1,0:T(8,128)(2,1)S(1)}, bf16[384,128]{1,0:T(8,128)(2,1)S(1)}, u32[]{:S(2)}, u32[]{:S(2)}) collective-permute-start(bf16[384,128]{1,0:T(8,128)(2,1)S(1)} %get-tuple-element.37), channel_id=1, source_target_pairs={{0,2},{1,3},{2,0},{3,1},{4,6},{5,7},{6,4},{7,5},{8,10},{9,11},{10,... | collective-permute-start | bytes 294920 | tf_op jit(solution)/shard_map/ppermute | solution.py:28
  10.6 3.1 %collective-permute-done.1.b_ref = bf16[384,128]{1,0:T(8,128)(2,1)S(1)} collective-permute-done((bf16[384,128]{1,0:T(8,128)(2,1)S(1)}, bf16[384,128]{1,0:T(8,128)(2,1)S(1)}, u32[]{:S(2)}, u32[]{:S(2)}) %collective-permute-start.1) | collective-permute-done | bytes 98336 | tf_op jit(solution)/shard_map/ppermute | solution.py:28
  13.7 0.6 join.3.a_ref
  14.2 2.9 %collective-permute-start.2 = (bf16[384,128]{1,0:T(8,128)(2,1)S(1)}, bf16[384,128]{1,0:T(8,128)(2,1)S(1)}, u32[]{:S(2)}, u32[]{:S(2)}) collective-permute-start(bf16[384,128]{1,0:T(8,128)(2,1)S(1)} %join.3.a_ref), channel_id=1, source_target_pairs={{0,8},{1,9},{2,10},{3,11},{4,12},{5,13},{6,14},{7,15},{8,0},{9,1},... | collective-permute-start | bytes 294920 | tf_op jit(solution)/shard_map/ppermute | solution.py:28
  17.1 4.5 %collective-permute-done.2.b_ref = bf16[384,128]{1,0:T(8,128)(2,1)S(1)} collective-permute-done((bf16[384,128]{1,0:T(8,128)(2,1)S(1)}, bf16[384,128]{1,0:T(8,128)(2,1)S(1)}, u32[]{:S(2)}, u32[]{:S(2)}) %collective-permute-start.2) | collective-permute-done | bytes 98336 | tf_op jit(solution)/shard_map/ppermute | solution.py:28
  21.6 0.6 join.4.a_ref
  22.2 0.6 collective-permute-start.3
  22.9 4.0 %collective-permute-done.3.b_ref = bf16[384,128]{1,0:T(8,128)(2,1)S(1)} collective-permute-done((bf16[384,128]{1,0:T(8,128)(2,1)S(1)}, bf16[384,128]{1,0:T(8,128)(2,1)S(1)}, u32[]{:S(2)}, u32[]{:S(2)}) %collective-permute-start.3) | collective-permute-done | bytes 98336 | tf_op jit(solution)/shard_map/ppermute | solution.py:28
  26.9 0.6 join.5.a_ref
  27.5 1.5 %collective-permute-start.4 = (bf16[384,128]{1,0:T(8,128)(2,1)S(1)}, bf16[384,128]{1,0:T(8,128)(2,1)S(1)}, u32[]{:S(2)}, u32[]{:S(2)}) collective-permute-start(bf16[384,128]{1,0:T(8,128)(2,1)S(1)} %join.5.a_ref), channel_id=1, source_target_pairs={{0,2},{1,3},{2,0},{3,1},{4,6},{5,7},{6,4},{7,5},{8,10},{9,11},{10,... | collective-permute-start | bytes 294920 | tf_op jit(solution)/shard_map/ppermute | solution.py:28
  29.0 3.2 %collective-permute-done.4.b_ref = bf16[384,128]{1,0:T(8,128)(2,1)S(1)} collective-permute-done((bf16[384,128]{1,0:T(8,128)(2,1)S(1)}, bf16[384,128]{1,0:T(8,128)(2,1)S(1)}, u32[]{:S(2)}, u32[]{:S(2)}) %collective-permute-start.4) | collective-permute-done | bytes 98336 | tf_op jit(solution)/shard_map/ppermute | solution.py:28
  32.2 0.6 pair.1.a_ref
  32.8 1.4 %collective-permute-done.5.b_ref = bf16[2,384,128]{2,1,0:T(8,128)(2,1)S(1)} collective-permute-done((bf16[2,384,128]{2,1,0:T(8,128)(2,1)S(1)}, bf16[2,384,128]{2,1,0:T(8,128)(2,1)S(1)}, u32[]{:S(2)}, u32[]{:S(2)}) %collective-permute-start.5) | collective-permute-done | bytes 196640 | tf_op jit(solution)/shard_map/ppermute | solution.py:28
  34.2 0.6 arrange.1
  34.8 8.0 %attention.1 = (f32[136,512]{1,0:T(8,128)S(1)}, f32[136,512]{1,0:T(8,128)S(1)}) custom-call(s32[5]{0:T(128)S(1)} %stack.30.place_ref, bf16[1024,128]{1,0:T(8,128)(2,1)S(1)} %get-tuple-element.38.q_ref, bf16[4096,128]{1,0:T(8,128)(2,1)S(1)} %bitcast.13, bf16[4096,128]{1,0:T(8,128)(2,1)S(1)} %bitcast.15), custom_call_target="tpu_custom_call" | custom-call | flops 2147483648 | bytes 2097152 | tf_op jit(solution)/shard_map/attention/pallas_call | solution.py:188
  43.0 1.6 %attend.1.at_ref = f32[512,1024]{1,0:T(8,128)S(1)} custom-call(s32[5]{0:T(128)S(1)} %stack.30.place_ref, bf16[1024,128]{1,0:T(8,128)(2,1)S(1)} %get-tuple-element.38.q_ref, bf16[512,128]{1,0:T(8,128)(2,1)S(1)} %get-tuple-element.39.c_ref), custom_call_target="tpu_custom_call" | custom-call | flops 1000000000 | bytes 100000 | tf_op jit(solution)/shard_map/attend/pallas_call | solution.py:33
  44.7 0.6 merge.3
  45.3 1.5 %collective-permute-start.7 = (f32[136,256]{1,0:T(8,128)S(1)}, f32[136,256]{1,0:T(8,128)S(1)}, u32[]{:S(2)}, u32[]{:S(2)}) collective-permute-start(f32[136,256]{1,0:T(8,128)S(1)} %get-tuple-element.44), channel_id=1, source_target_pairs={{0,2},{1,3},{2,0},{3,1},{4,6},{5,7},{6,4},{7,5},{8,10},{9,11},{10,... | collective-permute-start | bytes 417800 | tf_op jit(solution)/shard_map/ppermute | solution.py:28
  46.8 4.2 %gram.1.h_ref = f32[512,512]{1,0:T(8,128)S(1)} custom-call(s32[5]{0:T(128)S(1)} %stack.30.place_ref, f32[512,1024]{1,0:T(8,128)S(1)} %attend.1.at_ref), custom_call_target="tpu_custom_call" | custom-call | flops 4000000000 | bytes 100000 | tf_op jit(solution)/shard_map/gram/pallas_call | solution.py:33
  51.3 0.6 merge.4
  51.9 2.0 %collective-permute-start.8 = (f32[72,256]{1,0:T(8,128)S(1)}, f32[72,256]{1,0:T(8,128)S(1)}, u32[]{:S(2)}, u32[]{:S(2)}) collective-permute-start(f32[72,256]{1,0:T(8,128)S(1)} %get-tuple-element.48), channel_id=1, source_target_pairs={{0,8},{1,9},{2,10},{3,11},{4,12},{5,13},{6,14},{7,15},{8,0},{9,1},... | collective-permute-start | bytes 221192 | tf_op jit(solution)/shard_map/ppermute | solution.py:28
  53.9 4.7 %invert.4.inverse_ref = f32[128,128]{1,0:T(8,128)S(1)} custom-call(s32[5]{0:T(128)S(1)} %stack.30.place_ref, f32[512,512]{1,0:T(8,128)S(1)} %gram.1.h_ref), custom_call_target="tpu_custom_call" | custom-call | flops 5000000000 | bytes 100000 | tf_op jit(solution)/shard_map/invert/pallas_call | solution.py:33
  58.6 0.6 merge.5
  59.2 2.1 %collective-permute-start.9 = (f32[40,256]{1,0:T(8,128)S(1)}, f32[40,256]{1,0:T(8,128)S(1)}, u32[]{:S(2)}, u32[]{:S(2)}) collective-permute-start(f32[40,256]{1,0:T(8,128)S(1)} %get-tuple-element.52), channel_id=1, source_target_pairs={{0,4},{1,5},{2,6},{3,7},{4,0},{5,1},{6,2},{7,3},{8,12},{9,13},{10,... | collective-permute-start | bytes 122888 | tf_op jit(solution)/shard_map/ppermute | solution.py:28
  61.3 1.9 %update.4.h_ref = f32[512,512]{1,0:T(8,128)S(1)} custom-call(s32[5]{0:T(128)S(1)} %stack.30.place_ref, f32[512,512]{1,0:T(8,128)S(1)} %gram.1.h_ref, f32[128,128]{1,0:T(8,128)S(1)} %invert.4.inverse_ref), custom_call_target="tpu_custom_call" | custom-call | flops 2000000000 | bytes 100000 | tf_op jit(solution)/shard_map/update/pallas_call | solution.py:33
  63.3 0.6 finish.1.a_ref
  63.8 2.1 %collective-permute-start.10 = (f32[32,256]{1,0:T(8,128)S(1)}, f32[32,256]{1,0:T(8,128)S(1)}, u32[]{:S(2)}, u32[]{:S(2)}) collective-permute-start(f32[32,256]{1,0:T(8,128)S(1)} %finish.1.a_ref), channel_id=1, source_target_pairs={{0,4},{1,5},{2,6},{3,7},{4,0},{5,1},{6,2},{7,3},{8,12},{9,13},{10,... | collective-permute-start | bytes 98312 | tf_op jit(solution)/shard_map/ppermute | solution.py:28
  65.9 4.9 %invert.5.inverse_ref = f32[128,128]{1,0:T(8,128)S(1)} custom-call(s32[5]{0:T(128)S(1)} %stack.30.place_ref, f32[512,512]{1,0:T(8,128)S(1)} %update.4.h_ref), custom_call_target="tpu_custom_call" | custom-call | flops 5000000000 | bytes 100000 | tf_op jit(solution)/shard_map/invert/pallas_call | solution.py:33
  70.8 1.9 %update.5.h_ref = f32[512,512]{1,0:T(8,128)S(1)} custom-call(s32[5]{0:T(128)S(1)} %stack.30.place_ref, f32[512,512]{1,0:T(8,128)S(1)} %update.4.h_ref, f32[128,128]{1,0:T(8,128)S(1)} %invert.5.inverse_ref), custom_call_target="tpu_custom_call" | custom-call | flops 2000000000 | bytes 100000 | tf_op jit(solution)/shard_map/update/pallas_call | solution.py:33
  72.7 0.6 stack.32.a_ref
  73.2 1.3 %collective-permute-start.11 = (f32[64,256]{1,0:T(8,128)S(1)}, f32[64,256]{1,0:T(8,128)S(1)}, u32[]{:S(2)}, u32[]{:S(2)}) collective-permute-start(f32[64,256]{1,0:T(8,128)S(1)} %stack.32.a_ref), channel_id=1, source_target_pairs={{0,8},{1,9},{2,10},{3,11},{4,12},{5,13},{6,14},{7,15},{8,0},{9,1},... | collective-permute-start | bytes 196616 | tf_op jit(solution)/shard_map/ppermute | solution.py:28
  74.6 4.7 %invert.6.inverse_ref = f32[128,128]{1,0:T(8,128)S(1)} custom-call(s32[5]{0:T(128)S(1)} %stack.30.place_ref, f32[512,512]{1,0:T(8,128)S(1)} %update.5.h_ref), custom_call_target="tpu_custom_call" | custom-call | flops 5000000000 | bytes 100000 | tf_op jit(solution)/shard_map/invert/pallas_call | solution.py:33
  79.3 1.9 %update.6.h_ref = f32[512,512]{1,0:T(8,128)S(1)} custom-call(s32[5]{0:T(128)S(1)} %stack.30.place_ref, f32[512,512]{1,0:T(8,128)S(1)} %update.5.h_ref, f32[128,128]{1,0:T(8,128)S(1)} %invert.6.inverse_ref), custom_call_target="tpu_custom_call" | custom-call | flops 2000000000 | bytes 100000 | tf_op jit(solution)/shard_map/update/pallas_call | solution.py:33
  81.2 0.6 stack.33.a_ref
  81.7 1.3 %collective-permute-start.12 = (f32[128,256]{1,0:T(8,128)S(1)}, f32[128,256]{1,0:T(8,128)S(1)}, u32[]{:S(2)}, u32[]{:S(2)}) collective-permute-start(f32[128,256]{1,0:T(8,128)S(1)} %stack.33.a_ref), channel_id=1, source_target_pairs={{0,2},{1,3},{2,0},{3,1},{4,6},{5,7},{6,4},{7,5},{8,10},{9,11},{10,... | collective-permute-start | bytes 393224 | tf_op jit(solution)/shard_map/ppermute | solution.py:28
  83.0 4.7 %invert.7.inverse_ref = f32[128,128]{1,0:T(8,128)S(1)} custom-call(s32[5]{0:T(128)S(1)} %stack.30.place_ref, f32[512,512]{1,0:T(8,128)S(1)} %update.6.h_ref), custom_call_target="tpu_custom_call" | custom-call | flops 5000000000 | bytes 100000 | tf_op jit(solution)/shard_map/invert/pallas_call | solution.py:33
  87.7 0.6 stack.34.own_ref
  88.3 1.9 %update.7.minus_ref = f32[512,512]{1,0:T(8,128)S(1)} custom-call(s32[5]{0:T(128)S(1)} %stack.30.place_ref, f32[512,512]{1,0:T(8,128)S(1)} %update.6.h_ref, f32[128,128]{1,0:T(8,128)S(1)} %invert.7.inverse_ref), custom_call_target="tpu_custom_call" | custom-call | flops 2000000000 | bytes 100000 | tf_op jit(solution)/shard_map/update/pallas_call | solution.py:33
  90.2 5.3 %fit.1 = (f32[512,128]{1,0:T(8,128)}, f32[8,128]{1,0:T(8,128)S(1)}) custom-call(s32[5]{0:T(128)S(1)} %stack.30.place_ref, f32[512,512]{1,0:T(8,128)S(1)} %update.7.minus_ref, f32[512,1024]{1,0:T(8,128)S(1)} %attend.1.at_ref, f32[128,512]{1,0:T(8,128)S(1)} %stack.34.own_ref, f32[128,512]{1,0:T(8,128)S(1)} %collective-permute-done.13.other_ref), custom_call_target="tpu_custom_call" | custom-call | flops 1000000000 | bytes 100000 | tf_op jit(solution)/shard_map/fit/pallas_call | solution.py:33
  95.6 1.5 %collective-permute-start.14 = (f32[8,128]{1,0:T(8,128)S(1)}, f32[8,128]{1,0:T(8,128)S(1)}, u32[]{:S(2)}, u32[]{:S(2)}) collective-permute-start(f32[8,128]{1,0:T(8,128)S(1)} %get-tuple-element.65), channel_id=1, source_target_pairs={{0,16},{16,0},{1,17},{17,1},{2,18},{18,2},{3,19},{19,3},{4,20},{20... | collective-permute-start | bytes 12296 | tf_op jit(solution)/shard_map/ppermute | solution.py:28
  97.0 2.2 %collective-permute-done.14 = f32[8,128]{1,0:T(8,128)S(1)} collective-permute-done((f32[8,128]{1,0:T(8,128)S(1)}, f32[8,128]{1,0:T(8,128)S(1)}, u32[]{:S(2)}, u32[]{:S(2)}) %collective-permute-start.14) | collective-permute-done | bytes 4128 | tf_op jit(solution)/shard_map/ppermute | solution.py:28
  (21 shorter events, 1.4 us)
Async XLA Ops:
  1.4 1.2 %copy-start = (bf16[1,4096,128]{2,1,0:T(8,128)(2,1)S(1)}, bf16[1,4096,128]{2,1,0:T(8,128)(2,1)}, u32[]{:S(2)}) copy-start(bf16[1,4096,128]{2,1,0:T(8,128)(2,1)} %param.6) | copy-start | bytes 3145732
  2.6 0.9 copy-start.2
  3.6 0.7 copy-start.3
  4.3 30.6 %copy-start.1 = (bf16[1,4096,128]{2,1,0:T(8,128)(2,1)S(1)}, bf16[1,4096,128]{2,1,0:T(8,128)(2,1)}, u32[]{:S(2)}) copy-start(bf16[1,4096,128]{2,1,0:T(8,128)(2,1)} %param.6) | copy-start | bytes 3145732
  4.3 30.6 %copy-start.4 = (bf16[1,4096,128]{2,1,0:T(8,128)(2,1)S(1)}, bf16[1,4096,128]{2,1,0:T(8,128)(2,1)}, u32[]{:S(2)}) copy-start(bf16[1,4096,128]{2,1,0:T(8,128)(2,1)} %param.7) | copy-start | bytes 3145732
  5.4 1.6 %collective-permute-start = (bf16[2,384,128]{2,1,0:T(8,128)(2,1)S(1)}, bf16[2,384,128]{2,1,0:T(8,128)(2,1)S(1)}, u32[]{:S(2)}, u32[]{:S(2)}) collective-permute-start(bf16[2,384,128]{2,1,0:T(8,128)(2,1)S(1)} %get-tuple-element.35), channel_id=1, source_target_pairs={{0,1},{1,0},{2,3},{3,2},{4,5},{5,4},{6,7},{7,6},{8,9},{9,8},{10,11... | collective-permute-start | bytes 589832 | tf_op jit(solution)/shard_map/ppermute | solution.py:28
  7.6 6.0 %collective-permute-start.1 = (bf16[384,128]{1,0:T(8,128)(2,1)S(1)}, bf16[384,128]{1,0:T(8,128)(2,1)S(1)}, u32[]{:S(2)}, u32[]{:S(2)}) collective-permute-start(bf16[384,128]{1,0:T(8,128)(2,1)S(1)} %get-tuple-element.37), channel_id=1, source_target_pairs={{0,2},{1,3},{2,0},{3,1},{4,6},{5,7},{6,4},{7,5},{8,10},{9,11},{10,... | collective-permute-start | bytes 294920 | tf_op jit(solution)/shard_map/ppermute | solution.py:28
  14.2 7.4 %collective-permute-start.2 = (bf16[384,128]{1,0:T(8,128)(2,1)S(1)}, bf16[384,128]{1,0:T(8,128)(2,1)S(1)}, u32[]{:S(2)}, u32[]{:S(2)}) collective-permute-start(bf16[384,128]{1,0:T(8,128)(2,1)S(1)} %join.3.a_ref), channel_id=1, source_target_pairs={{0,8},{1,9},{2,10},{3,11},{4,12},{5,13},{6,14},{7,15},{8,0},{9,1},... | collective-permute-start | bytes 294920 | tf_op jit(solution)/shard_map/ppermute | solution.py:28
  22.2 4.7 %collective-permute-start.3 = (bf16[384,128]{1,0:T(8,128)(2,1)S(1)}, bf16[384,128]{1,0:T(8,128)(2,1)S(1)}, u32[]{:S(2)}, u32[]{:S(2)}) collective-permute-start(bf16[384,128]{1,0:T(8,128)(2,1)S(1)} %join.4.a_ref), channel_id=1, source_target_pairs={{0,4},{1,5},{2,6},{3,7},{4,0},{5,1},{6,2},{7,3},{8,12},{9,13},{10,... | collective-permute-start | bytes 294920 | tf_op jit(solution)/shard_map/ppermute | solution.py:28
  27.5 4.7 %collective-permute-start.4 = (bf16[384,128]{1,0:T(8,128)(2,1)S(1)}, bf16[384,128]{1,0:T(8,128)(2,1)S(1)}, u32[]{:S(2)}, u32[]{:S(2)}) collective-permute-start(bf16[384,128]{1,0:T(8,128)(2,1)S(1)} %join.5.a_ref), channel_id=1, source_target_pairs={{0,2},{1,3},{2,0},{3,1},{4,6},{5,7},{6,4},{7,5},{8,10},{9,11},{10,... | collective-permute-start | bytes 294920 | tf_op jit(solution)/shard_map/ppermute | solution.py:28
  32.7 1.5 %collective-permute-start.5 = (bf16[2,384,128]{2,1,0:T(8,128)(2,1)S(1)}, bf16[2,384,128]{2,1,0:T(8,128)(2,1)S(1)}, u32[]{:S(2)}, u32[]{:S(2)}) collective-permute-start(bf16[2,384,128]{2,1,0:T(8,128)(2,1)S(1)} %pair.1.a_ref), channel_id=1, source_target_pairs={{0,1},{1,0},{2,3},{3,2},{4,5},{5,4},{6,7},{7,6},{8,9},{9,8},{10,11... | collective-permute-start | bytes 589832 | tf_op jit(solution)/shard_map/ppermute | solution.py:28
  42.8 1.9 %collective-permute-start.6 = (f32[136,512]{1,0:T(8,128)S(1)}, f32[136,512]{1,0:T(8,128)S(1)}, u32[]{:S(2)}, u32[]{:S(2)}) collective-permute-start(f32[136,512]{1,0:T(8,128)S(1)} %get-tuple-element.40), channel_id=1, source_target_pairs={{0,1},{1,0},{2,3},{3,2},{4,5},{5,4},{6,7},{7,6},{8,9},{9,8},{10,11... | collective-permute-start | bytes 835592 | tf_op jit(solution)/shard_map/ppermute | solution.py:28
  45.3 6.0 %collective-permute-start.7 = (f32[136,256]{1,0:T(8,128)S(1)}, f32[136,256]{1,0:T(8,128)S(1)}, u32[]{:S(2)}, u32[]{:S(2)}) collective-permute-start(f32[136,256]{1,0:T(8,128)S(1)} %get-tuple-element.44), channel_id=1, source_target_pairs={{0,2},{1,3},{2,0},{3,1},{4,6},{5,7},{6,4},{7,5},{8,10},{9,11},{10,... | collective-permute-start | bytes 417800 | tf_op jit(solution)/shard_map/ppermute | solution.py:28
  51.9 6.7 %collective-permute-start.8 = (f32[72,256]{1,0:T(8,128)S(1)}, f32[72,256]{1,0:T(8,128)S(1)}, u32[]{:S(2)}, u32[]{:S(2)}) collective-permute-start(f32[72,256]{1,0:T(8,128)S(1)} %get-tuple-element.48), channel_id=1, source_target_pairs={{0,8},{1,9},{2,10},{3,11},{4,12},{5,13},{6,14},{7,15},{8,0},{9,1},... | collective-permute-start | bytes 221192 | tf_op jit(solution)/shard_map/ppermute | solution.py:28
  59.2 4.1 %collective-permute-start.9 = (f32[40,256]{1,0:T(8,128)S(1)}, f32[40,256]{1,0:T(8,128)S(1)}, u32[]{:S(2)}, u32[]{:S(2)}) collective-permute-start(f32[40,256]{1,0:T(8,128)S(1)} %get-tuple-element.52), channel_id=1, source_target_pairs={{0,4},{1,5},{2,6},{3,7},{4,0},{5,1},{6,2},{7,3},{8,12},{9,13},{10,... | collective-permute-start | bytes 122888 | tf_op jit(solution)/shard_map/ppermute | solution.py:28
  63.8 7.0 %collective-permute-start.10 = (f32[32,256]{1,0:T(8,128)S(1)}, f32[32,256]{1,0:T(8,128)S(1)}, u32[]{:S(2)}, u32[]{:S(2)}) collective-permute-start(f32[32,256]{1,0:T(8,128)S(1)} %finish.1.a_ref), channel_id=1, source_target_pairs={{0,4},{1,5},{2,6},{3,7},{4,0},{5,1},{6,2},{7,3},{8,12},{9,13},{10,... | collective-permute-start | bytes 98312 | tf_op jit(solution)/shard_map/ppermute | solution.py:28
  73.2 6.0 %collective-permute-start.11 = (f32[64,256]{1,0:T(8,128)S(1)}, f32[64,256]{1,0:T(8,128)S(1)}, u32[]{:S(2)}, u32[]{:S(2)}) collective-permute-start(f32[64,256]{1,0:T(8,128)S(1)} %stack.32.a_ref), channel_id=1, source_target_pairs={{0,8},{1,9},{2,10},{3,11},{4,12},{5,13},{6,14},{7,15},{8,0},{9,1},... | collective-permute-start | bytes 196616 | tf_op jit(solution)/shard_map/ppermute | solution.py:28
  81.7 5.9 %collective-permute-start.12 = (f32[128,256]{1,0:T(8,128)S(1)}, f32[128,256]{1,0:T(8,128)S(1)}, u32[]{:S(2)}, u32[]{:S(2)}) collective-permute-start(f32[128,256]{1,0:T(8,128)S(1)} %stack.33.a_ref), channel_id=1, source_target_pairs={{0,2},{1,3},{2,0},{3,1},{4,6},{5,7},{6,4},{7,5},{8,10},{9,11},{10,... | collective-permute-start | bytes 393224 | tf_op jit(solution)/shard_map/ppermute | solution.py:28
  88.3 2.0 %collective-permute-start.13 = (f32[128,512]{1,0:T(8,128)S(1)}, f32[128,512]{1,0:T(8,128)S(1)}, u32[]{:S(2)}, u32[]{:S(2)}) collective-permute-start(f32[128,512]{1,0:T(8,128)S(1)} %stack.34.own_ref), channel_id=1, source_target_pairs={{0,1},{1,0},{2,3},{3,2},{4,5},{5,4},{6,7},{7,6},{8,9},{9,8},{10,11... | collective-permute-start | bytes 786440 | tf_op jit(solution)/shard_map/ppermute | solution.py:28
  95.6 3.6 %collective-permute-start.14 = (f32[8,128]{1,0:T(8,128)S(1)}, f32[8,128]{1,0:T(8,128)S(1)}, u32[]{:S(2)}, u32[]{:S(2)}) collective-permute-start(f32[8,128]{1,0:T(8,128)S(1)} %get-tuple-element.65), channel_id=1, source_target_pairs={{0,16},{16,0},{1,17},{17,1},{2,18},{18,2},{3,19},{19,3},{4,20},{20... | collective-permute-start | bytes 12296 | tf_op jit(solution)/shard_map/ppermute | solution.py:28

commit v4 on v3

v4 whole, which is shorter than its diff:
```python
import functools
import math

import jax
import jax.numpy as jnp
from jax import lax
from jax.experimental import pallas as pl
from jax.experimental.pallas import tpu as pltpu
from jax.sharding import PartitionSpec as P

KBLK = 1024
PANEL = 128
SUB = 8
RIDGE_SHARE = 0.01
F32 = jnp.float32
BF16 = jnp.bfloat16
HIGH = lax.Precision.HIGHEST
VMEM_LIMIT = 48 * 1024 * 1024
VMEM = pl.BlockSpec(memory_space=pltpu.VMEM)
SMEM = pl.BlockSpec(memory_space=pltpu.SMEM)
NT = (((1,), (1,)), ((), ()))
TN = (((0,), (0,)), ((), ()))
NN = (((1,), (0,)), ((), ()))


def swap(array, axis, step):
    size = lax.axis_size(axis)
    return lax.ppermute(array, axis, [(i, i ^ step) for i in range(size)])


def call(kernel, ins, outs, cost=10**5, scratch=(), name=None, specs=None):
    return pl.pallas_call(
        kernel,
        in_specs=specs or [SMEM if x.size == 1 else VMEM for x in ins],
        out_specs=[VMEM] * len(outs),
        out_shape=[jax.ShapeDtypeStruct(shape, kind) for shape, kind in outs],
        scratch_shapes=list(scratch),
        compiler_params=pltpu.CompilerParams(vmem_limit_bytes=VMEM_LIMIT),
        cost_estimate=pl.CostEstimate(flops=cost, bytes_accessed=10**5, transcendentals=0),
        name=name,
    )(*ins)


def aligned(value, unit):
    return pl.ds(pl.multiple_of(value * unit, unit), unit)


def prepare_kernel(window, shard_ref, root_ref, q_hbm, kept_hbm, k_hbm, *refs):
    outs, k_ref, (q_ref, kept_ref, spots, picked, sems) = refs[:4], refs[4], refs[5:]
    slab, dims = k_ref.shape
    kept = kept_ref.shape[1]
    steps = sems.shape[0] - 2
    chunk = slab // steps
    loads = [pltpu.make_async_copy(kept_hbm, kept_ref, sems.at[steps])]
    for i in range(steps):
        part = pl.ds(i * chunk, chunk)
        loads.append(pltpu.make_async_copy(k_hbm.at[part], k_ref.at[part], sems.at[i]))
    loads.append(pltpu.make_async_copy(q_hbm, q_ref, sems.at[steps + 1]))
    for load in loads:
        load.start()
    base = shard_ref[0] * slab
    loads[0].wait()
    positions = kept_ref[...]
    before = jnp.sum((positions < base).astype(jnp.int32))
    start = jnp.minimum(before // 16, (kept - window) // 16)
    local = (positions - base).astype(F32)
    for i in range(0, kept, 128):
        spots[i : i + 128, :] = jnp.broadcast_to(local[:, i : i + 128], (128, 128)).T
    spot = pl.ds(pl.multiple_of(start * 16, 16), window)
    mine = spots[spot, :]
    column = lax.broadcasted_iota(jnp.int32, (window, 128), 1).astype(F32)
    rows = jnp.zeros((window, dims), F32)
    for i in range(steps):
        onehot = jnp.concatenate(
            [jnp.where(mine == column + float(j), 1.0, 0.0).astype(BF16) for j in range(i * chunk, (i + 1) * chunk, 128)],
            axis=1,
        )
        loads[1 + i].wait()
        rows += lax.dot_general(onehot, k_ref[i * chunk : (i + 1) * chunk, :], NN, preferred_element_type=F32)
    picked[...] = jnp.zeros_like(picked)
    picked[spot, :] = rows.astype(BF16)
    loads[-1].wait()
    share, part = q_ref.shape[0] // 4, kept // 4
    is_root = shard_ref[0] == root_ref[0]
    for s, out in enumerate(outs):
        place = (shard_ref[0] % 4) ^ s
        q = q_ref[aligned(place, share), :]
        out[:share, :] = jnp.where(is_root, q, jnp.zeros_like(q))
        out[share:, :] = picked[aligned(place, part), :]


def sum_kernel(*refs):
    total = refs[0][...]
    for ref in refs[1:-1]:
        total = total + ref[...]
    refs[-1][...] = total


def spread(shard, queries, kept, keys, roots):
    (rows, dims), (slab, _) = queries.shape, keys.shape
    count = kept.shape[1]
    devices = lax.axis_size("ctx")
    tall = ((rows + count) // 4, dims)
    anywhere = pl.BlockSpec(memory_space=pl.ANY)
    *pieces, keys = call(
        functools.partial(prepare_kernel, 4 * count // devices + 16),
        (shard, roots, queries, kept, keys),
        [(tall, BF16)] * 4 + [(keys.shape, BF16)],
        scratch=[
            pltpu.VMEM((rows, dims), BF16),
            pltpu.VMEM((1, count), jnp.int32),
            pltpu.VMEM((count, 128), F32),
            pltpu.VMEM((count, dims), BF16),
            pltpu.SemaphoreType.DMA((6,)),
        ],
        name="prepare",
        specs=[SMEM, SMEM, anywhere, anywhere, anywhere],
    )
    total = lambda arrays: call(sum_kernel, arrays, [(tall, BF16)], name="total")[0]
    piece = total([pieces[0]] + [swap(pieces[s], "ctx", s) for s in (1, 2, 3)])
    step = 4
    while step < devices:
        ways = math.gcd(devices // step, 4)
        piece = total([piece] + [swap(piece, "ctx", t * step) for t in range(1, ways)])
        step *= ways
    return [piece] + [swap(piece, "ctx", s) for s in (1, 2, 3)], keys


def turn_kernel(v_ref, vt_ref):
    dims = v_ref.shape[1]
    vt_ref[:dims, :] = v_ref[...].T
    vt_ref[dims:, :] = jnp.ones((vt_ref.shape[0] - dims, v_ref.shape[0]), BF16)


def attention_kernel(pieces, lanes, block, score_scale, *refs):
    q_refs, k_ref, vt_ref, before, out_ref = refs[:pieces], refs[pieces], refs[pieces + 1], refs[pieces + 2 : -1], refs[-1]
    dims = k_ref.shape[1]
    blocks = k_ref.shape[0] // block
    factor = score_scale * math.log2(math.e)
    skip = len(before) * lanes
    for ref in before:
        out_ref[:, :skip] = ref[...]

    def scores(i, b):
        return lax.dot_general(
            k_ref[b * block : (b + 1) * block, :], q_refs[i][:lanes, :], NT, preferred_element_type=F32
        )

    stages = [(i, b) for i in range(pieces) for b in range(blocks)]
    ahead = scores(*stages[0])
    for n, (i, b) in enumerate(stages):
        s = ahead
        if n + 1 < len(stages):
            ahead = scores(*stages[n + 1])
        at = slice(skip + i * lanes, skip + (i + 1) * lanes)
        top = jnp.max(s, axis=0, keepdims=True)
        e = jnp.exp2((s - top) * factor).astype(BF16)
        out = lax.dot_general(vt_ref[:, b * block : (b + 1) * block], e, NN, preferred_element_type=F32)
        top = top * factor
        total = out[dims : dims + 1, :]
        out = out[:dims, :]
        if b:
            old_top = out_ref[dims : dims + 1, at]
            joint = jnp.maximum(old_top, top)
            old_scale = jnp.exp2(old_top - joint)
            new_scale = jnp.exp2(top - joint)
            out = out_ref[:dims, at] * old_scale + out * new_scale
            total = out_ref[dims + 1 : dims + 2, at] * old_scale + total * new_scale
            top = joint
        out_ref[:dims, at] = out
        out_ref[dims:, at] = tail(top, total)


def attention(pieces, lanes, keys, turned, score_scale, before=()):
    slab, dims = keys.shape
    return call(
        functools.partial(attention_kernel, len(pieces), lanes, min(KBLK, slab), score_scale),
        (*pieces, keys, turned, *before),
        [((dims + SUB, lanes * (len(pieces) + len(before))), F32)],
        4 * lanes * len(pieces) * slab * dims,
        name="attention",
    )[0]


def merged(a_ref, b_ref):
    dims = a_ref.shape[0] - SUB
    a_top, b_top = a_ref[dims : dims + 1, :], b_ref[dims : dims + 1, :]
    top = jnp.maximum(a_top, b_top)
    a_scale, b_scale = jnp.exp2(a_top - top), jnp.exp2(b_top - top)
    total = a_ref[dims + 1 : dims + 2, :] * a_scale + b_ref[dims + 1 : dims + 2, :] * b_scale
    out = a_ref[:dims, :] * a_scale + b_ref[:dims, :] * b_scale
    return out, top, total


def tail(top, total):
    return jnp.concatenate([top, total, jnp.zeros((SUB - 2, top.shape[1]), F32)], axis=0)


def merge_lanes_kernel(a_ref, b_ref, keep_ref, send_ref):
    out, top, total = merged(a_ref, b_ref)
    dims, lanes = out.shape[0], keep_ref.shape[1]
    for ref, at in ((keep_ref, slice(0, lanes)), (send_ref, slice(lanes, 2 * lanes))):
        ref[:dims, :] = out[:, at]
        ref[dims:, :] = tail(top[:, at], total[:, at])


def merge_rows_kernel(step, shard_ref, a_ref, b_ref, keep_ref, send_ref, work):
    out, top, total = merged(a_ref, b_ref)
    rows = keep_ref.shape[0] - SUB
    work[...] = out
    bit = (shard_ref[0] // step) % 2
    for ref, which in ((keep_ref, bit), (send_ref, 1 - bit)):
        ref[:rows, :] = work[aligned(which, rows), :]
        ref[rows:, :] = tail(top, total)


def finish_kernel(a_ref, b_ref, out_ref):
    out, _, total = merged(a_ref, b_ref)
    out_ref[...] = out / total


def stack_rows_kernel(step, shard_ref, a_ref, b_ref, out_ref):
    rows = a_ref.shape[0]
    bit = (shard_ref[0] // step) % 2
    out_ref[aligned(bit, rows), :] = a_ref[...]
    out_ref[aligned(1 - bit, rows), :] = b_ref[...]


def stack_lanes_kernel(a_ref, b_ref, out_ref):
    lanes = a_ref.shape[1]
    out_ref[:, :lanes] = a_ref[...]
    out_ref[:, lanes:] = b_ref[...]


def target_rounds(shard, keep, came):
    dims, lanes = keep.shape[0] - SUB, keep.shape[1] // 2
    devices = lax.axis_size("ctx")
    keep, send = call(merge_lanes_kernel, (keep, came), [((dims + SUB, lanes), F32)] * 2, name="merge")
    came = yield swap(send, "ctx", 2)
    step, rows = devices // 2, dims
    while step >= 4:
        keep, send = call(
            functools.partial(merge_rows_kernel, step),
            (shard, keep, came),
            [((rows // 2 + SUB, lanes), F32)] * 2,
            scratch=[pltpu.VMEM((rows, lanes), F32)],
            name="merge",
        )
        came = yield swap(send, "ctx", step)
        rows //= 2
        step //= 2
    (block,) = call(finish_kernel, (keep, came), [((rows, lanes), F32)], name="finish")
    step = 4
    while step < devices:
        came = yield swap(block, "ctx", step)
        rows *= 2
        (block,) = call(functools.partial(stack_rows_kernel, step), (shard, block, came), [((rows, lanes), F32)], name="stack")
        step *= 2
    came = yield swap(block, "ctx", 2)
    (block,) = call(stack_lanes_kernel, (block, came), [((dims, 2 * lanes), F32)], name="stack")
    came = yield swap(block, "ctx", 1)
    return block, came


def attend_kernel(score_scale, shard_ref, *refs):
    pieces, at_ref, c_all = refs[:4], refs[4], refs[5]
    part, rows = c_all.shape[0] // 4, at_ref.shape[1] // 4
    places = [(shard_ref[0] % 4) ^ s for s in range(4)]
    for place, piece in zip(places, pieces):
        c_all[aligned(place, part), :] = piece[rows:, :]
    for place, piece in zip(places, pieces):
        scores = lax.dot_general(c_all[...], piece[:rows, :], NT, preferred_element_type=F32) * score_scale
        weights = jnp.exp(scores - jnp.max(scores, axis=0, keepdims=True))
        at_ref[:, aligned(place, rows)] = weights / jnp.sum(weights, axis=0, keepdims=True)


def gram_kernel(at_ref, h_ref):
    gram = lax.dot_general(at_ref[...], at_ref[...], NT, precision=HIGH, preferred_element_type=F32)
    kept = gram.shape[0]
    diagonal = lax.broadcasted_iota(jnp.int32, gram.shape, 0) == lax.broadcasted_iota(jnp.int32, gram.shape, 1)
    trace = jnp.sum(jnp.where(diagonal, gram, 0.0))
    h_ref[...] = gram + jnp.where(diagonal, RIDGE_SHARE * trace / kept, 0.0)


def invert_block(rows):
    count = len(rows)
    size = count * SUB
    lane = lax.broadcasted_iota(jnp.int32, (SUB, size), 1)
    sub = lax.broadcasted_iota(jnp.int32, (SUB, size), 0)
    spread = lambda array, column: jnp.broadcast_to(array[:, column : column + 1], (SUB, size))
    line = lambda array, row: jnp.broadcast_to(array[row : row + 1, :], (SUB, size))
    for k in range(count):
        base = k * SUB
        inside = (lane >= base) & (lane < base + SUB)
        columns = [spread(rows[k], base + j) for j in range(SUB)]
        work = jnp.where(inside, jnp.where(lane - base == sub, 1.0, 0.0), rows[k])
        for j in range(SUB):
            here = sub == j
            inverse = 1.0 / line(columns[j], j)
            step = lambda v: (lambda t: jnp.where(here, t, v - columns[j] * t))(line(v, j) * inverse)
            for i in range(j + 1, SUB):
                columns[i] = step(columns[i])
            work = step(work)
        lines = [line(work, j) for j in range(SUB)]
        updated = []
        for i in range(count):
            if i == k:
                updated.append(work)
                continue
            fresh = jnp.where(inside, 0.0, rows[i])
            for j in range(SUB):
                fresh = fresh - spread(rows[i], base + j) * lines[j]
            updated.append(fresh)
        rows = updated
    return rows


def invert_kernel(panel, h_ref, out_ref):
    at = slice(panel * PANEL, (panel + 1) * PANEL)
    block = h_ref[at, at]
    out_ref[...] = jnp.concatenate(
        invert_block([block[i * SUB : (i + 1) * SUB, :] for i in range(PANEL // SUB)]), axis=0
    )


def update_kernel(panel, h_ref, inverse_ref, out_ref):
    at = slice(panel * PANEL, (panel + 1) * PANEL)
    across = h_ref[at, :]
    turned = lax.dot_general(inverse_ref[...], across, NN, precision=HIGH, preferred_element_type=F32)
    out_ref[...] = h_ref[...] - lax.dot_general(across, turned, TN, precision=HIGH, preferred_element_type=F32)
    out_ref[:, at] = turned.T
    out_ref[at, :] = turned
    out_ref[at, at] = -inverse_ref[...]


def fit_kernel(shard_ref, minus_ref, at_ref, own_ref, other_ref, x_ref, err_ref, yt):
    lanes = own_ref.shape[1] // 2
    place = shard_ref[0] % 4
    for s, ref in ((1, own_ref), (3, own_ref), (0, other_ref), (2, other_ref)):
        half = s // 2
        yt[:, aligned(place ^ s, lanes)] = ref[:, half * lanes : (half + 1) * lanes]
    target = yt[...]
    attend = at_ref[...]
    cross = lax.dot_general(target, attend, NT, precision=HIGH, preferred_element_type=F32)
    fitted = -lax.dot_general(cross, minus_ref[...], NN, precision=HIGH, preferred_element_type=F32)
    x_ref[...] = fitted.T
    misfit = lax.dot_general(fitted, attend, NN, precision=HIGH, preferred_element_type=F32) - target
    error = jnp.sum(misfit * misfit) / jnp.sum(target * target)
    err_ref[...] = jnp.full(err_ref.shape, error, F32)


def per_device(queries, keys, values, kept, roots):
    rows, dims = queries.shape[2:]
    slab, count = keys.shape[1], kept.shape[1]
    lanes = rows // 4
    score_scale = 1.0 / math.sqrt(dims)
    shard = lax.axis_index("ctx").astype(jnp.int32).reshape(1)

    pieces, own_keys = spread(shard, queries[0, 0], kept, keys[0], roots)
    (turned,) = call(turn_kernel, (values[0],), [((dims + 16, slab), BF16)], name="turn")
    attend_to = functools.partial(attention, lanes=lanes, keys=own_keys, turned=turned, score_scale=score_scale)
    first = attend_to([pieces[0]])
    send = attend_to([pieces[2]], before=[first])
    keep = attend_to([pieces[1], pieces[3]])
    rounds = target_rounds(shard, keep, swap(send, "ctx", 1))
    came = next(rounds)
    ends = None

    def beside(arrays):
        nonlocal came, ends
        if ends is None:
            arrays, came = lax.optimization_barrier((arrays, came))
            try:
                came = rounds.send(came)
            except StopIteration as stop:
                ends = stop.value
        return arrays

    system_shape = ((count, count), F32)
    (attend,) = call(
        functools.partial(attend_kernel, score_scale),
        (shard, *pieces),
        [((count, rows), F32)],
        10**9,
        scratch=[pltpu.VMEM((count, dims), BF16)],
        name="attend",
    )
    (system,) = call(gram_kernel, (attend,), [system_shape], 4 * 10**9, name="gram")
    system = beside(system)
    panels = count // PANEL
    for panel in range(panels):
        (inverse,) = call(
            functools.partial(invert_kernel, panel), (system,), [((PANEL, PANEL), F32)], 5 * 10**9, name="invert"
        )
        inverse = beside(inverse)
        (system,) = call(
            functools.partial(update_kernel, panel), (system, inverse), [system_shape], 2 * 10**9, name="update"
        )
        if panel == 0 or panel == panels - 1:
            system = beside(system)
    while ends is None:
        system = beside(system)

    compact, error = call(
        fit_kernel,
        (shard, system, attend, *ends),
        [((count, dims), F32), ((SUB, 128), F32)],
        10**9,
        scratch=[pltpu.VMEM((dims, rows), F32)],
        name="fit",
    )
    heads = lax.axis_size("head")
    step = 1
    while step < heads:
        error = error + swap(error, "head", step)
        step *= 2
    return (compact[None], error[0, 0] / heads)


def solution(mesh):
    placed = (
        P("head", "ctx", None, None),
        P("head", "ctx", None),
        P("head", "ctx", None),
        P("head", None),
        P("head"),
    )
    return jax.shard_map(
        per_device,
        mesh=mesh,
        in_specs=placed,
        out_specs=(P("head", None, None), P()),
        check_vma=False,
    )
```

time: 102 us -> 87 us (0.85)
  Pallas kernels: 54.1 us -> 40.8 us
  starting transfers between devices: 20.6 us -> 18.7 us
    pallas_call x26 -> x25, Pallas kernels: 54.1 us -> 40.8 us  [call(): pl.pallas_call(kernel, in_specs=specs or [SMEM if x.size == 1 else VMEM f...]
    ppermute x15 -> x18, starting transfers between devices: 20.6 us -> 18.7 us  [swap(): return lax.ppermute(array, axis, [(i, i ^ step) for i in range(size)])]
    ppermute x15 -> x18, waiting for transfers between devices: 19.9 us -> 20.7 us  [swap(): return lax.ppermute(array, axis, [(i, i ^ step) for i in range(size)])]
    unnamed x10 -> x8, local copies, waits for them, and re-layouts: 2.86 us -> 2.85 us
  transfers between devices with their start and end apart: 15 -> 18, of which waited for: 9 -> 11; matrix products, arithmetic and copies ran while one was open for 0% -> 0% of each run, Pallas kernels for 28% -> 37%
where the time goes in v4:
time: 87 us; the launch traced here: 86.8 us
  Pallas kernels  40.8 us (47%)
  waiting for transfers between devices  20.7 us (24%)
  starting transfers between devices  18.7 us (21%)
  local copies, waits for them, and re-layouts  3.37 us (4%)
  between operations  3.28 us (4%)
    pallas_call x25, Pallas kernels, call(): pl.pallas_call(kernel, in_specs=specs or [SMEM if x.size == 1 else VMEM f...  40.8 us
    ppermute x18, waiting for transfers between devices, swap(): return lax.ppermute(array, axis, [(i, i ^ step) for i in range(size)])  20.7 us
    ppermute x18, starting transfers between devices, swap(): return lax.ppermute(array, axis, [(i, i ^ step) for i in range(size)])  18.7 us
    unnamed x8, local copies, waits for them, and re-layouts  2.85 us
  transfers between devices with their start and end apart: 18, of which 11 were waited for; matrix products, arithmetic and copies ran while one was open for 0% of the time, Pallas kernels for 37%

profile of v4, /device:TPU:0, one launch (start us, length us, event | category | flops | bytes accessed | tf_op | source)
XLA Modules:
  0.0 86.8 jit_solution(4587504306240908886)
XLA Ops:
  1.3 1.2 %copy-done = bf16[1,4096,128]{2,1,0:T(8,128)(2,1)S(1)} copy-done((bf16[1,4096,128]{2,1,0:T(8,128)(2,1)S(1)}, bf16[1,4096,128]{2,1,0:T(8,128)(2,1)}, u32[]{:S(2)}) %copy-start) | copy-done | bytes 1048600
  2.5 0.9 %copy-done.2 = bf16[1,1,1024,128]{3,2,1,0:T(8,128)(2,1)S(1)} copy-done((bf16[1,1,1024,128]{3,2,1,0:T(8,128)(2,1)S(1)}, bf16[1,1,1024,128]{3,2,1,0:T(8,128)(2,1)}, u32[]{:S(2)}) %copy-start.2) | copy-done | bytes 262168
  3.5 0.7 copy-done.3
  4.1 1.4 %prepare.1 = (bf16[384,128]{1,0:T(8,128)(2,1)S(1)}, bf16[384,128]{1,0:T(8,128)(2,1)S(1)}, bf16[384,128]{1,0:T(8,128)(2,1)S(1)}, bf16[384,128]{1,0:T(8,128)(2,1)S(1)}, bf16[4096,128]{1,0:T(8,128)(2,1)S(1)}) custom-call(s32[1]{0:T(128)} %bitcast.shard_ref, s32[1]{0:T(128)S(6)} %copy.7.root_ref, bf16[1024,128]{1,0:T(8,128)(2,1)S(1)} %bitcast.8, ...), custom_call_target="tpu_custom_call" | custom-call | flops 100000 | bytes 100000 | tf_op jit(solution)/shard_map/prepare/pallas_call | solution.py:32
  5.5 0.5 collective-permute-start
  6.0 2.6 %collective-permute-start.1 = (bf16[384,128]{1,0:T(8,128)(2,1)S(1)}, bf16[384,128]{1,0:T(8,128)(2,1)S(1)}, u32[]{:S(2)}, u32[]{:S(2)}) collective-permute-start(bf16[384,128]{1,0:T(8,128)(2,1)S(1)} %get-tuple-element.31), channel_id=1, source_target_pairs={{0,2},{1,3},{2,0},{3,1},{4,6},{5,7},{6,4},{7,5},{8,10},{9,11},{10,... | collective-permute-start | bytes 294920 | tf_op jit(solution)/shard_map/ppermute | solution.py:28
  8.6 0.1 collective-permute-start.2
  8.7 3.6 %collective-permute-done.1.refs_2_ = bf16[384,128]{1,0:T(8,128)(2,1)S(1)} collective-permute-done((bf16[384,128]{1,0:T(8,128)(2,1)S(1)}, bf16[384,128]{1,0:T(8,128)(2,1)S(1)}, u32[]{:S(2)}, u32[]{:S(2)}) %collective-permute-start.1) | collective-permute-done | bytes 98336 | tf_op jit(solution)/shard_map/ppermute | solution.py:28
  12.3 1.6 %collective-permute-done.2.refs_3_ = bf16[384,128]{1,0:T(8,128)(2,1)S(1)} collective-permute-done((bf16[384,128]{1,0:T(8,128)(2,1)S(1)}, bf16[384,128]{1,0:T(8,128)(2,1)S(1)}, u32[]{:S(2)}, u32[]{:S(2)}) %collective-permute-start.2) | collective-permute-done | bytes 98336 | tf_op jit(solution)/shard_map/ppermute | solution.py:28
  13.9 3.7 %collective-permute-start.5 = (bf16[384,128]{1,0:T(8,128)(2,1)S(1)}, bf16[384,128]{1,0:T(8,128)(2,1)S(1)}, u32[]{:S(2)}, u32[]{:S(2)}) collective-permute-start(bf16[384,128]{1,0:T(8,128)(2,1)S(1)} %total.2.refs_0_), channel_id=1, source_target_pairs={{0,12},{1,13},{2,14},{3,15},{4,8},{5,9},{6,10},{7,11},{8,4},{9,5},... | collective-permute-start | bytes 294920 | tf_op jit(solution)/shard_map/ppermute | solution.py:28
  17.6 0.7 collective-permute-start.3
  18.3 3.1 %collective-permute-done.5.refs_3_ = bf16[384,128]{1,0:T(8,128)(2,1)S(1)} collective-permute-done((bf16[384,128]{1,0:T(8,128)(2,1)S(1)}, bf16[384,128]{1,0:T(8,128)(2,1)S(1)}, u32[]{:S(2)}, u32[]{:S(2)}) %collective-permute-start.5) | collective-permute-done | bytes 98336 | tf_op jit(solution)/shard_map/ppermute | solution.py:28
  21.5 4.8 %collective-permute-done.4.refs_2_ = bf16[384,128]{1,0:T(8,128)(2,1)S(1)} collective-permute-done((bf16[384,128]{1,0:T(8,128)(2,1)S(1)}, bf16[384,128]{1,0:T(8,128)(2,1)S(1)}, u32[]{:S(2)}, u32[]{:S(2)}) %collective-permute-start.4) | collective-permute-done | bytes 98336 | tf_op jit(solution)/shard_map/ppermute | solution.py:28
  26.4 1.6 %collective-permute-start.7 = (bf16[384,128]{1,0:T(8,128)(2,1)S(1)}, bf16[384,128]{1,0:T(8,128)(2,1)S(1)}, u32[]{:S(2)}, u32[]{:S(2)}) collective-permute-start(bf16[384,128]{1,0:T(8,128)(2,1)S(1)} %total.3.refs_0_), channel_id=1, source_target_pairs={{0,2},{1,3},{2,0},{3,1},{4,6},{5,7},{6,4},{7,5},{8,10},{9,11},{10,... | collective-permute-start | bytes 294920 | tf_op jit(solution)/shard_map/ppermute | solution.py:28
  27.9 0.3 turn.1.refs_3_.refs_2_
  28.3 0.1 collective-permute-start.8
  28.4 0.6 collective-permute-start.6
  29.0 1.8 %attention.4.refs_3_ = f32[136,256]{1,0:T(8,128)S(1)} custom-call(bf16[384,128]{1,0:T(8,128)(2,1)S(1)} %total.3.refs_0_, bf16[4096,128]{1,0:T(8,128)(2,1)S(1)} %get-tuple-element.33.refs_2_.refs_1_, bf16[144,4096]{1,0:T(8,128)(2,1)S(1)} %turn.1.refs_3_.refs_2_), custom_call_target="tpu_custom_call" | custom-call | flops 536870912 | bytes 100000 | tf_op jit(solution)/shard_map/attention/pallas_call | solution.py:32
  30.8 0.3 collective-permute-done.7.refs_2_.refs_0_
  31.0 1.8 %attention.5 = f32[136,512]{1,0:T(8,128)S(1)} custom-call(bf16[384,128]{1,0:T(8,128)(2,1)S(1)} %collective-permute-done.7.refs_2_.refs_0_, bf16[4096,128]{1,0:T(8,128)(2,1)S(1)} %get-tuple-element.33.refs_2_.refs_1_, bf16[144,4096]{1,0:T(8,128)(2,1)S(1)} %turn.1.refs_3_.refs_2_, f32[136,256]{1,0:T(8,128)S(1)} %attention.4.refs_3_), custom_call_target="tpu_custom_call" | custom-call | flops 536870912 | bytes 100000 | tf_op jit(solution)/shard_map/attention/pallas_call | solution.py:32
  32.8 0.1 collective-permute-start.9
  32.9 0.2 collective-permute-done.8.refs_3_.refs_1_
  33.1 1.1 %attend.1.at_ref = f32[512,1024]{1,0:T(8,128)S(1)} custom-call(s32[1]{0:T(128)} %bitcast.shard_ref, bf16[384,128]{1,0:T(8,128)(2,1)S(1)} %total.3.refs_0_, bf16[384,128]{1,0:T(8,128)(2,1)S(1)} %collective-permute-done.6.refs_1_.refs_0_, bf16[384,128]{1,0:T(8,128)(2,1)S(1)} %collective-permute-done.7.refs_2_.refs_0_, ...), custom_call_target="tpu_custom_call" | custom-call | flops 1000000000 | bytes 100000 | tf_op jit(solution)/shard_map/attend/pallas_call | solution.py:32
  34.3 3.4 %attention.3.a_ref = f32[136,512]{1,0:T(8,128)S(1)} custom-call(bf16[384,128]{1,0:T(8,128)(2,1)S(1)} %collective-permute-done.6.refs_1_.refs_0_, bf16[384,128]{1,0:T(8,128)(2,1)S(1)} %collective-permute-done.8.refs_3_.refs_1_, bf16[4096,128]{1,0:T(8,128)(2,1)S(1)} %get-tuple-element.33.refs_2_.refs_1_, bf16[144,4096]{1,0:T(8,128)(2,1)S(1)} %turn.1.refs_3_.refs_2_), custom_call_target="tpu_custom_call" | custom-call | flops 1073741824 | bytes 100000 | tf_op jit(solution)/shard_map/attention/pallas_call | solution.py:32
  37.8 2.1 %collective-permute-start.10 = (f32[136,256]{1,0:T(8,128)S(1)}, f32[136,256]{1,0:T(8,128)S(1)}, u32[]{:S(2)}, u32[]{:S(2)}) collective-permute-start(f32[136,256]{1,0:T(8,128)S(1)} %get-tuple-element.34), channel_id=1, source_target_pairs={{0,2},{1,3},{2,0},{3,1},{4,6},{5,7},{6,4},{7,5},{8,10},{9,11},{10,... | collective-permute-start | bytes 417800 | tf_op jit(solution)/shard_map/ppermute | solution.py:28
  39.9 3.8 %gram.1.h_ref = f32[512,512]{1,0:T(8,128)S(1)} custom-call(f32[512,1024]{1,0:T(8,128)S(1)} %attend.1.at_ref), custom_call_target="tpu_custom_call" | custom-call | flops 4000000000 | bytes 100000 | tf_op jit(solution)/shard_map/gram/pallas_call | solution.py:32
  43.8 0.5 collective-permute-done.10.b_ref
  44.3 0.2 collective-permute-start.11
  44.5 4.1 %invert.4.inverse_ref = f32[128,128]{1,0:T(8,128)S(1)} custom-call(f32[512,512]{1,0:T(8,128)S(1)} %gram.1.h_ref), custom_call_target="tpu_custom_call" | custom-call | flops 5000000000 | bytes 100000 | tf_op jit(solution)/shard_map/invert/pallas_call | solution.py:32
  48.6 2.3 %collective-permute-done.11.b_ref = f32[72,256]{1,0:T(8,128)S(1)} collective-permute-done((f32[72,256]{1,0:T(8,128)S(1)}, f32[72,256]{1,0:T(8,128)S(1)}, u32[]{:S(2)}, u32[]{:S(2)}) %collective-permute-start.11) | collective-permute-done | bytes 73760 | tf_op jit(solution)/shard_map/ppermute | solution.py:28
  50.9 0.7 collective-permute-start.12
  51.6 1.3 %update.4.h_ref = f32[512,512]{1,0:T(8,128)S(1)} custom-call(f32[512,512]{1,0:T(8,128)S(1)} %gram.1.h_ref, f32[128,128]{1,0:T(8,128)S(1)} %invert.4.inverse_ref), custom_call_target="tpu_custom_call" | custom-call | flops 2000000000 | bytes 100000 | tf_op jit(solution)/shard_map/update/pallas_call | solution.py:32
  53.0 2.0 %collective-permute-done.12.b_ref = f32[40,256]{1,0:T(8,128)S(1)} collective-permute-done((f32[40,256]{1,0:T(8,128)S(1)}, f32[40,256]{1,0:T(8,128)S(1)}, u32[]{:S(2)}, u32[]{:S(2)}) %collective-permute-start.12) | collective-permute-done | bytes 40992 | tf_op jit(solution)/shard_map/ppermute | solution.py:28
  55.0 0.7 collective-permute-start.13
  55.7 4.1 %invert.5.inverse_ref = f32[128,128]{1,0:T(8,128)S(1)} custom-call(f32[512,512]{1,0:T(8,128)S(1)} %update.4.h_ref), custom_call_target="tpu_custom_call" | custom-call | flops 5000000000 | bytes 100000 | tf_op jit(solution)/shard_map/invert/pallas_call | solution.py:32
  59.9 1.3 %update.5.h_ref = f32[512,512]{1,0:T(8,128)S(1)} custom-call(f32[512,512]{1,0:T(8,128)S(1)} %update.4.h_ref, f32[128,128]{1,0:T(8,128)S(1)} %invert.5.inverse_ref), custom_call_target="tpu_custom_call" | custom-call | flops 2000000000 | bytes 100000 | tf_op jit(solution)/shard_map/update/pallas_call | solution.py:32
  61.2 1.3 %collective-permute-start.14 = (f32[64,256]{1,0:T(8,128)S(1)}, f32[64,256]{1,0:T(8,128)S(1)}, u32[]{:S(2)}, u32[]{:S(2)}) collective-permute-start(f32[64,256]{1,0:T(8,128)S(1)} %stack.3.a_ref), channel_id=1, source_target_pairs={{0,8},{1,9},{2,10},{3,11},{4,12},{5,13},{6,14},{7,15},{8,0},{9,1},... | collective-permute-start | bytes 196616 | tf_op jit(solution)/shard_map/ppermute | solution.py:28
  62.5 4.3 %invert.6.inverse_ref = f32[128,128]{1,0:T(8,128)S(1)} custom-call(f32[512,512]{1,0:T(8,128)S(1)} %update.5.h_ref), custom_call_target="tpu_custom_call" | custom-call | flops 5000000000 | bytes 100000 | tf_op jit(solution)/shard_map/invert/pallas_call | solution.py:32
  66.9 1.3 %update.6.h_ref = f32[512,512]{1,0:T(8,128)S(1)} custom-call(f32[512,512]{1,0:T(8,128)S(1)} %update.5.h_ref, f32[128,128]{1,0:T(8,128)S(1)} %invert.6.inverse_ref), custom_call_target="tpu_custom_call" | custom-call | flops 2000000000 | bytes 100000 | tf_op jit(solution)/shard_map/update/pallas_call | solution.py:32
  68.3 2.1 %collective-permute-start.15 = (f32[128,256]{1,0:T(8,128)S(1)}, f32[128,256]{1,0:T(8,128)S(1)}, u32[]{:S(2)}, u32[]{:S(2)}) collective-permute-start(f32[128,256]{1,0:T(8,128)S(1)} %stack.4.a_ref), channel_id=1, source_target_pairs={{0,2},{1,3},{2,0},{3,1},{4,6},{5,7},{6,4},{7,5},{8,10},{9,11},{10,... | collective-permute-start | bytes 393224 | tf_op jit(solution)/shard_map/ppermute | solution.py:28
  70.4 4.1 %invert.7.inverse_ref = f32[128,128]{1,0:T(8,128)S(1)} custom-call(f32[512,512]{1,0:T(8,128)S(1)} %update.6.h_ref), custom_call_target="tpu_custom_call" | custom-call | flops 5000000000 | bytes 100000 | tf_op jit(solution)/shard_map/invert/pallas_call | solution.py:32
  74.5 0.1 collective-permute-start.16
  74.6 1.3 %update.7.minus_ref = f32[512,512]{1,0:T(8,128)S(1)} custom-call(f32[512,512]{1,0:T(8,128)S(1)} %update.6.h_ref, f32[128,128]{1,0:T(8,128)S(1)} %invert.7.inverse_ref), custom_call_target="tpu_custom_call" | custom-call | flops 2000000000 | bytes 100000 | tf_op jit(solution)/shard_map/update/pallas_call | solution.py:32
  75.9 0.2 collective-permute-done.16.other_ref
  76.1 4.8 %fit.1 = (f32[512,128]{1,0:T(8,128)}, f32[8,128]{1,0:T(8,128)S(1)}) custom-call(s32[1]{0:T(128)} %bitcast.shard_ref, f32[512,512]{1,0:T(8,128)S(1)} %update.7.minus_ref, f32[512,1024]{1,0:T(8,128)S(1)} %attend.1.at_ref, f32[128,512]{1,0:T(8,128)S(1)} %stack.5.own_ref, f32[128,512]{1,0:T(8,128)S(1)} %collective-permute-done.16.other_ref), custom_call_target="tpu_custom_call" | custom-call | flops 1000000000 | bytes 100000 | tf_op jit(solution)/shard_map/fit/pallas_call | solution.py:32
  80.9 1.5 %collective-permute-start.17 = (f32[8,128]{1,0:T(8,128)S(1)}, f32[8,128]{1,0:T(8,128)S(1)}, u32[]{:S(2)}, u32[]{:S(2)}) collective-permute-start(f32[8,128]{1,0:T(8,128)S(1)} %get-tuple-element.55), channel_id=1, source_target_pairs={{0,16},{16,0},{1,17},{17,1},{2,18},{18,2},{3,19},{19,3},{4,20},{20... | collective-permute-start | bytes 12296 | tf_op jit(solution)/shard_map/ppermute | solution.py:28
  82.4 2.1 %collective-permute-done.17 = f32[8,128]{1,0:T(8,128)S(1)} collective-permute-done((f32[8,128]{1,0:T(8,128)S(1)}, f32[8,128]{1,0:T(8,128)S(1)}, u32[]{:S(2)}, u32[]{:S(2)}) %collective-permute-start.17) | collective-permute-done | bytes 4128 | tf_op jit(solution)/shard_map/ppermute | solution.py:28
  84.5 0.5 slice.3
  (23 shorter events, 0.3 us)
Async XLA Ops:
  1.3 1.2 %copy-start = (bf16[1,4096,128]{2,1,0:T(8,128)(2,1)S(1)}, bf16[1,4096,128]{2,1,0:T(8,128)(2,1)}, u32[]{:S(2)}) copy-start(bf16[1,4096,128]{2,1,0:T(8,128)(2,1)} %param.6) | copy-start | bytes 3145732
  2.5 0.9 %copy-start.2 = (bf16[1,1,1024,128]{3,2,1,0:T(8,128)(2,1)S(1)}, bf16[1,1,1024,128]{3,2,1,0:T(8,128)(2,1)}, u32[]{:S(2)}) copy-start(bf16[1,1,1024,128]{3,2,1,0:T(8,128)(2,1)} %param.5) | copy-start | bytes 786436
  3.5 0.7 copy-start.3
  4.1 23.8 %copy-start.1 = (bf16[1,4096,128]{2,1,0:T(8,128)(2,1)S(1)}, bf16[1,4096,128]{2,1,0:T(8,128)(2,1)}, u32[]{:S(2)}) copy-start(bf16[1,4096,128]{2,1,0:T(8,128)(2,1)} %param.7) | copy-start | bytes 3145732
  5.5 3.2 %collective-permute-start = (bf16[384,128]{1,0:T(8,128)(2,1)S(1)}, bf16[384,128]{1,0:T(8,128)(2,1)S(1)}, u32[]{:S(2)}, u32[]{:S(2)}) collective-permute-start(bf16[384,128]{1,0:T(8,128)(2,1)S(1)} %get-tuple-element.30), channel_id=1, source_target_pairs={{0,1},{1,0},{2,3},{3,2},{4,5},{5,4},{6,7},{7,6},{8,9},{9,8},{10,11... | collective-permute-start | bytes 294920 | tf_op jit(solution)/shard_map/ppermute | solution.py:28
  6.0 6.2 %collective-permute-start.1 = (bf16[384,128]{1,0:T(8,128)(2,1)S(1)}, bf16[384,128]{1,0:T(8,128)(2,1)S(1)}, u32[]{:S(2)}, u32[]{:S(2)}) collective-permute-start(bf16[384,128]{1,0:T(8,128)(2,1)S(1)} %get-tuple-element.31), channel_id=1, source_target_pairs={{0,2},{1,3},{2,0},{3,1},{4,6},{5,7},{6,4},{7,5},{8,10},{9,11},{10,... | collective-permute-start | bytes 294920 | tf_op jit(solution)/shard_map/ppermute | solution.py:28
  8.6 5.2 %collective-permute-start.2 = (bf16[384,128]{1,0:T(8,128)(2,1)S(1)}, bf16[384,128]{1,0:T(8,128)(2,1)S(1)}, u32[]{:S(2)}, u32[]{:S(2)}) collective-permute-start(bf16[384,128]{1,0:T(8,128)(2,1)S(1)} %get-tuple-element.32), channel_id=1, source_target_pairs={{0,3},{1,2},{2,1},{3,0},{4,7},{5,6},{6,5},{7,4},{8,11},{9,10},{10,... | collective-permute-start | bytes 294920 | tf_op jit(solution)/shard_map/ppermute | solution.py:28
  13.9 7.6 %collective-permute-start.5 = (bf16[384,128]{1,0:T(8,128)(2,1)S(1)}, bf16[384,128]{1,0:T(8,128)(2,1)S(1)}, u32[]{:S(2)}, u32[]{:S(2)}) collective-permute-start(bf16[384,128]{1,0:T(8,128)(2,1)S(1)} %total.2.refs_0_), channel_id=1, source_target_pairs={{0,12},{1,13},{2,14},{3,15},{4,8},{5,9},{6,10},{7,11},{8,4},{9,5},... | collective-permute-start | bytes 294920 | tf_op jit(solution)/shard_map/ppermute | solution.py:28
  17.6 8.7 %collective-permute-start.4 = (bf16[384,128]{1,0:T(8,128)(2,1)S(1)}, bf16[384,128]{1,0:T(8,128)(2,1)S(1)}, u32[]{:S(2)}, u32[]{:S(2)}) collective-permute-start(bf16[384,128]{1,0:T(8,128)(2,1)S(1)} %total.2.refs_0_), channel_id=1, source_target_pairs={{0,8},{1,9},{2,10},{3,11},{4,12},{5,13},{6,14},{7,15},{8,0},{9,1},... | collective-permute-start | bytes 294920 | tf_op jit(solution)/shard_map/ppermute | solution.py:28
  17.6 8.7 %collective-permute-start.3 = (bf16[384,128]{1,0:T(8,128)(2,1)S(1)}, bf16[384,128]{1,0:T(8,128)(2,1)S(1)}, u32[]{:S(2)}, u32[]{:S(2)}) collective-permute-start(bf16[384,128]{1,0:T(8,128)(2,1)S(1)} %total.2.refs_0_), channel_id=1, source_target_pairs={{0,4},{1,5},{2,6},{3,7},{4,0},{5,1},{6,2},{7,3},{8,12},{9,13},{10,... | collective-permute-start | bytes 294920 | tf_op jit(solution)/shard_map/ppermute | solution.py:28
  26.4 4.7 %collective-permute-start.7 = (bf16[384,128]{1,0:T(8,128)(2,1)S(1)}, bf16[384,128]{1,0:T(8,128)(2,1)S(1)}, u32[]{:S(2)}, u32[]{:S(2)}) collective-permute-start(bf16[384,128]{1,0:T(8,128)(2,1)S(1)} %total.3.refs_0_), channel_id=1, source_target_pairs={{0,2},{1,3},{2,0},{3,1},{4,6},{5,7},{6,4},{7,5},{8,10},{9,11},{10,... | collective-permute-start | bytes 294920 | tf_op jit(solution)/shard_map/ppermute | solution.py:28
  28.3 4.9 %collective-permute-start.8 = (bf16[384,128]{1,0:T(8,128)(2,1)S(1)}, bf16[384,128]{1,0:T(8,128)(2,1)S(1)}, u32[]{:S(2)}, u32[]{:S(2)}) collective-permute-start(bf16[384,128]{1,0:T(8,128)(2,1)S(1)} %total.3.refs_0_), channel_id=1, source_target_pairs={{0,3},{1,2},{2,1},{3,0},{4,7},{5,6},{6,5},{7,4},{8,11},{9,10},{10,... | collective-permute-start | bytes 294920 | tf_op jit(solution)/shard_map/ppermute | solution.py:28
  28.4 4.8 %collective-permute-start.6 = (bf16[384,128]{1,0:T(8,128)(2,1)S(1)}, bf16[384,128]{1,0:T(8,128)(2,1)S(1)}, u32[]{:S(2)}, u32[]{:S(2)}) collective-permute-start(bf16[384,128]{1,0:T(8,128)(2,1)S(1)} %total.3.refs_0_), channel_id=1, source_target_pairs={{0,1},{1,0},{2,3},{3,2},{4,5},{5,4},{6,7},{7,6},{8,9},{9,8},{10,11... | collective-permute-start | bytes 294920 | tf_op jit(solution)/shard_map/ppermute | solution.py:28
  32.8 4.9 %collective-permute-start.9 = (f32[136,512]{1,0:T(8,128)S(1)}, f32[136,512]{1,0:T(8,128)S(1)}, u32[]{:S(2)}, u32[]{:S(2)}) collective-permute-start(f32[136,512]{1,0:T(8,128)S(1)} %attention.5), channel_id=1, source_target_pairs={{0,1},{1,0},{2,3},{3,2},{4,5},{5,4},{6,7},{7,6},{8,9},{9,8},{10,11... | collective-permute-start | bytes 835592 | tf_op jit(solution)/shard_map/ppermute | solution.py:28
  37.8 6.4 %collective-permute-start.10 = (f32[136,256]{1,0:T(8,128)S(1)}, f32[136,256]{1,0:T(8,128)S(1)}, u32[]{:S(2)}, u32[]{:S(2)}) collective-permute-start(f32[136,256]{1,0:T(8,128)S(1)} %get-tuple-element.34), channel_id=1, source_target_pairs={{0,2},{1,3},{2,0},{3,1},{4,6},{5,7},{6,4},{7,5},{8,10},{9,11},{10,... | collective-permute-start | bytes 417800 | tf_op jit(solution)/shard_map/ppermute | solution.py:28
  44.3 6.6 %collective-permute-start.11 = (f32[72,256]{1,0:T(8,128)S(1)}, f32[72,256]{1,0:T(8,128)S(1)}, u32[]{:S(2)}, u32[]{:S(2)}) collective-permute-start(f32[72,256]{1,0:T(8,128)S(1)} %get-tuple-element.38), channel_id=1, source_target_pairs={{0,8},{1,9},{2,10},{3,11},{4,12},{5,13},{6,14},{7,15},{8,0},{9,1},... | collective-permute-start | bytes 221192 | tf_op jit(solution)/shard_map/ppermute | solution.py:28
  50.9 4.1 %collective-permute-start.12 = (f32[40,256]{1,0:T(8,128)S(1)}, f32[40,256]{1,0:T(8,128)S(1)}, u32[]{:S(2)}, u32[]{:S(2)}) collective-permute-start(f32[40,256]{1,0:T(8,128)S(1)} %get-tuple-element.42), channel_id=1, source_target_pairs={{0,4},{1,5},{2,6},{3,7},{4,0},{5,1},{6,2},{7,3},{8,12},{9,13},{10,... | collective-permute-start | bytes 122888 | tf_op jit(solution)/shard_map/ppermute | solution.py:28
  55.0 4.9 %collective-permute-start.13 = (f32[32,256]{1,0:T(8,128)S(1)}, f32[32,256]{1,0:T(8,128)S(1)}, u32[]{:S(2)}, u32[]{:S(2)}) collective-permute-start(f32[32,256]{1,0:T(8,128)S(1)} %finish.1.a_ref), channel_id=1, source_target_pairs={{0,4},{1,5},{2,6},{3,7},{4,0},{5,1},{6,2},{7,3},{8,12},{9,13},{10,... | collective-permute-start | bytes 98312 | tf_op jit(solution)/shard_map/ppermute | solution.py:28
  61.2 5.7 %collective-permute-start.14 = (f32[64,256]{1,0:T(8,128)S(1)}, f32[64,256]{1,0:T(8,128)S(1)}, u32[]{:S(2)}, u32[]{:S(2)}) collective-permute-start(f32[64,256]{1,0:T(8,128)S(1)} %stack.3.a_ref), channel_id=1, source_target_pairs={{0,8},{1,9},{2,10},{3,11},{4,12},{5,13},{6,14},{7,15},{8,0},{9,1},... | collective-permute-start | bytes 196616 | tf_op jit(solution)/shard_map/ppermute | solution.py:28
  68.3 6.2 %collective-permute-start.15 = (f32[128,256]{1,0:T(8,128)S(1)}, f32[128,256]{1,0:T(8,128)S(1)}, u32[]{:S(2)}, u32[]{:S(2)}) collective-permute-start(f32[128,256]{1,0:T(8,128)S(1)} %stack.4.a_ref), channel_id=1, source_target_pairs={{0,2},{1,3},{2,0},{3,1},{4,6},{5,7},{6,4},{7,5},{8,10},{9,11},{10,... | collective-permute-start | bytes 393224 | tf_op jit(solution)/shard_map/ppermute | solution.py:28
  74.5 1.6 %collective-permute-start.16 = (f32[128,512]{1,0:T(8,128)S(1)}, f32[128,512]{1,0:T(8,128)S(1)}, u32[]{:S(2)}, u32[]{:S(2)}) collective-permute-start(f32[128,512]{1,0:T(8,128)S(1)} %stack.5.own_ref), channel_id=1, source_target_pairs={{0,1},{1,0},{2,3},{3,2},{4,5},{5,4},{6,7},{7,6},{8,9},{9,8},{10,11... | collective-permute-start | bytes 786440 | tf_op jit(solution)/shard_map/ppermute | solution.py:28
  80.9 3.6 %collective-permute-start.17 = (f32[8,128]{1,0:T(8,128)S(1)}, f32[8,128]{1,0:T(8,128)S(1)}, u32[]{:S(2)}, u32[]{:S(2)}) collective-permute-start(f32[8,128]{1,0:T(8,128)S(1)} %get-tuple-element.55), channel_id=1, source_target_pairs={{0,16},{16,0},{1,17},{17,1},{2,18},{18,2},{3,19},{19,3},{4,20},{20... | collective-permute-start | bytes 12296 | tf_op jit(solution)/shard_map/ppermute | solution.py:28

commit v5 on v4

--- a/solution.py
+++ b/solution.py
@@ -14,10 +14,10 @@
 RIDGE_SHARE = 0.01
 F32 = jnp.float32
 BF16 = jnp.bfloat16
-HIGH = lax.Precision.HIGHEST
 VMEM_LIMIT = 48 * 1024 * 1024
 VMEM = pl.BlockSpec(memory_space=pltpu.VMEM)
 SMEM = pl.BlockSpec(memory_space=pltpu.SMEM)
+HBM = pl.BlockSpec(memory_space=pltpu.HBM)
 NT = (((1,), (1,)), ((), ()))
 TN = (((0,), (0,)), ((), ()))
 NN = (((1,), (0,)), ((), ()))
@@ -43,6 +43,22 @@
 
 def aligned(value, unit):
     return pl.ds(pl.multiple_of(value * unit, unit), unit)
+
+
+def halves(array):
+    high = array.astype(BF16)
+    return high, (array - high.astype(F32)).astype(BF16)
+
+
+def dot(left, right, dims):
+    return lax.dot_general(left, right, dims, preferred_element_type=F32)
+
+
+def product(left, right, dims):
+    (high, low), (right_high, right_low) = left, right
+    rows = high.shape[0]
+    both = dot(jnp.concatenate([high, low], axis=0), right_high, dims)
+    return both[:rows] + (both[rows:] + dot(high, right_low, dims))
 
 
 def prepare_kernel(window, shard_ref, root_ref, q_hbm, kept_hbm, k_hbm, *refs):
@@ -101,7 +117,6 @@
     count = kept.shape[1]
     devices = lax.axis_size("ctx")
     tall = ((rows + count) // 4, dims)
-    anywhere = pl.BlockSpec(memory_space=pl.ANY)
     *pieces, keys = call(
         functools.partial(prepare_kernel, 4 * count // devices + 16),
         (shard, roots, queries, kept, keys),
@@ -114,7 +129,7 @@
             pltpu.SemaphoreType.DMA((6,)),
         ],
         name="prepare",
-        specs=[SMEM, SMEM, anywhere, anywhere, anywhere],
+        specs=[SMEM, SMEM, HBM, HBM, HBM],
     )
     total = lambda arrays: call(sum_kernel, arrays, [(tall, BF16)], name="total")[0]
     piece = total([pieces[0]] + [swap(pieces[s], "ctx", s) for s in (1, 2, 3)])
@@ -263,19 +278,22 @@
 
 
 def attend_kernel(score_scale, shard_ref, *refs):
-    pieces, at_ref, c_all = refs[:4], refs[4], refs[5]
-    part, rows = c_all.shape[0] // 4, at_ref.shape[1] // 4
+    pieces, (high_ref, low_ref, c_all) = refs[:4], refs[4:]
+    part, rows = c_all.shape[0] // 4, high_ref.shape[1] // 4
     places = [(shard_ref[0] % 4) ^ s for s in range(4)]
     for place, piece in zip(places, pieces):
         c_all[aligned(place, part), :] = piece[rows:, :]
     for place, piece in zip(places, pieces):
         scores = lax.dot_general(c_all[...], piece[:rows, :], NT, preferred_element_type=F32) * score_scale
         weights = jnp.exp(scores - jnp.max(scores, axis=0, keepdims=True))
-        at_ref[:, aligned(place, rows)] = weights / jnp.sum(weights, axis=0, keepdims=True)
-
-
-def gram_kernel(at_ref, h_ref):
-    gram = lax.dot_general(at_ref[...], at_ref[...], NT, precision=HIGH, preferred_element_type=F32)
+        weights = weights * (1.0 / jnp.sum(weights, axis=0, keepdims=True))
+        high_ref[:, aligned(place, rows)], low_ref[:, aligned(place, rows)] = halves(weights)
+
+
+def gram_kernel(high_ref, low_ref, h_ref):
+    high, low = high_ref[...], low_ref[...]
+    cross = dot(high, low, NT)
+    gram = dot(high, high, NT) + (dot(low, low, NT) + (cross + cross.T))
     kept = gram.shape[0]
     diagonal = lax.broadcasted_iota(jnp.int32, gram.shape, 0) == lax.broadcasted_iota(jnp.int32, gram.shape, 1)
     trace = jnp.sum(jnp.where(diagonal, gram, 0.0))
@@ -287,30 +305,37 @@
     size = count * SUB
     lane = lax.broadcasted_iota(jnp.int32, (SUB, size), 1)
     sub = lax.broadcasted_iota(jnp.int32, (SUB, size), 0)
-    spread = lambda array, column: jnp.broadcast_to(array[:, column : column + 1], (SUB, size))
+    spread_lane = lambda array, column: jnp.broadcast_to(array[:, column : column + 1], (SUB, size))
     line = lambda array, row: jnp.broadcast_to(array[row : row + 1, :], (SUB, size))
     for k in range(count):
         base = k * SUB
         inside = (lane >= base) & (lane < base + SUB)
-        columns = [spread(rows[k], base + j) for j in range(SUB)]
+        columns = [spread_lane(rows[k], base + j) for j in range(SUB)]
         work = jnp.where(inside, jnp.where(lane - base == sub, 1.0, 0.0), rows[k])
-        for j in range(SUB):
-            here = sub == j
-            inverse = 1.0 / line(columns[j], j)
-            step = lambda v: (lambda t: jnp.where(here, t, v - columns[j] * t))(line(v, j) * inverse)
-            for i in range(j + 1, SUB):
+        for j in range(0, SUB, 2):
+            first, second = columns[j], columns[j + 1]
+            a, b, c, d = line(first, j), line(second, j), line(first, j + 1), line(second, j + 1)
+            inverse = 1.0 / (a * d - b * c)
+            at_first, at_second = sub == j, sub == j + 1
+
+            def step(v):
+                upper, lower = line(v, j), line(v, j + 1)
+                new_upper = (d * upper - b * lower) * inverse
+                new_lower = (a * lower - c * upper) * inverse
+                other = v - (first * new_upper + second * new_lower)
+                return jnp.where(at_first, new_upper, jnp.where(at_second, new_lower, other))
+
+            for i in range(j + 2, SUB):
                 columns[i] = step(columns[i])
             work = step(work)
         lines = [line(work, j) for j in range(SUB)]
-        updated = []
-        for i in range(count):
-            if i == k:
-                updated.append(work)
-                continue
-            fresh = jnp.where(inside, 0.0, rows[i])
-            for j in range(SUB):
-                fresh = fresh - spread(rows[i], base + j) * lines[j]
-            updated.append(fresh)
+        updated = list(rows)
+        updated[k] = work
+        for i in list(range(k + 1, count)) + list(range(k)):
+            terms = [spread_lane(rows[i], base + j) * lines[j] for j in range(SUB)]
+            while len(terms) > 1:
+                terms = [x + y for x, y in zip(terms[::2], terms[1::2])]
+            updated[i] = jnp.where(inside, 0.0, rows[i]) - terms[0]
         rows = updated
     return rows
 
@@ -325,28 +350,38 @@
 
 def update_kernel(panel, h_ref, inverse_ref, out_ref):
     at = slice(panel * PANEL, (panel + 1) * PANEL)
-    across = h_ref[at, :]
-    turned = lax.dot_general(inverse_ref[...], across, NN, precision=HIGH, preferred_element_type=F32)
-    out_ref[...] = h_ref[...] - lax.dot_general(across, turned, TN, precision=HIGH, preferred_element_type=F32)
+    turned = product(halves(inverse_ref[...]), halves(h_ref[at, :]), NN)
+    out_ref[...] = h_ref[...] - product(halves(h_ref[:, at]), halves(turned), NN)
     out_ref[:, at] = turned.T
     out_ref[at, :] = turned
     out_ref[at, at] = -inverse_ref[...]
 
 
-def fit_kernel(shard_ref, minus_ref, at_ref, own_ref, other_ref, x_ref, err_ref, yt):
+def fit_kernel(shard_ref, minus_ref, high_ref, low_ref, own_ref, other_ref, x_ref, err_ref, yt):
     lanes = own_ref.shape[1] // 2
     place = shard_ref[0] % 4
     for s, ref in ((1, own_ref), (3, own_ref), (0, other_ref), (2, other_ref)):
         half = s // 2
         yt[:, aligned(place ^ s, lanes)] = ref[:, half * lanes : (half + 1) * lanes]
     target = yt[...]
-    attend = at_ref[...]
-    cross = lax.dot_general(target, attend, NT, precision=HIGH, preferred_element_type=F32)
-    fitted = -lax.dot_general(cross, minus_ref[...], NN, precision=HIGH, preferred_element_type=F32)
-    x_ref[...] = fitted.T
-    misfit = lax.dot_general(fitted, attend, NN, precision=HIGH, preferred_element_type=F32) - target
+    attend = high_ref[...], low_ref[...]
+    cross = product(halves(target), attend, NT)
+    fitted = -product(halves(cross), halves(minus_ref[...]), NN)
+    x_ref[...] = fitted
+    misfit = product(halves(fitted), attend, NN) - target
     error = jnp.sum(misfit * misfit) / jnp.sum(target * target)
     err_ref[...] = jnp.full(err_ref.shape, error, F32)
+
+
+def flip_kernel(x_ref, out_ref):
+    out_ref[...] = x_ref[...].T
+
+
+def mean_kernel(heads, *refs):
+    total = refs[0][:1, :1]
+    for ref in refs[1:-1]:
+        total = total + ref[:1, :1]
+    refs[-1][...] = total / heads
 
 
 def per_device(queries, keys, values, kept, roots):
@@ -377,15 +412,15 @@
         return arrays
 
     system_shape = ((count, count), F32)
-    (attend,) = call(
+    attend = call(
         functools.partial(attend_kernel, score_scale),
         (shard, *pieces),
-        [((count, rows), F32)],
+        [((count, rows), BF16)] * 2,
         10**9,
         scratch=[pltpu.VMEM((count, dims), BF16)],
         name="attend",
     )
-    (system,) = call(gram_kernel, (attend,), [system_shape], 4 * 10**9, name="gram")
+    (system,) = call(gram_kernel, attend, [system_shape], 4 * 10**9, name="gram")
     system = beside(system)
     panels = count // PANEL
     for panel in range(panels):
@@ -401,20 +436,24 @@
     while ends is None:
         system = beside(system)
 
-    compact, error = call(
+    turned_fit, error = call(
         fit_kernel,
-        (shard, system, attend, *ends),
-        [((count, dims), F32), ((SUB, 128), F32)],
+        (shard, system, *attend, *ends),
+        [((dims, count), F32), ((SUB, 128), F32)],
         10**9,
         scratch=[pltpu.VMEM((dims, rows), F32)],
         name="fit",
     )
     heads = lax.axis_size("head")
-    step = 1
+    errors, step = [error], 1
     while step < heads:
-        error = error + swap(error, "head", step)
+        if len(errors) > 1:
+            errors = list(call(sum_kernel, errors, [((SUB, 128), F32)], name="total"))
+        errors.append(swap(errors[0], "head", step))
         step *= 2
-    return (compact[None], error[0, 0] / heads)
+    (compact,) = call(flip_kernel, (turned_fit,), [((count, dims), F32)], 10**6, name="flip")
+    (error,) = call(functools.partial(mean_kernel, heads), errors, [((1, 1), F32)], name="mean")
+    return (compact[None], error.reshape(()))
 
 
 def solution(mesh):

time: 87 us -> 82 us (0.943)
  Pallas kernels: 40.8 us -> 35.7 us
  waiting for transfers between devices: 20.7 us -> 22.5 us
  between operations: 3.28 us -> 1.49 us
    pallas_call x25 -> x27, Pallas kernels: 40.8 us -> 35.7 us  [call(): pl.pallas_call(kernel, in_specs=specs or [SMEM if x.size == 1 else VMEM f...]
    ppermute x18, waiting for transfers between devices: 20.7 us -> 22.5 us  [swap(): return lax.ppermute(array, axis, [(i, i ^ step) for i in range(size)])]
where the time goes in v5:
time: 82 us; the launch traced here: 81.8 us
  Pallas kernels  35.7 us (44%)
  waiting for transfers between devices  22.5 us (27%)
  starting transfers between devices  19.2 us (23%)
  local copies, waits for them, and re-layouts  2.85 us (3%)
  between operations  1.49 us (2%)
    pallas_call x27, Pallas kernels, call(): pl.pallas_call(kernel, in_specs=specs or [SMEM if x.size == 1 else VMEM f...  35.7 us
    ppermute x18, waiting for transfers between devices, swap(): return lax.ppermute(array, axis, [(i, i ^ step) for i in range(size)])  22.5 us
    ppermute x18, starting transfers between devices, swap(): return lax.ppermute(array, axis, [(i, i ^ step) for i in range(size)])  19.2 us
    unnamed x8, local copies, waits for them, and re-layouts  2.85 us
  transfers between devices with their start and end apart: 18, of which 11 were waited for; matrix products, arithmetic and copies ran while one was open for 0% of the time, Pallas kernels for 37%

profile of v5, /device:TPU:0, one launch (start us, length us, event | category | flops | bytes accessed | tf_op | source)
XLA Modules:
  0.0 81.8 jit_solution(5110142839064304402)
XLA Ops:
  1.3 1.2 %copy-done = bf16[1,4096,128]{2,1,0:T(8,128)(2,1)S(1)} copy-done((bf16[1,4096,128]{2,1,0:T(8,128)(2,1)S(1)}, bf16[1,4096,128]{2,1,0:T(8,128)(2,1)}, u32[]{:S(2)}) %copy-start) | copy-done | bytes 1048600
  2.5 0.9 %copy-done.2 = bf16[1,1,1024,128]{3,2,1,0:T(8,128)(2,1)S(1)} copy-done((bf16[1,1,1024,128]{3,2,1,0:T(8,128)(2,1)S(1)}, bf16[1,1,1024,128]{3,2,1,0:T(8,128)(2,1)}, u32[]{:S(2)}) %copy-start.2) | copy-done | bytes 262168
  3.5 0.7 copy-done.3
  4.1 1.4 %prepare.1 = (bf16[384,128]{1,0:T(8,128)(2,1)S(1)}, bf16[384,128]{1,0:T(8,128)(2,1)S(1)}, bf16[384,128]{1,0:T(8,128)(2,1)S(1)}, bf16[384,128]{1,0:T(8,128)(2,1)S(1)}, bf16[4096,128]{1,0:T(8,128)(2,1)S(1)}) custom-call(s32[1]{0:T(128)} %bitcast.shard_ref, s32[1]{0:T(128)S(6)} %copy.7.root_ref, bf16[1024,128]{1,0:T(8,128)(2,1)S(1)} %bitcast.8, ...), custom_call_target="tpu_custom_call" | custom-call | flops 100000 | bytes 100000 | tf_op jit(solution)/shard_map/prepare/pallas_call | solution.py:32
  5.5 0.5 collective-permute-start
  6.0 2.6 %collective-permute-start.1 = (bf16[384,128]{1,0:T(8,128)(2,1)S(1)}, bf16[384,128]{1,0:T(8,128)(2,1)S(1)}, u32[]{:S(2)}, u32[]{:S(2)}) collective-permute-start(bf16[384,128]{1,0:T(8,128)(2,1)S(1)} %get-tuple-element.33), channel_id=1, source_target_pairs={{0,2},{1,3},{2,0},{3,1},{4,6},{5,7},{6,4},{7,5},{8,10},{9,11},{10,... | collective-permute-start | bytes 294920 | tf_op jit(solution)/shard_map/ppermute | solution.py:28
  8.7 3.6 %collective-permute-done.1.refs_2_ = bf16[384,128]{1,0:T(8,128)(2,1)S(1)} collective-permute-done((bf16[384,128]{1,0:T(8,128)(2,1)S(1)}, bf16[384,128]{1,0:T(8,128)(2,1)S(1)}, u32[]{:S(2)}, u32[]{:S(2)}) %collective-permute-start.1) | collective-permute-done | bytes 98336 | tf_op jit(solution)/shard_map/ppermute | solution.py:28
  12.3 1.6 %collective-permute-done.2.refs_3_ = bf16[384,128]{1,0:T(8,128)(2,1)S(1)} collective-permute-done((bf16[384,128]{1,0:T(8,128)(2,1)S(1)}, bf16[384,128]{1,0:T(8,128)(2,1)S(1)}, u32[]{:S(2)}, u32[]{:S(2)}) %collective-permute-start.2) | collective-permute-done | bytes 98336 | tf_op jit(solution)/shard_map/ppermute | solution.py:28
  13.9 3.7 %collective-permute-start.5 = (bf16[384,128]{1,0:T(8,128)(2,1)S(1)}, bf16[384,128]{1,0:T(8,128)(2,1)S(1)}, u32[]{:S(2)}, u32[]{:S(2)}) collective-permute-start(bf16[384,128]{1,0:T(8,128)(2,1)S(1)} %total.2.refs_0_), channel_id=1, source_target_pairs={{0,12},{1,13},{2,14},{3,15},{4,8},{5,9},{6,10},{7,11},{8,4},{9,5},... | collective-permute-start | bytes 294920 | tf_op jit(solution)/shard_map/ppermute | solution.py:28
  17.6 0.7 collective-permute-start.3
  18.3 3.1 %collective-permute-done.5.refs_3_ = bf16[384,128]{1,0:T(8,128)(2,1)S(1)} collective-permute-done((bf16[384,128]{1,0:T(8,128)(2,1)S(1)}, bf16[384,128]{1,0:T(8,128)(2,1)S(1)}, u32[]{:S(2)}, u32[]{:S(2)}) %collective-permute-start.5) | collective-permute-done | bytes 98336 | tf_op jit(solution)/shard_map/ppermute | solution.py:28
  21.5 4.8 %collective-permute-done.4.refs_2_ = bf16[384,128]{1,0:T(8,128)(2,1)S(1)} collective-permute-done((bf16[384,128]{1,0:T(8,128)(2,1)S(1)}, bf16[384,128]{1,0:T(8,128)(2,1)S(1)}, u32[]{:S(2)}, u32[]{:S(2)}) %collective-permute-start.4) | collective-permute-done | bytes 98336 | tf_op jit(solution)/shard_map/ppermute | solution.py:28
  26.4 1.6 %collective-permute-start.7 = (bf16[384,128]{1,0:T(8,128)(2,1)S(1)}, bf16[384,128]{1,0:T(8,128)(2,1)S(1)}, u32[]{:S(2)}, u32[]{:S(2)}) collective-permute-start(bf16[384,128]{1,0:T(8,128)(2,1)S(1)} %total.3.refs_0_), channel_id=1, source_target_pairs={{0,2},{1,3},{2,0},{3,1},{4,6},{5,7},{6,4},{7,5},{8,10},{9,11},{10,... | collective-permute-start | bytes 294920 | tf_op jit(solution)/shard_map/ppermute | solution.py:28
  27.9 0.3 turn.1.refs_3_.refs_2_
  28.3 0.1 collective-permute-start.8
  28.4 0.6 collective-permute-start.6
  29.0 1.8 %attention.4.refs_3_ = f32[136,256]{1,0:T(8,128)S(1)} custom-call(bf16[384,128]{1,0:T(8,128)(2,1)S(1)} %total.3.refs_0_, bf16[4096,128]{1,0:T(8,128)(2,1)S(1)} %get-tuple-element.37.refs_2_.refs_1_, bf16[144,4096]{1,0:T(8,128)(2,1)S(1)} %turn.1.refs_3_.refs_2_), custom_call_target="tpu_custom_call" | custom-call | flops 536870912 | bytes 100000 | tf_op jit(solution)/shard_map/attention/pallas_call | solution.py:32
  30.8 0.3 collective-permute-done.7.refs_2_.refs_0_
  31.0 1.8 %attention.5 = f32[136,512]{1,0:T(8,128)S(1)} custom-call(bf16[384,128]{1,0:T(8,128)(2,1)S(1)} %collective-permute-done.7.refs_2_.refs_0_, bf16[4096,128]{1,0:T(8,128)(2,1)S(1)} %get-tuple-element.37.refs_2_.refs_1_, bf16[144,4096]{1,0:T(8,128)(2,1)S(1)} %turn.1.refs_3_.refs_2_, f32[136,256]{1,0:T(8,128)S(1)} %attention.4.refs_3_), custom_call_target="tpu_custom_call" | custom-call | flops 536870912 | bytes 100000 | tf_op jit(solution)/shard_map/attention/pallas_call | solution.py:32
  32.8 0.1 collective-permute-start.9
  32.9 0.2 collective-permute-done.8.refs_3_.refs_1_
  33.1 1.5 %attend.1 = (bf16[512,1024]{1,0:T(8,128)(2,1)S(1)}, bf16[512,1024]{1,0:T(8,128)(2,1)S(1)}) custom-call(s32[1]{0:T(128)} %bitcast.shard_ref, bf16[384,128]{1,0:T(8,128)(2,1)S(1)} %total.3.refs_0_, bf16[384,128]{1,0:T(8,128)(2,1)S(1)} %collective-permute-done.6.refs_1_.refs_0_, bf16[384,128]{1,0:T(8,128)(2,1)S(1)} %collective-permute-done.7.refs_2_.refs_0_, ...), custom_call_target="tpu_custom_call" | custom-call | flops 1000000000 | bytes 100000 | tf_op jit(solution)/shard_map/attend/pallas_call | solution.py:32
  34.7 3.4 %attention.3.a_ref = f32[136,512]{1,0:T(8,128)S(1)} custom-call(bf16[384,128]{1,0:T(8,128)(2,1)S(1)} %collective-permute-done.6.refs_1_.refs_0_, bf16[384,128]{1,0:T(8,128)(2,1)S(1)} %collective-permute-done.8.refs_3_.refs_1_, bf16[4096,128]{1,0:T(8,128)(2,1)S(1)} %get-tuple-element.37.refs_2_.refs_1_, bf16[144,4096]{1,0:T(8,128)(2,1)S(1)} %turn.1.refs_3_.refs_2_), custom_call_target="tpu_custom_call" | custom-call | flops 1073741824 | bytes 100000 | tf_op jit(solution)/shard_map/attention/pallas_call | solution.py:32
  38.2 2.1 %collective-permute-start.10 = (f32[136,256]{1,0:T(8,128)S(1)}, f32[136,256]{1,0:T(8,128)S(1)}, u32[]{:S(2)}, u32[]{:S(2)}) collective-permute-start(f32[136,256]{1,0:T(8,128)S(1)} %get-tuple-element.38), channel_id=1, source_target_pairs={{0,2},{1,3},{2,0},{3,1},{4,6},{5,7},{6,4},{7,5},{8,10},{9,11},{10,... | collective-permute-start | bytes 417800 | tf_op jit(solution)/shard_map/ppermute | solution.py:28
  40.3 2.0 %gram.1.h_ref = f32[512,512]{1,0:T(8,128)S(1)} custom-call(bf16[512,1024]{1,0:T(8,128)(2,1)S(1)} %get-tuple-element.35.high_ref, bf16[512,1024]{1,0:T(8,128)(2,1)S(1)} %get-tuple-element.36.low_ref), custom_call_target="tpu_custom_call" | custom-call | flops 4000000000 | bytes 100000 | tf_op jit(solution)/shard_map/gram/pallas_call | solution.py:32
  42.3 2.3 %collective-permute-done.10.b_ref = f32[136,256]{1,0:T(8,128)S(1)} collective-permute-done((f32[136,256]{1,0:T(8,128)S(1)}, f32[136,256]{1,0:T(8,128)S(1)}, u32[]{:S(2)}, u32[]{:S(2)}) %collective-permute-start.10) | collective-permute-done | bytes 139296 | tf_op jit(solution)/shard_map/ppermute | solution.py:28
  44.7 0.2 collective-permute-start.11
  44.9 4.3 %invert.4.inverse_ref = f32[128,128]{1,0:T(8,128)S(1)} custom-call(f32[512,512]{1,0:T(8,128)S(1)} %gram.1.h_ref), custom_call_target="tpu_custom_call" | custom-call | flops 5000000000 | bytes 100000 | tf_op jit(solution)/shard_map/invert/pallas_call | solution.py:32
  49.1 2.1 %collective-permute-done.11.b_ref = f32[72,256]{1,0:T(8,128)S(1)} collective-permute-done((f32[72,256]{1,0:T(8,128)S(1)}, f32[72,256]{1,0:T(8,128)S(1)}, u32[]{:S(2)}, u32[]{:S(2)}) %collective-permute-start.11) | collective-permute-done | bytes 73760 | tf_op jit(solution)/shard_map/ppermute | solution.py:28
  51.3 0.9 %collective-permute-start.12 = (f32[40,256]{1,0:T(8,128)S(1)}, f32[40,256]{1,0:T(8,128)S(1)}, u32[]{:S(2)}, u32[]{:S(2)}) collective-permute-start(f32[40,256]{1,0:T(8,128)S(1)} %get-tuple-element.46), channel_id=1, source_target_pairs={{0,4},{1,5},{2,6},{3,7},{4,0},{5,1},{6,2},{7,3},{8,12},{9,13},{10,... | collective-permute-start | bytes 122888 | tf_op jit(solution)/shard_map/ppermute | solution.py:28
  52.1 0.8 update.4.h_ref
  53.0 2.4 %collective-permute-done.12.b_ref = f32[40,256]{1,0:T(8,128)S(1)} collective-permute-done((f32[40,256]{1,0:T(8,128)S(1)}, f32[40,256]{1,0:T(8,128)S(1)}, u32[]{:S(2)}, u32[]{:S(2)}) %collective-permute-start.12) | collective-permute-done | bytes 40992 | tf_op jit(solution)/shard_map/ppermute | solution.py:28
  55.4 0.9 %collective-permute-start.13 = (f32[32,256]{1,0:T(8,128)S(1)}, f32[32,256]{1,0:T(8,128)S(1)}, u32[]{:S(2)}, u32[]{:S(2)}) collective-permute-start(f32[32,256]{1,0:T(8,128)S(1)} %finish.1.a_ref), channel_id=1, source_target_pairs={{0,4},{1,5},{2,6},{3,7},{4,0},{5,1},{6,2},{7,3},{8,12},{9,13},{10,... | collective-permute-start | bytes 98312 | tf_op jit(solution)/shard_map/ppermute | solution.py:28
  56.2 4.1 %invert.5.inverse_ref = f32[128,128]{1,0:T(8,128)S(1)} custom-call(f32[512,512]{1,0:T(8,128)S(1)} %update.4.h_ref), custom_call_target="tpu_custom_call" | custom-call | flops 5000000000 | bytes 100000 | tf_op jit(solution)/shard_map/invert/pallas_call | solution.py:32
  60.3 0.8 update.5.h_ref
  61.2 1.2 %collective-permute-start.14 = (f32[64,256]{1,0:T(8,128)S(1)}, f32[64,256]{1,0:T(8,128)S(1)}, u32[]{:S(2)}, u32[]{:S(2)}) collective-permute-start(f32[64,256]{1,0:T(8,128)S(1)} %stack.3.a_ref), channel_id=1, source_target_pairs={{0,8},{1,9},{2,10},{3,11},{4,12},{5,13},{6,14},{7,15},{8,0},{9,1},... | collective-permute-start | bytes 196616 | tf_op jit(solution)/shard_map/ppermute | solution.py:28
  62.3 4.1 %invert.6.inverse_ref = f32[128,128]{1,0:T(8,128)S(1)} custom-call(f32[512,512]{1,0:T(8,128)S(1)} %update.5.h_ref), custom_call_target="tpu_custom_call" | custom-call | flops 5000000000 | bytes 100000 | tf_op jit(solution)/shard_map/invert/pallas_call | solution.py:32
  66.4 0.8 update.6.h_ref
  67.3 2.5 %collective-permute-start.15 = (f32[128,256]{1,0:T(8,128)S(1)}, f32[128,256]{1,0:T(8,128)S(1)}, u32[]{:S(2)}, u32[]{:S(2)}) collective-permute-start(f32[128,256]{1,0:T(8,128)S(1)} %stack.4.a_ref), channel_id=1, source_target_pairs={{0,2},{1,3},{2,0},{3,1},{4,6},{5,7},{6,4},{7,5},{8,10},{9,11},{10,... | collective-permute-start | bytes 393224 | tf_op jit(solution)/shard_map/ppermute | solution.py:28
  69.7 4.3 %invert.7.inverse_ref = f32[128,128]{1,0:T(8,128)S(1)} custom-call(f32[512,512]{1,0:T(8,128)S(1)} %update.6.h_ref), custom_call_target="tpu_custom_call" | custom-call | flops 5000000000 | bytes 100000 | tf_op jit(solution)/shard_map/invert/pallas_call | solution.py:32
  74.1 0.1 collective-permute-start.16
  74.1 0.8 update.7.minus_ref
  74.9 0.7 collective-permute-done.16.other_ref
  75.7 1.9 %fit.1 = (f32[128,512]{1,0:T(8,128)S(1)}, f32[8,128]{1,0:T(8,128)S(1)}) custom-call(s32[1]{0:T(128)} %bitcast.shard_ref, f32[512,512]{1,0:T(8,128)S(1)} %update.7.minus_ref, bf16[512,1024]{1,0:T(8,128)(2,1)S(1)} %get-tuple-element.35.high_ref, bf16[512,1024]{1,0:T(8,128)(2,1)S(1)} %get-tuple-element.36.low_ref, f32[128,512]{1,0:T(8,128)S(1)} %stack.5.own_ref, ...), custom_call_target="tpu_custom_call" | custom-call | flops 1000000000 | bytes 100000 | tf_op jit(solution)/shard_map/fit/pallas_call | solution.py:32
  77.6 1.6 %collective-permute-start.17 = (f32[8,128]{1,0:T(8,128)S(1)}, f32[8,128]{1,0:T(8,128)S(1)}, u32[]{:S(2)}, u32[]{:S(2)}) collective-permute-start(f32[8,128]{1,0:T(8,128)S(1)} %get-tuple-element.59.refs_0_), channel_id=1, source_target_pairs={{0,16},{16,0},{1,17},{17,1},{2,18},{18,2},{3,19},{19,3},{4,20},{20... | collective-permute-start | bytes 12296 | tf_op jit(solution)/shard_map/ppermute | solution.py:28
  79.1 0.8 %flip.1 = f32[512,128]{1,0:T(8,128)} custom-call(f32[128,512]{1,0:T(8,128)S(1)} %get-tuple-element.58.x_ref), custom_call_target="tpu_custom_call" | custom-call | flops 1000000 | bytes 100000 | tf_op jit(solution)/shard_map/flip/pallas_call | solution.py:32
  80.0 1.3 %collective-permute-done.17.refs_1_ = f32[8,128]{1,0:T(8,128)S(1)} collective-permute-done((f32[8,128]{1,0:T(8,128)S(1)}, f32[8,128]{1,0:T(8,128)S(1)}, u32[]{:S(2)}, u32[]{:S(2)}) %collective-permute-start.17) | collective-permute-done | bytes 4128 | tf_op jit(solution)/shard_map/ppermute | solution.py:28
  81.3 0.5 mean.1
  (23 shorter events, 0.4 us)
Async XLA Ops:
  1.3 1.2 %copy-start = (bf16[1,4096,128]{2,1,0:T(8,128)(2,1)S(1)}, bf16[1,4096,128]{2,1,0:T(8,128)(2,1)}, u32[]{:S(2)}) copy-start(bf16[1,4096,128]{2,1,0:T(8,128)(2,1)} %param.6) | copy-start | bytes 3145732
  2.5 0.9 %copy-start.2 = (bf16[1,1,1024,128]{3,2,1,0:T(8,128)(2,1)S(1)}, bf16[1,1,1024,128]{3,2,1,0:T(8,128)(2,1)}, u32[]{:S(2)}) copy-start(bf16[1,1,1024,128]{3,2,1,0:T(8,128)(2,1)} %param.5) | copy-start | bytes 786436
  3.5 0.7 copy-start.3
  4.1 23.8 %copy-start.1 = (bf16[1,4096,128]{2,1,0:T(8,128)(2,1)S(1)}, bf16[1,4096,128]{2,1,0:T(8,128)(2,1)}, u32[]{:S(2)}) copy-start(bf16[1,4096,128]{2,1,0:T(8,128)(2,1)} %param.7) | copy-start | bytes 3145732
  5.5 3.2 %collective-permute-start = (bf16[384,128]{1,0:T(8,128)(2,1)S(1)}, bf16[384,128]{1,0:T(8,128)(2,1)S(1)}, u32[]{:S(2)}, u32[]{:S(2)}) collective-permute-start(bf16[384,128]{1,0:T(8,128)(2,1)S(1)} %get-tuple-element.32), channel_id=1, source_target_pairs={{0,1},{1,0},{2,3},{3,2},{4,5},{5,4},{6,7},{7,6},{8,9},{9,8},{10,11... | collective-permute-start | bytes 294920 | tf_op jit(solution)/shard_map/ppermute | solution.py:28
  6.0 6.2 %collective-permute-start.1 = (bf16[384,128]{1,0:T(8,128)(2,1)S(1)}, bf16[384,128]{1,0:T(8,128)(2,1)S(1)}, u32[]{:S(2)}, u32[]{:S(2)}) collective-permute-start(bf16[384,128]{1,0:T(8,128)(2,1)S(1)} %get-tuple-element.33), channel_id=1, source_target_pairs={{0,2},{1,3},{2,0},{3,1},{4,6},{5,7},{6,4},{7,5},{8,10},{9,11},{10,... | collective-permute-start | bytes 294920 | tf_op jit(solution)/shard_map/ppermute | solution.py:28
  8.6 5.2 %collective-permute-start.2 = (bf16[384,128]{1,0:T(8,128)(2,1)S(1)}, bf16[384,128]{1,0:T(8,128)(2,1)S(1)}, u32[]{:S(2)}, u32[]{:S(2)}) collective-permute-start(bf16[384,128]{1,0:T(8,128)(2,1)S(1)} %get-tuple-element.34), channel_id=1, source_target_pairs={{0,3},{1,2},{2,1},{3,0},{4,7},{5,6},{6,5},{7,4},{8,11},{9,10},{10,... | collective-permute-start | bytes 294920 | tf_op jit(solution)/shard_map/ppermute | solution.py:28
  13.9 7.6 %collective-permute-start.5 = (bf16[384,128]{1,0:T(8,128)(2,1)S(1)}, bf16[384,128]{1,0:T(8,128)(2,1)S(1)}, u32[]{:S(2)}, u32[]{:S(2)}) collective-permute-start(bf16[384,128]{1,0:T(8,128)(2,1)S(1)} %total.2.refs_0_), channel_id=1, source_target_pairs={{0,12},{1,13},{2,14},{3,15},{4,8},{5,9},{6,10},{7,11},{8,4},{9,5},... | collective-permute-start | bytes 294920 | tf_op jit(solution)/shard_map/ppermute | solution.py:28
  17.6 8.7 %collective-permute-start.4 = (bf16[384,128]{1,0:T(8,128)(2,1)S(1)}, bf16[384,128]{1,0:T(8,128)(2,1)S(1)}, u32[]{:S(2)}, u32[]{:S(2)}) collective-permute-start(bf16[384,128]{1,0:T(8,128)(2,1)S(1)} %total.2.refs_0_), channel_id=1, source_target_pairs={{0,8},{1,9},{2,10},{3,11},{4,12},{5,13},{6,14},{7,15},{8,0},{9,1},... | collective-permute-start | bytes 294920 | tf_op jit(solution)/shard_map/ppermute | solution.py:28
  17.6 8.7 %collective-permute-start.3 = (bf16[384,128]{1,0:T(8,128)(2,1)S(1)}, bf16[384,128]{1,0:T(8,128)(2,1)S(1)}, u32[]{:S(2)}, u32[]{:S(2)}) collective-permute-start(bf16[384,128]{1,0:T(8,128)(2,1)S(1)} %total.2.refs_0_), channel_id=1, source_target_pairs={{0,4},{1,5},{2,6},{3,7},{4,0},{5,1},{6,2},{7,3},{8,12},{9,13},{10,... | collective-permute-start | bytes 294920 | tf_op jit(solution)/shard_map/ppermute | solution.py:28
  26.4 4.7 %collective-permute-start.7 = (bf16[384,128]{1,0:T(8,128)(2,1)S(1)}, bf16[384,128]{1,0:T(8,128)(2,1)S(1)}, u32[]{:S(2)}, u32[]{:S(2)}) collective-permute-start(bf16[384,128]{1,0:T(8,128)(2,1)S(1)} %total.3.refs_0_), channel_id=1, source_target_pairs={{0,2},{1,3},{2,0},{3,1},{4,6},{5,7},{6,4},{7,5},{8,10},{9,11},{10,... | collective-permute-start | bytes 294920 | tf_op jit(solution)/shard_map/ppermute | solution.py:28
  28.3 4.9 %collective-permute-start.8 = (bf16[384,128]{1,0:T(8,128)(2,1)S(1)}, bf16[384,128]{1,0:T(8,128)(2,1)S(1)}, u32[]{:S(2)}, u32[]{:S(2)}) collective-permute-start(bf16[384,128]{1,0:T(8,128)(2,1)S(1)} %total.3.refs_0_), channel_id=1, source_target_pairs={{0,3},{1,2},{2,1},{3,0},{4,7},{5,6},{6,5},{7,4},{8,11},{9,10},{10,... | collective-permute-start | bytes 294920 | tf_op jit(solution)/shard_map/ppermute | solution.py:28
  28.4 4.8 %collective-permute-start.6 = (bf16[384,128]{1,0:T(8,128)(2,1)S(1)}, bf16[384,128]{1,0:T(8,128)(2,1)S(1)}, u32[]{:S(2)}, u32[]{:S(2)}) collective-permute-start(bf16[384,128]{1,0:T(8,128)(2,1)S(1)} %total.3.refs_0_), channel_id=1, source_target_pairs={{0,1},{1,0},{2,3},{3,2},{4,5},{5,4},{6,7},{7,6},{8,9},{9,8},{10,11... | collective-permute-start | bytes 294920 | tf_op jit(solution)/shard_map/ppermute | solution.py:28
  32.8 5.3 %collective-permute-start.9 = (f32[136,512]{1,0:T(8,128)S(1)}, f32[136,512]{1,0:T(8,128)S(1)}, u32[]{:S(2)}, u32[]{:S(2)}) collective-permute-start(f32[136,512]{1,0:T(8,128)S(1)} %attention.5), channel_id=1, source_target_pairs={{0,1},{1,0},{2,3},{3,2},{4,5},{5,4},{6,7},{7,6},{8,9},{9,8},{10,11... | collective-permute-start | bytes 835592 | tf_op jit(solution)/shard_map/ppermute | solution.py:28
  38.2 6.4 %collective-permute-start.10 = (f32[136,256]{1,0:T(8,128)S(1)}, f32[136,256]{1,0:T(8,128)S(1)}, u32[]{:S(2)}, u32[]{:S(2)}) collective-permute-start(f32[136,256]{1,0:T(8,128)S(1)} %get-tuple-element.38), channel_id=1, source_target_pairs={{0,2},{1,3},{2,0},{3,1},{4,6},{5,7},{6,4},{7,5},{8,10},{9,11},{10,... | collective-permute-start | bytes 417800 | tf_op jit(solution)/shard_map/ppermute | solution.py:28
  44.7 6.6 %collective-permute-start.11 = (f32[72,256]{1,0:T(8,128)S(1)}, f32[72,256]{1,0:T(8,128)S(1)}, u32[]{:S(2)}, u32[]{:S(2)}) collective-permute-start(f32[72,256]{1,0:T(8,128)S(1)} %get-tuple-element.42), channel_id=1, source_target_pairs={{0,8},{1,9},{2,10},{3,11},{4,12},{5,13},{6,14},{7,15},{8,0},{9,1},... | collective-permute-start | bytes 221192 | tf_op jit(solution)/shard_map/ppermute | solution.py:28
  51.3 4.1 %collective-permute-start.12 = (f32[40,256]{1,0:T(8,128)S(1)}, f32[40,256]{1,0:T(8,128)S(1)}, u32[]{:S(2)}, u32[]{:S(2)}) collective-permute-start(f32[40,256]{1,0:T(8,128)S(1)} %get-tuple-element.46), channel_id=1, source_target_pairs={{0,4},{1,5},{2,6},{3,7},{4,0},{5,1},{6,2},{7,3},{8,12},{9,13},{10,... | collective-permute-start | bytes 122888 | tf_op jit(solution)/shard_map/ppermute | solution.py:28
  55.4 4.9 %collective-permute-start.13 = (f32[32,256]{1,0:T(8,128)S(1)}, f32[32,256]{1,0:T(8,128)S(1)}, u32[]{:S(2)}, u32[]{:S(2)}) collective-permute-start(f32[32,256]{1,0:T(8,128)S(1)} %finish.1.a_ref), channel_id=1, source_target_pairs={{0,4},{1,5},{2,6},{3,7},{4,0},{5,1},{6,2},{7,3},{8,12},{9,13},{10,... | collective-permute-start | bytes 98312 | tf_op jit(solution)/shard_map/ppermute | solution.py:28
  61.2 5.3 %collective-permute-start.14 = (f32[64,256]{1,0:T(8,128)S(1)}, f32[64,256]{1,0:T(8,128)S(1)}, u32[]{:S(2)}, u32[]{:S(2)}) collective-permute-start(f32[64,256]{1,0:T(8,128)S(1)} %stack.3.a_ref), channel_id=1, source_target_pairs={{0,8},{1,9},{2,10},{3,11},{4,12},{5,13},{6,14},{7,15},{8,0},{9,1},... | collective-permute-start | bytes 196616 | tf_op jit(solution)/shard_map/ppermute | solution.py:28
  67.3 6.8 %collective-permute-start.15 = (f32[128,256]{1,0:T(8,128)S(1)}, f32[128,256]{1,0:T(8,128)S(1)}, u32[]{:S(2)}, u32[]{:S(2)}) collective-permute-start(f32[128,256]{1,0:T(8,128)S(1)} %stack.4.a_ref), channel_id=1, source_target_pairs={{0,2},{1,3},{2,0},{3,1},{4,6},{5,7},{6,4},{7,5},{8,10},{9,11},{10,... | collective-permute-start | bytes 393224 | tf_op jit(solution)/shard_map/ppermute | solution.py:28
  74.1 1.6 %collective-permute-start.16 = (f32[128,512]{1,0:T(8,128)S(1)}, f32[128,512]{1,0:T(8,128)S(1)}, u32[]{:S(2)}, u32[]{:S(2)}) collective-permute-start(f32[128,512]{1,0:T(8,128)S(1)} %stack.5.own_ref), channel_id=1, source_target_pairs={{0,1},{1,0},{2,3},{3,2},{4,5},{5,4},{6,7},{7,6},{8,9},{9,8},{10,11... | collective-permute-start | bytes 786440 | tf_op jit(solution)/shard_map/ppermute | solution.py:28
  77.6 3.7 %collective-permute-start.17 = (f32[8,128]{1,0:T(8,128)S(1)}, f32[8,128]{1,0:T(8,128)S(1)}, u32[]{:S(2)}, u32[]{:S(2)}) collective-permute-start(f32[8,128]{1,0:T(8,128)S(1)} %get-tuple-element.59.refs_0_), channel_id=1, source_target_pairs={{0,16},{16,0},{1,17},{17,1},{2,18},{18,2},{3,19},{19,3},{4,20},{20... | collective-permute-start | bytes 12296 | tf_op jit(solution)/shard_map/ppermute | solution.py:28

commit v6 on v5

--- a/solution.py
+++ b/solution.py
@@ -9,7 +9,7 @@
 from jax.sharding import PartitionSpec as P
 
 KBLK = 1024
-PANEL = 128
+PANEL = 64
 SUB = 8
 RIDGE_SHARE = 0.01
 F32 = jnp.float32
@@ -62,7 +62,7 @@
 
 
 def prepare_kernel(window, shard_ref, root_ref, q_hbm, kept_hbm, k_hbm, *refs):
-    outs, k_ref, (q_ref, kept_ref, spots, picked, sems) = refs[:4], refs[4], refs[5:]
+    keep_ref, send_ref, k_ref, q_ref, kept_ref, spots, picked, sems = refs
     slab, dims = k_ref.shape
     kept = kept_ref.shape[1]
     steps = sems.shape[0] - 2
@@ -98,11 +98,13 @@
     loads[-1].wait()
     share, part = q_ref.shape[0] // 4, kept // 4
     is_root = shard_ref[0] == root_ref[0]
-    for s, out in enumerate(outs):
+    tall = share + part
+    for s in range(4):
+        out, at = (keep_ref, send_ref)[s % 2], s // 2 * tall
         place = (shard_ref[0] % 4) ^ s
         q = q_ref[aligned(place, share), :]
-        out[:share, :] = jnp.where(is_root, q, jnp.zeros_like(q))
-        out[share:, :] = picked[aligned(place, part), :]
+        out[at : at + share, :] = jnp.where(is_root, q, jnp.zeros_like(q))
+        out[at + share : at + tall, :] = picked[aligned(place, part), :]
 
 
 def sum_kernel(*refs):
@@ -112,15 +114,29 @@
     refs[-1][...] = total
 
 
+def halve_kernel(a_ref, b_ref, near_ref, far_ref):
+    rows = near_ref.shape[0]
+    near_ref[...] = a_ref[:rows, :] + b_ref[:rows, :]
+    far_ref[...] = a_ref[rows:, :] + b_ref[rows:, :]
+
+
+def stack_kernel(a_ref, b_ref, out_ref):
+    rows = a_ref.shape[0]
+    out_ref[:rows, :] = a_ref[...]
+    out_ref[rows:, :] = b_ref[...]
+
+
 def spread(shard, queries, kept, keys, roots):
     (rows, dims), (slab, _) = queries.shape, keys.shape
     count = kept.shape[1]
     devices = lax.axis_size("ctx")
-    tall = ((rows + count) // 4, dims)
-    *pieces, keys = call(
+    quarter = ((rows + count) // 4, dims)
+    half = (2 * quarter[0], dims)
+    in_hbm = lambda x: pltpu.with_memory_space_constraint(x, pltpu.HBM)
+    keep, send, keys = call(
         functools.partial(prepare_kernel, 4 * count // devices + 16),
-        (shard, roots, queries, kept, keys),
-        [(tall, BF16)] * 4 + [(keys.shape, BF16)],
+        (shard, roots, in_hbm(queries), in_hbm(kept), in_hbm(keys)),
+        [(half, BF16)] * 2 + [(keys.shape, BF16)],
         scratch=[
             pltpu.VMEM((rows, dims), BF16),
             pltpu.VMEM((1, count), jnp.int32),
@@ -131,14 +147,17 @@
         name="prepare",
         specs=[SMEM, SMEM, HBM, HBM, HBM],
     )
-    total = lambda arrays: call(sum_kernel, arrays, [(tall, BF16)], name="total")[0]
-    piece = total([pieces[0]] + [swap(pieces[s], "ctx", s) for s in (1, 2, 3)])
+    near, far = call(halve_kernel, (keep, swap(send, "ctx", 1)), [(quarter, BF16)] * 2, name="halve")
+    total = lambda arrays: call(sum_kernel, arrays, [(quarter, BF16)], name="total")[0]
+    near = total([near, swap(far, "ctx", 2)])
     step = 4
     while step < devices:
         ways = math.gcd(devices // step, 4)
-        piece = total([piece] + [swap(piece, "ctx", t * step) for t in range(1, ways)])
+        near = total([near] + [swap(near, "ctx", t * step) for t in range(1, ways)])
         step *= ways
-    return [piece] + [swap(piece, "ctx", s) for s in (1, 2, 3)], keys
+    far = swap(near, "ctx", 2)
+    (both,) = call(stack_kernel, (near, far), [(half, BF16)], name="stack")
+    return near, far, swap(both, "ctx", 1), keys
 
 
 def turn_kernel(v_ref, vt_ref):
@@ -147,8 +166,13 @@
     vt_ref[dims:, :] = jnp.ones((vt_ref.shape[0] - dims, v_ref.shape[0]), BF16)
 
 
-def attention_kernel(pieces, lanes, block, score_scale, *refs):
-    q_refs, k_ref, vt_ref, before, out_ref = refs[:pieces], refs[pieces], refs[pieces + 1], refs[pieces + 2 : -1], refs[-1]
+def quarters_of(ref, rows, tall):
+    return [ref[i : i + rows, :] for i in range(0, ref.shape[0], tall)]
+
+
+def attention_kernel(lanes, tall, block, score_scale, q_ref, k_ref, vt_ref, *refs):
+    before, out_ref = refs[:-1], refs[-1]
+    quarters = quarters_of(q_ref, lanes, tall)
     dims = k_ref.shape[1]
     blocks = k_ref.shape[0] // block
     factor = score_scale * math.log2(math.e)
@@ -158,10 +182,10 @@
 
     def scores(i, b):
         return lax.dot_general(
-            k_ref[b * block : (b + 1) * block, :], q_refs[i][:lanes, :], NT, preferred_element_type=F32
+            k_ref[b * block : (b + 1) * block, :], quarters[i], NT, preferred_element_type=F32
         )
 
-    stages = [(i, b) for i in range(pieces) for b in range(blocks)]
+    stages = [(i, b) for i in range(len(quarters)) for b in range(blocks)]
     ahead = scores(*stages[0])
     for n, (i, b) in enumerate(stages):
         s = ahead
@@ -186,13 +210,14 @@
         out_ref[dims:, at] = tail(top, total)
 
 
-def attention(pieces, lanes, keys, turned, score_scale, before=()):
+def attention(piece, lanes, tall, keys, turned, score_scale, before=()):
     slab, dims = keys.shape
+    count = piece.shape[0] // tall
     return call(
-        functools.partial(attention_kernel, len(pieces), lanes, min(KBLK, slab), score_scale),
-        (*pieces, keys, turned, *before),
-        [((dims + SUB, lanes * (len(pieces) + len(before))), F32)],
-        4 * lanes * len(pieces) * slab * dims,
+        functools.partial(attention_kernel, lanes, tall, min(KBLK, slab), score_scale),
+        (piece, keys, turned, *before),
+        [((dims + SUB, lanes * (count + len(before))), F32)],
+        4 * lanes * count * slab * dims,
         name="attention",
     )[0]
 
@@ -277,14 +302,15 @@
     return block, came
 
 
-def attend_kernel(score_scale, shard_ref, *refs):
-    pieces, (high_ref, low_ref, c_all) = refs[:4], refs[4:]
+def attend_kernel(score_scale, shard_ref, near_ref, far_ref, other_ref, high_ref, low_ref, c_all):
     part, rows = c_all.shape[0] // 4, high_ref.shape[1] // 4
+    tall = part + rows
+    pieces = [(near_ref, 0), (other_ref, 0), (far_ref, 0), (other_ref, tall)]
     places = [(shard_ref[0] % 4) ^ s for s in range(4)]
-    for place, piece in zip(places, pieces):
-        c_all[aligned(place, part), :] = piece[rows:, :]
-    for place, piece in zip(places, pieces):
-        scores = lax.dot_general(c_all[...], piece[:rows, :], NT, preferred_element_type=F32) * score_scale
+    for place, (ref, at) in zip(places, pieces):
+        c_all[aligned(place, part), :] = ref[at + rows : at + tall, :]
+    for place, (ref, at) in zip(places, pieces):
+        scores = lax.dot_general(c_all[...], ref[at : at + rows, :], NT, preferred_element_type=F32) * score_scale
         weights = jnp.exp(scores - jnp.max(scores, axis=0, keepdims=True))
         weights = weights * (1.0 / jnp.sum(weights, axis=0, keepdims=True))
         high_ref[:, aligned(place, rows)], low_ref[:, aligned(place, rows)] = halves(weights)
@@ -337,24 +363,65 @@
                 terms = [x + y for x, y in zip(terms[::2], terms[1::2])]
             updated[i] = jnp.where(inside, 0.0, rows[i]) - terms[0]
         rows = updated
-    return rows
-
-
-def invert_kernel(panel, h_ref, out_ref):
+        yield
+    return jnp.concatenate(rows, axis=0)
+
+
+def inverse_beside(block, work=()):
+    work = list(work)
+    groups = invert_block([block[i : i + SUB, :] for i in range(0, block.shape[0], SUB)])
+    while True:
+        try:
+            next(groups)
+        except StopIteration as stop:
+            for piece in work:
+                piece()
+            return stop.value
+        if work:
+            work.pop(0)()
+
+
+def invert_kernel(h_ref, out_ref):
+    out_ref[...] = inverse_beside(h_ref[:PANEL, :PANEL])
+
+
+def sweep_kernel(panel, h_ref, inverse_ref, out_ref, *next_ref):
+    size = h_ref.shape[0]
     at = slice(panel * PANEL, (panel + 1) * PANEL)
-    block = h_ref[at, at]
-    out_ref[...] = jnp.concatenate(
-        invert_block([block[i * SUB : (i + 1) * SUB, :] for i in range(PANEL // SUB)]), axis=0
-    )
-
-
-def update_kernel(panel, h_ref, inverse_ref, out_ref):
-    at = slice(panel * PANEL, (panel + 1) * PANEL)
-    turned = product(halves(inverse_ref[...]), halves(h_ref[at, :]), NN)
-    out_ref[...] = h_ref[...] - product(halves(h_ref[:, at]), halves(turned), NN)
-    out_ref[:, at] = turned.T
-    out_ref[at, :] = turned
-    out_ref[at, at] = -inverse_ref[...]
+    wide = slice(panel * PANEL // 128 * 128, panel * PANEL // 128 * 128 + 128)
+    offset = at.start - wide.start
+    inverse = inverse_ref[...]
+    turned = product(halves(inverse), halves(h_ref[at, :]), NN)
+    padded = jnp.concatenate(
+        [turned if i == offset else jnp.zeros_like(turned) for i in range(0, 128, PANEL)], axis=0
+    )
+    split = halves(padded)
+    columns = padded.T
+    lane = lax.broadcasted_iota(jnp.int32, (128, 128), 1)
+    inside = (lane >= offset) & (lane < offset + PANEL)
+
+    def rows_update(i):
+        def piece():
+            rows = slice(i, i + 128)
+            old = h_ref[rows, :]
+            out_ref[rows, :] = old - product(halves(h_ref[rows, wide]), split, NN)
+            out_ref[rows, wide] = jnp.where(inside, columns[rows, :], out_ref[rows, wide])
+            if i == wide.start:
+                out_ref[at, :] = turned
+                out_ref[at, at] = -inverse
+
+        return piece
+
+    work = [rows_update(i) for i in range(0, size, 128)]
+    if next_ref:
+        after = slice(at.stop, at.stop + PANEL)
+        block = h_ref[after, after] - product(
+            halves(h_ref[after, wide]), tuple(x[:, after] for x in split), NN
+        )
+        next_ref[0][...] = inverse_beside(block, work)
+    else:
+        for piece in work:
+            piece()
 
 
 def fit_kernel(shard_ref, minus_ref, high_ref, low_ref, own_ref, other_ref, x_ref, err_ref, yt):
@@ -391,12 +458,13 @@
     score_scale = 1.0 / math.sqrt(dims)
     shard = lax.axis_index("ctx").astype(jnp.int32).reshape(1)
 
-    pieces, own_keys = spread(shard, queries[0, 0], kept, keys[0], roots)
+    near, far, other, own_keys = spread(shard, queries[0, 0], kept, keys[0], roots)
     (turned,) = call(turn_kernel, (values[0],), [((dims + 16, slab), BF16)], name="turn")
-    attend_to = functools.partial(attention, lanes=lanes, keys=own_keys, turned=turned, score_scale=score_scale)
-    first = attend_to([pieces[0]])
-    send = attend_to([pieces[2]], before=[first])
-    keep = attend_to([pieces[1], pieces[3]])
+    attend_to = functools.partial(
+        attention, lanes=lanes, tall=near.shape[0], keys=own_keys, turned=turned, score_scale=score_scale
+    )
+    send = attend_to(far, before=[attend_to(near)])
+    keep = attend_to(other)
     rounds = target_rounds(shard, keep, swap(send, "ctx", 1))
     came = next(rounds)
     ends = None
@@ -414,24 +482,30 @@
     system_shape = ((count, count), F32)
     attend = call(
         functools.partial(attend_kernel, score_scale),
-        (shard, *pieces),
+        (shard, near, far, other),
         [((count, rows), BF16)] * 2,
         10**9,
         scratch=[pltpu.VMEM((count, dims), BF16)],
         name="attend",
     )
     (system,) = call(gram_kernel, attend, [system_shape], 4 * 10**9, name="gram")
-    system = beside(system)
     panels = count // PANEL
+    block_shape = ((PANEL, PANEL), F32)
+    (inverse,) = call(invert_kernel, (system,), [block_shape], 10**9, name="invert")
+    system, inverse = beside((system, inverse))
     for panel in range(panels):
-        (inverse,) = call(
-            functools.partial(invert_kernel, panel), (system,), [((PANEL, PANEL), F32)], 5 * 10**9, name="invert"
+        last = panel == panels - 1
+        system, *inverse = call(
+            functools.partial(sweep_kernel, panel),
+            (system, inverse),
+            [system_shape] if last else [system_shape, block_shape],
+            2 * 10**9,
+            name="sweep",
         )
-        inverse = beside(inverse)
-        (system,) = call(
-            functools.partial(update_kernel, panel), (system, inverse), [system_shape], 2 * 10**9, name="update"
-        )
-        if panel == 0 or panel == panels - 1:
+        inverse = None if last else inverse[0]
+        if inverse is not None:
+            system, inverse = beside((system, inverse))
+        else:
             system = beside(system)
     while ends is None:
         system = beside(system)

time: 82 us -> 78.9 us (0.962)
  waiting for transfers between devices: 22.5 us -> 28.1 us
  starting transfers between devices: 19.2 us -> 16.2 us
  local copies, waits for them, and re-layouts: 2.85 us -> 0.01 us
  Pallas kernels: 35.7 us -> 33 us
    ppermute x18 -> x16, waiting for transfers between devices: 22.5 us -> 28.1 us  [swap(): return lax.ppermute(array, axis, [(i, i ^ step) for i in range(size)])]
    ppermute x18 -> x16, starting transfers between devices: 19.2 us -> 16.2 us  [swap(): return lax.ppermute(array, axis, [(i, i ^ step) for i in range(size)])]
    unnamed x8 -> x2, local copies, waits for them, and re-layouts: 2.85 us -> 0.01 us
    pallas_call x27 -> x30, Pallas kernels: 35.7 us -> 33 us  [call(): pl.pallas_call(kernel, in_specs=specs or [SMEM if x.size == 1 else VMEM f...]
  transfers between devices with their start and end apart: 18 -> 16, of which waited for: 11 -> 12; matrix products, arithmetic and copies ran while one was open for 0% -> 0% of each run, Pallas kernels for 37% -> 32%
where the time goes in v6:
time: 78.9 us; the launch traced here: 78.8 us
  Pallas kernels  33 us (42%)
  waiting for transfers between devices  28.1 us (36%)
  starting transfers between devices  16.2 us (21%)
  between operations  1.5 us (2%)
    pallas_call x30, Pallas kernels, call(): pl.pallas_call(kernel, in_specs=specs or [SMEM if x.size == 1 else VMEM f...  33 us
    ppermute x16, waiting for transfers between devices, swap(): return lax.ppermute(array, axis, [(i, i ^ step) for i in range(size)])  28.1 us
    ppermute x16, starting transfers between devices, swap(): return lax.ppermute(array, axis, [(i, i ^ step) for i in range(size)])  16.2 us
  transfers between devices with their start and end apart: 16, of which 12 were waited for; matrix products, arithmetic and copies ran while one was open for 0% of the time, Pallas kernels for 32%

profile of v6, /device:TPU:0, one launch (start us, length us, event | category | flops | bytes accessed | tf_op | source)
XLA Modules:
  0.0 78.8 jit_solution(12613029555965135088)
XLA Ops:
  1.3 2.1 %prepare.1 = (bf16[768,128]{1,0:T(8,128)(2,1)S(1)}, bf16[768,128]{1,0:T(8,128)(2,1)S(1)}, bf16[4096,128]{1,0:T(8,128)(2,1)S(1)}) custom-call(s32[1]{0:T(128)} %bitcast.shard_ref, s32[1]{0:T(128)S(6)} %copy.7.root_ref, bf16[1024,128]{1,0:T(8,128)(2,1)} %bitcast.9, s32[1,512]{1,0:T(1,128)} %kept_hbm.1, bf16[4096,128]{1,0:T(8,128)(2,1)} %bitcast.7), custom_call_target="tpu_custom_call" | custom-call | flops 100000 | bytes 100000 | tf_op jit(solution)/shard_map/prepare/pallas_call | solution.py:32
  3.4 0.5 collective-permute-start
  3.9 1.1 %collective-permute-done.b_ref = bf16[768,128]{1,0:T(8,128)(2,1)S(1)} collective-permute-done((bf16[768,128]{1,0:T(8,128)(2,1)S(1)}, bf16[768,128]{1,0:T(8,128)(2,1)S(1)}, u32[]{:S(2)}, u32[]{:S(2)}) %collective-permute-start) | collective-permute-done | bytes 196640 | tf_op jit(solution)/shard_map/ppermute | solution.py:28
  5.0 3.0 %collective-permute-start.1 = (bf16[384,128]{1,0:T(8,128)(2,1)S(1)}, bf16[384,128]{1,0:T(8,128)(2,1)S(1)}, u32[]{:S(2)}, u32[]{:S(2)}) collective-permute-start(bf16[384,128]{1,0:T(8,128)(2,1)S(1)} %get-tuple-element.55), channel_id=1, source_target_pairs={{0,2},{1,3},{2,0},{3,1},{4,6},{5,7},{6,4},{7,5},{8,10},{9,11},{10,... | collective-permute-start | bytes 294920 | tf_op jit(solution)/shard_map/ppermute | solution.py:28
  8.0 3.1 %collective-permute-done.1.refs_1_ = bf16[384,128]{1,0:T(8,128)(2,1)S(1)} collective-permute-done((bf16[384,128]{1,0:T(8,128)(2,1)S(1)}, bf16[384,128]{1,0:T(8,128)(2,1)S(1)}, u32[]{:S(2)}, u32[]{:S(2)}) %collective-permute-start.1) | collective-permute-done | bytes 98336 | tf_op jit(solution)/shard_map/ppermute | solution.py:28
  11.1 3.9 %collective-permute-start.4 = (bf16[384,128]{1,0:T(8,128)(2,1)S(1)}, bf16[384,128]{1,0:T(8,128)(2,1)S(1)}, u32[]{:S(2)}, u32[]{:S(2)}) collective-permute-start(bf16[384,128]{1,0:T(8,128)(2,1)S(1)} %total.2.refs_0_), channel_id=1, source_target_pairs={{0,12},{1,13},{2,14},{3,15},{4,8},{5,9},{6,10},{7,11},{8,4},{9,5},... | collective-permute-start | bytes 294920 | tf_op jit(solution)/shard_map/ppermute | solution.py:28
  15.0 0.0 collective-permute-start.3
  15.0 0.6 collective-permute-start.2
  15.6 3.1 %collective-permute-done.4.refs_3_ = bf16[384,128]{1,0:T(8,128)(2,1)S(1)} collective-permute-done((bf16[384,128]{1,0:T(8,128)(2,1)S(1)}, bf16[384,128]{1,0:T(8,128)(2,1)S(1)}, u32[]{:S(2)}, u32[]{:S(2)}) %collective-permute-start.4) | collective-permute-done | bytes 98336 | tf_op jit(solution)/shard_map/ppermute | solution.py:28
  18.7 4.0 %collective-permute-done.3.refs_2_ = bf16[384,128]{1,0:T(8,128)(2,1)S(1)} collective-permute-done((bf16[384,128]{1,0:T(8,128)(2,1)S(1)}, bf16[384,128]{1,0:T(8,128)(2,1)S(1)}, u32[]{:S(2)}, u32[]{:S(2)}) %collective-permute-start.3) | collective-permute-done | bytes 98336 | tf_op jit(solution)/shard_map/ppermute | solution.py:28
  22.7 0.0 collective-permute-done.2.refs_1_
  22.8 1.6 %collective-permute-start.5 = (bf16[384,128]{1,0:T(8,128)(2,1)S(1)}, bf16[384,128]{1,0:T(8,128)(2,1)S(1)}, u32[]{:S(2)}, u32[]{:S(2)}) collective-permute-start(bf16[384,128]{1,0:T(8,128)(2,1)S(1)} %total.3.a_ref.near_ref.q_ref), channel_id=1, source_target_pairs={{0,2},{1,3},{2,0},{3,1},{4,6},{5,7},{6,4},{7,5},{8,10},{9,11},{10,... | collective-permute-start | bytes 294920 | tf_op jit(solution)/shard_map/ppermute | solution.py:28
  24.4 3.1 %collective-permute-done.5.b_ref.far_ref.q_ref = bf16[384,128]{1,0:T(8,128)(2,1)S(1)} collective-permute-done((bf16[384,128]{1,0:T(8,128)(2,1)S(1)}, bf16[384,128]{1,0:T(8,128)(2,1)S(1)}, u32[]{:S(2)}, u32[]{:S(2)}) %collective-permute-start.5) | collective-permute-done | bytes 98336 | tf_op jit(solution)/shard_map/ppermute | solution.py:28
  27.5 0.1 collective-permute-start.6
  27.6 0.3 turn.1.vt_ref
  27.9 1.8 %attention.4.refs_0_ = f32[136,256]{1,0:T(8,128)S(1)} custom-call(bf16[384,128]{1,0:T(8,128)(2,1)S(1)} %total.3.a_ref.near_ref.q_ref, bf16[4096,128]{1,0:T(8,128)(2,1)S(1)} %get-tuple-element.58.k_ref, bf16[144,4096]{1,0:T(8,128)(2,1)S(1)} %turn.1.vt_ref), custom_call_target="tpu_custom_call" | custom-call | flops 536870912 | bytes 100000 | tf_op jit(solution)/shard_map/attention/pallas_call | solution.py:32
  29.7 1.8 %attention.5 = f32[136,512]{1,0:T(8,128)S(1)} custom-call(bf16[384,128]{1,0:T(8,128)(2,1)S(1)} %collective-permute-done.5.b_ref.far_ref.q_ref, bf16[4096,128]{1,0:T(8,128)(2,1)S(1)} %get-tuple-element.58.k_ref, bf16[144,4096]{1,0:T(8,128)(2,1)S(1)} %turn.1.vt_ref, f32[136,256]{1,0:T(8,128)S(1)} %attention.4.refs_0_), custom_call_target="tpu_custom_call" | custom-call | flops 536870912 | bytes 100000 | tf_op jit(solution)/shard_map/attention/pallas_call | solution.py:32
  31.5 0.6 collective-permute-start.7
  32.0 1.5 %attend.1 = (bf16[512,1024]{1,0:T(8,128)(2,1)S(1)}, bf16[512,1024]{1,0:T(8,128)(2,1)S(1)}) custom-call(s32[1]{0:T(128)} %bitcast.shard_ref, bf16[384,128]{1,0:T(8,128)(2,1)S(1)} %total.3.a_ref.near_ref.q_ref, bf16[384,128]{1,0:T(8,128)(2,1)S(1)} %collective-permute-done.5.b_ref.far_ref.q_ref, bf16[768,128]{1,0:T(8,128)(2,1)S(1)} %collective-permute-done.6.other_ref.q_ref), custom_call_target="tpu_custom_call" | custom-call | flops 1000000000 | bytes 100000 | tf_op jit(solution)/shard_map/attend/pallas_call | solution.py:32
  33.6 3.5 %attention.3.a_ref = f32[136,512]{1,0:T(8,128)S(1)} custom-call(bf16[768,128]{1,0:T(8,128)(2,1)S(1)} %collective-permute-done.6.other_ref.q_ref, bf16[4096,128]{1,0:T(8,128)(2,1)S(1)} %get-tuple-element.58.k_ref, bf16[144,4096]{1,0:T(8,128)(2,1)S(1)} %turn.1.vt_ref), custom_call_target="tpu_custom_call" | custom-call | flops 1073741824 | bytes 100000 | tf_op jit(solution)/shard_map/attention/pallas_call | solution.py:32
  37.1 1.6 %collective-permute-start.8 = (f32[136,256]{1,0:T(8,128)S(1)}, f32[136,256]{1,0:T(8,128)S(1)}, u32[]{:S(2)}, u32[]{:S(2)}) collective-permute-start(f32[136,256]{1,0:T(8,128)S(1)} %get-tuple-element.59), channel_id=1, source_target_pairs={{0,2},{1,3},{2,0},{3,1},{4,6},{5,7},{6,4},{7,5},{8,10},{9,11},{10,... | collective-permute-start | bytes 417800 | tf_op jit(solution)/shard_map/ppermute | solution.py:28
  38.7 2.0 %gram.1.h_ref = f32[512,512]{1,0:T(8,128)S(1)} custom-call(bf16[512,1024]{1,0:T(8,128)(2,1)S(1)} %get-tuple-element.56.high_ref, bf16[512,1024]{1,0:T(8,128)(2,1)S(1)} %get-tuple-element.57.low_ref), custom_call_target="tpu_custom_call" | custom-call | flops 4000000000 | bytes 100000 | tf_op jit(solution)/shard_map/gram/pallas_call | solution.py:32
  40.7 1.7 %invert.1.inverse_ref = f32[64,64]{1,0:T(8,128)S(1)} custom-call(f32[512,512]{1,0:T(8,128)S(1)} %gram.1.h_ref), custom_call_target="tpu_custom_call" | custom-call | flops 1000000000 | bytes 100000 | tf_op jit(solution)/shard_map/invert/pallas_call | solution.py:32
  42.4 0.4 collective-permute-done.8.b_ref
  42.8 0.6 collective-permute-start.9
  43.5 2.0 %sweep.8 = (f32[512,512]{1,0:T(8,128)S(1)}, f32[64,64]{1,0:T(8,128)S(1)}) custom-call(f32[512,512]{1,0:T(8,128)S(1)} %gram.1.h_ref, f32[64,64]{1,0:T(8,128)S(1)} %invert.1.inverse_ref), custom_call_target="tpu_custom_call" | custom-call | flops 2000000000 | bytes 100000 | tf_op jit(solution)/shard_map/sweep/pallas_call | solution.py:32
  45.5 3.4 %collective-permute-done.9.b_ref = f32[72,256]{1,0:T(8,128)S(1)} collective-permute-done((f32[72,256]{1,0:T(8,128)S(1)}, f32[72,256]{1,0:T(8,128)S(1)}, u32[]{:S(2)}, u32[]{:S(2)}) %collective-permute-start.9) | collective-permute-done | bytes 73760 | tf_op jit(solution)/shard_map/ppermute | solution.py:28
  48.9 0.1 collective-permute-start.10
  49.0 1.9 %sweep.9 = (f32[512,512]{1,0:T(8,128)S(1)}, f32[64,64]{1,0:T(8,128)S(1)}) custom-call(f32[512,512]{1,0:T(8,128)S(1)} %get-tuple-element.67.h_ref, f32[64,64]{1,0:T(8,128)S(1)} %get-tuple-element.68.inverse_ref), custom_call_target="tpu_custom_call" | custom-call | flops 2000000000 | bytes 100000 | tf_op jit(solution)/shard_map/sweep/pallas_call | solution.py:32
  50.9 2.3 %collective-permute-done.10.b_ref = f32[40,256]{1,0:T(8,128)S(1)} collective-permute-done((f32[40,256]{1,0:T(8,128)S(1)}, f32[40,256]{1,0:T(8,128)S(1)}, u32[]{:S(2)}, u32[]{:S(2)}) %collective-permute-start.10) | collective-permute-done | bytes 40992 | tf_op jit(solution)/shard_map/ppermute | solution.py:28
  53.2 0.1 collective-permute-start.11
  53.3 2.0 %sweep.10 = (f32[512,512]{1,0:T(8,128)S(1)}, f32[64,64]{1,0:T(8,128)S(1)}) custom-call(f32[512,512]{1,0:T(8,128)S(1)} %get-tuple-element.74.h_ref, f32[64,64]{1,0:T(8,128)S(1)} %get-tuple-element.75.inverse_ref), custom_call_target="tpu_custom_call" | custom-call | flops 2000000000 | bytes 100000 | tf_op jit(solution)/shard_map/sweep/pallas_call | solution.py:32
  55.3 2.0 %collective-permute-done.11.b_ref = f32[32,256]{1,0:T(8,128)S(1)} collective-permute-done((f32[32,256]{1,0:T(8,128)S(1)}, f32[32,256]{1,0:T(8,128)S(1)}, u32[]{:S(2)}, u32[]{:S(2)}) %collective-permute-start.11) | collective-permute-done | bytes 32800 | tf_op jit(solution)/shard_map/ppermute | solution.py:28
  57.4 0.1 collective-permute-start.12
  57.5 1.9 %sweep.11 = (f32[512,512]{1,0:T(8,128)S(1)}, f32[64,64]{1,0:T(8,128)S(1)}) custom-call(f32[512,512]{1,0:T(8,128)S(1)} %get-tuple-element.80.h_ref, f32[64,64]{1,0:T(8,128)S(1)} %get-tuple-element.81.inverse_ref), custom_call_target="tpu_custom_call" | custom-call | flops 2000000000 | bytes 100000 | tf_op jit(solution)/shard_map/sweep/pallas_call | solution.py:32
  59.4 3.3 %collective-permute-done.12.b_ref = f32[64,256]{1,0:T(8,128)S(1)} collective-permute-done((f32[64,256]{1,0:T(8,128)S(1)}, f32[64,256]{1,0:T(8,128)S(1)}, u32[]{:S(2)}, u32[]{:S(2)}) %collective-permute-start.12) | collective-permute-done | bytes 65568 | tf_op jit(solution)/shard_map/ppermute | solution.py:28
  62.8 1.9 %collective-permute-start.13 = (f32[128,256]{1,0:T(8,128)S(1)}, f32[128,256]{1,0:T(8,128)S(1)}, u32[]{:S(2)}, u32[]{:S(2)}) collective-permute-start(f32[128,256]{1,0:T(8,128)S(1)} %stack.6.a_ref), channel_id=1, source_target_pairs={{0,2},{1,3},{2,0},{3,1},{4,6},{5,7},{6,4},{7,5},{8,10},{9,11},{10,... | collective-permute-start | bytes 393224 | tf_op jit(solution)/shard_map/ppermute | solution.py:28
  64.7 2.1 %sweep.12 = (f32[512,512]{1,0:T(8,128)S(1)}, f32[64,64]{1,0:T(8,128)S(1)}) custom-call(f32[512,512]{1,0:T(8,128)S(1)} %get-tuple-element.85.h_ref, f32[64,64]{1,0:T(8,128)S(1)} %get-tuple-element.86.inverse_ref), custom_call_target="tpu_custom_call" | custom-call | flops 2000000000 | bytes 100000 | tf_op jit(solution)/shard_map/sweep/pallas_call | solution.py:32
  66.8 1.0 %collective-permute-done.13.b_ref = f32[128,256]{1,0:T(8,128)S(1)} collective-permute-done((f32[128,256]{1,0:T(8,128)S(1)}, f32[128,256]{1,0:T(8,128)S(1)}, u32[]{:S(2)}, u32[]{:S(2)}) %collective-permute-start.13) | collective-permute-done | bytes 131104 | tf_op jit(solution)/shard_map/ppermute | solution.py:28
  67.8 0.1 collective-permute-start.14
  67.9 1.9 %sweep.13 = (f32[512,512]{1,0:T(8,128)S(1)}, f32[64,64]{1,0:T(8,128)S(1)}) custom-call(f32[512,512]{1,0:T(8,128)S(1)} %get-tuple-element.90.h_ref, f32[64,64]{1,0:T(8,128)S(1)} %get-tuple-element.91.inverse_ref), custom_call_target="tpu_custom_call" | custom-call | flops 2000000000 | bytes 100000 | tf_op jit(solution)/shard_map/sweep/pallas_call | solution.py:32
  69.8 2.1 %sweep.14 = (f32[512,512]{1,0:T(8,128)S(1)}, f32[64,64]{1,0:T(8,128)S(1)}) custom-call(f32[512,512]{1,0:T(8,128)S(1)} %get-tuple-element.95.h_ref, f32[64,64]{1,0:T(8,128)S(1)} %get-tuple-element.96.inverse_ref), custom_call_target="tpu_custom_call" | custom-call | flops 2000000000 | bytes 100000 | tf_op jit(solution)/shard_map/sweep/pallas_call | solution.py:32
  72.0 0.7 sweep.15.minus_ref
  72.7 1.9 %fit.1 = (f32[128,512]{1,0:T(8,128)S(1)}, f32[8,128]{1,0:T(8,128)S(1)}) custom-call(s32[1]{0:T(128)} %bitcast.shard_ref, f32[512,512]{1,0:T(8,128)S(1)} %sweep.15.minus_ref, bf16[512,1024]{1,0:T(8,128)(2,1)S(1)} %get-tuple-element.56.high_ref, bf16[512,1024]{1,0:T(8,128)(2,1)S(1)} %get-tuple-element.57.low_ref, f32[128,512]{1,0:T(8,128)S(1)} %stack.7.own_ref, ...), custom_call_target="tpu_custom_call" | custom-call | flops 1000000000 | bytes 100000 | tf_op jit(solution)/shard_map/fit/pallas_call | solution.py:32
  74.6 1.6 %collective-permute-start.15 = (f32[8,128]{1,0:T(8,128)S(1)}, f32[8,128]{1,0:T(8,128)S(1)}, u32[]{:S(2)}, u32[]{:S(2)}) collective-permute-start(f32[8,128]{1,0:T(8,128)S(1)} %get-tuple-element.101.refs_0_), channel_id=1, source_target_pairs={{0,16},{16,0},{1,17},{17,1},{2,18},{18,2},{3,19},{19,3},{4,20},{20... | collective-permute-start | bytes 12296 | tf_op jit(solution)/shard_map/ppermute | solution.py:28
  76.2 0.8 %flip.1 = f32[512,128]{1,0:T(8,128)} custom-call(f32[128,512]{1,0:T(8,128)S(1)} %get-tuple-element.100.x_ref), custom_call_target="tpu_custom_call" | custom-call | flops 1000000 | bytes 100000 | tf_op jit(solution)/shard_map/flip/pallas_call | solution.py:32
  77.0 1.3 %collective-permute-done.15.refs_1_ = f32[8,128]{1,0:T(8,128)S(1)} collective-permute-done((f32[8,128]{1,0:T(8,128)S(1)}, f32[8,128]{1,0:T(8,128)S(1)}, u32[]{:S(2)}, u32[]{:S(2)}) %collective-permute-start.15) | collective-permute-done | bytes 4128 | tf_op jit(solution)/shard_map/ppermute | solution.py:28
  78.3 0.5 mean.1
  (16 shorter events, 0.3 us)
Async XLA Ops:
  1.3 26.3 %copy-start = (bf16[1,4096,128]{2,1,0:T(8,128)(2,1)S(1)}, bf16[1,4096,128]{2,1,0:T(8,128)(2,1)}, u32[]{:S(2)}) copy-start(bf16[1,4096,128]{2,1,0:T(8,128)(2,1)} %param.7) | copy-start | bytes 3145732
  3.4 1.6 %collective-permute-start = (bf16[768,128]{1,0:T(8,128)(2,1)S(1)}, bf16[768,128]{1,0:T(8,128)(2,1)S(1)}, u32[]{:S(2)}, u32[]{:S(2)}) collective-permute-start(bf16[768,128]{1,0:T(8,128)(2,1)S(1)} %get-tuple-element.53), channel_id=1, source_target_pairs={{0,1},{1,0},{2,3},{3,2},{4,5},{5,4},{6,7},{7,6},{8,9},{9,8},{10,11... | collective-permute-start | bytes 589832 | tf_op jit(solution)/shard_map/ppermute | solution.py:28
  5.0 6.1 %collective-permute-start.1 = (bf16[384,128]{1,0:T(8,128)(2,1)S(1)}, bf16[384,128]{1,0:T(8,128)(2,1)S(1)}, u32[]{:S(2)}, u32[]{:S(2)}) collective-permute-start(bf16[384,128]{1,0:T(8,128)(2,1)S(1)} %get-tuple-element.55), channel_id=1, source_target_pairs={{0,2},{1,3},{2,0},{3,1},{4,6},{5,7},{6,4},{7,5},{8,10},{9,11},{10,... | collective-permute-start | bytes 294920 | tf_op jit(solution)/shard_map/ppermute | solution.py:28
  11.1 7.6 %collective-permute-start.4 = (bf16[384,128]{1,0:T(8,128)(2,1)S(1)}, bf16[384,128]{1,0:T(8,128)(2,1)S(1)}, u32[]{:S(2)}, u32[]{:S(2)}) collective-permute-start(bf16[384,128]{1,0:T(8,128)(2,1)S(1)} %total.2.refs_0_), channel_id=1, source_target_pairs={{0,12},{1,13},{2,14},{3,15},{4,8},{5,9},{6,10},{7,11},{8,4},{9,5},... | collective-permute-start | bytes 294920 | tf_op jit(solution)/shard_map/ppermute | solution.py:28
  15.0 7.7 %collective-permute-start.3 = (bf16[384,128]{1,0:T(8,128)(2,1)S(1)}, bf16[384,128]{1,0:T(8,128)(2,1)S(1)}, u32[]{:S(2)}, u32[]{:S(2)}) collective-permute-start(bf16[384,128]{1,0:T(8,128)(2,1)S(1)} %total.2.refs_0_), channel_id=1, source_target_pairs={{0,8},{1,9},{2,10},{3,11},{4,12},{5,13},{6,14},{7,15},{8,0},{9,1},... | collective-permute-start | bytes 294920 | tf_op jit(solution)/shard_map/ppermute | solution.py:28
  15.0 7.7 %collective-permute-start.2 = (bf16[384,128]{1,0:T(8,128)(2,1)S(1)}, bf16[384,128]{1,0:T(8,128)(2,1)S(1)}, u32[]{:S(2)}, u32[]{:S(2)}) collective-permute-start(bf16[384,128]{1,0:T(8,128)(2,1)S(1)} %total.2.refs_0_), channel_id=1, source_target_pairs={{0,4},{1,5},{2,6},{3,7},{4,0},{5,1},{6,2},{7,3},{8,12},{9,13},{10,... | collective-permute-start | bytes 294920 | tf_op jit(solution)/shard_map/ppermute | solution.py:28
  22.8 4.7 %collective-permute-start.5 = (bf16[384,128]{1,0:T(8,128)(2,1)S(1)}, bf16[384,128]{1,0:T(8,128)(2,1)S(1)}, u32[]{:S(2)}, u32[]{:S(2)}) collective-permute-start(bf16[384,128]{1,0:T(8,128)(2,1)S(1)} %total.3.a_ref.near_ref.q_ref), channel_id=1, source_target_pairs={{0,2},{1,3},{2,0},{3,1},{4,6},{5,7},{6,4},{7,5},{8,10},{9,11},{10,... | collective-permute-start | bytes 294920 | tf_op jit(solution)/shard_map/ppermute | solution.py:28
  27.5 4.6 %collective-permute-start.6 = (bf16[768,128]{1,0:T(8,128)(2,1)S(1)}, bf16[768,128]{1,0:T(8,128)(2,1)S(1)}, u32[]{:S(2)}, u32[]{:S(2)}) collective-permute-start(bf16[768,128]{1,0:T(8,128)(2,1)S(1)} %stack.4), channel_id=1, source_target_pairs={{0,1},{1,0},{2,3},{3,2},{4,5},{5,4},{6,7},{7,6},{8,9},{9,8},{10,11... | collective-permute-start | bytes 589832 | tf_op jit(solution)/shard_map/ppermute | solution.py:28
  31.5 5.6 %collective-permute-start.7 = (f32[136,512]{1,0:T(8,128)S(1)}, f32[136,512]{1,0:T(8,128)S(1)}, u32[]{:S(2)}, u32[]{:S(2)}) collective-permute-start(f32[136,512]{1,0:T(8,128)S(1)} %attention.5), channel_id=1, source_target_pairs={{0,1},{1,0},{2,3},{3,2},{4,5},{5,4},{6,7},{7,6},{8,9},{9,8},{10,11... | collective-permute-start | bytes 835592 | tf_op jit(solution)/shard_map/ppermute | solution.py:28
  37.1 5.7 %collective-permute-start.8 = (f32[136,256]{1,0:T(8,128)S(1)}, f32[136,256]{1,0:T(8,128)S(1)}, u32[]{:S(2)}, u32[]{:S(2)}) collective-permute-start(f32[136,256]{1,0:T(8,128)S(1)} %get-tuple-element.59), channel_id=1, source_target_pairs={{0,2},{1,3},{2,0},{3,1},{4,6},{5,7},{6,4},{7,5},{8,10},{9,11},{10,... | collective-permute-start | bytes 417800 | tf_op jit(solution)/shard_map/ppermute | solution.py:28
  42.8 6.1 %collective-permute-start.9 = (f32[72,256]{1,0:T(8,128)S(1)}, f32[72,256]{1,0:T(8,128)S(1)}, u32[]{:S(2)}, u32[]{:S(2)}) collective-permute-start(f32[72,256]{1,0:T(8,128)S(1)} %get-tuple-element.66), channel_id=1, source_target_pairs={{0,8},{1,9},{2,10},{3,11},{4,12},{5,13},{6,14},{7,15},{8,0},{9,1},... | collective-permute-start | bytes 221192 | tf_op jit(solution)/shard_map/ppermute | solution.py:28
  48.9 4.3 %collective-permute-start.10 = (f32[40,256]{1,0:T(8,128)S(1)}, f32[40,256]{1,0:T(8,128)S(1)}, u32[]{:S(2)}, u32[]{:S(2)}) collective-permute-start(f32[40,256]{1,0:T(8,128)S(1)} %get-tuple-element.73), channel_id=1, source_target_pairs={{0,4},{1,5},{2,6},{3,7},{4,0},{5,1},{6,2},{7,3},{8,12},{9,13},{10,... | collective-permute-start | bytes 122888 | tf_op jit(solution)/shard_map/ppermute | solution.py:28
  53.2 4.1 %collective-permute-start.11 = (f32[32,256]{1,0:T(8,128)S(1)}, f32[32,256]{1,0:T(8,128)S(1)}, u32[]{:S(2)}, u32[]{:S(2)}) collective-permute-start(f32[32,256]{1,0:T(8,128)S(1)} %finish.1.a_ref), channel_id=1, source_target_pairs={{0,4},{1,5},{2,6},{3,7},{4,0},{5,1},{6,2},{7,3},{8,12},{9,13},{10,... | collective-permute-start | bytes 98312 | tf_op jit(solution)/shard_map/ppermute | solution.py:28
  57.4 5.4 %collective-permute-start.12 = (f32[64,256]{1,0:T(8,128)S(1)}, f32[64,256]{1,0:T(8,128)S(1)}, u32[]{:S(2)}, u32[]{:S(2)}) collective-permute-start(f32[64,256]{1,0:T(8,128)S(1)} %stack.5.a_ref), channel_id=1, source_target_pairs={{0,8},{1,9},{2,10},{3,11},{4,12},{5,13},{6,14},{7,15},{8,0},{9,1},... | collective-permute-start | bytes 196616 | tf_op jit(solution)/shard_map/ppermute | solution.py:28
  62.8 5.0 %collective-permute-start.13 = (f32[128,256]{1,0:T(8,128)S(1)}, f32[128,256]{1,0:T(8,128)S(1)}, u32[]{:S(2)}, u32[]{:S(2)}) collective-permute-start(f32[128,256]{1,0:T(8,128)S(1)} %stack.6.a_ref), channel_id=1, source_target_pairs={{0,2},{1,3},{2,0},{3,1},{4,6},{5,7},{6,4},{7,5},{8,10},{9,11},{10,... | collective-permute-start | bytes 393224 | tf_op jit(solution)/shard_map/ppermute | solution.py:28
  67.8 2.0 %collective-permute-start.14 = (f32[128,512]{1,0:T(8,128)S(1)}, f32[128,512]{1,0:T(8,128)S(1)}, u32[]{:S(2)}, u32[]{:S(2)}) collective-permute-start(f32[128,512]{1,0:T(8,128)S(1)} %stack.7.own_ref), channel_id=1, source_target_pairs={{0,1},{1,0},{2,3},{3,2},{4,5},{5,4},{6,7},{7,6},{8,9},{9,8},{10,11... | collective-permute-start | bytes 786440 | tf_op jit(solution)/shard_map/ppermute | solution.py:28
  74.6 3.7 %collective-permute-start.15 = (f32[8,128]{1,0:T(8,128)S(1)}, f32[8,128]{1,0:T(8,128)S(1)}, u32[]{:S(2)}, u32[]{:S(2)}) collective-permute-start(f32[8,128]{1,0:T(8,128)S(1)} %get-tuple-element.101.refs_0_), channel_id=1, source_target_pairs={{0,16},{16,0},{1,17},{17,1},{2,18},{18,2},{3,19},{19,3},{4,20},{20... | collective-permute-start | bytes 12296 | tf_op jit(solution)/shard_map/ppermute | solution.py:28

commit v7 on v6

--- a/solution.py
+++ b/solution.py
@@ -126,7 +126,7 @@
     out_ref[rows:, :] = b_ref[...]
 
 
-def spread(shard, queries, kept, keys, roots):
+def spread(shard, queries, kept, keys, roots, values, attend_to):
     (rows, dims), (slab, _) = queries.shape, keys.shape
     count = kept.shape[1]
     devices = lax.axis_size("ctx")
@@ -149,15 +149,24 @@
     )
     near, far = call(halve_kernel, (keep, swap(send, "ctx", 1)), [(quarter, BF16)] * 2, name="halve")
     total = lambda arrays: call(sum_kernel, arrays, [(quarter, BF16)], name="total")[0]
-    near = total([near, swap(far, "ctx", 2)])
+    came = swap(far, "ctx", 2)
+    (turned,) = call(turn_kernel, (values,), [((dims + 16, slab), BF16)], 10**7, name="turn")
+    came, turned = lax.optimization_barrier((came, turned))
+    near = total([near, came])
     step = 4
     while step < devices:
         ways = math.gcd(devices // step, 4)
         near = total([near] + [swap(near, "ctx", t * step) for t in range(1, ways)])
         step *= ways
     far = swap(near, "ctx", 2)
+    first = attend_to(near, keys, turned)
+    far, first = lax.optimization_barrier((far, first))
     (both,) = call(stack_kernel, (near, far), [(half, BF16)], name="stack")
-    return near, far, swap(both, "ctx", 1), keys
+    other = swap(both, "ctx", 1)
+    send = attend_to(far, keys, turned, before=[first])
+    other, send = lax.optimization_barrier((other, send))
+    came = swap(send, "ctx", 1)
+    return near, far, other, attend_to(other, keys, turned), came
 
 
 def turn_kernel(v_ref, vt_ref):
@@ -210,7 +219,7 @@
         out_ref[dims:, at] = tail(top, total)
 
 
-def attention(piece, lanes, tall, keys, turned, score_scale, before=()):
+def attention(lanes, tall, score_scale, piece, keys, turned, before=()):
     slab, dims = keys.shape
     count = piece.shape[0] // tall
     return call(
@@ -222,13 +231,13 @@
     )[0]
 
 
-def merged(a_ref, b_ref):
-    dims = a_ref.shape[0] - SUB
-    a_top, b_top = a_ref[dims : dims + 1, :], b_ref[dims : dims + 1, :]
-    top = jnp.maximum(a_top, b_top)
-    a_scale, b_scale = jnp.exp2(a_top - top), jnp.exp2(b_top - top)
-    total = a_ref[dims + 1 : dims + 2, :] * a_scale + b_ref[dims + 1 : dims + 2, :] * b_scale
-    out = a_ref[:dims, :] * a_scale + b_ref[:dims, :] * b_scale
+def merged(*refs):
+    dims = refs[0].shape[0] - SUB
+    tops = [ref[dims : dims + 1, :] for ref in refs]
+    top = functools.reduce(jnp.maximum, tops)
+    scales = [jnp.exp2(t - top) for t in tops]
+    total = sum(ref[dims + 1 : dims + 2, :] * scale for ref, scale in zip(refs, scales))
+    out = sum(ref[:dims, :] * scale for ref, scale in zip(refs, scales))
     return out, top, total
 
 
@@ -244,26 +253,30 @@
         ref[dims:, :] = tail(top[:, at], total[:, at])
 
 
-def merge_rows_kernel(step, shard_ref, a_ref, b_ref, keep_ref, send_ref, work):
-    out, top, total = merged(a_ref, b_ref)
-    rows = keep_ref.shape[0] - SUB
+def merge_rows_kernel(step, shard_ref, *refs):
+    work, refs = refs[-1], refs[:-1]
+    ways = sum(1 for ref in refs if ref.shape[0] != refs[0].shape[0])
+    ins, outs = refs[:-ways], refs[-ways:]
+    out, top, total = merged(*ins)
+    rows = outs[0].shape[0] - SUB
     work[...] = out
-    bit = (shard_ref[0] // step) % 2
-    for ref, which in ((keep_ref, bit), (send_ref, 1 - bit)):
-        ref[:rows, :] = work[aligned(which, rows), :]
+    digit = (shard_ref[0] // step) % ways
+    for t, ref in enumerate(outs):
+        ref[:rows, :] = work[aligned(digit ^ t, rows), :]
         ref[rows:, :] = tail(top, total)
 
 
-def finish_kernel(a_ref, b_ref, out_ref):
-    out, _, total = merged(a_ref, b_ref)
-    out_ref[...] = out / total
-
-
-def stack_rows_kernel(step, shard_ref, a_ref, b_ref, out_ref):
-    rows = a_ref.shape[0]
-    bit = (shard_ref[0] // step) % 2
-    out_ref[aligned(bit, rows), :] = a_ref[...]
-    out_ref[aligned(1 - bit, rows), :] = b_ref[...]
+def finish_kernel(*refs):
+    out, _, total = merged(*refs[:-1])
+    refs[-1][...] = out / total
+
+
+def stack_rows_kernel(step, shard_ref, *refs):
+    ins, out_ref = refs[:-1], refs[-1]
+    rows = ins[0].shape[0]
+    digit = (shard_ref[0] // step) % len(ins)
+    for t, ref in enumerate(ins):
+        out_ref[aligned(digit ^ t, rows), :] = ref[...]
 
 
 def stack_lanes_kernel(a_ref, b_ref, out_ref):
@@ -276,30 +289,34 @@
     dims, lanes = keep.shape[0] - SUB, keep.shape[1] // 2
     devices = lax.axis_size("ctx")
     keep, send = call(merge_lanes_kernel, (keep, came), [((dims + SUB, lanes), F32)] * 2, name="merge")
-    came = yield swap(send, "ctx", 2)
-    step, rows = devices // 2, dims
-    while step >= 4:
-        keep, send = call(
+    came = yield [swap(send, "ctx", 2)]
+    digits, step = [], devices
+    while step > 4:
+        ways = math.gcd(step // 4, 4)
+        step //= ways
+        digits.append((step, ways))
+    rows = dims
+    for step, ways in digits:
+        keep, *send = call(
             functools.partial(merge_rows_kernel, step),
-            (shard, keep, came),
-            [((rows // 2 + SUB, lanes), F32)] * 2,
+            (shard, keep, *came),
+            [((rows // ways + SUB, lanes), F32)] * ways,
             scratch=[pltpu.VMEM((rows, lanes), F32)],
             name="merge",
         )
-        came = yield swap(send, "ctx", step)
-        rows //= 2
-        step //= 2
-    (block,) = call(finish_kernel, (keep, came), [((rows, lanes), F32)], name="finish")
-    step = 4
-    while step < devices:
-        came = yield swap(block, "ctx", step)
-        rows *= 2
-        (block,) = call(functools.partial(stack_rows_kernel, step), (shard, block, came), [((rows, lanes), F32)], name="stack")
-        step *= 2
-    came = yield swap(block, "ctx", 2)
-    (block,) = call(stack_lanes_kernel, (block, came), [((dims, 2 * lanes), F32)], name="stack")
-    came = yield swap(block, "ctx", 1)
-    return block, came
+        came = yield [swap(x, "ctx", t * step) for t, x in enumerate(send, 1)]
+        rows //= ways
+    (block,) = call(finish_kernel, (keep, *came), [((rows, lanes), F32)], name="finish")
+    for step, ways in reversed(digits):
+        came = yield [swap(block, "ctx", t * step) for t in range(1, ways)]
+        rows *= ways
+        (block,) = call(
+            functools.partial(stack_rows_kernel, step), (shard, block, *came), [((rows, lanes), F32)], name="stack"
+        )
+    came = yield [swap(block, "ctx", 2)]
+    (block,) = call(stack_lanes_kernel, (block, *came), [((dims, 2 * lanes), F32)], name="stack")
+    came = yield [swap(block, "ctx", 1)]
+    return block, *came
 
 
 def attend_kernel(score_scale, shard_ref, near_ref, far_ref, other_ref, high_ref, low_ref, c_all):
@@ -458,14 +475,9 @@
     score_scale = 1.0 / math.sqrt(dims)
     shard = lax.axis_index("ctx").astype(jnp.int32).reshape(1)
 
-    near, far, other, own_keys = spread(shard, queries[0, 0], kept, keys[0], roots)
-    (turned,) = call(turn_kernel, (values[0],), [((dims + 16, slab), BF16)], name="turn")
-    attend_to = functools.partial(
-        attention, lanes=lanes, tall=near.shape[0], keys=own_keys, turned=turned, score_scale=score_scale
-    )
-    send = attend_to(far, before=[attend_to(near)])
-    keep = attend_to(other)
-    rounds = target_rounds(shard, keep, swap(send, "ctx", 1))
+    attend_to = functools.partial(attention, lanes, (rows + count) // 4, score_scale)
+    near, far, other, keep, came = spread(shard, queries[0, 0], kept, keys[0], roots, values[0], attend_to)
+    rounds = target_rounds(shard, keep, came)
     came = next(rounds)
     ends = None
 
@@ -503,10 +515,8 @@
             name="sweep",
         )
         inverse = None if last else inverse[0]
-        if inverse is not None:
+        if panel % 2 == 1 or panel >= panels - 2:
             system, inverse = beside((system, inverse))
-        else:
-            system = beside(system)
     while ends is None:
         system = beside(system)
 

time: 78.9 us -> 73.1 us (0.926)
  waiting for transfers between devices: 28.1 us -> 14.5 us
  starting transfers between devices: 16.2 us -> 24 us
    ppermute x16 -> x18, waiting for transfers between devices: 28.1 us -> 14.5 us  [swap(): return lax.ppermute(array, axis, [(i, i ^ step) for i in range(size)])]
    ppermute x16 -> x18, starting transfers between devices: 16.2 us -> 24 us  [swap(): return lax.ppermute(array, axis, [(i, i ^ step) for i in range(size)])]
    pallas_call x30 -> x28, Pallas kernels: 33 us -> 32.9 us  [call(): pl.pallas_call(kernel, in_specs=specs or [SMEM if x.size == 1 else VMEM f...]
  transfers between devices with their start and end apart: 16 -> 18, of which waited for: 12 -> 8; matrix products, arithmetic and copies ran while one was open for 0% -> 0% of each run, Pallas kernels for 32% -> 38%
where the time goes in v7:
time: 73.1 us; the launch traced here: 73 us
  Pallas kernels  32.9 us (45%)
  starting transfers between devices  24 us (33%)
  waiting for transfers between devices  14.5 us (20%)
  between operations  1.62 us (2%)
    pallas_call x28, Pallas kernels, call(): pl.pallas_call(kernel, in_specs=specs or [SMEM if x.size == 1 else VMEM f...  32.9 us
    ppermute x18, starting transfers between devices, swap(): return lax.ppermute(array, axis, [(i, i ^ step) for i in range(size)])  24 us
    ppermute x18, waiting for transfers between devices, swap(): return lax.ppermute(array, axis, [(i, i ^ step) for i in range(size)])  14.5 us
  transfers between devices with their start and end apart: 18, of which 8 were waited for; matrix products, arithmetic and copies ran while one was open for 0% of the time, Pallas kernels for 38%

profile of v7, /device:TPU:0, one launch (start us, length us, event | category | flops | bytes accessed | tf_op | source)
XLA Modules:
  0.0 73.0 jit_solution(7021550873046914774)
XLA Ops:
  1.4 2.0 %prepare.1 = (bf16[768,128]{1,0:T(8,128)(2,1)S(1)}, bf16[768,128]{1,0:T(8,128)(2,1)S(1)}, bf16[4096,128]{1,0:T(8,128)(2,1)S(1)}) custom-call(s32[1]{0:T(128)} %bitcast.shard_ref, s32[1]{0:T(128)S(6)} %copy.7.root_ref, bf16[1024,128]{1,0:T(8,128)(2,1)} %bitcast.9, s32[1,512]{1,0:T(1,128)} %kept_hbm.1, bf16[4096,128]{1,0:T(8,128)(2,1)} %bitcast.7), custom_call_target="tpu_custom_call" | custom-call | flops 100000 | bytes 100000 | tf_op jit(solution)/shard_map/prepare/pallas_call | solution.py:32
  3.4 0.5 collective-permute-start
  3.9 1.1 %collective-permute-done.b_ref = bf16[768,128]{1,0:T(8,128)(2,1)S(1)} collective-permute-done((bf16[768,128]{1,0:T(8,128)(2,1)S(1)}, bf16[768,128]{1,0:T(8,128)(2,1)S(1)}, u32[]{:S(2)}, u32[]{:S(2)}) %collective-permute-start) | collective-permute-done | bytes 196640 | tf_op jit(solution)/shard_map/ppermute | solution.py:28
  5.0 3.0 %collective-permute-start.1 = (bf16[384,128]{1,0:T(8,128)(2,1)S(1)}, bf16[384,128]{1,0:T(8,128)(2,1)S(1)}, u32[]{:S(2)}, u32[]{:S(2)}) collective-permute-start(bf16[384,128]{1,0:T(8,128)(2,1)S(1)} %get-tuple-element.59), channel_id=1, source_target_pairs={{0,2},{1,3},{2,0},{3,1},{4,6},{5,7},{6,4},{7,5},{8,10},{9,11},{10,... | collective-permute-start | bytes 294920 | tf_op jit(solution)/shard_map/ppermute | solution.py:28
  8.0 0.3 turn.1.vt_ref
  8.3 2.8 %collective-permute-done.1.refs_1_ = bf16[384,128]{1,0:T(8,128)(2,1)S(1)} collective-permute-done((bf16[384,128]{1,0:T(8,128)(2,1)S(1)}, bf16[384,128]{1,0:T(8,128)(2,1)S(1)}, u32[]{:S(2)}, u32[]{:S(2)}) %collective-permute-start.1) | collective-permute-done | bytes 98336 | tf_op jit(solution)/shard_map/ppermute | solution.py:28
  11.1 3.9 %collective-permute-start.4 = (bf16[384,128]{1,0:T(8,128)(2,1)S(1)}, bf16[384,128]{1,0:T(8,128)(2,1)S(1)}, u32[]{:S(2)}, u32[]{:S(2)}) collective-permute-start(bf16[384,128]{1,0:T(8,128)(2,1)S(1)} %total.2.refs_0_), channel_id=1, source_target_pairs={{0,12},{1,13},{2,14},{3,15},{4,8},{5,9},{6,10},{7,11},{8,4},{9,5},... | collective-permute-start | bytes 294920 | tf_op jit(solution)/shard_map/ppermute | solution.py:28
  15.0 0.6 collective-permute-start.2
  15.6 3.1 %collective-permute-done.4.refs_3_ = bf16[384,128]{1,0:T(8,128)(2,1)S(1)} collective-permute-done((bf16[384,128]{1,0:T(8,128)(2,1)S(1)}, bf16[384,128]{1,0:T(8,128)(2,1)S(1)}, u32[]{:S(2)}, u32[]{:S(2)}) %collective-permute-start.4) | collective-permute-done | bytes 98336 | tf_op jit(solution)/shard_map/ppermute | solution.py:28
  18.7 4.0 %collective-permute-done.3.refs_2_ = bf16[384,128]{1,0:T(8,128)(2,1)S(1)} collective-permute-done((bf16[384,128]{1,0:T(8,128)(2,1)S(1)}, bf16[384,128]{1,0:T(8,128)(2,1)S(1)}, u32[]{:S(2)}, u32[]{:S(2)}) %collective-permute-start.3) | collective-permute-done | bytes 98336 | tf_op jit(solution)/shard_map/ppermute | solution.py:28
  22.7 0.0 collective-permute-done.2.refs_1_
  22.8 1.6 %collective-permute-start.5 = (bf16[384,128]{1,0:T(8,128)(2,1)S(1)}, bf16[384,128]{1,0:T(8,128)(2,1)S(1)}, u32[]{:S(2)}, u32[]{:S(2)}) collective-permute-start(bf16[384,128]{1,0:T(8,128)(2,1)S(1)} %total.3.q_ref.a_ref.near_ref), channel_id=1, source_target_pairs={{0,2},{1,3},{2,0},{3,1},{4,6},{5,7},{6,4},{7,5},{8,10},{9,11},{10,... | collective-permute-start | bytes 294920 | tf_op jit(solution)/shard_map/ppermute | solution.py:28
  24.4 1.8 %attention.3.refs_0_ = f32[136,256]{1,0:T(8,128)S(1)} custom-call(bf16[384,128]{1,0:T(8,128)(2,1)S(1)} %total.3.q_ref.a_ref.near_ref, bf16[4096,128]{1,0:T(8,128)(2,1)S(1)} %get-tuple-element.61.k_ref, bf16[144,4096]{1,0:T(8,128)(2,1)S(1)} %turn.1.vt_ref), custom_call_target="tpu_custom_call" | custom-call | flops 536870912 | bytes 100000 | tf_op jit(solution)/shard_map/attention/pallas_call | solution.py:32
  26.1 1.3 %collective-permute-done.5.b_ref.q_ref.far_ref = bf16[384,128]{1,0:T(8,128)(2,1)S(1)} collective-permute-done((bf16[384,128]{1,0:T(8,128)(2,1)S(1)}, bf16[384,128]{1,0:T(8,128)(2,1)S(1)}, u32[]{:S(2)}, u32[]{:S(2)}) %collective-permute-start.5) | collective-permute-done | bytes 98336 | tf_op jit(solution)/shard_map/ppermute | solution.py:28
  27.5 0.1 collective-permute-start.6
  27.5 1.8 %attention.4 = f32[136,512]{1,0:T(8,128)S(1)} custom-call(bf16[384,128]{1,0:T(8,128)(2,1)S(1)} %collective-permute-done.5.b_ref.q_ref.far_ref, bf16[4096,128]{1,0:T(8,128)(2,1)S(1)} %get-tuple-element.61.k_ref, bf16[144,4096]{1,0:T(8,128)(2,1)S(1)} %turn.1.vt_ref, f32[136,256]{1,0:T(8,128)S(1)} %attention.3.refs_0_), custom_call_target="tpu_custom_call" | custom-call | flops 536870912 | bytes 100000 | tf_op jit(solution)/shard_map/attention/pallas_call | solution.py:32
  29.3 0.0 collective-permute-done.6.other_ref.q_ref
  29.4 0.6 collective-permute-start.7
  29.9 1.5 %attend.1 = (bf16[512,1024]{1,0:T(8,128)(2,1)S(1)}, bf16[512,1024]{1,0:T(8,128)(2,1)S(1)}) custom-call(s32[1]{0:T(128)} %bitcast.shard_ref, bf16[384,128]{1,0:T(8,128)(2,1)S(1)} %total.3.q_ref.a_ref.near_ref, bf16[384,128]{1,0:T(8,128)(2,1)S(1)} %collective-permute-done.5.b_ref.q_ref.far_ref, bf16[768,128]{1,0:T(8,128)(2,1)S(1)} %collective-permute-done.6.other_ref.q_ref), custom_call_target="tpu_custom_call" | custom-call | flops 1000000000 | bytes 100000 | tf_op jit(solution)/shard_map/attend/pallas_call | solution.py:32
  31.5 3.5 %attention.5.a_ref = f32[136,512]{1,0:T(8,128)S(1)} custom-call(bf16[768,128]{1,0:T(8,128)(2,1)S(1)} %collective-permute-done.6.other_ref.q_ref, bf16[4096,128]{1,0:T(8,128)(2,1)S(1)} %get-tuple-element.61.k_ref, bf16[144,4096]{1,0:T(8,128)(2,1)S(1)} %turn.1.vt_ref), custom_call_target="tpu_custom_call" | custom-call | flops 1073741824 | bytes 100000 | tf_op jit(solution)/shard_map/attention/pallas_call | solution.py:32
  35.0 1.6 %collective-permute-start.8 = (f32[136,256]{1,0:T(8,128)S(1)}, f32[136,256]{1,0:T(8,128)S(1)}, u32[]{:S(2)}, u32[]{:S(2)}) collective-permute-start(f32[136,256]{1,0:T(8,128)S(1)} %get-tuple-element.69), channel_id=1, source_target_pairs={{0,2},{1,3},{2,0},{3,1},{4,6},{5,7},{6,4},{7,5},{8,10},{9,11},{10,... | collective-permute-start | bytes 417800 | tf_op jit(solution)/shard_map/ppermute | solution.py:28
  36.6 2.0 %gram.1.h_ref = f32[512,512]{1,0:T(8,128)S(1)} custom-call(bf16[512,1024]{1,0:T(8,128)(2,1)S(1)} %get-tuple-element.66.high_ref, bf16[512,1024]{1,0:T(8,128)(2,1)S(1)} %get-tuple-element.67.low_ref), custom_call_target="tpu_custom_call" | custom-call | flops 4000000000 | bytes 100000 | tf_op jit(solution)/shard_map/gram/pallas_call | solution.py:32
  38.6 1.7 %invert.1.inverse_ref = f32[64,64]{1,0:T(8,128)S(1)} custom-call(f32[512,512]{1,0:T(8,128)S(1)} %gram.1.h_ref), custom_call_target="tpu_custom_call" | custom-call | flops 1000000000 | bytes 100000 | tf_op jit(solution)/shard_map/invert/pallas_call | solution.py:32
  40.3 0.4 collective-permute-done.8.refs_1_
  40.7 0.6 collective-permute-start.9
  41.3 2.5 %collective-permute-start.10 = (f32[40,256]{1,0:T(8,128)S(1)}, f32[40,256]{1,0:T(8,128)S(1)}, u32[]{:S(2)}, u32[]{:S(2)}) collective-permute-start(f32[40,256]{1,0:T(8,128)S(1)} %get-tuple-element.79), channel_id=1, source_target_pairs={{0,8},{1,9},{2,10},{3,11},{4,12},{5,13},{6,14},{7,15},{8,0},{9,1},... | collective-permute-start | bytes 122888 | tf_op jit(solution)/shard_map/ppermute | solution.py:28
  43.8 1.3 %collective-permute-start.11 = (f32[40,256]{1,0:T(8,128)S(1)}, f32[40,256]{1,0:T(8,128)S(1)}, u32[]{:S(2)}, u32[]{:S(2)}) collective-permute-start(f32[40,256]{1,0:T(8,128)S(1)} %get-tuple-element.80), channel_id=1, source_target_pairs={{0,12},{1,13},{2,14},{3,15},{4,8},{5,9},{6,10},{7,11},{8,4},{9,5},... | collective-permute-start | bytes 122888 | tf_op jit(solution)/shard_map/ppermute | solution.py:28
  45.1 2.0 %sweep.8 = (f32[512,512]{1,0:T(8,128)S(1)}, f32[64,64]{1,0:T(8,128)S(1)}) custom-call(f32[512,512]{1,0:T(8,128)S(1)} %gram.1.h_ref, f32[64,64]{1,0:T(8,128)S(1)} %invert.1.inverse_ref), custom_call_target="tpu_custom_call" | custom-call | flops 2000000000 | bytes 100000 | tf_op jit(solution)/shard_map/sweep/pallas_call | solution.py:32
  47.2 1.9 %sweep.9 = (f32[512,512]{1,0:T(8,128)S(1)}, f32[64,64]{1,0:T(8,128)S(1)}) custom-call(f32[512,512]{1,0:T(8,128)S(1)} %get-tuple-element.72.h_ref, f32[64,64]{1,0:T(8,128)S(1)} %get-tuple-element.73.inverse_ref), custom_call_target="tpu_custom_call" | custom-call | flops 2000000000 | bytes 100000 | tf_op jit(solution)/shard_map/sweep/pallas_call | solution.py:32
  49.1 0.0 collective-permute-done.10.refs_2_
  49.1 0.6 collective-permute-done.11.refs_3_
  49.7 2.0 %collective-permute-start.14 = (f32[32,256]{1,0:T(8,128)S(1)}, f32[32,256]{1,0:T(8,128)S(1)}, u32[]{:S(2)}, u32[]{:S(2)}) collective-permute-start(f32[32,256]{1,0:T(8,128)S(1)} %finish.1.refs_0_), channel_id=1, source_target_pairs={{0,12},{1,13},{2,14},{3,15},{4,8},{5,9},{6,10},{7,11},{8,4},{9,5},... | collective-permute-start | bytes 98312 | tf_op jit(solution)/shard_map/ppermute | solution.py:28
  51.7 0.0 collective-permute-start.13
  51.7 2.4 %collective-permute-start.12 = (f32[32,256]{1,0:T(8,128)S(1)}, f32[32,256]{1,0:T(8,128)S(1)}, u32[]{:S(2)}, u32[]{:S(2)}) collective-permute-start(f32[32,256]{1,0:T(8,128)S(1)} %finish.1.refs_0_), channel_id=1, source_target_pairs={{0,4},{1,5},{2,6},{3,7},{4,0},{5,1},{6,2},{7,3},{8,12},{9,13},{10,... | collective-permute-start | bytes 98312 | tf_op jit(solution)/shard_map/ppermute | solution.py:28
  54.1 2.0 %sweep.10 = (f32[512,512]{1,0:T(8,128)S(1)}, f32[64,64]{1,0:T(8,128)S(1)}) custom-call(f32[512,512]{1,0:T(8,128)S(1)} %get-tuple-element.81.h_ref, f32[64,64]{1,0:T(8,128)S(1)} %get-tuple-element.82.inverse_ref), custom_call_target="tpu_custom_call" | custom-call | flops 2000000000 | bytes 100000 | tf_op jit(solution)/shard_map/sweep/pallas_call | solution.py:32
  56.2 1.9 %sweep.11 = (f32[512,512]{1,0:T(8,128)S(1)}, f32[64,64]{1,0:T(8,128)S(1)}) custom-call(f32[512,512]{1,0:T(8,128)S(1)} %get-tuple-element.83.h_ref, f32[64,64]{1,0:T(8,128)S(1)} %get-tuple-element.84.inverse_ref), custom_call_target="tpu_custom_call" | custom-call | flops 2000000000 | bytes 100000 | tf_op jit(solution)/shard_map/sweep/pallas_call | solution.py:32
  58.1 0.0 collective-permute-done.14.refs_3_
  58.2 1.7 %collective-permute-start.15 = (f32[128,256]{1,0:T(8,128)S(1)}, f32[128,256]{1,0:T(8,128)S(1)}, u32[]{:S(2)}, u32[]{:S(2)}) collective-permute-start(f32[128,256]{1,0:T(8,128)S(1)} %stack.4.a_ref), channel_id=1, source_target_pairs={{0,2},{1,3},{2,0},{3,1},{4,6},{5,7},{6,4},{7,5},{8,10},{9,11},{10,... | collective-permute-start | bytes 393224 | tf_op jit(solution)/shard_map/ppermute | solution.py:28
  59.8 2.1 %sweep.12 = (f32[512,512]{1,0:T(8,128)S(1)}, f32[64,64]{1,0:T(8,128)S(1)}) custom-call(f32[512,512]{1,0:T(8,128)S(1)} %get-tuple-element.91.h_ref, f32[64,64]{1,0:T(8,128)S(1)} %get-tuple-element.92.inverse_ref), custom_call_target="tpu_custom_call" | custom-call | flops 2000000000 | bytes 100000 | tf_op jit(solution)/shard_map/sweep/pallas_call | solution.py:32
  62.0 1.9 %sweep.13 = (f32[512,512]{1,0:T(8,128)S(1)}, f32[64,64]{1,0:T(8,128)S(1)}) custom-call(f32[512,512]{1,0:T(8,128)S(1)} %get-tuple-element.93.h_ref, f32[64,64]{1,0:T(8,128)S(1)} %get-tuple-element.94.inverse_ref), custom_call_target="tpu_custom_call" | custom-call | flops 2000000000 | bytes 100000 | tf_op jit(solution)/shard_map/sweep/pallas_call | solution.py:32
  63.9 0.1 collective-permute-start.16
  64.0 2.1 %sweep.14 = (f32[512,512]{1,0:T(8,128)S(1)}, f32[64,64]{1,0:T(8,128)S(1)}) custom-call(f32[512,512]{1,0:T(8,128)S(1)} %get-tuple-element.100.h_ref, f32[64,64]{1,0:T(8,128)S(1)} %get-tuple-element.101.inverse_ref), custom_call_target="tpu_custom_call" | custom-call | flops 2000000000 | bytes 100000 | tf_op jit(solution)/shard_map/sweep/pallas_call | solution.py:32
  66.1 0.7 sweep.15.minus_ref
  66.9 1.9 %fit.1 = (f32[128,512]{1,0:T(8,128)S(1)}, f32[8,128]{1,0:T(8,128)S(1)}) custom-call(s32[1]{0:T(128)} %bitcast.shard_ref, f32[512,512]{1,0:T(8,128)S(1)} %sweep.15.minus_ref, bf16[512,1024]{1,0:T(8,128)(2,1)S(1)} %get-tuple-element.66.high_ref, bf16[512,1024]{1,0:T(8,128)(2,1)S(1)} %get-tuple-element.67.low_ref, f32[128,512]{1,0:T(8,128)S(1)} %stack.5.own_ref, ...), custom_call_target="tpu_custom_call" | custom-call | flops 1000000000 | bytes 100000 | tf_op jit(solution)/shard_map/fit/pallas_call | solution.py:32
  68.8 1.6 %collective-permute-start.17 = (f32[8,128]{1,0:T(8,128)S(1)}, f32[8,128]{1,0:T(8,128)S(1)}, u32[]{:S(2)}, u32[]{:S(2)}) collective-permute-start(f32[8,128]{1,0:T(8,128)S(1)} %get-tuple-element.109.refs_0_), channel_id=1, source_target_pairs={{0,16},{16,0},{1,17},{17,1},{2,18},{18,2},{3,19},{19,3},{4,20},{20... | collective-permute-start | bytes 12296 | tf_op jit(solution)/shard_map/ppermute | solution.py:28
  70.3 0.8 %flip.1 = f32[512,128]{1,0:T(8,128)} custom-call(f32[128,512]{1,0:T(8,128)S(1)} %get-tuple-element.108.x_ref), custom_call_target="tpu_custom_call" | custom-call | flops 1000000 | bytes 100000 | tf_op jit(solution)/shard_map/flip/pallas_call | solution.py:32
  71.2 1.3 %collective-permute-done.17.refs_1_ = f32[8,128]{1,0:T(8,128)S(1)} collective-permute-done((f32[8,128]{1,0:T(8,128)S(1)}, f32[8,128]{1,0:T(8,128)S(1)}, u32[]{:S(2)}, u32[]{:S(2)}) %collective-permute-start.17) | collective-permute-done | bytes 4128 | tf_op jit(solution)/shard_map/ppermute | solution.py:28
  72.5 0.5 mean.1
  (18 shorter events, 0.3 us)
Async XLA Ops:
  0.6 7.3 %copy-start = (bf16[1,4096,128]{2,1,0:T(8,128)(2,1)S(1)}, bf16[1,4096,128]{2,1,0:T(8,128)(2,1)}, u32[]{:S(2)}) copy-start(bf16[1,4096,128]{2,1,0:T(8,128)(2,1)} %param.7) | copy-start | bytes 3145732
  3.4 1.6 %collective-permute-start = (bf16[768,128]{1,0:T(8,128)(2,1)S(1)}, bf16[768,128]{1,0:T(8,128)(2,1)S(1)}, u32[]{:S(2)}, u32[]{:S(2)}) collective-permute-start(bf16[768,128]{1,0:T(8,128)(2,1)S(1)} %get-tuple-element.57), channel_id=1, source_target_pairs={{0,1},{1,0},{2,3},{3,2},{4,5},{5,4},{6,7},{7,6},{8,9},{9,8},{10,11... | collective-permute-start | bytes 589832 | tf_op jit(solution)/shard_map/ppermute | solution.py:28
  5.0 6.0 %collective-permute-start.1 = (bf16[384,128]{1,0:T(8,128)(2,1)S(1)}, bf16[384,128]{1,0:T(8,128)(2,1)S(1)}, u32[]{:S(2)}, u32[]{:S(2)}) collective-permute-start(bf16[384,128]{1,0:T(8,128)(2,1)S(1)} %get-tuple-element.59), channel_id=1, source_target_pairs={{0,2},{1,3},{2,0},{3,1},{4,6},{5,7},{6,4},{7,5},{8,10},{9,11},{10,... | collective-permute-start | bytes 294920 | tf_op jit(solution)/shard_map/ppermute | solution.py:28
  11.1 7.6 %collective-permute-start.4 = (bf16[384,128]{1,0:T(8,128)(2,1)S(1)}, bf16[384,128]{1,0:T(8,128)(2,1)S(1)}, u32[]{:S(2)}, u32[]{:S(2)}) collective-permute-start(bf16[384,128]{1,0:T(8,128)(2,1)S(1)} %total.2.refs_0_), channel_id=1, source_target_pairs={{0,12},{1,13},{2,14},{3,15},{4,8},{5,9},{6,10},{7,11},{8,4},{9,5},... | collective-permute-start | bytes 294920 | tf_op jit(solution)/shard_map/ppermute | solution.py:28
  15.0 7.7 %collective-permute-start.3 = (bf16[384,128]{1,0:T(8,128)(2,1)S(1)}, bf16[384,128]{1,0:T(8,128)(2,1)S(1)}, u32[]{:S(2)}, u32[]{:S(2)}) collective-permute-start(bf16[384,128]{1,0:T(8,128)(2,1)S(1)} %total.2.refs_0_), channel_id=1, source_target_pairs={{0,8},{1,9},{2,10},{3,11},{4,12},{5,13},{6,14},{7,15},{8,0},{9,1},... | collective-permute-start | bytes 294920 | tf_op jit(solution)/shard_map/ppermute | solution.py:28
  15.0 7.7 %collective-permute-start.2 = (bf16[384,128]{1,0:T(8,128)(2,1)S(1)}, bf16[384,128]{1,0:T(8,128)(2,1)S(1)}, u32[]{:S(2)}, u32[]{:S(2)}) collective-permute-start(bf16[384,128]{1,0:T(8,128)(2,1)S(1)} %total.2.refs_0_), channel_id=1, source_target_pairs={{0,4},{1,5},{2,6},{3,7},{4,0},{5,1},{6,2},{7,3},{8,12},{9,13},{10,... | collective-permute-start | bytes 294920 | tf_op jit(solution)/shard_map/ppermute | solution.py:28
  22.8 4.7 %collective-permute-start.5 = (bf16[384,128]{1,0:T(8,128)(2,1)S(1)}, bf16[384,128]{1,0:T(8,128)(2,1)S(1)}, u32[]{:S(2)}, u32[]{:S(2)}) collective-permute-start(bf16[384,128]{1,0:T(8,128)(2,1)S(1)} %total.3.q_ref.a_ref.near_ref), channel_id=1, source_target_pairs={{0,2},{1,3},{2,0},{3,1},{4,6},{5,7},{6,4},{7,5},{8,10},{9,11},{10,... | collective-permute-start | bytes 294920 | tf_op jit(solution)/shard_map/ppermute | solution.py:28
  27.5 1.9 %collective-permute-start.6 = (bf16[768,128]{1,0:T(8,128)(2,1)S(1)}, bf16[768,128]{1,0:T(8,128)(2,1)S(1)}, u32[]{:S(2)}, u32[]{:S(2)}) collective-permute-start(bf16[768,128]{1,0:T(8,128)(2,1)S(1)} %stack.3), channel_id=1, source_target_pairs={{0,1},{1,0},{2,3},{3,2},{4,5},{5,4},{6,7},{7,6},{8,9},{9,8},{10,11... | collective-permute-start | bytes 589832 | tf_op jit(solution)/shard_map/ppermute | solution.py:28
  29.4 5.6 %collective-permute-start.7 = (f32[136,512]{1,0:T(8,128)S(1)}, f32[136,512]{1,0:T(8,128)S(1)}, u32[]{:S(2)}, u32[]{:S(2)}) collective-permute-start(f32[136,512]{1,0:T(8,128)S(1)} %attention.4), channel_id=1, source_target_pairs={{0,1},{1,0},{2,3},{3,2},{4,5},{5,4},{6,7},{7,6},{8,9},{9,8},{10,11... | collective-permute-start | bytes 835592 | tf_op jit(solution)/shard_map/ppermute | solution.py:28
  35.0 5.7 %collective-permute-start.8 = (f32[136,256]{1,0:T(8,128)S(1)}, f32[136,256]{1,0:T(8,128)S(1)}, u32[]{:S(2)}, u32[]{:S(2)}) collective-permute-start(f32[136,256]{1,0:T(8,128)S(1)} %get-tuple-element.69), channel_id=1, source_target_pairs={{0,2},{1,3},{2,0},{3,1},{4,6},{5,7},{6,4},{7,5},{8,10},{9,11},{10,... | collective-permute-start | bytes 417800 | tf_op jit(solution)/shard_map/ppermute | solution.py:28
  40.7 8.4 %collective-permute-start.9 = (f32[40,256]{1,0:T(8,128)S(1)}, f32[40,256]{1,0:T(8,128)S(1)}, u32[]{:S(2)}, u32[]{:S(2)}) collective-permute-start(f32[40,256]{1,0:T(8,128)S(1)} %get-tuple-element.78), channel_id=1, source_target_pairs={{0,4},{1,5},{2,6},{3,7},{4,0},{5,1},{6,2},{7,3},{8,12},{9,13},{10,... | collective-permute-start | bytes 122888 | tf_op jit(solution)/shard_map/ppermute | solution.py:28
  41.3 7.8 %collective-permute-start.10 = (f32[40,256]{1,0:T(8,128)S(1)}, f32[40,256]{1,0:T(8,128)S(1)}, u32[]{:S(2)}, u32[]{:S(2)}) collective-permute-start(f32[40,256]{1,0:T(8,128)S(1)} %get-tuple-element.79), channel_id=1, source_target_pairs={{0,8},{1,9},{2,10},{3,11},{4,12},{5,13},{6,14},{7,15},{8,0},{9,1},... | collective-permute-start | bytes 122888 | tf_op jit(solution)/shard_map/ppermute | solution.py:28
  43.8 5.8 %collective-permute-start.11 = (f32[40,256]{1,0:T(8,128)S(1)}, f32[40,256]{1,0:T(8,128)S(1)}, u32[]{:S(2)}, u32[]{:S(2)}) collective-permute-start(f32[40,256]{1,0:T(8,128)S(1)} %get-tuple-element.80), channel_id=1, source_target_pairs={{0,12},{1,13},{2,14},{3,15},{4,8},{5,9},{6,10},{7,11},{8,4},{9,5},... | collective-permute-start | bytes 122888 | tf_op jit(solution)/shard_map/ppermute | solution.py:28
  49.7 8.4 %collective-permute-start.14 = (f32[32,256]{1,0:T(8,128)S(1)}, f32[32,256]{1,0:T(8,128)S(1)}, u32[]{:S(2)}, u32[]{:S(2)}) collective-permute-start(f32[32,256]{1,0:T(8,128)S(1)} %finish.1.refs_0_), channel_id=1, source_target_pairs={{0,12},{1,13},{2,14},{3,15},{4,8},{5,9},{6,10},{7,11},{8,4},{9,5},... | collective-permute-start | bytes 98312 | tf_op jit(solution)/shard_map/ppermute | solution.py:28
  51.7 6.4 %collective-permute-start.13 = (f32[32,256]{1,0:T(8,128)S(1)}, f32[32,256]{1,0:T(8,128)S(1)}, u32[]{:S(2)}, u32[]{:S(2)}) collective-permute-start(f32[32,256]{1,0:T(8,128)S(1)} %finish.1.refs_0_), channel_id=1, source_target_pairs={{0,8},{1,9},{2,10},{3,11},{4,12},{5,13},{6,14},{7,15},{8,0},{9,1},... | collective-permute-start | bytes 98312 | tf_op jit(solution)/shard_map/ppermute | solution.py:28
  51.7 6.4 %collective-permute-start.12 = (f32[32,256]{1,0:T(8,128)S(1)}, f32[32,256]{1,0:T(8,128)S(1)}, u32[]{:S(2)}, u32[]{:S(2)}) collective-permute-start(f32[32,256]{1,0:T(8,128)S(1)} %finish.1.refs_0_), channel_id=1, source_target_pairs={{0,4},{1,5},{2,6},{3,7},{4,0},{5,1},{6,2},{7,3},{8,12},{9,13},{10,... | collective-permute-start | bytes 98312 | tf_op jit(solution)/shard_map/ppermute | solution.py:28
  58.2 5.7 %collective-permute-start.15 = (f32[128,256]{1,0:T(8,128)S(1)}, f32[128,256]{1,0:T(8,128)S(1)}, u32[]{:S(2)}, u32[]{:S(2)}) collective-permute-start(f32[128,256]{1,0:T(8,128)S(1)} %stack.4.a_ref), channel_id=1, source_target_pairs={{0,2},{1,3},{2,0},{3,1},{4,6},{5,7},{6,4},{7,5},{8,10},{9,11},{10,... | collective-permute-start | bytes 393224 | tf_op jit(solution)/shard_map/ppermute | solution.py:28
  63.9 2.2 %collective-permute-start.16 = (f32[128,512]{1,0:T(8,128)S(1)}, f32[128,512]{1,0:T(8,128)S(1)}, u32[]{:S(2)}, u32[]{:S(2)}) collective-permute-start(f32[128,512]{1,0:T(8,128)S(1)} %stack.5.own_ref), channel_id=1, source_target_pairs={{0,1},{1,0},{2,3},{3,2},{4,5},{5,4},{6,7},{7,6},{8,9},{9,8},{10,11... | collective-permute-start | bytes 786440 | tf_op jit(solution)/shard_map/ppermute | solution.py:28
  68.8 3.7 %collective-permute-start.17 = (f32[8,128]{1,0:T(8,128)S(1)}, f32[8,128]{1,0:T(8,128)S(1)}, u32[]{:S(2)}, u32[]{:S(2)}) collective-permute-start(f32[8,128]{1,0:T(8,128)S(1)} %get-tuple-element.109.refs_0_), channel_id=1, source_target_pairs={{0,16},{16,0},{1,17},{17,1},{2,18},{18,2},{3,19},{19,3},{4,20},{20... | collective-permute-start | bytes 12296 | tf_op jit(solution)/shard_map/ppermute | solution.py:28

commit v8 on v7

--- a/solution.py
+++ b/solution.py
@@ -290,11 +290,7 @@
     devices = lax.axis_size("ctx")
     keep, send = call(merge_lanes_kernel, (keep, came), [((dims + SUB, lanes), F32)] * 2, name="merge")
     came = yield [swap(send, "ctx", 2)]
-    digits, step = [], devices
-    while step > 4:
-        ways = math.gcd(step // 4, 4)
-        step //= ways
-        digits.append((step, ways))
+    digits = [(step, 2) for step in (2**i for i in range(2, devices.bit_length() - 1))]
     rows = dims
     for step, ways in digits:
         keep, *send = call(
@@ -515,7 +511,7 @@
             name="sweep",
         )
         inverse = None if last else inverse[0]
-        if panel % 2 == 1 or panel >= panels - 2:
+        if panel not in (panels - 7, panels - 3):
             system, inverse = beside((system, inverse))
     while ends is None:
         system = beside(system)

time: 73.1 us -> 73.4 us (level)
  waiting for transfers between devices: 14.5 us -> 18.3 us
  starting transfers between devices: 24 us -> 20.5 us
    ppermute x18 -> x16, waiting for transfers between devices: 14.5 us -> 18.3 us  [swap(): return lax.ppermute(array, axis, [(i, i ^ step) for i in range(size)])]
    ppermute x18 -> x16, starting transfers between devices: 24 us -> 20.5 us  [swap(): return lax.ppermute(array, axis, [(i, i ^ step) for i in range(size)])]
    pallas_call x28 -> x30, Pallas kernels: 32.9 us -> 32.9 us  [call(): pl.pallas_call(kernel, in_specs=specs or [SMEM if x.size == 1 else VMEM f...]
  transfers between devices with their start and end apart: 18 -> 16, of which waited for: 8 -> 12; matrix products, arithmetic and copies ran while one was open for 0% -> 0% of each run, Pallas kernels for 38% -> 39%
where the time goes in v8:
time: 73.4 us; the launch traced here: 73.2 us
  Pallas kernels  32.9 us (45%)
  starting transfers between devices  20.5 us (28%)
  waiting for transfers between devices  18.3 us (25%)
  between operations  1.58 us (2%)
    pallas_call x30, Pallas kernels, call(): pl.pallas_call(kernel, in_specs=specs or [SMEM if x.size == 1 else VMEM f...  32.9 us
    ppermute x16, starting transfers between devices, swap(): return lax.ppermute(array, axis, [(i, i ^ step) for i in range(size)])  20.5 us
    ppermute x16, waiting for transfers between devices, swap(): return lax.ppermute(array, axis, [(i, i ^ step) for i in range(size)])  18.3 us
  transfers between devices with their start and end apart: 16, of which 12 were waited for; matrix products, arithmetic and copies ran while one was open for 0% of the time, Pallas kernels for 39%

profile of v8, /device:TPU:0, one launch (start us, length us, event | category | flops | bytes accessed | tf_op | source)
XLA Modules:
  0.0 73.2 jit_solution(11787745712617439052)
XLA Ops:
  1.4 2.0 %prepare.1 = (bf16[768,128]{1,0:T(8,128)(2,1)S(1)}, bf16[768,128]{1,0:T(8,128)(2,1)S(1)}, bf16[4096,128]{1,0:T(8,128)(2,1)S(1)}) custom-call(s32[1]{0:T(128)} %bitcast.shard_ref, s32[1]{0:T(128)S(6)} %copy.7.root_ref, bf16[1024,128]{1,0:T(8,128)(2,1)} %bitcast.9, s32[1,512]{1,0:T(1,128)} %kept_hbm.1, bf16[4096,128]{1,0:T(8,128)(2,1)} %bitcast.7), custom_call_target="tpu_custom_call" | custom-call | flops 100000 | bytes 100000 | tf_op jit(solution)/shard_map/prepare/pallas_call | solution.py:32
  3.4 0.5 collective-permute-start
  3.9 1.1 %collective-permute-done.b_ref = bf16[768,128]{1,0:T(8,128)(2,1)S(1)} collective-permute-done((bf16[768,128]{1,0:T(8,128)(2,1)S(1)}, bf16[768,128]{1,0:T(8,128)(2,1)S(1)}, u32[]{:S(2)}, u32[]{:S(2)}) %collective-permute-start) | collective-permute-done | bytes 196640 | tf_op jit(solution)/shard_map/ppermute | solution.py:28
  5.0 3.0 %collective-permute-start.1 = (bf16[384,128]{1,0:T(8,128)(2,1)S(1)}, bf16[384,128]{1,0:T(8,128)(2,1)S(1)}, u32[]{:S(2)}, u32[]{:S(2)}) collective-permute-start(bf16[384,128]{1,0:T(8,128)(2,1)S(1)} %get-tuple-element.60), channel_id=1, source_target_pairs={{0,2},{1,3},{2,0},{3,1},{4,6},{5,7},{6,4},{7,5},{8,10},{9,11},{10,... | collective-permute-start | bytes 294920 | tf_op jit(solution)/shard_map/ppermute | solution.py:28
  8.0 0.3 turn.1.vt_ref
  8.3 2.8 %collective-permute-done.1.refs_1_ = bf16[384,128]{1,0:T(8,128)(2,1)S(1)} collective-permute-done((bf16[384,128]{1,0:T(8,128)(2,1)S(1)}, bf16[384,128]{1,0:T(8,128)(2,1)S(1)}, u32[]{:S(2)}, u32[]{:S(2)}) %collective-permute-start.1) | collective-permute-done | bytes 98336 | tf_op jit(solution)/shard_map/ppermute | solution.py:28
  11.1 3.9 %collective-permute-start.4 = (bf16[384,128]{1,0:T(8,128)(2,1)S(1)}, bf16[384,128]{1,0:T(8,128)(2,1)S(1)}, u32[]{:S(2)}, u32[]{:S(2)}) collective-permute-start(bf16[384,128]{1,0:T(8,128)(2,1)S(1)} %total.2.refs_0_), channel_id=1, source_target_pairs={{0,12},{1,13},{2,14},{3,15},{4,8},{5,9},{6,10},{7,11},{8,4},{9,5},... | collective-permute-start | bytes 294920 | tf_op jit(solution)/shard_map/ppermute | solution.py:28
  15.0 0.6 collective-permute-start.2
  15.6 3.1 %collective-permute-done.4.refs_3_ = bf16[384,128]{1,0:T(8,128)(2,1)S(1)} collective-permute-done((bf16[384,128]{1,0:T(8,128)(2,1)S(1)}, bf16[384,128]{1,0:T(8,128)(2,1)S(1)}, u32[]{:S(2)}, u32[]{:S(2)}) %collective-permute-start.4) | collective-permute-done | bytes 98336 | tf_op jit(solution)/shard_map/ppermute | solution.py:28
  18.7 4.0 %collective-permute-done.3.refs_2_ = bf16[384,128]{1,0:T(8,128)(2,1)S(1)} collective-permute-done((bf16[384,128]{1,0:T(8,128)(2,1)S(1)}, bf16[384,128]{1,0:T(8,128)(2,1)S(1)}, u32[]{:S(2)}, u32[]{:S(2)}) %collective-permute-start.3) | collective-permute-done | bytes 98336 | tf_op jit(solution)/shard_map/ppermute | solution.py:28
  22.7 0.0 collective-permute-done.2.refs_1_
  22.8 1.6 %collective-permute-start.5 = (bf16[384,128]{1,0:T(8,128)(2,1)S(1)}, bf16[384,128]{1,0:T(8,128)(2,1)S(1)}, u32[]{:S(2)}, u32[]{:S(2)}) collective-permute-start(bf16[384,128]{1,0:T(8,128)(2,1)S(1)} %total.3.q_ref.a_ref.near_ref), channel_id=1, source_target_pairs={{0,2},{1,3},{2,0},{3,1},{4,6},{5,7},{6,4},{7,5},{8,10},{9,11},{10,... | collective-permute-start | bytes 294920 | tf_op jit(solution)/shard_map/ppermute | solution.py:28
  24.4 1.8 %attention.3.refs_0_ = f32[136,256]{1,0:T(8,128)S(1)} custom-call(bf16[384,128]{1,0:T(8,128)(2,1)S(1)} %total.3.q_ref.a_ref.near_ref, bf16[4096,128]{1,0:T(8,128)(2,1)S(1)} %get-tuple-element.62.k_ref, bf16[144,4096]{1,0:T(8,128)(2,1)S(1)} %turn.1.vt_ref), custom_call_target="tpu_custom_call" | custom-call | flops 536870912 | bytes 100000 | tf_op jit(solution)/shard_map/attention/pallas_call | solution.py:32
  26.1 1.3 %collective-permute-done.5.b_ref.q_ref.far_ref = bf16[384,128]{1,0:T(8,128)(2,1)S(1)} collective-permute-done((bf16[384,128]{1,0:T(8,128)(2,1)S(1)}, bf16[384,128]{1,0:T(8,128)(2,1)S(1)}, u32[]{:S(2)}, u32[]{:S(2)}) %collective-permute-start.5) | collective-permute-done | bytes 98336 | tf_op jit(solution)/shard_map/ppermute | solution.py:28
  27.5 0.1 collective-permute-start.6
  27.5 1.8 %attention.4 = f32[136,512]{1,0:T(8,128)S(1)} custom-call(bf16[384,128]{1,0:T(8,128)(2,1)S(1)} %collective-permute-done.5.b_ref.q_ref.far_ref, bf16[4096,128]{1,0:T(8,128)(2,1)S(1)} %get-tuple-element.62.k_ref, bf16[144,4096]{1,0:T(8,128)(2,1)S(1)} %turn.1.vt_ref, f32[136,256]{1,0:T(8,128)S(1)} %attention.3.refs_0_), custom_call_target="tpu_custom_call" | custom-call | flops 536870912 | bytes 100000 | tf_op jit(solution)/shard_map/attention/pallas_call | solution.py:32
  29.3 0.0 collective-permute-done.6.other_ref.q_ref
  29.4 0.6 collective-permute-start.7
  29.9 1.5 %attend.1 = (bf16[512,1024]{1,0:T(8,128)(2,1)S(1)}, bf16[512,1024]{1,0:T(8,128)(2,1)S(1)}) custom-call(s32[1]{0:T(128)} %bitcast.shard_ref, bf16[384,128]{1,0:T(8,128)(2,1)S(1)} %total.3.q_ref.a_ref.near_ref, bf16[384,128]{1,0:T(8,128)(2,1)S(1)} %collective-permute-done.5.b_ref.q_ref.far_ref, bf16[768,128]{1,0:T(8,128)(2,1)S(1)} %collective-permute-done.6.other_ref.q_ref), custom_call_target="tpu_custom_call" | custom-call | flops 1000000000 | bytes 100000 | tf_op jit(solution)/shard_map/attend/pallas_call | solution.py:32
  31.5 3.5 %attention.5.a_ref = f32[136,512]{1,0:T(8,128)S(1)} custom-call(bf16[768,128]{1,0:T(8,128)(2,1)S(1)} %collective-permute-done.6.other_ref.q_ref, bf16[4096,128]{1,0:T(8,128)(2,1)S(1)} %get-tuple-element.62.k_ref, bf16[144,4096]{1,0:T(8,128)(2,1)S(1)} %turn.1.vt_ref), custom_call_target="tpu_custom_call" | custom-call | flops 1073741824 | bytes 100000 | tf_op jit(solution)/shard_map/attention/pallas_call | solution.py:32
  35.0 1.6 %collective-permute-start.8 = (f32[136,256]{1,0:T(8,128)S(1)}, f32[136,256]{1,0:T(8,128)S(1)}, u32[]{:S(2)}, u32[]{:S(2)}) collective-permute-start(f32[136,256]{1,0:T(8,128)S(1)} %get-tuple-element.70), channel_id=1, source_target_pairs={{0,2},{1,3},{2,0},{3,1},{4,6},{5,7},{6,4},{7,5},{8,10},{9,11},{10,... | collective-permute-start | bytes 417800 | tf_op jit(solution)/shard_map/ppermute | solution.py:28
  36.6 2.0 %gram.1.h_ref = f32[512,512]{1,0:T(8,128)S(1)} custom-call(bf16[512,1024]{1,0:T(8,128)(2,1)S(1)} %get-tuple-element.67.high_ref, bf16[512,1024]{1,0:T(8,128)(2,1)S(1)} %get-tuple-element.68.low_ref), custom_call_target="tpu_custom_call" | custom-call | flops 4000000000 | bytes 100000 | tf_op jit(solution)/shard_map/gram/pallas_call | solution.py:32
  38.6 1.7 %invert.1.inverse_ref = f32[64,64]{1,0:T(8,128)S(1)} custom-call(f32[512,512]{1,0:T(8,128)S(1)} %gram.1.h_ref), custom_call_target="tpu_custom_call" | custom-call | flops 1000000000 | bytes 100000 | tf_op jit(solution)/shard_map/invert/pallas_call | solution.py:32
  40.3 0.4 collective-permute-done.8.refs_1_
  40.7 0.6 collective-permute-start.9
  41.3 2.0 %sweep.8 = (f32[512,512]{1,0:T(8,128)S(1)}, f32[64,64]{1,0:T(8,128)S(1)}) custom-call(f32[512,512]{1,0:T(8,128)S(1)} %gram.1.h_ref, f32[64,64]{1,0:T(8,128)S(1)} %invert.1.inverse_ref), custom_call_target="tpu_custom_call" | custom-call | flops 2000000000 | bytes 100000 | tf_op jit(solution)/shard_map/sweep/pallas_call | solution.py:32
  43.3 1.8 %collective-permute-done.9.refs_1_ = f32[72,256]{1,0:T(8,128)S(1)} collective-permute-done((f32[72,256]{1,0:T(8,128)S(1)}, f32[72,256]{1,0:T(8,128)S(1)}, u32[]{:S(2)}, u32[]{:S(2)}) %collective-permute-start.9) | collective-permute-done | bytes 73760 | tf_op jit(solution)/shard_map/ppermute | solution.py:28
  45.1 1.1 %collective-permute-start.10 = (f32[40,256]{1,0:T(8,128)S(1)}, f32[40,256]{1,0:T(8,128)S(1)}, u32[]{:S(2)}, u32[]{:S(2)}) collective-permute-start(f32[40,256]{1,0:T(8,128)S(1)} %get-tuple-element.86), channel_id=1, source_target_pairs={{0,8},{1,9},{2,10},{3,11},{4,12},{5,13},{6,14},{7,15},{8,0},{9,1},... | collective-permute-start | bytes 122888 | tf_op jit(solution)/shard_map/ppermute | solution.py:28
  46.3 1.9 %sweep.9 = (f32[512,512]{1,0:T(8,128)S(1)}, f32[64,64]{1,0:T(8,128)S(1)}) custom-call(f32[512,512]{1,0:T(8,128)S(1)} %get-tuple-element.78.h_ref, f32[64,64]{1,0:T(8,128)S(1)} %get-tuple-element.79.inverse_ref), custom_call_target="tpu_custom_call" | custom-call | flops 2000000000 | bytes 100000 | tf_op jit(solution)/shard_map/sweep/pallas_call | solution.py:32
  48.2 2.0 %sweep.10 = (f32[512,512]{1,0:T(8,128)S(1)}, f32[64,64]{1,0:T(8,128)S(1)}) custom-call(f32[512,512]{1,0:T(8,128)S(1)} %get-tuple-element.80.h_ref, f32[64,64]{1,0:T(8,128)S(1)} %get-tuple-element.81.inverse_ref), custom_call_target="tpu_custom_call" | custom-call | flops 2000000000 | bytes 100000 | tf_op jit(solution)/shard_map/sweep/pallas_call | solution.py:32
  50.2 0.3 collective-permute-done.10.refs_1_
  50.5 1.6 %collective-permute-start.11 = (f32[32,256]{1,0:T(8,128)S(1)}, f32[32,256]{1,0:T(8,128)S(1)}, u32[]{:S(2)}, u32[]{:S(2)}) collective-permute-start(f32[32,256]{1,0:T(8,128)S(1)} %finish.1.refs_0_), channel_id=1, source_target_pairs={{0,8},{1,9},{2,10},{3,11},{4,12},{5,13},{6,14},{7,15},{8,0},{9,1},... | collective-permute-start | bytes 98312 | tf_op jit(solution)/shard_map/ppermute | solution.py:28
  52.2 1.9 %sweep.11 = (f32[512,512]{1,0:T(8,128)S(1)}, f32[64,64]{1,0:T(8,128)S(1)}) custom-call(f32[512,512]{1,0:T(8,128)S(1)} %get-tuple-element.87.h_ref, f32[64,64]{1,0:T(8,128)S(1)} %get-tuple-element.88.inverse_ref), custom_call_target="tpu_custom_call" | custom-call | flops 2000000000 | bytes 100000 | tf_op jit(solution)/shard_map/sweep/pallas_call | solution.py:32
  54.1 1.3 %collective-permute-done.11.refs_1_ = f32[32,256]{1,0:T(8,128)S(1)} collective-permute-done((f32[32,256]{1,0:T(8,128)S(1)}, f32[32,256]{1,0:T(8,128)S(1)}, u32[]{:S(2)}, u32[]{:S(2)}) %collective-permute-start.11) | collective-permute-done | bytes 32800 | tf_op jit(solution)/shard_map/ppermute | solution.py:28
  55.4 2.1 %collective-permute-start.12 = (f32[64,256]{1,0:T(8,128)S(1)}, f32[64,256]{1,0:T(8,128)S(1)}, u32[]{:S(2)}, u32[]{:S(2)}) collective-permute-start(f32[64,256]{1,0:T(8,128)S(1)} %stack.5.refs_0_), channel_id=1, source_target_pairs={{0,4},{1,5},{2,6},{3,7},{4,0},{5,1},{6,2},{7,3},{8,12},{9,13},{10,... | collective-permute-start | bytes 196616 | tf_op jit(solution)/shard_map/ppermute | solution.py:28
  57.6 2.1 %sweep.12 = (f32[512,512]{1,0:T(8,128)S(1)}, f32[64,64]{1,0:T(8,128)S(1)}) custom-call(f32[512,512]{1,0:T(8,128)S(1)} %get-tuple-element.93.h_ref, f32[64,64]{1,0:T(8,128)S(1)} %get-tuple-element.94.inverse_ref), custom_call_target="tpu_custom_call" | custom-call | flops 2000000000 | bytes 100000 | tf_op jit(solution)/shard_map/sweep/pallas_call | solution.py:32
  59.7 0.1 collective-permute-done.12.refs_1_
  59.8 1.6 %collective-permute-start.13 = (f32[128,256]{1,0:T(8,128)S(1)}, f32[128,256]{1,0:T(8,128)S(1)}, u32[]{:S(2)}, u32[]{:S(2)}) collective-permute-start(f32[128,256]{1,0:T(8,128)S(1)} %stack.6.a_ref), channel_id=1, source_target_pairs={{0,2},{1,3},{2,0},{3,1},{4,6},{5,7},{6,4},{7,5},{8,10},{9,11},{10,... | collective-permute-start | bytes 393224 | tf_op jit(solution)/shard_map/ppermute | solution.py:28
  61.5 1.9 %sweep.13 = (f32[512,512]{1,0:T(8,128)S(1)}, f32[64,64]{1,0:T(8,128)S(1)}) custom-call(f32[512,512]{1,0:T(8,128)S(1)} %get-tuple-element.98.h_ref, f32[64,64]{1,0:T(8,128)S(1)} %get-tuple-element.99.inverse_ref), custom_call_target="tpu_custom_call" | custom-call | flops 2000000000 | bytes 100000 | tf_op jit(solution)/shard_map/sweep/pallas_call | solution.py:32
  63.4 2.1 %sweep.14 = (f32[512,512]{1,0:T(8,128)S(1)}, f32[64,64]{1,0:T(8,128)S(1)}) custom-call(f32[512,512]{1,0:T(8,128)S(1)} %get-tuple-element.100.h_ref, f32[64,64]{1,0:T(8,128)S(1)} %get-tuple-element.101.inverse_ref), custom_call_target="tpu_custom_call" | custom-call | flops 2000000000 | bytes 100000 | tf_op jit(solution)/shard_map/sweep/pallas_call | solution.py:32
  65.5 0.1 collective-permute-start.14
  65.6 0.7 sweep.15.minus_ref
  66.4 0.8 %collective-permute-done.14.other_ref = f32[128,512]{1,0:T(8,128)S(1)} collective-permute-done((f32[128,512]{1,0:T(8,128)S(1)}, f32[128,512]{1,0:T(8,128)S(1)}, u32[]{:S(2)}, u32[]{:S(2)}) %collective-permute-start.14) | collective-permute-done | bytes 262176 | tf_op jit(solution)/shard_map/ppermute | solution.py:28
  67.1 1.9 %fit.1 = (f32[128,512]{1,0:T(8,128)S(1)}, f32[8,128]{1,0:T(8,128)S(1)}) custom-call(s32[1]{0:T(128)} %bitcast.shard_ref, f32[512,512]{1,0:T(8,128)S(1)} %sweep.15.minus_ref, bf16[512,1024]{1,0:T(8,128)(2,1)S(1)} %get-tuple-element.67.high_ref, bf16[512,1024]{1,0:T(8,128)(2,1)S(1)} %get-tuple-element.68.low_ref, f32[128,512]{1,0:T(8,128)S(1)} %stack.7.own_ref, ...), custom_call_target="tpu_custom_call" | custom-call | flops 1000000000 | bytes 100000 | tf_op jit(solution)/shard_map/fit/pallas_call | solution.py:32
  69.0 1.6 %collective-permute-start.15 = (f32[8,128]{1,0:T(8,128)S(1)}, f32[8,128]{1,0:T(8,128)S(1)}, u32[]{:S(2)}, u32[]{:S(2)}) collective-permute-start(f32[8,128]{1,0:T(8,128)S(1)} %get-tuple-element.111.refs_0_), channel_id=1, source_target_pairs={{0,16},{16,0},{1,17},{17,1},{2,18},{18,2},{3,19},{19,3},{4,20},{20... | collective-permute-start | bytes 12296 | tf_op jit(solution)/shard_map/ppermute | solution.py:28
  70.6 0.8 %flip.1 = f32[512,128]{1,0:T(8,128)} custom-call(f32[128,512]{1,0:T(8,128)S(1)} %get-tuple-element.110.x_ref), custom_call_target="tpu_custom_call" | custom-call | flops 1000000 | bytes 100000 | tf_op jit(solution)/shard_map/flip/pallas_call | solution.py:32
  71.4 1.3 %collective-permute-done.15.refs_1_ = f32[8,128]{1,0:T(8,128)S(1)} collective-permute-done((f32[8,128]{1,0:T(8,128)S(1)}, f32[8,128]{1,0:T(8,128)S(1)}, u32[]{:S(2)}, u32[]{:S(2)}) %collective-permute-start.15) | collective-permute-done | bytes 4128 | tf_op jit(solution)/shard_map/ppermute | solution.py:28
  72.7 0.5 mean.1
  (16 shorter events, 0.3 us)
Async XLA Ops:
  0.6 7.3 %copy-start = (bf16[1,4096,128]{2,1,0:T(8,128)(2,1)S(1)}, bf16[1,4096,128]{2,1,0:T(8,128)(2,1)}, u32[]{:S(2)}) copy-start(bf16[1,4096,128]{2,1,0:T(8,128)(2,1)} %param.7) | copy-start | bytes 3145732
  3.4 1.6 %collective-permute-start = (bf16[768,128]{1,0:T(8,128)(2,1)S(1)}, bf16[768,128]{1,0:T(8,128)(2,1)S(1)}, u32[]{:S(2)}, u32[]{:S(2)}) collective-permute-start(bf16[768,128]{1,0:T(8,128)(2,1)S(1)} %get-tuple-element.58), channel_id=1, source_target_pairs={{0,1},{1,0},{2,3},{3,2},{4,5},{5,4},{6,7},{7,6},{8,9},{9,8},{10,11... | collective-permute-start | bytes 589832 | tf_op jit(solution)/shard_map/ppermute | solution.py:28
  5.0 6.0 %collective-permute-start.1 = (bf16[384,128]{1,0:T(8,128)(2,1)S(1)}, bf16[384,128]{1,0:T(8,128)(2,1)S(1)}, u32[]{:S(2)}, u32[]{:S(2)}) collective-permute-start(bf16[384,128]{1,0:T(8,128)(2,1)S(1)} %get-tuple-element.60), channel_id=1, source_target_pairs={{0,2},{1,3},{2,0},{3,1},{4,6},{5,7},{6,4},{7,5},{8,10},{9,11},{10,... | collective-permute-start | bytes 294920 | tf_op jit(solution)/shard_map/ppermute | solution.py:28
  11.1 7.6 %collective-permute-start.4 = (bf16[384,128]{1,0:T(8,128)(2,1)S(1)}, bf16[384,128]{1,0:T(8,128)(2,1)S(1)}, u32[]{:S(2)}, u32[]{:S(2)}) collective-permute-start(bf16[384,128]{1,0:T(8,128)(2,1)S(1)} %total.2.refs_0_), channel_id=1, source_target_pairs={{0,12},{1,13},{2,14},{3,15},{4,8},{5,9},{6,10},{7,11},{8,4},{9,5},... | collective-permute-start | bytes 294920 | tf_op jit(solution)/shard_map/ppermute | solution.py:28
  15.0 7.7 %collective-permute-start.3 = (bf16[384,128]{1,0:T(8,128)(2,1)S(1)}, bf16[384,128]{1,0:T(8,128)(2,1)S(1)}, u32[]{:S(2)}, u32[]{:S(2)}) collective-permute-start(bf16[384,128]{1,0:T(8,128)(2,1)S(1)} %total.2.refs_0_), channel_id=1, source_target_pairs={{0,8},{1,9},{2,10},{3,11},{4,12},{5,13},{6,14},{7,15},{8,0},{9,1},... | collective-permute-start | bytes 294920 | tf_op jit(solution)/shard_map/ppermute | solution.py:28
  15.0 7.7 %collective-permute-start.2 = (bf16[384,128]{1,0:T(8,128)(2,1)S(1)}, bf16[384,128]{1,0:T(8,128)(2,1)S(1)}, u32[]{:S(2)}, u32[]{:S(2)}) collective-permute-start(bf16[384,128]{1,0:T(8,128)(2,1)S(1)} %total.2.refs_0_), channel_id=1, source_target_pairs={{0,4},{1,5},{2,6},{3,7},{4,0},{5,1},{6,2},{7,3},{8,12},{9,13},{10,... | collective-permute-start | bytes 294920 | tf_op jit(solution)/shard_map/ppermute | solution.py:28
  22.8 4.7 %collective-permute-start.5 = (bf16[384,128]{1,0:T(8,128)(2,1)S(1)}, bf16[384,128]{1,0:T(8,128)(2,1)S(1)}, u32[]{:S(2)}, u32[]{:S(2)}) collective-permute-start(bf16[384,128]{1,0:T(8,128)(2,1)S(1)} %total.3.q_ref.a_ref.near_ref), channel_id=1, source_target_pairs={{0,2},{1,3},{2,0},{3,1},{4,6},{5,7},{6,4},{7,5},{8,10},{9,11},{10,... | collective-permute-start | bytes 294920 | tf_op jit(solution)/shard_map/ppermute | solution.py:28
  27.5 1.9 %collective-permute-start.6 = (bf16[768,128]{1,0:T(8,128)(2,1)S(1)}, bf16[768,128]{1,0:T(8,128)(2,1)S(1)}, u32[]{:S(2)}, u32[]{:S(2)}) collective-permute-start(bf16[768,128]{1,0:T(8,128)(2,1)S(1)} %stack.4), channel_id=1, source_target_pairs={{0,1},{1,0},{2,3},{3,2},{4,5},{5,4},{6,7},{7,6},{8,9},{9,8},{10,11... | collective-permute-start | bytes 589832 | tf_op jit(solution)/shard_map/ppermute | solution.py:28
  29.4 5.6 %collective-permute-start.7 = (f32[136,512]{1,0:T(8,128)S(1)}, f32[136,512]{1,0:T(8,128)S(1)}, u32[]{:S(2)}, u32[]{:S(2)}) collective-permute-start(f32[136,512]{1,0:T(8,128)S(1)} %attention.4), channel_id=1, source_target_pairs={{0,1},{1,0},{2,3},{3,2},{4,5},{5,4},{6,7},{7,6},{8,9},{9,8},{10,11... | collective-permute-start | bytes 835592 | tf_op jit(solution)/shard_map/ppermute | solution.py:28
  35.0 5.7 %collective-permute-start.8 = (f32[136,256]{1,0:T(8,128)S(1)}, f32[136,256]{1,0:T(8,128)S(1)}, u32[]{:S(2)}, u32[]{:S(2)}) collective-permute-start(f32[136,256]{1,0:T(8,128)S(1)} %get-tuple-element.70), channel_id=1, source_target_pairs={{0,2},{1,3},{2,0},{3,1},{4,6},{5,7},{6,4},{7,5},{8,10},{9,11},{10,... | collective-permute-start | bytes 417800 | tf_op jit(solution)/shard_map/ppermute | solution.py:28
  40.7 4.4 %collective-permute-start.9 = (f32[72,256]{1,0:T(8,128)S(1)}, f32[72,256]{1,0:T(8,128)S(1)}, u32[]{:S(2)}, u32[]{:S(2)}) collective-permute-start(f32[72,256]{1,0:T(8,128)S(1)} %get-tuple-element.77), channel_id=1, source_target_pairs={{0,4},{1,5},{2,6},{3,7},{4,0},{5,1},{6,2},{7,3},{8,12},{9,13},{10,... | collective-permute-start | bytes 221192 | tf_op jit(solution)/shard_map/ppermute | solution.py:28
  45.1 5.4 %collective-permute-start.10 = (f32[40,256]{1,0:T(8,128)S(1)}, f32[40,256]{1,0:T(8,128)S(1)}, u32[]{:S(2)}, u32[]{:S(2)}) collective-permute-start(f32[40,256]{1,0:T(8,128)S(1)} %get-tuple-element.86), channel_id=1, source_target_pairs={{0,8},{1,9},{2,10},{3,11},{4,12},{5,13},{6,14},{7,15},{8,0},{9,1},... | collective-permute-start | bytes 122888 | tf_op jit(solution)/shard_map/ppermute | solution.py:28
  50.5 4.9 %collective-permute-start.11 = (f32[32,256]{1,0:T(8,128)S(1)}, f32[32,256]{1,0:T(8,128)S(1)}, u32[]{:S(2)}, u32[]{:S(2)}) collective-permute-start(f32[32,256]{1,0:T(8,128)S(1)} %finish.1.refs_0_), channel_id=1, source_target_pairs={{0,8},{1,9},{2,10},{3,11},{4,12},{5,13},{6,14},{7,15},{8,0},{9,1},... | collective-permute-start | bytes 98312 | tf_op jit(solution)/shard_map/ppermute | solution.py:28
  55.4 4.4 %collective-permute-start.12 = (f32[64,256]{1,0:T(8,128)S(1)}, f32[64,256]{1,0:T(8,128)S(1)}, u32[]{:S(2)}, u32[]{:S(2)}) collective-permute-start(f32[64,256]{1,0:T(8,128)S(1)} %stack.5.refs_0_), channel_id=1, source_target_pairs={{0,4},{1,5},{2,6},{3,7},{4,0},{5,1},{6,2},{7,3},{8,12},{9,13},{10,... | collective-permute-start | bytes 196616 | tf_op jit(solution)/shard_map/ppermute | solution.py:28
  59.8 5.7 %collective-permute-start.13 = (f32[128,256]{1,0:T(8,128)S(1)}, f32[128,256]{1,0:T(8,128)S(1)}, u32[]{:S(2)}, u32[]{:S(2)}) collective-permute-start(f32[128,256]{1,0:T(8,128)S(1)} %stack.6.a_ref), channel_id=1, source_target_pairs={{0,2},{1,3},{2,0},{3,1},{4,6},{5,7},{6,4},{7,5},{8,10},{9,11},{10,... | collective-permute-start | bytes 393224 | tf_op jit(solution)/shard_map/ppermute | solution.py:28
  65.5 1.6 %collective-permute-start.14 = (f32[128,512]{1,0:T(8,128)S(1)}, f32[128,512]{1,0:T(8,128)S(1)}, u32[]{:S(2)}, u32[]{:S(2)}) collective-permute-start(f32[128,512]{1,0:T(8,128)S(1)} %stack.7.own_ref), channel_id=1, source_target_pairs={{0,1},{1,0},{2,3},{3,2},{4,5},{5,4},{6,7},{7,6},{8,9},{9,8},{10,11... | collective-permute-start | bytes 786440 | tf_op jit(solution)/shard_map/ppermute | solution.py:28
  69.0 3.7 %collective-permute-start.15 = (f32[8,128]{1,0:T(8,128)S(1)}, f32[8,128]{1,0:T(8,128)S(1)}, u32[]{:S(2)}, u32[]{:S(2)}) collective-permute-start(f32[8,128]{1,0:T(8,128)S(1)} %get-tuple-element.111.refs_0_), channel_id=1, source_target_pairs={{0,16},{16,0},{1,17},{17,1},{2,18},{18,2},{3,19},{19,3},{4,20},{20... | collective-permute-start | bytes 12296 | tf_op jit(solution)/shard_map/ppermute | solution.py:28

commit v9 on v8

--- a/solution.py
+++ b/solution.py
@@ -59,6 +59,52 @@
     rows = high.shape[0]
     both = dot(jnp.concatenate([high, low], axis=0), right_high, dims)
     return both[:rows] + (both[rows:] + dot(high, right_low, dims))
+
+
+def pack(out, top, total):
+    rows = out.shape[0] // 2
+    mean = out * (1.0 / total)
+    code = (jnp.max(jnp.abs(mean), axis=0, keepdims=True) * 2.0**27).astype(jnp.int32) + 1
+    fixed = jnp.round(mean * (32767.0 / (code.astype(F32) * 2.0**-27))).astype(jnp.int32)
+    words = (fixed[:rows] << 16) | (fixed[rows:] & 0xFFFF)
+    level = jnp.floor(top + jnp.log2(total))
+    rest = (total * jnp.exp2(top - level) * 2.0**28).astype(jnp.int32)
+    blank = jnp.zeros((SUB - 3, top.shape[1]), jnp.int32)
+    return jnp.concatenate([words, code, level.astype(jnp.int32), rest, blank], axis=0)
+
+
+def means(packed):
+    rows = packed.shape[0] - SUB
+    words = packed[:rows]
+    fixed = jnp.concatenate([words >> 16, (words << 16) >> 16], axis=0)
+    return fixed.astype(F32) * (packed[rows : rows + 1].astype(F32) * (2.0**-27 / 32767.0))
+
+
+def tail(top, total):
+    return jnp.concatenate([top, total, jnp.zeros((SUB - 2, top.shape[1]), F32)], axis=0)
+
+
+def partial_of(ref):
+    rows = ref.shape[0] - SUB
+    if ref.dtype == F32:
+        return ref[:rows, :], ref[rows : rows + 1, :], ref[rows + 1 : rows + 2, :]
+    packed = ref[...]
+    rest = packed[rows + 2 : rows + 3].astype(F32) * 2.0**-28
+    return means(packed) * rest, packed[rows + 1 : rows + 2].astype(F32), rest
+
+
+def put_partial(ref, out, top, total):
+    if ref.dtype == F32:
+        ref[: out.shape[0], :] = out
+        ref[out.shape[0] :, :] = tail(top, total)
+    else:
+        ref[...] = pack(out, top, total)
+
+
+def partial_shape(rows, lanes, packed):
+    if packed and rows % 16 == 0:
+        return (rows // 2 + SUB, lanes), jnp.int32
+    return (rows + SUB, lanes), F32
 
 
 def prepare_kernel(window, shard_ref, root_ref, q_hbm, kept_hbm, k_hbm, *refs):
@@ -162,11 +208,14 @@
     first = attend_to(near, keys, turned)
     far, first = lax.optimization_barrier((far, first))
     (both,) = call(stack_kernel, (near, far), [(half, BF16)], name="stack")
-    other = swap(both, "ctx", 1)
-    send = attend_to(far, keys, turned, before=[first])
-    other, send = lax.optimization_barrier((other, send))
-    came = swap(send, "ctx", 1)
-    return near, far, other, attend_to(other, keys, turned), came
+    other, came = swap(both, "ctx", 1), [swap(first, "ctx", 1)]
+    second = attend_to(far, keys, turned)
+    other, second = lax.optimization_barrier((other, second))
+    came.append(swap(second, "ctx", 3))
+    third = attend_to(other, keys, turned, start=quarter[0])
+    came.append(swap(third, "ctx", 2))
+    other, third = lax.optimization_barrier((other, third))
+    return near, far, other, attend_to(other, keys, turned, packed=False), came
 
 
 def turn_kernel(v_ref, vt_ref):
@@ -175,95 +224,63 @@
     vt_ref[dims:, :] = jnp.ones((vt_ref.shape[0] - dims, v_ref.shape[0]), BF16)
 
 
-def quarters_of(ref, rows, tall):
-    return [ref[i : i + rows, :] for i in range(0, ref.shape[0], tall)]
-
-
-def attention_kernel(lanes, tall, block, score_scale, q_ref, k_ref, vt_ref, *refs):
-    before, out_ref = refs[:-1], refs[-1]
-    quarters = quarters_of(q_ref, lanes, tall)
+def attention_kernel(start, block, score_scale, q_ref, k_ref, vt_ref, out_ref):
     dims = k_ref.shape[1]
-    blocks = k_ref.shape[0] // block
+    lanes = out_ref.shape[1]
     factor = score_scale * math.log2(math.e)
-    skip = len(before) * lanes
-    for ref in before:
-        out_ref[:, :skip] = ref[...]
-
-    def scores(i, b):
-        return lax.dot_general(
-            k_ref[b * block : (b + 1) * block, :], quarters[i], NT, preferred_element_type=F32
-        )
-
-    stages = [(i, b) for i in range(len(quarters)) for b in range(blocks)]
-    ahead = scores(*stages[0])
-    for n, (i, b) in enumerate(stages):
+    queries = q_ref[start : start + lanes, :]
+    scores = lambda b: dot(k_ref[b : b + block, :], queries, NT)
+    slab = k_ref.shape[0]
+    ahead = scores(0)
+    for b in range(0, slab, block):
         s = ahead
-        if n + 1 < len(stages):
-            ahead = scores(*stages[n + 1])
-        at = slice(skip + i * lanes, skip + (i + 1) * lanes)
+        if b + block < slab:
+            ahead = scores(b + block)
         top = jnp.max(s, axis=0, keepdims=True)
         e = jnp.exp2((s - top) * factor).astype(BF16)
-        out = lax.dot_general(vt_ref[:, b * block : (b + 1) * block], e, NN, preferred_element_type=F32)
+        out = dot(vt_ref[:, b : b + block], e, NN)
         top = top * factor
         total = out[dims : dims + 1, :]
         out = out[:dims, :]
         if b:
-            old_top = out_ref[dims : dims + 1, at]
             joint = jnp.maximum(old_top, top)
             old_scale = jnp.exp2(old_top - joint)
             new_scale = jnp.exp2(top - joint)
-            out = out_ref[:dims, at] * old_scale + out * new_scale
-            total = out_ref[dims + 1 : dims + 2, at] * old_scale + total * new_scale
+            out = old_out * old_scale + out * new_scale
+            total = old_total * old_scale + total * new_scale
             top = joint
-        out_ref[:dims, at] = out
-        out_ref[dims:, at] = tail(top, total)
-
-
-def attention(lanes, tall, score_scale, piece, keys, turned, before=()):
+        old_out, old_top, old_total = out, top, total
+    put_partial(out_ref, out, top, total)
+
+
+def attention(lanes, score_scale, piece, keys, turned, start=0, packed=True):
     slab, dims = keys.shape
-    count = piece.shape[0] // tall
     return call(
-        functools.partial(attention_kernel, lanes, tall, min(KBLK, slab), score_scale),
-        (piece, keys, turned, *before),
-        [((dims + SUB, lanes * (count + len(before))), F32)],
-        4 * lanes * count * slab * dims,
+        functools.partial(attention_kernel, start, min(KBLK, slab), score_scale),
+        (piece, keys, turned),
+        [partial_shape(dims, lanes, packed)],
+        10**6,
         name="attention",
     )[0]
 
 
 def merged(*refs):
-    dims = refs[0].shape[0] - SUB
-    tops = [ref[dims : dims + 1, :] for ref in refs]
-    top = functools.reduce(jnp.maximum, tops)
-    scales = [jnp.exp2(t - top) for t in tops]
-    total = sum(ref[dims + 1 : dims + 2, :] * scale for ref, scale in zip(refs, scales))
-    out = sum(ref[:dims, :] * scale for ref, scale in zip(refs, scales))
+    parts = [partial_of(ref) for ref in refs]
+    top = functools.reduce(jnp.maximum, [part[1] for part in parts])
+    scales = [jnp.exp2(part[1] - top) for part in parts]
+    total = sum(part[2] * scale for part, scale in zip(parts, scales))
+    out = sum(part[0] * scale for part, scale in zip(parts, scales))
     return out, top, total
 
 
-def tail(top, total):
-    return jnp.concatenate([top, total, jnp.zeros((SUB - 2, top.shape[1]), F32)], axis=0)
-
-
-def merge_lanes_kernel(a_ref, b_ref, keep_ref, send_ref):
-    out, top, total = merged(a_ref, b_ref)
-    dims, lanes = out.shape[0], keep_ref.shape[1]
-    for ref, at in ((keep_ref, slice(0, lanes)), (send_ref, slice(lanes, 2 * lanes))):
-        ref[:dims, :] = out[:, at]
-        ref[dims:, :] = tail(top[:, at], total[:, at])
-
-
-def merge_rows_kernel(step, shard_ref, *refs):
-    work, refs = refs[-1], refs[:-1]
-    ways = sum(1 for ref in refs if ref.shape[0] != refs[0].shape[0])
-    ins, outs = refs[:-ways], refs[-ways:]
+def merge_kernel(step, shard_ref, *refs):
+    ins, (keep_ref, send_ref, work) = refs[:-3], refs[-3:]
     out, top, total = merged(*ins)
-    rows = outs[0].shape[0] - SUB
+    rows = out.shape[0] // 2
     work[...] = out
-    digit = (shard_ref[0] // step) % ways
-    for t, ref in enumerate(outs):
-        ref[:rows, :] = work[aligned(digit ^ t, rows), :]
-        ref[rows:, :] = tail(top, total)
+    bit = (shard_ref[0] // step) % 2
+    put_partial(keep_ref, work[aligned(bit, rows), :], top, total)
+    put_partial(send_ref, work[aligned(1 - bit, rows), :], top, total)
 
 
 def finish_kernel(*refs):
@@ -271,46 +288,45 @@
     refs[-1][...] = out / total
 
 
-def stack_rows_kernel(step, shard_ref, *refs):
-    ins, out_ref = refs[:-1], refs[-1]
-    rows = ins[0].shape[0]
-    digit = (shard_ref[0] // step) % len(ins)
-    for t, ref in enumerate(ins):
-        out_ref[aligned(digit ^ t, rows), :] = ref[...]
-
-
-def stack_lanes_kernel(a_ref, b_ref, out_ref):
-    lanes = a_ref.shape[1]
-    out_ref[:, :lanes] = a_ref[...]
-    out_ref[:, lanes:] = b_ref[...]
+def stack_rows_kernel(step, shard_ref, a_ref, b_ref, out_ref):
+    rows = a_ref.shape[0]
+    bit = (shard_ref[0] // step) % 2
+    out_ref[aligned(bit, rows), :] = a_ref[...]
+    out_ref[aligned(1 - bit, rows), :] = b_ref[...]
+
+
+def pack_kernel(y_ref, out_ref):
+    one = jnp.ones((1, y_ref.shape[1]), F32)
+    out_ref[...] = pack(y_ref[...], one * 0.0, one)
 
 
 def target_rounds(shard, keep, came):
-    dims, lanes = keep.shape[0] - SUB, keep.shape[1] // 2
+    dims, lanes = keep.shape[0] - SUB, keep.shape[1]
     devices = lax.axis_size("ctx")
-    keep, send = call(merge_lanes_kernel, (keep, came), [((dims + SUB, lanes), F32)] * 2, name="merge")
-    came = yield [swap(send, "ctx", 2)]
-    digits = [(step, 2) for step in (2**i for i in range(2, devices.bit_length() - 1))]
+    came = yield came
+    steps = [2**i for i in range(2, devices.bit_length() - 1)]
     rows = dims
-    for step, ways in digits:
-        keep, *send = call(
-            functools.partial(merge_rows_kernel, step),
+    for step in steps:
+        keep, send = call(
+            functools.partial(merge_kernel, step),
             (shard, keep, *came),
-            [((rows // ways + SUB, lanes), F32)] * ways,
+            [partial_shape(rows // 2, lanes, packed) for packed in (False, True)],
             scratch=[pltpu.VMEM((rows, lanes), F32)],
             name="merge",
         )
-        came = yield [swap(x, "ctx", t * step) for t, x in enumerate(send, 1)]
-        rows //= ways
+        came = yield [swap(send, "ctx", step)]
+        rows //= 2
     (block,) = call(finish_kernel, (keep, *came), [((rows, lanes), F32)], name="finish")
-    for step, ways in reversed(digits):
-        came = yield [swap(block, "ctx", t * step) for t in range(1, ways)]
-        rows *= ways
+    for step in reversed(steps):
+        came = yield [swap(block, "ctx", step)]
+        rows *= 2
         (block,) = call(
             functools.partial(stack_rows_kernel, step), (shard, block, *came), [((rows, lanes), F32)], name="stack"
         )
+    shape, kind = partial_shape(dims, lanes, True)
+    (block,) = call(pack_kernel, (block,), [(shape, kind)], name="pack")
     came = yield [swap(block, "ctx", 2)]
-    (block,) = call(stack_lanes_kernel, (block, *came), [((dims, 2 * lanes), F32)], name="stack")
+    (block,) = call(stack_kernel, (block, *came), [((2 * shape[0], lanes), kind)], name="stack")
     came = yield [swap(block, "ctx", 1)]
     return block, *came
 
@@ -438,11 +454,11 @@
 
 
 def fit_kernel(shard_ref, minus_ref, high_ref, low_ref, own_ref, other_ref, x_ref, err_ref, yt):
-    lanes = own_ref.shape[1] // 2
+    rows, lanes = own_ref.shape[0] // 2, own_ref.shape[1]
     place = shard_ref[0] % 4
     for s, ref in ((1, own_ref), (3, own_ref), (0, other_ref), (2, other_ref)):
         half = s // 2
-        yt[:, aligned(place ^ s, lanes)] = ref[:, half * lanes : (half + 1) * lanes]
+        yt[:, aligned(place ^ s, lanes)] = means(ref[half * rows : (half + 1) * rows, :])
     target = yt[...]
     attend = high_ref[...], low_ref[...]
     cross = product(halves(target), attend, NT)
@@ -471,7 +487,7 @@
     score_scale = 1.0 / math.sqrt(dims)
     shard = lax.axis_index("ctx").astype(jnp.int32).reshape(1)
 
-    attend_to = functools.partial(attention, lanes, (rows + count) // 4, score_scale)
+    attend_to = functools.partial(attention, lanes, score_scale)
     near, far, other, keep, came = spread(shard, queries[0, 0], kept, keys[0], roots, values[0], attend_to)
     rounds = target_rounds(shard, keep, came)
     came = next(rounds)
@@ -492,15 +508,16 @@
         functools.partial(attend_kernel, score_scale),
         (shard, near, far, other),
         [((count, rows), BF16)] * 2,
-        10**9,
+        10**6,
         scratch=[pltpu.VMEM((count, dims), BF16)],
         name="attend",
     )
+    attend = beside(attend)
     (system,) = call(gram_kernel, attend, [system_shape], 4 * 10**9, name="gram")
+    system = beside(system)
     panels = count // PANEL
     block_shape = ((PANEL, PANEL), F32)
     (inverse,) = call(invert_kernel, (system,), [block_shape], 10**9, name="invert")
-    system, inverse = beside((system, inverse))
     for panel in range(panels):
         last = panel == panels - 1
         system, *inverse = call(
@@ -511,7 +528,7 @@
             name="sweep",
         )
         inverse = None if last else inverse[0]
-        if panel not in (panels - 7, panels - 3):
+        if panel in (0, 2, 3, 5, 6):
             system, inverse = beside((system, inverse))
     while ends is None:
         system = beside(system)

time: 73.4 us -> 72.5 us (0.988)
  starting transfers between devices: 20.5 us -> 18.8 us
    ppermute x16 -> x17, starting transfers between devices: 20.5 us -> 18.8 us  [swap(): return lax.ppermute(array, axis, [(i, i ^ step) for i in range(size)])]
    ppermute x16 -> x17, waiting for transfers between devices: 18.3 us -> 18.6 us  [swap(): return lax.ppermute(array, axis, [(i, i ^ step) for i in range(size)])]
    pallas_call x30 -> x31, Pallas kernels: 32.9 us -> 33.2 us  [call(): pl.pallas_call(kernel, in_specs=specs or [SMEM if x.size == 1 else VMEM f...]
  transfers between devices with their start and end apart: 16 -> 17, of which waited for: 12 -> 11; matrix products, arithmetic and copies ran while one was open for 0% -> 0% of each run, Pallas kernels for 39% -> 36%
where the time goes in v9:
time: 72.5 us; the launch traced here: 72.3 us
  Pallas kernels  33.2 us (46%)
  starting transfers between devices  18.8 us (26%)
  waiting for transfers between devices  18.6 us (26%)
  between operations  1.62 us (2%)
    pallas_call x31, Pallas kernels, call(): pl.pallas_call(kernel, in_specs=specs or [SMEM if x.size == 1 else VMEM f...  33.2 us
    ppermute x17, starting transfers between devices, swap(): return lax.ppermute(array, axis, [(i, i ^ step) for i in range(size)])  18.8 us
    ppermute x17, waiting for transfers between devices, swap(): return lax.ppermute(array, axis, [(i, i ^ step) for i in range(size)])  18.6 us
  transfers between devices with their start and end apart: 17, of which 11 were waited for; matrix products, arithmetic and copies ran while one was open for 0% of the time, Pallas kernels for 36%

profile of v9, /device:TPU:0, one launch (start us, length us, event | category | flops | bytes accessed | tf_op | source)
XLA Modules:
  0.0 72.3 jit_solution(11820887808492207319)
XLA Ops:
  1.4 2.0 %prepare.1 = (bf16[768,128]{1,0:T(8,128)(2,1)S(1)}, bf16[768,128]{1,0:T(8,128)(2,1)S(1)}, bf16[4096,128]{1,0:T(8,128)(2,1)S(1)}) custom-call(s32[1]{0:T(128)} %bitcast.shard_ref, s32[1]{0:T(128)S(6)} %copy.7.root_ref, bf16[1024,128]{1,0:T(8,128)(2,1)} %bitcast.9, s32[1,512]{1,0:T(1,128)} %kept_hbm.1, bf16[4096,128]{1,0:T(8,128)(2,1)} %bitcast.7), custom_call_target="tpu_custom_call" | custom-call | flops 100000 | bytes 100000 | tf_op jit(solution)/shard_map/prepare/pallas_call | solution.py:32
  3.4 0.5 collective-permute-start
  3.9 1.1 %collective-permute-done.b_ref = bf16[768,128]{1,0:T(8,128)(2,1)S(1)} collective-permute-done((bf16[768,128]{1,0:T(8,128)(2,1)S(1)}, bf16[768,128]{1,0:T(8,128)(2,1)S(1)}, u32[]{:S(2)}, u32[]{:S(2)}) %collective-permute-start) | collective-permute-done | bytes 196640 | tf_op jit(solution)/shard_map/ppermute | solution.py:28
  5.0 3.0 %collective-permute-start.1 = (bf16[384,128]{1,0:T(8,128)(2,1)S(1)}, bf16[384,128]{1,0:T(8,128)(2,1)S(1)}, u32[]{:S(2)}, u32[]{:S(2)}) collective-permute-start(bf16[384,128]{1,0:T(8,128)(2,1)S(1)} %get-tuple-element.61), channel_id=1, source_target_pairs={{0,2},{1,3},{2,0},{3,1},{4,6},{5,7},{6,4},{7,5},{8,10},{9,11},{10,... | collective-permute-start | bytes 294920 | tf_op jit(solution)/shard_map/ppermute | solution.py:28
  7.9 0.3 turn.1.vt_ref
  8.3 2.8 %collective-permute-done.1.refs_1_ = bf16[384,128]{1,0:T(8,128)(2,1)S(1)} collective-permute-done((bf16[384,128]{1,0:T(8,128)(2,1)S(1)}, bf16[384,128]{1,0:T(8,128)(2,1)S(1)}, u32[]{:S(2)}, u32[]{:S(2)}) %collective-permute-start.1) | collective-permute-done | bytes 98336 | tf_op jit(solution)/shard_map/ppermute | solution.py:28
  11.1 3.9 %collective-permute-start.4 = (bf16[384,128]{1,0:T(8,128)(2,1)S(1)}, bf16[384,128]{1,0:T(8,128)(2,1)S(1)}, u32[]{:S(2)}, u32[]{:S(2)}) collective-permute-start(bf16[384,128]{1,0:T(8,128)(2,1)S(1)} %total.2.refs_0_), channel_id=1, source_target_pairs={{0,12},{1,13},{2,14},{3,15},{4,8},{5,9},{6,10},{7,11},{8,4},{9,5},... | collective-permute-start | bytes 294920 | tf_op jit(solution)/shard_map/ppermute | solution.py:28
  15.0 0.6 collective-permute-start.2
  15.6 3.1 %collective-permute-done.4.refs_3_ = bf16[384,128]{1,0:T(8,128)(2,1)S(1)} collective-permute-done((bf16[384,128]{1,0:T(8,128)(2,1)S(1)}, bf16[384,128]{1,0:T(8,128)(2,1)S(1)}, u32[]{:S(2)}, u32[]{:S(2)}) %collective-permute-start.4) | collective-permute-done | bytes 98336 | tf_op jit(solution)/shard_map/ppermute | solution.py:28
  18.7 4.0 %collective-permute-done.3.refs_2_ = bf16[384,128]{1,0:T(8,128)(2,1)S(1)} collective-permute-done((bf16[384,128]{1,0:T(8,128)(2,1)S(1)}, bf16[384,128]{1,0:T(8,128)(2,1)S(1)}, u32[]{:S(2)}, u32[]{:S(2)}) %collective-permute-start.3) | collective-permute-done | bytes 98336 | tf_op jit(solution)/shard_map/ppermute | solution.py:28
  22.7 1.6 %collective-permute-start.5 = (bf16[384,128]{1,0:T(8,128)(2,1)S(1)}, bf16[384,128]{1,0:T(8,128)(2,1)S(1)}, u32[]{:S(2)}, u32[]{:S(2)}) collective-permute-start(bf16[384,128]{1,0:T(8,128)(2,1)S(1)} %total.3.q_ref.a_ref.near_ref), channel_id=1, source_target_pairs={{0,2},{1,3},{2,0},{3,1},{4,6},{5,7},{6,4},{7,5},{8,10},{9,11},{10,... | collective-permute-start | bytes 294920 | tf_op jit(solution)/shard_map/ppermute | solution.py:28
  24.3 1.8 %attention.4 = s32[72,256]{1,0:T(8,128)S(1)} custom-call(bf16[384,128]{1,0:T(8,128)(2,1)S(1)} %total.3.q_ref.a_ref.near_ref, bf16[4096,128]{1,0:T(8,128)(2,1)S(1)} %get-tuple-element.63.k_ref, bf16[144,4096]{1,0:T(8,128)(2,1)S(1)} %turn.1.vt_ref), custom_call_target="tpu_custom_call" | custom-call | flops 1000000 | bytes 100000 | tf_op jit(solution)/shard_map/attention/pallas_call | solution.py:32
  26.1 1.3 %collective-permute-done.5.b_ref.q_ref.far_ref = bf16[384,128]{1,0:T(8,128)(2,1)S(1)} collective-permute-done((bf16[384,128]{1,0:T(8,128)(2,1)S(1)}, bf16[384,128]{1,0:T(8,128)(2,1)S(1)}, u32[]{:S(2)}, u32[]{:S(2)}) %collective-permute-start.5) | collective-permute-done | bytes 98336 | tf_op jit(solution)/shard_map/ppermute | solution.py:28
  27.4 0.1 collective-permute-start.6
  27.5 0.5 collective-permute-start.7
  28.0 1.8 %attention.5 = s32[72,256]{1,0:T(8,128)S(1)} custom-call(bf16[384,128]{1,0:T(8,128)(2,1)S(1)} %collective-permute-done.5.b_ref.q_ref.far_ref, bf16[4096,128]{1,0:T(8,128)(2,1)S(1)} %get-tuple-element.63.k_ref, bf16[144,4096]{1,0:T(8,128)(2,1)S(1)} %turn.1.vt_ref), custom_call_target="tpu_custom_call" | custom-call | flops 1000000 | bytes 100000 | tf_op jit(solution)/shard_map/attention/pallas_call | solution.py:32
  29.9 1.8 %attention.6 = s32[72,256]{1,0:T(8,128)S(1)} custom-call(bf16[768,128]{1,0:T(8,128)(2,1)S(1)} %collective-permute-done.6.q_ref.other_ref, bf16[4096,128]{1,0:T(8,128)(2,1)S(1)} %get-tuple-element.63.k_ref, bf16[144,4096]{1,0:T(8,128)(2,1)S(1)} %turn.1.vt_ref), custom_call_target="tpu_custom_call" | custom-call | flops 1000000 | bytes 100000 | tf_op jit(solution)/shard_map/attention/pallas_call | solution.py:32
  31.7 1.6 %collective-permute-start.9 = (s32[72,256]{1,0:T(8,128)S(1)}, s32[72,256]{1,0:T(8,128)S(1)}, u32[]{:S(2)}, u32[]{:S(2)}) collective-permute-start(s32[72,256]{1,0:T(8,128)S(1)} %attention.6), channel_id=1, source_target_pairs={{0,2},{1,3},{2,0},{3,1},{4,6},{5,7},{6,4},{7,5},{8,10},{9,11},{10,... | collective-permute-start | bytes 221192 | tf_op jit(solution)/shard_map/ppermute | solution.py:28
  33.3 1.8 %attention.7.refs_0_ = f32[136,256]{1,0:T(8,128)S(1)} custom-call(bf16[768,128]{1,0:T(8,128)(2,1)S(1)} %collective-permute-done.6.q_ref.other_ref, bf16[4096,128]{1,0:T(8,128)(2,1)S(1)} %get-tuple-element.63.k_ref, bf16[144,4096]{1,0:T(8,128)(2,1)S(1)} %turn.1.vt_ref), custom_call_target="tpu_custom_call" | custom-call | flops 1000000 | bytes 100000 | tf_op jit(solution)/shard_map/attention/pallas_call | solution.py:32
  35.0 1.5 %attend.1 = (bf16[512,1024]{1,0:T(8,128)(2,1)S(1)}, bf16[512,1024]{1,0:T(8,128)(2,1)S(1)}) custom-call(s32[1]{0:T(128)} %bitcast.shard_ref, bf16[384,128]{1,0:T(8,128)(2,1)S(1)} %total.3.q_ref.a_ref.near_ref, bf16[384,128]{1,0:T(8,128)(2,1)S(1)} %collective-permute-done.5.b_ref.q_ref.far_ref, bf16[768,128]{1,0:T(8,128)(2,1)S(1)} %collective-permute-done.6.q_ref.other_ref), custom_call_target="tpu_custom_call" | custom-call | flops 1000000 | bytes 100000 | tf_op jit(solution)/shard_map/attend/pallas_call | solution.py:32
  36.6 1.2 %collective-permute-done.8.refs_2_ = s32[72,256]{1,0:T(8,128)S(1)} collective-permute-done((s32[72,256]{1,0:T(8,128)S(1)}, s32[72,256]{1,0:T(8,128)S(1)}, u32[]{:S(2)}, u32[]{:S(2)}) %collective-permute-start.8) | collective-permute-done | bytes 73760 | tf_op jit(solution)/shard_map/ppermute | solution.py:28
  37.8 0.2 merge.2
  38.0 0.6 collective-permute-start.10
  38.5 2.0 %gram.1.h_ref = f32[512,512]{1,0:T(8,128)S(1)} custom-call(bf16[512,1024]{1,0:T(8,128)(2,1)S(1)} %get-tuple-element.72.high_ref, bf16[512,1024]{1,0:T(8,128)(2,1)S(1)} %get-tuple-element.73.low_ref), custom_call_target="tpu_custom_call" | custom-call | flops 4000000000 | bytes 100000 | tf_op jit(solution)/shard_map/gram/pallas_call | solution.py:32
  40.5 1.5 %collective-permute-done.10.refs_1_ = s32[40,256]{1,0:T(8,128)S(1)} collective-permute-done((s32[40,256]{1,0:T(8,128)S(1)}, s32[40,256]{1,0:T(8,128)S(1)}, u32[]{:S(2)}, u32[]{:S(2)}) %collective-permute-start.10) | collective-permute-done | bytes 40992 | tf_op jit(solution)/shard_map/ppermute | solution.py:28
  42.0 1.7 %invert.1.inverse_ref = f32[64,64]{1,0:T(8,128)S(1)} custom-call(f32[512,512]{1,0:T(8,128)S(1)} %gram.1.h_ref), custom_call_target="tpu_custom_call" | custom-call | flops 1000000000 | bytes 100000 | tf_op jit(solution)/shard_map/invert/pallas_call | solution.py:32
  43.8 0.1 merge.3
  43.8 1.1 %collective-permute-start.11 = (s32[24,256]{1,0:T(8,128)S(1)}, s32[24,256]{1,0:T(8,128)S(1)}, u32[]{:S(2)}, u32[]{:S(2)}) collective-permute-start(s32[24,256]{1,0:T(8,128)S(1)} %get-tuple-element.83), channel_id=1, source_target_pairs={{0,8},{1,9},{2,10},{3,11},{4,12},{5,13},{6,14},{7,15},{8,0},{9,1},... | collective-permute-start | bytes 73736 | tf_op jit(solution)/shard_map/ppermute | solution.py:28
  45.0 2.0 %sweep.8 = (f32[512,512]{1,0:T(8,128)S(1)}, f32[64,64]{1,0:T(8,128)S(1)}) custom-call(f32[512,512]{1,0:T(8,128)S(1)} %gram.1.h_ref, f32[64,64]{1,0:T(8,128)S(1)} %invert.1.inverse_ref), custom_call_target="tpu_custom_call" | custom-call | flops 2000000000 | bytes 100000 | tf_op jit(solution)/shard_map/sweep/pallas_call | solution.py:32
  47.0 1.8 %collective-permute-done.11.refs_1_ = s32[24,256]{1,0:T(8,128)S(1)} collective-permute-done((s32[24,256]{1,0:T(8,128)S(1)}, s32[24,256]{1,0:T(8,128)S(1)}, u32[]{:S(2)}, u32[]{:S(2)}) %collective-permute-start.11) | collective-permute-done | bytes 24608 | tf_op jit(solution)/shard_map/ppermute | solution.py:28
  48.9 0.9 %collective-permute-start.12 = (f32[32,256]{1,0:T(8,128)S(1)}, f32[32,256]{1,0:T(8,128)S(1)}, u32[]{:S(2)}, u32[]{:S(2)}) collective-permute-start(f32[32,256]{1,0:T(8,128)S(1)} %finish.1.a_ref), channel_id=1, source_target_pairs={{0,8},{1,9},{2,10},{3,11},{4,12},{5,13},{6,14},{7,15},{8,0},{9,1},... | collective-permute-start | bytes 98312 | tf_op jit(solution)/shard_map/ppermute | solution.py:28
  49.8 1.9 %sweep.9 = (f32[512,512]{1,0:T(8,128)S(1)}, f32[64,64]{1,0:T(8,128)S(1)}) custom-call(f32[512,512]{1,0:T(8,128)S(1)} %get-tuple-element.84.h_ref, f32[64,64]{1,0:T(8,128)S(1)} %get-tuple-element.85.inverse_ref), custom_call_target="tpu_custom_call" | custom-call | flops 2000000000 | bytes 100000 | tf_op jit(solution)/shard_map/sweep/pallas_call | solution.py:32
  51.7 2.0 %sweep.10 = (f32[512,512]{1,0:T(8,128)S(1)}, f32[64,64]{1,0:T(8,128)S(1)}) custom-call(f32[512,512]{1,0:T(8,128)S(1)} %get-tuple-element.86.h_ref, f32[64,64]{1,0:T(8,128)S(1)} %get-tuple-element.87.inverse_ref), custom_call_target="tpu_custom_call" | custom-call | flops 2000000000 | bytes 100000 | tf_op jit(solution)/shard_map/sweep/pallas_call | solution.py:32
  53.7 0.1 collective-permute-done.12.b_ref
  53.9 2.0 %collective-permute-start.13 = (f32[64,256]{1,0:T(8,128)S(1)}, f32[64,256]{1,0:T(8,128)S(1)}, u32[]{:S(2)}, u32[]{:S(2)}) collective-permute-start(f32[64,256]{1,0:T(8,128)S(1)} %stack.5.a_ref), channel_id=1, source_target_pairs={{0,4},{1,5},{2,6},{3,7},{4,0},{5,1},{6,2},{7,3},{8,12},{9,13},{10,... | collective-permute-start | bytes 196616 | tf_op jit(solution)/shard_map/ppermute | solution.py:28
  55.8 1.9 %sweep.11 = (f32[512,512]{1,0:T(8,128)S(1)}, f32[64,64]{1,0:T(8,128)S(1)}) custom-call(f32[512,512]{1,0:T(8,128)S(1)} %get-tuple-element.92.h_ref, f32[64,64]{1,0:T(8,128)S(1)} %get-tuple-element.93.inverse_ref), custom_call_target="tpu_custom_call" | custom-call | flops 2000000000 | bytes 100000 | tf_op jit(solution)/shard_map/sweep/pallas_call | solution.py:32
  57.7 0.5 collective-permute-done.13.b_ref
  58.3 0.8 %collective-permute-start.14 = (s32[72,256]{1,0:T(8,128)S(1)}, s32[72,256]{1,0:T(8,128)S(1)}, u32[]{:S(2)}, u32[]{:S(2)}) collective-permute-start(s32[72,256]{1,0:T(8,128)S(1)} %pack.1.a_ref), channel_id=1, source_target_pairs={{0,2},{1,3},{2,0},{3,1},{4,6},{5,7},{6,4},{7,5},{8,10},{9,11},{10,... | collective-permute-start | bytes 221192 | tf_op jit(solution)/shard_map/ppermute | solution.py:28
  59.1 2.1 %sweep.12 = (f32[512,512]{1,0:T(8,128)S(1)}, f32[64,64]{1,0:T(8,128)S(1)}) custom-call(f32[512,512]{1,0:T(8,128)S(1)} %get-tuple-element.97.h_ref, f32[64,64]{1,0:T(8,128)S(1)} %get-tuple-element.98.inverse_ref), custom_call_target="tpu_custom_call" | custom-call | flops 2000000000 | bytes 100000 | tf_op jit(solution)/shard_map/sweep/pallas_call | solution.py:32
  61.2 1.9 %sweep.13 = (f32[512,512]{1,0:T(8,128)S(1)}, f32[64,64]{1,0:T(8,128)S(1)}) custom-call(f32[512,512]{1,0:T(8,128)S(1)} %get-tuple-element.99.h_ref, f32[64,64]{1,0:T(8,128)S(1)} %get-tuple-element.100.inverse_ref), custom_call_target="tpu_custom_call" | custom-call | flops 2000000000 | bytes 100000 | tf_op jit(solution)/shard_map/sweep/pallas_call | solution.py:32
  63.2 0.1 collective-permute-start.15
  63.2 2.1 %sweep.14 = (f32[512,512]{1,0:T(8,128)S(1)}, f32[64,64]{1,0:T(8,128)S(1)}) custom-call(f32[512,512]{1,0:T(8,128)S(1)} %get-tuple-element.104.h_ref, f32[64,64]{1,0:T(8,128)S(1)} %get-tuple-element.105.inverse_ref), custom_call_target="tpu_custom_call" | custom-call | flops 2000000000 | bytes 100000 | tf_op jit(solution)/shard_map/sweep/pallas_call | solution.py:32
  65.4 0.7 %sweep.15.minus_ref = f32[512,512]{1,0:T(8,128)S(1)} custom-call(f32[512,512]{1,0:T(8,128)S(1)} %get-tuple-element.109.h_ref, f32[64,64]{1,0:T(8,128)S(1)} %get-tuple-element.110.inverse_ref), custom_call_target="tpu_custom_call" | custom-call | flops 2000000000 | bytes 100000 | tf_op jit(solution)/shard_map/sweep/pallas_call | solution.py:32
  66.1 1.9 %fit.1 = (f32[128,512]{1,0:T(8,128)S(1)}, f32[8,128]{1,0:T(8,128)S(1)}) custom-call(s32[1]{0:T(128)} %bitcast.shard_ref, f32[512,512]{1,0:T(8,128)S(1)} %sweep.15.minus_ref, bf16[512,1024]{1,0:T(8,128)(2,1)S(1)} %get-tuple-element.72.high_ref, bf16[512,1024]{1,0:T(8,128)(2,1)S(1)} %get-tuple-element.73.low_ref, s32[144,256]{1,0:T(8,128)S(1)} %stack.7.own_ref, ...), custom_call_target="tpu_custom_call" | custom-call | flops 1000000000 | bytes 100000 | tf_op jit(solution)/shard_map/fit/pallas_call | solution.py:32
  68.1 1.6 %collective-permute-start.16 = (f32[8,128]{1,0:T(8,128)S(1)}, f32[8,128]{1,0:T(8,128)S(1)}, u32[]{:S(2)}, u32[]{:S(2)}) collective-permute-start(f32[8,128]{1,0:T(8,128)S(1)} %get-tuple-element.113.refs_0_), channel_id=1, source_target_pairs={{0,16},{16,0},{1,17},{17,1},{2,18},{18,2},{3,19},{19,3},{4,20},{20... | collective-permute-start | bytes 12296 | tf_op jit(solution)/shard_map/ppermute | solution.py:28
  69.7 0.8 %flip.1 = f32[512,128]{1,0:T(8,128)} custom-call(f32[128,512]{1,0:T(8,128)S(1)} %get-tuple-element.112.x_ref), custom_call_target="tpu_custom_call" | custom-call | flops 1000000 | bytes 100000 | tf_op jit(solution)/shard_map/flip/pallas_call | solution.py:32
  70.5 1.3 %collective-permute-done.16.refs_1_ = f32[8,128]{1,0:T(8,128)S(1)} collective-permute-done((f32[8,128]{1,0:T(8,128)S(1)}, f32[8,128]{1,0:T(8,128)S(1)}, u32[]{:S(2)}, u32[]{:S(2)}) %collective-permute-start.16) | collective-permute-done | bytes 4128 | tf_op jit(solution)/shard_map/ppermute | solution.py:28
  71.8 0.5 mean.1
  (19 shorter events, 0.2 us)
Async XLA Ops:
  0.6 7.3 %copy-start = (bf16[1,4096,128]{2,1,0:T(8,128)(2,1)S(1)}, bf16[1,4096,128]{2,1,0:T(8,128)(2,1)}, u32[]{:S(2)}) copy-start(bf16[1,4096,128]{2,1,0:T(8,128)(2,1)} %param.7) | copy-start | bytes 3145732
  3.4 1.6 %collective-permute-start = (bf16[768,128]{1,0:T(8,128)(2,1)S(1)}, bf16[768,128]{1,0:T(8,128)(2,1)S(1)}, u32[]{:S(2)}, u32[]{:S(2)}) collective-permute-start(bf16[768,128]{1,0:T(8,128)(2,1)S(1)} %get-tuple-element.59), channel_id=1, source_target_pairs={{0,1},{1,0},{2,3},{3,2},{4,5},{5,4},{6,7},{7,6},{8,9},{9,8},{10,11... | collective-permute-start | bytes 589832 | tf_op jit(solution)/shard_map/ppermute | solution.py:28
  5.0 6.0 %collective-permute-start.1 = (bf16[384,128]{1,0:T(8,128)(2,1)S(1)}, bf16[384,128]{1,0:T(8,128)(2,1)S(1)}, u32[]{:S(2)}, u32[]{:S(2)}) collective-permute-start(bf16[384,128]{1,0:T(8,128)(2,1)S(1)} %get-tuple-element.61), channel_id=1, source_target_pairs={{0,2},{1,3},{2,0},{3,1},{4,6},{5,7},{6,4},{7,5},{8,10},{9,11},{10,... | collective-permute-start | bytes 294920 | tf_op jit(solution)/shard_map/ppermute | solution.py:28
  11.1 7.6 %collective-permute-start.4 = (bf16[384,128]{1,0:T(8,128)(2,1)S(1)}, bf16[384,128]{1,0:T(8,128)(2,1)S(1)}, u32[]{:S(2)}, u32[]{:S(2)}) collective-permute-start(bf16[384,128]{1,0:T(8,128)(2,1)S(1)} %total.2.refs_0_), channel_id=1, source_target_pairs={{0,12},{1,13},{2,14},{3,15},{4,8},{5,9},{6,10},{7,11},{8,4},{9,5},... | collective-permute-start | bytes 294920 | tf_op jit(solution)/shard_map/ppermute | solution.py:28
  15.0 7.7 %collective-permute-start.3 = (bf16[384,128]{1,0:T(8,128)(2,1)S(1)}, bf16[384,128]{1,0:T(8,128)(2,1)S(1)}, u32[]{:S(2)}, u32[]{:S(2)}) collective-permute-start(bf16[384,128]{1,0:T(8,128)(2,1)S(1)} %total.2.refs_0_), channel_id=1, source_target_pairs={{0,8},{1,9},{2,10},{3,11},{4,12},{5,13},{6,14},{7,15},{8,0},{9,1},... | collective-permute-start | bytes 294920 | tf_op jit(solution)/shard_map/ppermute | solution.py:28
  15.0 7.7 %collective-permute-start.2 = (bf16[384,128]{1,0:T(8,128)(2,1)S(1)}, bf16[384,128]{1,0:T(8,128)(2,1)S(1)}, u32[]{:S(2)}, u32[]{:S(2)}) collective-permute-start(bf16[384,128]{1,0:T(8,128)(2,1)S(1)} %total.2.refs_0_), channel_id=1, source_target_pairs={{0,4},{1,5},{2,6},{3,7},{4,0},{5,1},{6,2},{7,3},{8,12},{9,13},{10,... | collective-permute-start | bytes 294920 | tf_op jit(solution)/shard_map/ppermute | solution.py:28
  22.7 4.7 %collective-permute-start.5 = (bf16[384,128]{1,0:T(8,128)(2,1)S(1)}, bf16[384,128]{1,0:T(8,128)(2,1)S(1)}, u32[]{:S(2)}, u32[]{:S(2)}) collective-permute-start(bf16[384,128]{1,0:T(8,128)(2,1)S(1)} %total.3.q_ref.a_ref.near_ref), channel_id=1, source_target_pairs={{0,2},{1,3},{2,0},{3,1},{4,6},{5,7},{6,4},{7,5},{8,10},{9,11},{10,... | collective-permute-start | bytes 294920 | tf_op jit(solution)/shard_map/ppermute | solution.py:28
  27.4 2.4 %collective-permute-start.6 = (bf16[768,128]{1,0:T(8,128)(2,1)S(1)}, bf16[768,128]{1,0:T(8,128)(2,1)S(1)}, u32[]{:S(2)}, u32[]{:S(2)}) collective-permute-start(bf16[768,128]{1,0:T(8,128)(2,1)S(1)} %stack.4), channel_id=1, source_target_pairs={{0,1},{1,0},{2,3},{3,2},{4,5},{5,4},{6,7},{7,6},{8,9},{9,8},{10,11... | collective-permute-start | bytes 589832 | tf_op jit(solution)/shard_map/ppermute | solution.py:28
  27.5 9.1 %collective-permute-start.7 = (s32[72,256]{1,0:T(8,128)S(1)}, s32[72,256]{1,0:T(8,128)S(1)}, u32[]{:S(2)}, u32[]{:S(2)}) collective-permute-start(s32[72,256]{1,0:T(8,128)S(1)} %attention.4), channel_id=1, source_target_pairs={{0,1},{1,0},{2,3},{3,2},{4,5},{5,4},{6,7},{7,6},{8,9},{9,8},{10,11... | collective-permute-start | bytes 221192 | tf_op jit(solution)/shard_map/ppermute | solution.py:28
  31.7 4.9 %collective-permute-start.9 = (s32[72,256]{1,0:T(8,128)S(1)}, s32[72,256]{1,0:T(8,128)S(1)}, u32[]{:S(2)}, u32[]{:S(2)}) collective-permute-start(s32[72,256]{1,0:T(8,128)S(1)} %attention.6), channel_id=1, source_target_pairs={{0,2},{1,3},{2,0},{3,1},{4,6},{5,7},{6,4},{7,5},{8,10},{9,11},{10,... | collective-permute-start | bytes 221192 | tf_op jit(solution)/shard_map/ppermute | solution.py:28
  33.3 4.5 %collective-permute-start.8 = (s32[72,256]{1,0:T(8,128)S(1)}, s32[72,256]{1,0:T(8,128)S(1)}, u32[]{:S(2)}, u32[]{:S(2)}) collective-permute-start(s32[72,256]{1,0:T(8,128)S(1)} %attention.5), channel_id=1, source_target_pairs={{0,3},{1,2},{2,1},{3,0},{4,7},{5,6},{6,5},{7,4},{8,11},{9,10},{10,... | collective-permute-start | bytes 221192 | tf_op jit(solution)/shard_map/ppermute | solution.py:28
  38.0 4.1 %collective-permute-start.10 = (s32[40,256]{1,0:T(8,128)S(1)}, s32[40,256]{1,0:T(8,128)S(1)}, u32[]{:S(2)}, u32[]{:S(2)}) collective-permute-start(s32[40,256]{1,0:T(8,128)S(1)} %get-tuple-element.77), channel_id=1, source_target_pairs={{0,4},{1,5},{2,6},{3,7},{4,0},{5,1},{6,2},{7,3},{8,12},{9,13},{10,... | collective-permute-start | bytes 122888 | tf_op jit(solution)/shard_map/ppermute | solution.py:28
  43.8 5.0 %collective-permute-start.11 = (s32[24,256]{1,0:T(8,128)S(1)}, s32[24,256]{1,0:T(8,128)S(1)}, u32[]{:S(2)}, u32[]{:S(2)}) collective-permute-start(s32[24,256]{1,0:T(8,128)S(1)} %get-tuple-element.83), channel_id=1, source_target_pairs={{0,8},{1,9},{2,10},{3,11},{4,12},{5,13},{6,14},{7,15},{8,0},{9,1},... | collective-permute-start | bytes 73736 | tf_op jit(solution)/shard_map/ppermute | solution.py:28
  48.9 5.0 %collective-permute-start.12 = (f32[32,256]{1,0:T(8,128)S(1)}, f32[32,256]{1,0:T(8,128)S(1)}, u32[]{:S(2)}, u32[]{:S(2)}) collective-permute-start(f32[32,256]{1,0:T(8,128)S(1)} %finish.1.a_ref), channel_id=1, source_target_pairs={{0,8},{1,9},{2,10},{3,11},{4,12},{5,13},{6,14},{7,15},{8,0},{9,1},... | collective-permute-start | bytes 98312 | tf_op jit(solution)/shard_map/ppermute | solution.py:28
  53.9 4.3 %collective-permute-start.13 = (f32[64,256]{1,0:T(8,128)S(1)}, f32[64,256]{1,0:T(8,128)S(1)}, u32[]{:S(2)}, u32[]{:S(2)}) collective-permute-start(f32[64,256]{1,0:T(8,128)S(1)} %stack.5.a_ref), channel_id=1, source_target_pairs={{0,4},{1,5},{2,6},{3,7},{4,0},{5,1},{6,2},{7,3},{8,12},{9,13},{10,... | collective-permute-start | bytes 196616 | tf_op jit(solution)/shard_map/ppermute | solution.py:28
  58.3 4.9 %collective-permute-start.14 = (s32[72,256]{1,0:T(8,128)S(1)}, s32[72,256]{1,0:T(8,128)S(1)}, u32[]{:S(2)}, u32[]{:S(2)}) collective-permute-start(s32[72,256]{1,0:T(8,128)S(1)} %pack.1.a_ref), channel_id=1, source_target_pairs={{0,2},{1,3},{2,0},{3,1},{4,6},{5,7},{6,4},{7,5},{8,10},{9,11},{10,... | collective-permute-start | bytes 221192 | tf_op jit(solution)/shard_map/ppermute | solution.py:28
  63.2 2.2 %collective-permute-start.15 = (s32[144,256]{1,0:T(8,128)S(1)}, s32[144,256]{1,0:T(8,128)S(1)}, u32[]{:S(2)}, u32[]{:S(2)}) collective-permute-start(s32[144,256]{1,0:T(8,128)S(1)} %stack.7.own_ref), channel_id=1, source_target_pairs={{0,1},{1,0},{2,3},{3,2},{4,5},{5,4},{6,7},{7,6},{8,9},{9,8},{10,11... | collective-permute-start | bytes 442376 | tf_op jit(solution)/shard_map/ppermute | solution.py:28
  68.1 3.7 %collective-permute-start.16 = (f32[8,128]{1,0:T(8,128)S(1)}, f32[8,128]{1,0:T(8,128)S(1)}, u32[]{:S(2)}, u32[]{:S(2)}) collective-permute-start(f32[8,128]{1,0:T(8,128)S(1)} %get-tuple-element.113.refs_0_), channel_id=1, source_target_pairs={{0,16},{16,0},{1,17},{17,1},{2,18},{18,2},{3,19},{19,3},{4,20},{20... | collective-permute-start | bytes 12296 | tf_op jit(solution)/shard_map/ppermute | solution.py:28

commit v10 on v9

--- a/solution.py
+++ b/solution.py
@@ -107,17 +107,34 @@
     return (rows + SUB, lanes), F32
 
 
-def prepare_kernel(window, shard_ref, root_ref, q_hbm, kept_hbm, k_hbm, *refs):
-    keep_ref, send_ref, k_ref, q_ref, kept_ref, spots, picked, sems = refs
+def quarters_out(keep_ref, send_ref, shard, rows, get):
+    for s in range(4):
+        at = s // 2 * rows
+        (keep_ref, send_ref)[s % 2][at : at + rows, :] = get(aligned((shard % 4) ^ s, rows))
+
+
+def root_kernel(shard_ref, root_ref, q_hbm, keep_ref, send_ref, q_ref, sem):
+    load = pltpu.make_async_copy(q_hbm, q_ref, sem)
+    load.start()
+    load.wait()
+    is_root = shard_ref[0] == root_ref[0]
+
+    def get(at):
+        q = q_ref[at, :]
+        return jnp.where(is_root, q, jnp.zeros_like(q))
+
+    quarters_out(keep_ref, send_ref, shard_ref[0], q_ref.shape[0] // 4, get)
+
+
+def pick_kernel(window, shard_ref, kept_hbm, k_hbm, keep_ref, send_ref, k_ref, kept_ref, spots, picked, sems):
     slab, dims = k_ref.shape
     kept = kept_ref.shape[1]
-    steps = sems.shape[0] - 2
+    steps = sems.shape[0] - 1
     chunk = slab // steps
     loads = [pltpu.make_async_copy(kept_hbm, kept_ref, sems.at[steps])]
     for i in range(steps):
         part = pl.ds(i * chunk, chunk)
         loads.append(pltpu.make_async_copy(k_hbm.at[part], k_ref.at[part], sems.at[i]))
-    loads.append(pltpu.make_async_copy(q_hbm, q_ref, sems.at[steps + 1]))
     for load in loads:
         load.start()
     base = shard_ref[0] * slab
@@ -138,19 +155,10 @@
             axis=1,
         )
         loads[1 + i].wait()
-        rows += lax.dot_general(onehot, k_ref[i * chunk : (i + 1) * chunk, :], NN, preferred_element_type=F32)
+        rows += dot(onehot, k_ref[i * chunk : (i + 1) * chunk, :], NN)
     picked[...] = jnp.zeros_like(picked)
     picked[spot, :] = rows.astype(BF16)
-    loads[-1].wait()
-    share, part = q_ref.shape[0] // 4, kept // 4
-    is_root = shard_ref[0] == root_ref[0]
-    tall = share + part
-    for s in range(4):
-        out, at = (keep_ref, send_ref)[s % 2], s // 2 * tall
-        place = (shard_ref[0] % 4) ^ s
-        q = q_ref[aligned(place, share), :]
-        out[at : at + share, :] = jnp.where(is_root, q, jnp.zeros_like(q))
-        out[at + share : at + tall, :] = picked[aligned(place, part), :]
+    quarters_out(keep_ref, send_ref, shard_ref[0], kept // 4, lambda at: picked[at, :])
 
 
 def sum_kernel(*refs):
@@ -172,50 +180,88 @@
     out_ref[rows:, :] = b_ref[...]
 
 
+def total(arrays):
+    return call(sum_kernel, arrays, [(arrays[0].shape, arrays[0].dtype)], name="total")[0]
+
+
+def after(first, then):
+    return lax.optimization_barrier((first, then))
+
+
+def halved(keep, send):
+    rows, dims = keep.shape
+    return call(halve_kernel, (keep, swap(send, "ctx", 1)), [((rows // 2, dims), BF16)] * 2, name="halve")
+
+
+def across_groups(near, beside):
+    step, devices = 4, lax.axis_size("ctx")
+    while step < devices:
+        ways = math.gcd(devices // step, 4)
+        came = [swap(near, "ctx", t * step) for t in range(1, ways)]
+        if step == 4:
+            beside, came = after(beside, came)
+        near = total([near] + came)
+        step *= ways
+    return near, beside
+
+
+def both_of(near, far):
+    return call(stack_kernel, (near, far), [((2 * near.shape[0], near.shape[1]), BF16)], name="stack")[0]
+
+
 def spread(shard, queries, kept, keys, roots, values, attend_to):
     (rows, dims), (slab, _) = queries.shape, keys.shape
     count = kept.shape[1]
-    devices = lax.axis_size("ctx")
-    quarter = ((rows + count) // 4, dims)
-    half = (2 * quarter[0], dims)
     in_hbm = lambda x: pltpu.with_memory_space_constraint(x, pltpu.HBM)
+    keep, send = call(
+        root_kernel,
+        (shard, roots, in_hbm(queries)),
+        [((rows // 2, dims), BF16)] * 2,
+        scratch=[pltpu.VMEM((rows, dims), BF16), pltpu.SemaphoreType.DMA],
+        name="root",
+        specs=[SMEM, SMEM, HBM],
+    )
+    near, far = halved(keep, send)
+    came = swap(far, "ctx", 2)
     keep, send, keys = call(
-        functools.partial(prepare_kernel, 4 * count // devices + 16),
-        (shard, roots, in_hbm(queries), in_hbm(kept), in_hbm(keys)),
-        [(half, BF16)] * 2 + [(keys.shape, BF16)],
+        functools.partial(pick_kernel, 4 * count // lax.axis_size("ctx") + 16),
+        (shard, in_hbm(kept), in_hbm(keys)),
+        [((count // 2, dims), BF16)] * 2 + [(keys.shape, BF16)],
         scratch=[
-            pltpu.VMEM((rows, dims), BF16),
             pltpu.VMEM((1, count), jnp.int32),
             pltpu.VMEM((count, 128), F32),
             pltpu.VMEM((count, dims), BF16),
-            pltpu.SemaphoreType.DMA((6,)),
+            pltpu.SemaphoreType.DMA((5,)),
         ],
-        name="prepare",
-        specs=[SMEM, SMEM, HBM, HBM, HBM],
+        name="pick",
+        specs=[SMEM, HBM, HBM],
     )
-    near, far = call(halve_kernel, (keep, swap(send, "ctx", 1)), [(quarter, BF16)] * 2, name="halve")
-    total = lambda arrays: call(sum_kernel, arrays, [(quarter, BF16)], name="total")[0]
-    came = swap(far, "ctx", 2)
     (turned,) = call(turn_kernel, (values,), [((dims + 16, slab), BF16)], 10**7, name="turn")
-    came, turned = lax.optimization_barrier((came, turned))
+    kept_near, kept_far = halved(keep, send)
+    kept_near = total([kept_near, swap(kept_far, "ctx", 2)])
+    (kept_near, turned), came = after((kept_near, turned), came)
     near = total([near, came])
-    step = 4
-    while step < devices:
-        ways = math.gcd(devices // step, 4)
-        near = total([near] + [swap(near, "ctx", t * step) for t in range(1, ways)])
-        step *= ways
+    steps = [2**i for i in range(2, lax.axis_size("ctx").bit_length() - 1)]
+    for step in steps[:1]:
+        kept_near = total([kept_near, swap(kept_near, "ctx", step)])
+    near, kept_near = across_groups(near, kept_near)
+    for step in steps[1:]:
+        kept_near = total([kept_near, swap(kept_near, "ctx", step)])
+
     far = swap(near, "ctx", 2)
     first = attend_to(near, keys, turned)
-    far, first = lax.optimization_barrier((far, first))
-    (both,) = call(stack_kernel, (near, far), [(half, BF16)], name="stack")
-    other, came = swap(both, "ctx", 1), [swap(first, "ctx", 1)]
+    (first, kept_near), far = after((first, kept_near), far)
+    other, came = swap(both_of(near, far), "ctx", 1), [swap(first, "ctx", 1)]
+    kept_far = swap(kept_near, "ctx", 2)
     second = attend_to(far, keys, turned)
-    other, second = lax.optimization_barrier((other, second))
+    other, second, kept_far = lax.optimization_barrier((other, second, kept_far))
     came.append(swap(second, "ctx", 3))
-    third = attend_to(other, keys, turned, start=quarter[0])
+    kept_other = swap(both_of(kept_near, kept_far), "ctx", 1)
+    third = attend_to(other, keys, turned, start=rows // 4)
     came.append(swap(third, "ctx", 2))
-    other, third = lax.optimization_barrier((other, third))
-    return near, far, other, attend_to(other, keys, turned, packed=False), came
+    other, third = after(other, third)
+    keep = attend_to(other, keys, turned, packed=False)
+    return (near, far, other), (kept_near, kept_far, kept_other), keep, came
 
 
 def turn_kernel(v_ref, vt_ref):
@@ -331,18 +377,23 @@
     return block, *came
 
 
-def attend_kernel(score_scale, shard_ref, near_ref, far_ref, other_ref, high_ref, low_ref, c_all):
-    part, rows = c_all.shape[0] // 4, high_ref.shape[1] // 4
-    tall = part + rows
-    pieces = [(near_ref, 0), (other_ref, 0), (far_ref, 0), (other_ref, tall)]
-    places = [(shard_ref[0] % 4) ^ s for s in range(4)]
-    for place, (ref, at) in zip(places, pieces):
-        c_all[aligned(place, part), :] = ref[at + rows : at + tall, :]
-    for place, (ref, at) in zip(places, pieces):
-        scores = lax.dot_general(c_all[...], ref[at : at + rows, :], NT, preferred_element_type=F32) * score_scale
+def attend_kernel(score_scale, shard_ref, *refs):
+    queries, kept, (high_ref, low_ref, c_all) = refs[:3], refs[3:6], refs[6:]
+
+    def quarters(near_ref, far_ref, other_ref):
+        rows = near_ref.shape[0]
+        return rows, [near_ref[...], other_ref[:rows, :], far_ref[...], other_ref[rows:, :]]
+
+    rows, pieces = quarters(*kept)
+    for s, piece in enumerate(pieces):
+        c_all[aligned((shard_ref[0] % 4) ^ s, rows), :] = piece
+    rows, pieces = quarters(*queries)
+    for s, piece in enumerate(pieces):
+        scores = dot(c_all[...], piece, NT) * score_scale
         weights = jnp.exp(scores - jnp.max(scores, axis=0, keepdims=True))
         weights = weights * (1.0 / jnp.sum(weights, axis=0, keepdims=True))
-        high_ref[:, aligned(place, rows)], low_ref[:, aligned(place, rows)] = halves(weights)
+        at = aligned((shard_ref[0] % 4) ^ s, rows)
+        high_ref[:, at], low_ref[:, at] = halves(weights)
 
 
 def gram_kernel(high_ref, low_ref, h_ref):
@@ -488,7 +539,7 @@
     shard = lax.axis_index("ctx").astype(jnp.int32).reshape(1)
 
     attend_to = functools.partial(attention, lanes, score_scale)
-    near, far, other, keep, came = spread(shard, queries[0, 0], kept, keys[0], roots, values[0], attend_to)
+    pieces, kept_pieces, keep, came = spread(shard, queries[0, 0], kept, keys[0], roots, values[0], attend_to)
     rounds = target_rounds(shard, keep, came)
     came = next(rounds)
     ends = None
@@ -506,7 +557,7 @@
     system_shape = ((count, count), F32)
     attend = call(
         functools.partial(attend_kernel, score_scale),
-        (shard, near, far, other),
+        (shard, *pieces, *kept_pieces),
         [((count, rows), BF16)] * 2,
         10**6,
         scratch=[pltpu.VMEM((count, dims), BF16)],

time: 72.5 us -> 74.6 us (1.029)
  starting transfers between devices: 18.8 us -> 25.4 us
  waiting for transfers between devices: 18.6 us -> 13.1 us
  Pallas kernels: 33.2 us -> 34.2 us
    ppermute x17 -> x23, starting transfers between devices: 18.8 us -> 25.4 us  [swap(): return lax.ppermute(array, axis, [(i, i ^ step) for i in range(size)])]
    ppermute x17 -> x23, waiting for transfers between devices: 18.6 us -> 13.1 us  [swap(): return lax.ppermute(array, axis, [(i, i ^ step) for i in range(size)])]
    pallas_call x31 -> x37, Pallas kernels: 33.2 us -> 34.2 us  [call(): pl.pallas_call(kernel, in_specs=specs or [SMEM if x.size == 1 else VMEM f...]
  transfers between devices with their start and end apart: 17 -> 23, of which waited for: 11 -> 8; matrix products, arithmetic and copies ran while one was open for 0% -> 0% of each run, Pallas kernels for 36% -> 37%
where the time goes in v10:
time: 74.6 us; the launch traced here: 74.4 us
  Pallas kernels  34.2 us (46%)
  starting transfers between devices  25.4 us (34%)
  waiting for transfers between devices  13.1 us (18%)
  between operations  1.71 us (2%)
    pallas_call x37, Pallas kernels, call(): pl.pallas_call(kernel, in_specs=specs or [SMEM if x.size == 1 else VMEM f...  34.2 us
    ppermute x23, starting transfers between devices, swap(): return lax.ppermute(array, axis, [(i, i ^ step) for i in range(size)])  25.4 us
    ppermute x23, waiting for transfers between devices, swap(): return lax.ppermute(array, axis, [(i, i ^ step) for i in range(size)])  13.1 us
  transfers between devices with their start and end apart: 23, of which 8 were waited for; matrix products, arithmetic and copies ran while one was open for 0% of the time, Pallas kernels for 37%

profile of v10, /device:TPU:0, one launch (start us, length us, event | category | flops | bytes accessed | tf_op | source)
XLA Modules:
  0.0 74.4 jit_solution(9038720533986428684)
XLA Ops:
  1.4 1.0 %root.1 = (bf16[512,128]{1,0:T(8,128)(2,1)S(1)}, bf16[512,128]{1,0:T(8,128)(2,1)S(1)}) custom-call(s32[1]{0:T(128)} %bitcast.shard_ref, s32[1]{0:T(128)S(6)} %copy.7.root_ref, bf16[1024,128]{1,0:T(8,128)(2,1)} %bitcast.8), custom_call_target="tpu_custom_call" | custom-call | flops 100000 | bytes 100000 | tf_op jit(solution)/shard_map/root/pallas_call | solution.py:32
  2.4 0.5 collective-permute-start
  2.9 1.9 %pick.1 = (bf16[256,128]{1,0:T(8,128)(2,1)S(1)}, bf16[256,128]{1,0:T(8,128)(2,1)S(1)}, bf16[4096,128]{1,0:T(8,128)(2,1)S(1)}) custom-call(s32[1]{0:T(128)} %bitcast.shard_ref, s32[1,512]{1,0:T(1,128)} %kept_hbm.1, bf16[4096,128]{1,0:T(8,128)(2,1)} %bitcast.7), custom_call_target="tpu_custom_call" | custom-call | flops 100000 | bytes 100000 | tf_op jit(solution)/shard_map/pick/pallas_call | solution.py:32
  5.0 3.0 %collective-permute-start.3 = (bf16[256,128]{1,0:T(8,128)(2,1)S(1)}, bf16[256,128]{1,0:T(8,128)(2,1)S(1)}, u32[]{:S(2)}, u32[]{:S(2)}) collective-permute-start(bf16[256,128]{1,0:T(8,128)(2,1)S(1)} %get-tuple-element.76), channel_id=1, source_target_pairs={{0,2},{1,3},{2,0},{3,1},{4,6},{5,7},{6,4},{7,5},{8,10},{9,11},{10,... | collective-permute-start | bytes 196616 | tf_op jit(solution)/shard_map/ppermute | solution.py:28
  8.0 0.9 %collective-permute-start.2 = (bf16[128,128]{1,0:T(8,128)(2,1)S(1)}, bf16[128,128]{1,0:T(8,128)(2,1)S(1)}, u32[]{:S(2)}, u32[]{:S(2)}) collective-permute-start(bf16[128,128]{1,0:T(8,128)(2,1)S(1)} %get-tuple-element.75), channel_id=1, source_target_pairs={{0,2},{1,3},{2,0},{3,1},{4,6},{5,7},{6,4},{7,5},{8,10},{9,11},{10,... | collective-permute-start | bytes 98312 | tf_op jit(solution)/shard_map/ppermute | solution.py:28
  8.9 0.3 turn.1.vt_ref
  9.2 2.8 %collective-permute-done.2.refs_1_ = bf16[128,128]{1,0:T(8,128)(2,1)S(1)} collective-permute-done((bf16[128,128]{1,0:T(8,128)(2,1)S(1)}, bf16[128,128]{1,0:T(8,128)(2,1)S(1)}, u32[]{:S(2)}, u32[]{:S(2)}) %collective-permute-start.2) | collective-permute-done | bytes 32800 | tf_op jit(solution)/shard_map/ppermute | solution.py:28
  12.1 3.7 %collective-permute-start.7 = (bf16[256,128]{1,0:T(8,128)(2,1)S(1)}, bf16[256,128]{1,0:T(8,128)(2,1)S(1)}, u32[]{:S(2)}, u32[]{:S(2)}) collective-permute-start(bf16[256,128]{1,0:T(8,128)(2,1)S(1)} %total.6.refs_0_), channel_id=1, source_target_pairs={{0,12},{1,13},{2,14},{3,15},{4,8},{5,9},{6,10},{7,11},{8,4},{9,5},... | collective-permute-start | bytes 196616 | tf_op jit(solution)/shard_map/ppermute | solution.py:28
  15.8 0.8 %collective-permute-start.5 = (bf16[256,128]{1,0:T(8,128)(2,1)S(1)}, bf16[256,128]{1,0:T(8,128)(2,1)S(1)}, u32[]{:S(2)}, u32[]{:S(2)}) collective-permute-start(bf16[256,128]{1,0:T(8,128)(2,1)S(1)} %total.6.refs_0_), channel_id=1, source_target_pairs={{0,4},{1,5},{2,6},{3,7},{4,0},{5,1},{6,2},{7,3},{8,12},{9,13},{10,... | collective-permute-start | bytes 196616 | tf_op jit(solution)/shard_map/ppermute | solution.py:28
  16.5 1.3 %collective-permute-start.4 = (bf16[128,128]{1,0:T(8,128)(2,1)S(1)}, bf16[128,128]{1,0:T(8,128)(2,1)S(1)}, u32[]{:S(2)}, u32[]{:S(2)}) collective-permute-start(bf16[128,128]{1,0:T(8,128)(2,1)S(1)} %total.5.refs_0_), channel_id=1, source_target_pairs={{0,4},{1,5},{2,6},{3,7},{4,0},{5,1},{6,2},{7,3},{8,12},{9,13},{10,... | collective-permute-start | bytes 98312 | tf_op jit(solution)/shard_map/ppermute | solution.py:28
  17.8 3.6 %collective-permute-done.4.refs_1_ = bf16[128,128]{1,0:T(8,128)(2,1)S(1)} collective-permute-done((bf16[128,128]{1,0:T(8,128)(2,1)S(1)}, bf16[128,128]{1,0:T(8,128)(2,1)S(1)}, u32[]{:S(2)}, u32[]{:S(2)}) %collective-permute-start.4) | collective-permute-done | bytes 32800 | tf_op jit(solution)/shard_map/ppermute | solution.py:28
  21.5 1.4 %collective-permute-start.9 = (bf16[256,128]{1,0:T(8,128)(2,1)S(1)}, bf16[256,128]{1,0:T(8,128)(2,1)S(1)}, u32[]{:S(2)}, u32[]{:S(2)}) collective-permute-start(bf16[256,128]{1,0:T(8,128)(2,1)S(1)} %total.8.q_ref.a_ref.refs_0_), channel_id=1, source_target_pairs={{0,2},{1,3},{2,0},{3,1},{4,6},{5,7},{6,4},{7,5},{8,10},{9,11},{10,... | collective-permute-start | bytes 196616 | tf_op jit(solution)/shard_map/ppermute | solution.py:28
  22.9 1.5 %collective-permute-start.8 = (bf16[128,128]{1,0:T(8,128)(2,1)S(1)}, bf16[128,128]{1,0:T(8,128)(2,1)S(1)}, u32[]{:S(2)}, u32[]{:S(2)}) collective-permute-start(bf16[128,128]{1,0:T(8,128)(2,1)S(1)} %total.7.refs_0_), channel_id=1, source_target_pairs={{0,8},{1,9},{2,10},{3,11},{4,12},{5,13},{6,14},{7,15},{8,0},{9,1},... | collective-permute-start | bytes 98312 | tf_op jit(solution)/shard_map/ppermute | solution.py:28
  24.4 1.8 %attention.4 = s32[72,256]{1,0:T(8,128)S(1)} custom-call(bf16[256,128]{1,0:T(8,128)(2,1)S(1)} %total.8.q_ref.a_ref.refs_0_, bf16[4096,128]{1,0:T(8,128)(2,1)S(1)} %get-tuple-element.82.k_ref, bf16[144,4096]{1,0:T(8,128)(2,1)S(1)} %turn.1.vt_ref), custom_call_target="tpu_custom_call" | custom-call | flops 1000000 | bytes 100000 | tf_op jit(solution)/shard_map/attention/pallas_call | solution.py:32
  26.2 1.5 %collective-permute-done.8.refs_1_ = bf16[128,128]{1,0:T(8,128)(2,1)S(1)} collective-permute-done((bf16[128,128]{1,0:T(8,128)(2,1)S(1)}, bf16[128,128]{1,0:T(8,128)(2,1)S(1)}, u32[]{:S(2)}, u32[]{:S(2)}) %collective-permute-start.8) | collective-permute-done | bytes 32800 | tf_op jit(solution)/shard_map/ppermute | solution.py:28
  27.9 0.7 collective-permute-start.11
  28.6 0.2 collective-permute-start.13
  28.8 1.8 %attention.5 = s32[72,256]{1,0:T(8,128)S(1)} custom-call(bf16[256,128]{1,0:T(8,128)(2,1)S(1)} %collective-permute-done.9.b_ref.q_ref.refs_1_, bf16[4096,128]{1,0:T(8,128)(2,1)S(1)} %get-tuple-element.82.k_ref, bf16[144,4096]{1,0:T(8,128)(2,1)S(1)} %turn.1.vt_ref), custom_call_target="tpu_custom_call" | custom-call | flops 1000000 | bytes 100000 | tf_op jit(solution)/shard_map/attention/pallas_call | solution.py:32
  30.6 1.3 %collective-permute-done.11.b_ref.refs_4_ = bf16[128,128]{1,0:T(8,128)(2,1)S(1)} collective-permute-done((bf16[128,128]{1,0:T(8,128)(2,1)S(1)}, bf16[128,128]{1,0:T(8,128)(2,1)S(1)}, u32[]{:S(2)}, u32[]{:S(2)}) %collective-permute-start.11) | collective-permute-done | bytes 32800 | tf_op jit(solution)/shard_map/ppermute | solution.py:28
  31.9 1.8 %attention.6 = s32[72,256]{1,0:T(8,128)S(1)} custom-call(bf16[512,128]{1,0:T(8,128)(2,1)S(1)} %collective-permute-done.10.q_ref.refs_2_, bf16[4096,128]{1,0:T(8,128)(2,1)S(1)} %get-tuple-element.82.k_ref, bf16[144,4096]{1,0:T(8,128)(2,1)S(1)} %turn.1.vt_ref), custom_call_target="tpu_custom_call" | custom-call | flops 1000000 | bytes 100000 | tf_op jit(solution)/shard_map/attention/pallas_call | solution.py:32
  33.7 0.7 collective-permute-start.15
  34.4 1.5 %collective-permute-start.12 = (bf16[256,128]{1,0:T(8,128)(2,1)S(1)}, bf16[256,128]{1,0:T(8,128)(2,1)S(1)}, u32[]{:S(2)}, u32[]{:S(2)}) collective-permute-start(bf16[256,128]{1,0:T(8,128)(2,1)S(1)} %stack.6), channel_id=1, source_target_pairs={{0,1},{1,0},{2,3},{3,2},{4,5},{5,4},{6,7},{7,6},{8,9},{9,8},{10,11... | collective-permute-start | bytes 196616 | tf_op jit(solution)/shard_map/ppermute | solution.py:28
  35.9 1.8 %attention.7.refs_0_ = f32[136,256]{1,0:T(8,128)S(1)} custom-call(bf16[512,128]{1,0:T(8,128)(2,1)S(1)} %collective-permute-done.10.q_ref.refs_2_, bf16[4096,128]{1,0:T(8,128)(2,1)S(1)} %get-tuple-element.82.k_ref, bf16[144,4096]{1,0:T(8,128)(2,1)S(1)} %turn.1.vt_ref), custom_call_target="tpu_custom_call" | custom-call | flops 1000000 | bytes 100000 | tf_op jit(solution)/shard_map/attention/pallas_call | solution.py:32
  37.7 1.5 %attend.1 = (bf16[512,1024]{1,0:T(8,128)(2,1)S(1)}, bf16[512,1024]{1,0:T(8,128)(2,1)S(1)}) custom-call(s32[1]{0:T(128)} %bitcast.shard_ref, bf16[256,128]{1,0:T(8,128)(2,1)S(1)} %total.8.q_ref.a_ref.refs_0_, bf16[256,128]{1,0:T(8,128)(2,1)S(1)} %collective-permute-done.9.b_ref.q_ref.refs_1_, bf16[512,128]{1,0:T(8,128)(2,1)S(1)} %collective-permute-done.10.q_ref.refs_2_, ...), custom_call_target="tpu_custom_call" | custom-call | flops 1000000 | bytes 100000 | tf_op jit(solution)/shard_map/attend/pallas_call | solution.py:32
  39.2 0.2 merge.2
  39.4 1.2 %collective-permute-start.16 = (s32[40,256]{1,0:T(8,128)S(1)}, s32[40,256]{1,0:T(8,128)S(1)}, u32[]{:S(2)}, u32[]{:S(2)}) collective-permute-start(s32[40,256]{1,0:T(8,128)S(1)} %get-tuple-element.99), channel_id=1, source_target_pairs={{0,4},{1,5},{2,6},{3,7},{4,0},{5,1},{6,2},{7,3},{8,12},{9,13},{10,... | collective-permute-start | bytes 122888 | tf_op jit(solution)/shard_map/ppermute | solution.py:28
  40.6 2.0 %gram.1.h_ref = f32[512,512]{1,0:T(8,128)S(1)} custom-call(bf16[512,1024]{1,0:T(8,128)(2,1)S(1)} %get-tuple-element.94.high_ref, bf16[512,1024]{1,0:T(8,128)(2,1)S(1)} %get-tuple-element.95.low_ref), custom_call_target="tpu_custom_call" | custom-call | flops 4000000000 | bytes 100000 | tf_op jit(solution)/shard_map/gram/pallas_call | solution.py:32
  42.6 0.8 %collective-permute-done.16.refs_1_ = s32[40,256]{1,0:T(8,128)S(1)} collective-permute-done((s32[40,256]{1,0:T(8,128)S(1)}, s32[40,256]{1,0:T(8,128)S(1)}, u32[]{:S(2)}, u32[]{:S(2)}) %collective-permute-start.16) | collective-permute-done | bytes 40992 | tf_op jit(solution)/shard_map/ppermute | solution.py:28
  43.5 1.7 %invert.1.inverse_ref = f32[64,64]{1,0:T(8,128)S(1)} custom-call(f32[512,512]{1,0:T(8,128)S(1)} %gram.1.h_ref), custom_call_target="tpu_custom_call" | custom-call | flops 1000000000 | bytes 100000 | tf_op jit(solution)/shard_map/invert/pallas_call | solution.py:32
  45.3 1.7 %collective-permute-start.17 = (s32[24,256]{1,0:T(8,128)S(1)}, s32[24,256]{1,0:T(8,128)S(1)}, u32[]{:S(2)}, u32[]{:S(2)}) collective-permute-start(s32[24,256]{1,0:T(8,128)S(1)} %get-tuple-element.105), channel_id=1, source_target_pairs={{0,8},{1,9},{2,10},{3,11},{4,12},{5,13},{6,14},{7,15},{8,0},{9,1},... | collective-permute-start | bytes 73736 | tf_op jit(solution)/shard_map/ppermute | solution.py:28
  47.0 2.0 %sweep.8 = (f32[512,512]{1,0:T(8,128)S(1)}, f32[64,64]{1,0:T(8,128)S(1)}) custom-call(f32[512,512]{1,0:T(8,128)S(1)} %gram.1.h_ref, f32[64,64]{1,0:T(8,128)S(1)} %invert.1.inverse_ref), custom_call_target="tpu_custom_call" | custom-call | flops 2000000000 | bytes 100000 | tf_op jit(solution)/shard_map/sweep/pallas_call | solution.py:32
  49.0 1.1 %collective-permute-done.17.refs_1_ = s32[24,256]{1,0:T(8,128)S(1)} collective-permute-done((s32[24,256]{1,0:T(8,128)S(1)}, s32[24,256]{1,0:T(8,128)S(1)}, u32[]{:S(2)}, u32[]{:S(2)}) %collective-permute-start.17) | collective-permute-done | bytes 24608 | tf_op jit(solution)/shard_map/ppermute | solution.py:28
  50.1 1.7 %collective-permute-start.18 = (f32[32,256]{1,0:T(8,128)S(1)}, f32[32,256]{1,0:T(8,128)S(1)}, u32[]{:S(2)}, u32[]{:S(2)}) collective-permute-start(f32[32,256]{1,0:T(8,128)S(1)} %finish.1.a_ref), channel_id=1, source_target_pairs={{0,8},{1,9},{2,10},{3,11},{4,12},{5,13},{6,14},{7,15},{8,0},{9,1},... | collective-permute-start | bytes 98312 | tf_op jit(solution)/shard_map/ppermute | solution.py:28
  51.8 1.9 %sweep.9 = (f32[512,512]{1,0:T(8,128)S(1)}, f32[64,64]{1,0:T(8,128)S(1)}) custom-call(f32[512,512]{1,0:T(8,128)S(1)} %get-tuple-element.106.h_ref, f32[64,64]{1,0:T(8,128)S(1)} %get-tuple-element.107.inverse_ref), custom_call_target="tpu_custom_call" | custom-call | flops 2000000000 | bytes 100000 | tf_op jit(solution)/shard_map/sweep/pallas_call | solution.py:32
  53.7 2.0 %sweep.10 = (f32[512,512]{1,0:T(8,128)S(1)}, f32[64,64]{1,0:T(8,128)S(1)}) custom-call(f32[512,512]{1,0:T(8,128)S(1)} %get-tuple-element.108.h_ref, f32[64,64]{1,0:T(8,128)S(1)} %get-tuple-element.109.inverse_ref), custom_call_target="tpu_custom_call" | custom-call | flops 2000000000 | bytes 100000 | tf_op jit(solution)/shard_map/sweep/pallas_call | solution.py:32
  55.8 1.8 %collective-permute-start.19 = (f32[64,256]{1,0:T(8,128)S(1)}, f32[64,256]{1,0:T(8,128)S(1)}, u32[]{:S(2)}, u32[]{:S(2)}) collective-permute-start(f32[64,256]{1,0:T(8,128)S(1)} %stack.7.a_ref), channel_id=1, source_target_pairs={{0,4},{1,5},{2,6},{3,7},{4,0},{5,1},{6,2},{7,3},{8,12},{9,13},{10,... | collective-permute-start | bytes 196616 | tf_op jit(solution)/shard_map/ppermute | solution.py:28
  57.5 1.9 %sweep.11 = (f32[512,512]{1,0:T(8,128)S(1)}, f32[64,64]{1,0:T(8,128)S(1)}) custom-call(f32[512,512]{1,0:T(8,128)S(1)} %get-tuple-element.114.h_ref, f32[64,64]{1,0:T(8,128)S(1)} %get-tuple-element.115.inverse_ref), custom_call_target="tpu_custom_call" | custom-call | flops 2000000000 | bytes 100000 | tf_op jit(solution)/shard_map/sweep/pallas_call | solution.py:32
  59.5 0.6 collective-permute-done.19.b_ref
  60.2 1.1 %collective-permute-start.20 = (s32[72,256]{1,0:T(8,128)S(1)}, s32[72,256]{1,0:T(8,128)S(1)}, u32[]{:S(2)}, u32[]{:S(2)}) collective-permute-start(s32[72,256]{1,0:T(8,128)S(1)} %pack.1.a_ref), channel_id=1, source_target_pairs={{0,2},{1,3},{2,0},{3,1},{4,6},{5,7},{6,4},{7,5},{8,10},{9,11},{10,... | collective-permute-start | bytes 221192 | tf_op jit(solution)/shard_map/ppermute | solution.py:28
  61.2 2.1 %sweep.12 = (f32[512,512]{1,0:T(8,128)S(1)}, f32[64,64]{1,0:T(8,128)S(1)}) custom-call(f32[512,512]{1,0:T(8,128)S(1)} %get-tuple-element.119.h_ref, f32[64,64]{1,0:T(8,128)S(1)} %get-tuple-element.120.inverse_ref), custom_call_target="tpu_custom_call" | custom-call | flops 2000000000 | bytes 100000 | tf_op jit(solution)/shard_map/sweep/pallas_call | solution.py:32
  63.4 1.9 %sweep.13 = (f32[512,512]{1,0:T(8,128)S(1)}, f32[64,64]{1,0:T(8,128)S(1)}) custom-call(f32[512,512]{1,0:T(8,128)S(1)} %get-tuple-element.121.h_ref, f32[64,64]{1,0:T(8,128)S(1)} %get-tuple-element.122.inverse_ref), custom_call_target="tpu_custom_call" | custom-call | flops 2000000000 | bytes 100000 | tf_op jit(solution)/shard_map/sweep/pallas_call | solution.py:32
  65.4 2.1 %sweep.14 = (f32[512,512]{1,0:T(8,128)S(1)}, f32[64,64]{1,0:T(8,128)S(1)}) custom-call(f32[512,512]{1,0:T(8,128)S(1)} %get-tuple-element.126.h_ref, f32[64,64]{1,0:T(8,128)S(1)} %get-tuple-element.127.inverse_ref), custom_call_target="tpu_custom_call" | custom-call | flops 2000000000 | bytes 100000 | tf_op jit(solution)/shard_map/sweep/pallas_call | solution.py:32
  67.5 0.7 sweep.15.minus_ref
  68.3 1.9 %fit.1 = (f32[128,512]{1,0:T(8,128)S(1)}, f32[8,128]{1,0:T(8,128)S(1)}) custom-call(s32[1]{0:T(128)} %bitcast.shard_ref, f32[512,512]{1,0:T(8,128)S(1)} %sweep.15.minus_ref, bf16[512,1024]{1,0:T(8,128)(2,1)S(1)} %get-tuple-element.94.high_ref, bf16[512,1024]{1,0:T(8,128)(2,1)S(1)} %get-tuple-element.95.low_ref, s32[144,256]{1,0:T(8,128)S(1)} %stack.9.own_ref, ...), custom_call_target="tpu_custom_call" | custom-call | flops 1000000000 | bytes 100000 | tf_op jit(solution)/shard_map/fit/pallas_call | solution.py:32
  70.2 1.5 %collective-permute-start.22 = (f32[8,128]{1,0:T(8,128)S(1)}, f32[8,128]{1,0:T(8,128)S(1)}, u32[]{:S(2)}, u32[]{:S(2)}) collective-permute-start(f32[8,128]{1,0:T(8,128)S(1)} %get-tuple-element.135.refs_0_), channel_id=1, source_target_pairs={{0,16},{16,0},{1,17},{17,1},{2,18},{18,2},{3,19},{19,3},{4,20},{20... | collective-permute-start | bytes 12296 | tf_op jit(solution)/shard_map/ppermute | solution.py:28
  71.8 0.8 %flip.1 = f32[512,128]{1,0:T(8,128)} custom-call(f32[128,512]{1,0:T(8,128)S(1)} %get-tuple-element.134.x_ref), custom_call_target="tpu_custom_call" | custom-call | flops 1000000 | bytes 100000 | tf_op jit(solution)/shard_map/flip/pallas_call | solution.py:32
  72.6 1.3 %collective-permute-done.22.refs_1_ = f32[8,128]{1,0:T(8,128)S(1)} collective-permute-done((f32[8,128]{1,0:T(8,128)S(1)}, f32[8,128]{1,0:T(8,128)S(1)}, u32[]{:S(2)}, u32[]{:S(2)}) %collective-permute-start.22) | collective-permute-done | bytes 4128 | tf_op jit(solution)/shard_map/ppermute | solution.py:28
  73.9 0.5 mean.1
  (37 shorter events, 0.6 us)
Async XLA Ops:
  0.6 8.3 %copy-start = (bf16[1,4096,128]{2,1,0:T(8,128)(2,1)S(1)}, bf16[1,4096,128]{2,1,0:T(8,128)(2,1)}, u32[]{:S(2)}) copy-start(bf16[1,4096,128]{2,1,0:T(8,128)(2,1)} %param.7) | copy-start | bytes 3145732
  2.4 2.6 %collective-permute-start = (bf16[512,128]{1,0:T(8,128)(2,1)S(1)}, bf16[512,128]{1,0:T(8,128)(2,1)S(1)}, u32[]{:S(2)}, u32[]{:S(2)}) collective-permute-start(bf16[512,128]{1,0:T(8,128)(2,1)S(1)} %get-tuple-element.70), channel_id=1, source_target_pairs={{0,1},{1,0},{2,3},{3,2},{4,5},{5,4},{6,7},{7,6},{8,9},{9,8},{10,11... | collective-permute-start | bytes 393224 | tf_op jit(solution)/shard_map/ppermute | solution.py:28
  4.8 3.2 %collective-permute-start.1 = (bf16[256,128]{1,0:T(8,128)(2,1)S(1)}, bf16[256,128]{1,0:T(8,128)(2,1)S(1)}, u32[]{:S(2)}, u32[]{:S(2)}) collective-permute-start(bf16[256,128]{1,0:T(8,128)(2,1)S(1)} %get-tuple-element.73), channel_id=1, source_target_pairs={{0,1},{1,0},{2,3},{3,2},{4,5},{5,4},{6,7},{7,6},{8,9},{9,8},{10,11... | collective-permute-start | bytes 196616 | tf_op jit(solution)/shard_map/ppermute | solution.py:28
  5.0 7.0 %collective-permute-start.3 = (bf16[256,128]{1,0:T(8,128)(2,1)S(1)}, bf16[256,128]{1,0:T(8,128)(2,1)S(1)}, u32[]{:S(2)}, u32[]{:S(2)}) collective-permute-start(bf16[256,128]{1,0:T(8,128)(2,1)S(1)} %get-tuple-element.76), channel_id=1, source_target_pairs={{0,2},{1,3},{2,0},{3,1},{4,6},{5,7},{6,4},{7,5},{8,10},{9,11},{10,... | collective-permute-start | bytes 196616 | tf_op jit(solution)/shard_map/ppermute | solution.py:28
  8.0 4.0 %collective-permute-start.2 = (bf16[128,128]{1,0:T(8,128)(2,1)S(1)}, bf16[128,128]{1,0:T(8,128)(2,1)S(1)}, u32[]{:S(2)}, u32[]{:S(2)}) collective-permute-start(bf16[128,128]{1,0:T(8,128)(2,1)S(1)} %get-tuple-element.75), channel_id=1, source_target_pairs={{0,2},{1,3},{2,0},{3,1},{4,6},{5,7},{6,4},{7,5},{8,10},{9,11},{10,... | collective-permute-start | bytes 98312 | tf_op jit(solution)/shard_map/ppermute | solution.py:28
  12.1 9.4 %collective-permute-start.7 = (bf16[256,128]{1,0:T(8,128)(2,1)S(1)}, bf16[256,128]{1,0:T(8,128)(2,1)S(1)}, u32[]{:S(2)}, u32[]{:S(2)}) collective-permute-start(bf16[256,128]{1,0:T(8,128)(2,1)S(1)} %total.6.refs_0_), channel_id=1, source_target_pairs={{0,12},{1,13},{2,14},{3,15},{4,8},{5,9},{6,10},{7,11},{8,4},{9,5},... | collective-permute-start | bytes 196616 | tf_op jit(solution)/shard_map/ppermute | solution.py:28
  15.7 5.7 %collective-permute-start.6 = (bf16[256,128]{1,0:T(8,128)(2,1)S(1)}, bf16[256,128]{1,0:T(8,128)(2,1)S(1)}, u32[]{:S(2)}, u32[]{:S(2)}) collective-permute-start(bf16[256,128]{1,0:T(8,128)(2,1)S(1)} %total.6.refs_0_), channel_id=1, source_target_pairs={{0,8},{1,9},{2,10},{3,11},{4,12},{5,13},{6,14},{7,15},{8,0},{9,1},... | collective-permute-start | bytes 196616 | tf_op jit(solution)/shard_map/ppermute | solution.py:28
  15.8 5.7 %collective-permute-start.5 = (bf16[256,128]{1,0:T(8,128)(2,1)S(1)}, bf16[256,128]{1,0:T(8,128)(2,1)S(1)}, u32[]{:S(2)}, u32[]{:S(2)}) collective-permute-start(bf16[256,128]{1,0:T(8,128)(2,1)S(1)} %total.6.refs_0_), channel_id=1, source_target_pairs={{0,4},{1,5},{2,6},{3,7},{4,0},{5,1},{6,2},{7,3},{8,12},{9,13},{10,... | collective-permute-start | bytes 196616 | tf_op jit(solution)/shard_map/ppermute | solution.py:28
  16.5 4.9 %collective-permute-start.4 = (bf16[128,128]{1,0:T(8,128)(2,1)S(1)}, bf16[128,128]{1,0:T(8,128)(2,1)S(1)}, u32[]{:S(2)}, u32[]{:S(2)}) collective-permute-start(bf16[128,128]{1,0:T(8,128)(2,1)S(1)} %total.5.refs_0_), channel_id=1, source_target_pairs={{0,4},{1,5},{2,6},{3,7},{4,0},{5,1},{6,2},{7,3},{8,12},{9,13},{10,... | collective-permute-start | bytes 98312 | tf_op jit(solution)/shard_map/ppermute | solution.py:28
  21.5 6.3 %collective-permute-start.9 = (bf16[256,128]{1,0:T(8,128)(2,1)S(1)}, bf16[256,128]{1,0:T(8,128)(2,1)S(1)}, u32[]{:S(2)}, u32[]{:S(2)}) collective-permute-start(bf16[256,128]{1,0:T(8,128)(2,1)S(1)} %total.8.q_ref.a_ref.refs_0_), channel_id=1, source_target_pairs={{0,2},{1,3},{2,0},{3,1},{4,6},{5,7},{6,4},{7,5},{8,10},{9,11},{10,... | collective-permute-start | bytes 196616 | tf_op jit(solution)/shard_map/ppermute | solution.py:28
  22.9 4.8 %collective-permute-start.8 = (bf16[128,128]{1,0:T(8,128)(2,1)S(1)}, bf16[128,128]{1,0:T(8,128)(2,1)S(1)}, u32[]{:S(2)}, u32[]{:S(2)}) collective-permute-start(bf16[128,128]{1,0:T(8,128)(2,1)S(1)} %total.7.refs_0_), channel_id=1, source_target_pairs={{0,8},{1,9},{2,10},{3,11},{4,12},{5,13},{6,14},{7,15},{8,0},{9,1},... | collective-permute-start | bytes 98312 | tf_op jit(solution)/shard_map/ppermute | solution.py:28
  27.8 4.1 %collective-permute-start.10 = (bf16[512,128]{1,0:T(8,128)(2,1)S(1)}, bf16[512,128]{1,0:T(8,128)(2,1)S(1)}, u32[]{:S(2)}, u32[]{:S(2)}) collective-permute-start(bf16[512,128]{1,0:T(8,128)(2,1)S(1)} %stack.5), channel_id=1, source_target_pairs={{0,1},{1,0},{2,3},{3,2},{4,5},{5,4},{6,7},{7,6},{8,9},{9,8},{10,11... | collective-permute-start | bytes 393224 | tf_op jit(solution)/shard_map/ppermute | solution.py:28
  27.9 4.0 %collective-permute-start.11 = (bf16[128,128]{1,0:T(8,128)(2,1)S(1)}, bf16[128,128]{1,0:T(8,128)(2,1)S(1)}, u32[]{:S(2)}, u32[]{:S(2)}) collective-permute-start(bf16[128,128]{1,0:T(8,128)(2,1)S(1)} %total.9.a_ref.refs_3_), channel_id=1, source_target_pairs={{0,2},{1,3},{2,0},{3,1},{4,6},{5,7},{6,4},{7,5},{8,10},{9,11},{10,... | collective-permute-start | bytes 98312 | tf_op jit(solution)/shard_map/ppermute | solution.py:28
  28.6 10.6 %collective-permute-start.13 = (s32[72,256]{1,0:T(8,128)S(1)}, s32[72,256]{1,0:T(8,128)S(1)}, u32[]{:S(2)}, u32[]{:S(2)}) collective-permute-start(s32[72,256]{1,0:T(8,128)S(1)} %attention.4), channel_id=1, source_target_pairs={{0,1},{1,0},{2,3},{3,2},{4,5},{5,4},{6,7},{7,6},{8,9},{9,8},{10,11... | collective-permute-start | bytes 221192 | tf_op jit(solution)/shard_map/ppermute | solution.py:28
  33.7 5.6 %collective-permute-start.15 = (s32[72,256]{1,0:T(8,128)S(1)}, s32[72,256]{1,0:T(8,128)S(1)}, u32[]{:S(2)}, u32[]{:S(2)}) collective-permute-start(s32[72,256]{1,0:T(8,128)S(1)} %attention.6), channel_id=1, source_target_pairs={{0,2},{1,3},{2,0},{3,1},{4,6},{5,7},{6,4},{7,5},{8,10},{9,11},{10,... | collective-permute-start | bytes 221192 | tf_op jit(solution)/shard_map/ppermute | solution.py:28
  34.4 4.8 %collective-permute-start.14 = (s32[72,256]{1,0:T(8,128)S(1)}, s32[72,256]{1,0:T(8,128)S(1)}, u32[]{:S(2)}, u32[]{:S(2)}) collective-permute-start(s32[72,256]{1,0:T(8,128)S(1)} %attention.5), channel_id=1, source_target_pairs={{0,3},{1,2},{2,1},{3,0},{4,7},{5,6},{6,5},{7,4},{8,11},{9,10},{10,... | collective-permute-start | bytes 221192 | tf_op jit(solution)/shard_map/ppermute | solution.py:28
  34.4 3.2 %collective-permute-start.12 = (bf16[256,128]{1,0:T(8,128)(2,1)S(1)}, bf16[256,128]{1,0:T(8,128)(2,1)S(1)}, u32[]{:S(2)}, u32[]{:S(2)}) collective-permute-start(bf16[256,128]{1,0:T(8,128)(2,1)S(1)} %stack.6), channel_id=1, source_target_pairs={{0,1},{1,0},{2,3},{3,2},{4,5},{5,4},{6,7},{7,6},{8,9},{9,8},{10,11... | collective-permute-start | bytes 196616 | tf_op jit(solution)/shard_map/ppermute | solution.py:28
  39.4 4.1 %collective-permute-start.16 = (s32[40,256]{1,0:T(8,128)S(1)}, s32[40,256]{1,0:T(8,128)S(1)}, u32[]{:S(2)}, u32[]{:S(2)}) collective-permute-start(s32[40,256]{1,0:T(8,128)S(1)} %get-tuple-element.99), channel_id=1, source_target_pairs={{0,4},{1,5},{2,6},{3,7},{4,0},{5,1},{6,2},{7,3},{8,12},{9,13},{10,... | collective-permute-start | bytes 122888 | tf_op jit(solution)/shard_map/ppermute | solution.py:28
  45.3 4.8 %collective-permute-start.17 = (s32[24,256]{1,0:T(8,128)S(1)}, s32[24,256]{1,0:T(8,128)S(1)}, u32[]{:S(2)}, u32[]{:S(2)}) collective-permute-start(s32[24,256]{1,0:T(8,128)S(1)} %get-tuple-element.105), channel_id=1, source_target_pairs={{0,8},{1,9},{2,10},{3,11},{4,12},{5,13},{6,14},{7,15},{8,0},{9,1},... | collective-permute-start | bytes 73736 | tf_op jit(solution)/shard_map/ppermute | solution.py:28
  50.1 5.6 %collective-permute-start.18 = (f32[32,256]{1,0:T(8,128)S(1)}, f32[32,256]{1,0:T(8,128)S(1)}, u32[]{:S(2)}, u32[]{:S(2)}) collective-permute-start(f32[32,256]{1,0:T(8,128)S(1)} %finish.1.a_ref), channel_id=1, source_target_pairs={{0,8},{1,9},{2,10},{3,11},{4,12},{5,13},{6,14},{7,15},{8,0},{9,1},... | collective-permute-start | bytes 98312 | tf_op jit(solution)/shard_map/ppermute | solution.py:28
  55.8 4.3 %collective-permute-start.19 = (f32[64,256]{1,0:T(8,128)S(1)}, f32[64,256]{1,0:T(8,128)S(1)}, u32[]{:S(2)}, u32[]{:S(2)}) collective-permute-start(f32[64,256]{1,0:T(8,128)S(1)} %stack.7.a_ref), channel_id=1, source_target_pairs={{0,4},{1,5},{2,6},{3,7},{4,0},{5,1},{6,2},{7,3},{8,12},{9,13},{10,... | collective-permute-start | bytes 196616 | tf_op jit(solution)/shard_map/ppermute | solution.py:28
  60.2 5.1 %collective-permute-start.20 = (s32[72,256]{1,0:T(8,128)S(1)}, s32[72,256]{1,0:T(8,128)S(1)}, u32[]{:S(2)}, u32[]{:S(2)}) collective-permute-start(s32[72,256]{1,0:T(8,128)S(1)} %pack.1.a_ref), channel_id=1, source_target_pairs={{0,2},{1,3},{2,0},{3,1},{4,6},{5,7},{6,4},{7,5},{8,10},{9,11},{10,... | collective-permute-start | bytes 221192 | tf_op jit(solution)/shard_map/ppermute | solution.py:28
  65.3 2.2 %collective-permute-start.21 = (s32[144,256]{1,0:T(8,128)S(1)}, s32[144,256]{1,0:T(8,128)S(1)}, u32[]{:S(2)}, u32[]{:S(2)}) collective-permute-start(s32[144,256]{1,0:T(8,128)S(1)} %stack.9.own_ref), channel_id=1, source_target_pairs={{0,1},{1,0},{2,3},{3,2},{4,5},{5,4},{6,7},{7,6},{8,9},{9,8},{10,11... | collective-permute-start | bytes 442376 | tf_op jit(solution)/shard_map/ppermute | solution.py:28
  70.2 3.7 %collective-permute-start.22 = (f32[8,128]{1,0:T(8,128)S(1)}, f32[8,128]{1,0:T(8,128)S(1)}, u32[]{:S(2)}, u32[]{:S(2)}) collective-permute-start(f32[8,128]{1,0:T(8,128)S(1)} %get-tuple-element.135.refs_0_), channel_id=1, source_target_pairs={{0,16},{16,0},{1,17},{17,1},{2,18},{18,2},{3,19},{19,3},{4,20},{20... | collective-permute-start | bytes 12296 | tf_op jit(solution)/shard_map/ppermute | solution.py:28

commit v11 on v9

--- a/solution.py
+++ b/solution.py
@@ -26,6 +26,11 @@
 def swap(array, axis, step):
     size = lax.axis_size(axis)
     return lax.ppermute(array, axis, [(i, i ^ step) for i in range(size)])
+
+
+def one_way(array, step, core):
+    size = lax.axis_size("ctx")
+    return lax.ppermute(array, "ctx", [(i, i ^ step) for i in range(size) if i % 2 == core])
 
 
 def call(kernel, ins, outs, cost=10**5, scratch=(), name=None, specs=None):
@@ -208,14 +213,23 @@
     first = attend_to(near, keys, turned)
     far, first = lax.optimization_barrier((far, first))
     (both,) = call(stack_kernel, (near, far), [(half, BF16)], name="stack")
-    other, came = swap(both, "ctx", 1), [swap(first, "ctx", 1)]
+    other = swap(both, "ctx", 1)
+    partials, handed = [first], [one_way(first, 1, 0)]
     second = attend_to(far, keys, turned)
     other, second = lax.optimization_barrier((other, second))
-    came.append(swap(second, "ctx", 3))
+    partials.append(second)
+    handed.append(one_way(second, 1, 0))
     third = attend_to(other, keys, turned, start=quarter[0])
-    came.append(swap(third, "ctx", 2))
-    other, third = lax.optimization_barrier((other, third))
-    return near, far, other, attend_to(other, keys, turned, packed=False), came
+    partials.append(third)
+    handed.append(one_way(third, 1, 0))
+    shape, kind = partial_shape(values.shape[1], 2 * (rows // 4), True)
+    (send,) = call(far_half_kernel, (second, third, handed[1], handed[2]), [(shape, kind)], name="far_half")
+    other, send = lax.optimization_barrier((other, send))
+    came = one_way(send, 2, 1)
+    fourth = attend_to(other, keys, turned)
+    partials.append(fourth)
+    handed.append(one_way(fourth, 1, 0))
+    return near, far, other, (first, fourth, handed[0], handed[3], came)
 
 
 def turn_kernel(v_ref, vt_ref):
@@ -264,8 +278,7 @@
     )[0]
 
 
-def merged(*refs):
-    parts = [partial_of(ref) for ref in refs]
+def join(*parts):
     top = functools.reduce(jnp.maximum, [part[1] for part in parts])
     scales = [jnp.exp2(part[1] - top) for part in parts]
     total = sum(part[2] * scale for part, scale in zip(parts, scales))
@@ -273,9 +286,25 @@
     return out, top, total
 
 
-def merge_kernel(step, shard_ref, *refs):
-    ins, (keep_ref, send_ref, work) = refs[:-3], refs[-3:]
-    out, top, total = merged(*ins)
+def merged(*refs):
+    return join(*[partial_of(ref) for ref in refs])
+
+
+def far_half_kernel(second_ref, third_ref, handed_second_ref, handed_third_ref, out_ref):
+    lanes = second_ref.shape[1]
+    out_ref[:, :lanes] = pack(*merged(third_ref, handed_second_ref))
+    out_ref[:, lanes:] = pack(*merged(second_ref, handed_third_ref))
+
+
+def near_half_kernel(step, shard_ref, first_ref, fourth_ref, handed_first_ref, handed_fourth_ref, came_ref, keep_ref, send_ref, work):
+    lanes = first_ref.shape[1]
+    own = [merged(fourth_ref, handed_first_ref), merged(first_ref, handed_fourth_ref)]
+    own = [jnp.concatenate(pair, axis=1) for pair in zip(*own)]
+    out, top, total = join(tuple(own), partial_of(came_ref))
+    split_rows(step, shard_ref, out, top, total, keep_ref, send_ref, work)
+
+
+def split_rows(step, shard_ref, out, top, total, keep_ref, send_ref, work):
     rows = out.shape[0] // 2
     work[...] = out
     bit = (shard_ref[0] // step) % 2
@@ -283,6 +312,10 @@
     put_partial(send_ref, work[aligned(1 - bit, rows), :], top, total)
 
 
+def merge_kernel(step, shard_ref, *refs):
+    split_rows(step, shard_ref, *merged(*refs[:-3]), *refs[-3:])
+
+
 def finish_kernel(*refs):
     out, _, total = merged(*refs[:-1])
     refs[-1][...] = out / total
@@ -300,34 +333,35 @@
     out_ref[...] = pack(y_ref[...], one * 0.0, one)
 
 
-def target_rounds(shard, keep, came):
-    dims, lanes = keep.shape[0] - SUB, keep.shape[1]
+def target_rounds(shard, parts):
+    dims, lanes = 2 * (parts[0].shape[0] - SUB), 2 * parts[0].shape[1]
     devices = lax.axis_size("ctx")
-    came = yield came
+    parts = yield list(parts)
     steps = [2**i for i in range(2, devices.bit_length() - 1)]
-    rows = dims
+    rows, kernel = dims, near_half_kernel
     for step in steps:
         keep, send = call(
-            functools.partial(merge_kernel, step),
-            (shard, keep, *came),
+            functools.partial(kernel, step),
+            (shard, *parts),
             [partial_shape(rows // 2, lanes, packed) for packed in (False, True)],
             scratch=[pltpu.VMEM((rows, lanes), F32)],
             name="merge",
         )
-        came = yield [swap(send, "ctx", step)]
+        came = yield [one_way(send, step, 1)]
+        parts, kernel = (keep, *came), merge_kernel
         rows //= 2
-    (block,) = call(finish_kernel, (keep, *came), [((rows, lanes), F32)], name="finish")
+    (block,) = call(finish_kernel, parts, [((rows, lanes), F32)], name="finish")
     for step in reversed(steps):
-        came = yield [swap(block, "ctx", step)]
+        came = yield [one_way(block, step, 1)]
         rows *= 2
         (block,) = call(
             functools.partial(stack_rows_kernel, step), (shard, block, *came), [((rows, lanes), F32)], name="stack"
         )
     shape, kind = partial_shape(dims, lanes, True)
     (block,) = call(pack_kernel, (block,), [(shape, kind)], name="pack")
-    came = yield [swap(block, "ctx", 2)]
+    came = yield [one_way(block, 2, 1)]
     (block,) = call(stack_kernel, (block, *came), [((2 * shape[0], lanes), kind)], name="stack")
-    came = yield [swap(block, "ctx", 1)]
+    came = yield [one_way(block, 1, 1)]
     return block, *came
 
 
@@ -455,10 +489,10 @@
 
 def fit_kernel(shard_ref, minus_ref, high_ref, low_ref, own_ref, other_ref, x_ref, err_ref, yt):
     rows, lanes = own_ref.shape[0] // 2, own_ref.shape[1]
-    place = shard_ref[0] % 4
-    for s, ref in ((1, own_ref), (3, own_ref), (0, other_ref), (2, other_ref)):
-        half = s // 2
-        yt[:, aligned(place ^ s, lanes)] = means(ref[half * rows : (half + 1) * rows, :])
+    is_core_1, y = shard_ref[0] % 2 == 1, shard_ref[0] // 2 % 2
+    packed = jnp.where(is_core_1, own_ref[...], other_ref[...])
+    for half in range(2):
+        yt[:, aligned(y ^ half, lanes)] = means(packed[half * rows : (half + 1) * rows])
     target = yt[...]
     attend = high_ref[...], low_ref[...]
     cross = product(halves(target), attend, NT)
@@ -488,8 +522,8 @@
     shard = lax.axis_index("ctx").astype(jnp.int32).reshape(1)
 
     attend_to = functools.partial(attention, lanes, score_scale)
-    near, far, other, keep, came = spread(shard, queries[0, 0], kept, keys[0], roots, values[0], attend_to)
-    rounds = target_rounds(shard, keep, came)
+    near, far, other, parts = spread(shard, queries[0, 0], kept, keys[0], roots, values[0], attend_to)
+    rounds = target_rounds(shard, parts)
     came = next(rounds)
     ends = None
 

time: 72.5 us -> 88 us (1.21)
  starting transfers between devices: 18.8 us -> 26.7 us
  waiting for transfers between devices: 18.6 us -> 25.7 us
    ppermute x0 -> x11, starting transfers between devices: none -> 15.4 us  [one_way(): lax.ppermute(array, 'ctx', [(i, i ^ step) for i in range(size) if i % 2 =...]
    ppermute x0 -> x11, waiting for transfers between devices: none -> 12.2 us  [one_way(): lax.ppermute(array, 'ctx', [(i, i ^ step) for i in range(size) if i % 2 =...]
    ppermute x17 -> x8, starting transfers between devices: 18.8 us -> 11.2 us  [swap(): return lax.ppermute(array, axis, [(i, i ^ step) for i in range(size)])]
    ppermute x17 -> x8, waiting for transfers between devices: 18.6 us -> 13.5 us  [swap(): return lax.ppermute(array, axis, [(i, i ^ step) for i in range(size)])]
    pallas_call x31 -> x32, Pallas kernels: 33.2 us -> 33.5 us  [call(): pl.pallas_call(kernel, in_specs=specs or [SMEM if x.size == 1 else VMEM f...]
  transfers between devices with their start and end apart: 17 -> 19, of which waited for: 11 -> 8; matrix products, arithmetic and copies ran while one was open for 0% -> 0% of each run, Pallas kernels for 36% -> 28%
where the time goes in v11:
time: 88 us; the launch traced here: 87.6 us
  Pallas kernels  33.5 us (38%)
  starting transfers between devices  26.7 us (30%)
  waiting for transfers between devices  25.7 us (29%)
  between operations  1.74 us (2%)
    pallas_call x32, Pallas kernels, call(): pl.pallas_call(kernel, in_specs=specs or [SMEM if x.size == 1 else VMEM f...  33.5 us
    ppermute x11, starting transfers between devices, one_way(): lax.ppermute(array, 'ctx', [(i, i ^ step) for i in range(size) if i % 2 =...  15.4 us
    ppermute x8, waiting for transfers between devices, swap(): return lax.ppermute(array, axis, [(i, i ^ step) for i in range(size)])  13.5 us
    ppermute x11, waiting for transfers between devices, one_way(): lax.ppermute(array, 'ctx', [(i, i ^ step) for i in range(size) if i % 2 =...  12.2 us
    ppermute x8, starting transfers between devices, swap(): return lax.ppermute(array, axis, [(i, i ^ step) for i in range(size)])  11.2 us
  transfers between devices with their start and end apart: 19, of which 8 were waited for; matrix products, arithmetic and copies ran while one was open for 0% of the time, Pallas kernels for 28%

profile of v11, /device:TPU:0, one launch (start us, length us, event | category | flops | bytes accessed | tf_op | source)
XLA Modules:
  0.0 87.6 jit_solution(15244106400772413451)
XLA Ops:
  1.4 2.0 %prepare.1 = (bf16[768,128]{1,0:T(8,128)(2,1)S(1)}, bf16[768,128]{1,0:T(8,128)(2,1)S(1)}, bf16[4096,128]{1,0:T(8,128)(2,1)S(1)}) custom-call(s32[1]{0:T(128)} %bitcast.shard_ref, s32[1]{0:T(128)S(6)} %copy.7.root_ref, bf16[1024,128]{1,0:T(8,128)(2,1)} %bitcast.9, s32[1,512]{1,0:T(1,128)} %kept_hbm.1, bf16[4096,128]{1,0:T(8,128)(2,1)} %bitcast.7), custom_call_target="tpu_custom_call" | custom-call | flops 100000 | bytes 100000 | tf_op jit(solution)/shard_map/prepare/pallas_call | solution.py:37
  3.4 0.5 collective-permute-start
  3.9 1.1 %collective-permute-done.b_ref = bf16[768,128]{1,0:T(8,128)(2,1)S(1)} collective-permute-done((bf16[768,128]{1,0:T(8,128)(2,1)S(1)}, bf16[768,128]{1,0:T(8,128)(2,1)S(1)}, u32[]{:S(2)}, u32[]{:S(2)}) %collective-permute-start) | collective-permute-done | bytes 196640 | tf_op jit(solution)/shard_map/ppermute | solution.py:28
  5.0 3.0 %collective-permute-start.1 = (bf16[384,128]{1,0:T(8,128)(2,1)S(1)}, bf16[384,128]{1,0:T(8,128)(2,1)S(1)}, u32[]{:S(2)}, u32[]{:S(2)}) collective-permute-start(bf16[384,128]{1,0:T(8,128)(2,1)S(1)} %get-tuple-element.64), channel_id=1, source_target_pairs={{0,2},{1,3},{2,0},{3,1},{4,6},{5,7},{6,4},{7,5},{8,10},{9,11},{10,... | collective-permute-start | bytes 294920 | tf_op jit(solution)/shard_map/ppermute | solution.py:28
  7.9 0.3 turn.1.vt_ref
  8.3 2.8 %collective-permute-done.1.refs_1_ = bf16[384,128]{1,0:T(8,128)(2,1)S(1)} collective-permute-done((bf16[384,128]{1,0:T(8,128)(2,1)S(1)}, bf16[384,128]{1,0:T(8,128)(2,1)S(1)}, u32[]{:S(2)}, u32[]{:S(2)}) %collective-permute-start.1) | collective-permute-done | bytes 98336 | tf_op jit(solution)/shard_map/ppermute | solution.py:28
  11.1 3.9 %collective-permute-start.4 = (bf16[384,128]{1,0:T(8,128)(2,1)S(1)}, bf16[384,128]{1,0:T(8,128)(2,1)S(1)}, u32[]{:S(2)}, u32[]{:S(2)}) collective-permute-start(bf16[384,128]{1,0:T(8,128)(2,1)S(1)} %total.2.refs_0_), channel_id=1, source_target_pairs={{0,12},{1,13},{2,14},{3,15},{4,8},{5,9},{6,10},{7,11},{8,4},{9,5},... | collective-permute-start | bytes 294920 | tf_op jit(solution)/shard_map/ppermute | solution.py:28
  15.0 0.6 collective-permute-start.2
  15.6 3.1 %collective-permute-done.4.refs_3_ = bf16[384,128]{1,0:T(8,128)(2,1)S(1)} collective-permute-done((bf16[384,128]{1,0:T(8,128)(2,1)S(1)}, bf16[384,128]{1,0:T(8,128)(2,1)S(1)}, u32[]{:S(2)}, u32[]{:S(2)}) %collective-permute-start.4) | collective-permute-done | bytes 98336 | tf_op jit(solution)/shard_map/ppermute | solution.py:28
  18.7 4.0 %collective-permute-done.3.refs_2_ = bf16[384,128]{1,0:T(8,128)(2,1)S(1)} collective-permute-done((bf16[384,128]{1,0:T(8,128)(2,1)S(1)}, bf16[384,128]{1,0:T(8,128)(2,1)S(1)}, u32[]{:S(2)}, u32[]{:S(2)}) %collective-permute-start.3) | collective-permute-done | bytes 98336 | tf_op jit(solution)/shard_map/ppermute | solution.py:28
  22.7 1.6 %collective-permute-start.5 = (bf16[384,128]{1,0:T(8,128)(2,1)S(1)}, bf16[384,128]{1,0:T(8,128)(2,1)S(1)}, u32[]{:S(2)}, u32[]{:S(2)}) collective-permute-start(bf16[384,128]{1,0:T(8,128)(2,1)S(1)} %total.3.q_ref.a_ref.near_ref), channel_id=1, source_target_pairs={{0,2},{1,3},{2,0},{3,1},{4,6},{5,7},{6,4},{7,5},{8,10},{9,11},{10,... | collective-permute-start | bytes 294920 | tf_op jit(solution)/shard_map/ppermute | solution.py:28
  24.3 1.8 %attention.4.first_ref = s32[72,256]{1,0:T(8,128)S(1)} custom-call(bf16[384,128]{1,0:T(8,128)(2,1)S(1)} %total.3.q_ref.a_ref.near_ref, bf16[4096,128]{1,0:T(8,128)(2,1)S(1)} %get-tuple-element.66.k_ref, bf16[144,4096]{1,0:T(8,128)(2,1)S(1)} %turn.1.vt_ref), custom_call_target="tpu_custom_call" | custom-call | flops 1000000 | bytes 100000 | tf_op jit(solution)/shard_map/attention/pallas_call | solution.py:37
  26.1 1.3 %collective-permute-done.5.b_ref.q_ref.far_ref = bf16[384,128]{1,0:T(8,128)(2,1)S(1)} collective-permute-done((bf16[384,128]{1,0:T(8,128)(2,1)S(1)}, bf16[384,128]{1,0:T(8,128)(2,1)S(1)}, u32[]{:S(2)}, u32[]{:S(2)}) %collective-permute-start.5) | collective-permute-done | bytes 98336 | tf_op jit(solution)/shard_map/ppermute | solution.py:28
  27.5 1.8 %attention.5.second_ref = s32[72,256]{1,0:T(8,128)S(1)} custom-call(bf16[384,128]{1,0:T(8,128)(2,1)S(1)} %collective-permute-done.5.b_ref.q_ref.far_ref, bf16[4096,128]{1,0:T(8,128)(2,1)S(1)} %get-tuple-element.66.k_ref, bf16[144,4096]{1,0:T(8,128)(2,1)S(1)} %turn.1.vt_ref), custom_call_target="tpu_custom_call" | custom-call | flops 1000000 | bytes 100000 | tf_op jit(solution)/shard_map/attention/pallas_call | solution.py:37
  29.4 1.8 %attention.6.third_ref = s32[72,256]{1,0:T(8,128)S(1)} custom-call(bf16[768,128]{1,0:T(8,128)(2,1)S(1)} %collective-permute-done.6.q_ref.other_ref, bf16[4096,128]{1,0:T(8,128)(2,1)S(1)} %get-tuple-element.66.k_ref, bf16[144,4096]{1,0:T(8,128)(2,1)S(1)} %turn.1.vt_ref), custom_call_target="tpu_custom_call" | custom-call | flops 1000000 | bytes 100000 | tf_op jit(solution)/shard_map/attention/pallas_call | solution.py:37
  31.2 2.4 %collective-permute-start.8 = (s32[72,256]{1,0:T(8,128)S(1)}, s32[72,256]{1,0:T(8,128)S(1)}, u32[]{:S(2)}, u32[]{:S(2)}) collective-permute-start(s32[72,256]{1,0:T(8,128)S(1)} %attention.6.third_ref), channel_id=1, source_target_pairs={{0,1},{2,3},{4,5},{6,7},{8,9},{10,11},{12,13},{14,15},{16,17},{18,... | collective-permute-start | bytes 221192 | tf_op jit(solution)/shard_map/ppermute | solution.py:33
  33.6 1.3 %collective-permute-start.7 = (s32[72,256]{1,0:T(8,128)S(1)}, s32[72,256]{1,0:T(8,128)S(1)}, u32[]{:S(2)}, u32[]{:S(2)}) collective-permute-start(s32[72,256]{1,0:T(8,128)S(1)} %attention.5.second_ref), channel_id=1, source_target_pairs={{0,1},{2,3},{4,5},{6,7},{8,9},{10,11},{12,13},{14,15},{16,17},{18,... | collective-permute-start | bytes 221192 | tf_op jit(solution)/shard_map/ppermute | solution.py:33
  34.9 0.9 %collective-permute-done.7.handed_second_ref = s32[72,256]{1,0:T(8,128)S(1)} collective-permute-done((s32[72,256]{1,0:T(8,128)S(1)}, s32[72,256]{1,0:T(8,128)S(1)}, u32[]{:S(2)}, u32[]{:S(2)}) %collective-permute-start.7) | collective-permute-done | bytes 73760 | tf_op jit(solution)/shard_map/ppermute | solution.py:33
  35.8 0.2 far_half.1
  36.0 0.7 collective-permute-start.11
  36.6 4.7 %collective-permute-start.9 = (s32[72,256]{1,0:T(8,128)S(1)}, s32[72,256]{1,0:T(8,128)S(1)}, u32[]{:S(2)}, u32[]{:S(2)}) collective-permute-start(s32[72,256]{1,0:T(8,128)S(1)} %attention.4.first_ref), channel_id=1, source_target_pairs={{0,1},{2,3},{4,5},{6,7},{8,9},{10,11},{12,13},{14,15},{16,17},{18,... | collective-permute-start | bytes 221192 | tf_op jit(solution)/shard_map/ppermute | solution.py:33
  41.4 1.8 %attention.7.fourth_ref = s32[72,256]{1,0:T(8,128)S(1)} custom-call(bf16[768,128]{1,0:T(8,128)(2,1)S(1)} %collective-permute-done.6.q_ref.other_ref, bf16[4096,128]{1,0:T(8,128)(2,1)S(1)} %get-tuple-element.66.k_ref, bf16[144,4096]{1,0:T(8,128)(2,1)S(1)} %turn.1.vt_ref), custom_call_target="tpu_custom_call" | custom-call | flops 1000000 | bytes 100000 | tf_op jit(solution)/shard_map/attention/pallas_call | solution.py:37
  43.2 1.3 %collective-permute-start.10 = (s32[72,256]{1,0:T(8,128)S(1)}, s32[72,256]{1,0:T(8,128)S(1)}, u32[]{:S(2)}, u32[]{:S(2)}) collective-permute-start(s32[72,256]{1,0:T(8,128)S(1)} %attention.7.fourth_ref), channel_id=1, source_target_pairs={{0,1},{2,3},{4,5},{6,7},{8,9},{10,11},{12,13},{14,15},{16,17},{18,... | collective-permute-start | bytes 221192 | tf_op jit(solution)/shard_map/ppermute | solution.py:33
  44.5 1.5 %attend.1 = (bf16[512,1024]{1,0:T(8,128)(2,1)S(1)}, bf16[512,1024]{1,0:T(8,128)(2,1)S(1)}) custom-call(s32[1]{0:T(128)} %bitcast.shard_ref, bf16[384,128]{1,0:T(8,128)(2,1)S(1)} %total.3.q_ref.a_ref.near_ref, bf16[384,128]{1,0:T(8,128)(2,1)S(1)} %collective-permute-done.5.b_ref.q_ref.far_ref, bf16[768,128]{1,0:T(8,128)(2,1)S(1)} %collective-permute-done.6.q_ref.other_ref), custom_call_target="tpu_custom_call" | custom-call | flops 1000000 | bytes 100000 | tf_op jit(solution)/shard_map/attend/pallas_call | solution.py:37
  46.1 0.3 merge.2
  46.4 0.8 collective-permute-start.12
  47.3 2.0 %gram.1.h_ref = f32[512,512]{1,0:T(8,128)S(1)} custom-call(bf16[512,1024]{1,0:T(8,128)(2,1)S(1)} %get-tuple-element.76.high_ref, bf16[512,1024]{1,0:T(8,128)(2,1)S(1)} %get-tuple-element.77.low_ref), custom_call_target="tpu_custom_call" | custom-call | flops 4000000000 | bytes 100000 | tf_op jit(solution)/shard_map/gram/pallas_call | solution.py:37
  49.3 1.6 %invert.1.inverse_ref = f32[64,64]{1,0:T(8,128)S(1)} custom-call(f32[512,512]{1,0:T(8,128)S(1)} %gram.1.h_ref), custom_call_target="tpu_custom_call" | custom-call | flops 1000000000 | bytes 100000 | tf_op jit(solution)/shard_map/invert/pallas_call | solution.py:37
  50.8 0.1 merge.3
  50.9 0.7 collective-permute-start.13
  51.6 2.0 %sweep.8 = (f32[512,512]{1,0:T(8,128)S(1)}, f32[64,64]{1,0:T(8,128)S(1)}) custom-call(f32[512,512]{1,0:T(8,128)S(1)} %gram.1.h_ref, f32[64,64]{1,0:T(8,128)S(1)} %invert.1.inverse_ref), custom_call_target="tpu_custom_call" | custom-call | flops 2000000000 | bytes 100000 | tf_op jit(solution)/shard_map/sweep/pallas_call | solution.py:37
  53.7 0.7 collective-permute-start.14
  54.3 1.9 %sweep.9 = (f32[512,512]{1,0:T(8,128)S(1)}, f32[64,64]{1,0:T(8,128)S(1)}) custom-call(f32[512,512]{1,0:T(8,128)S(1)} %get-tuple-element.90.h_ref, f32[64,64]{1,0:T(8,128)S(1)} %get-tuple-element.91.inverse_ref), custom_call_target="tpu_custom_call" | custom-call | flops 2000000000 | bytes 100000 | tf_op jit(solution)/shard_map/sweep/pallas_call | solution.py:37
  56.2 2.0 %sweep.10 = (f32[512,512]{1,0:T(8,128)S(1)}, f32[64,64]{1,0:T(8,128)S(1)}) custom-call(f32[512,512]{1,0:T(8,128)S(1)} %get-tuple-element.92.h_ref, f32[64,64]{1,0:T(8,128)S(1)} %get-tuple-element.93.inverse_ref), custom_call_target="tpu_custom_call" | custom-call | flops 2000000000 | bytes 100000 | tf_op jit(solution)/shard_map/sweep/pallas_call | solution.py:37
  58.3 0.7 collective-permute-start.15
  59.0 1.9 %sweep.11 = (f32[512,512]{1,0:T(8,128)S(1)}, f32[64,64]{1,0:T(8,128)S(1)}) custom-call(f32[512,512]{1,0:T(8,128)S(1)} %get-tuple-element.98.h_ref, f32[64,64]{1,0:T(8,128)S(1)} %get-tuple-element.99.inverse_ref), custom_call_target="tpu_custom_call" | custom-call | flops 2000000000 | bytes 100000 | tf_op jit(solution)/shard_map/sweep/pallas_call | solution.py:37
  61.0 0.9 %collective-permute-start.16 = (s32[72,512]{1,0:T(8,128)S(1)}, s32[72,512]{1,0:T(8,128)S(1)}, u32[]{:S(2)}, u32[]{:S(2)}) collective-permute-start(s32[72,512]{1,0:T(8,128)S(1)} %pack.1.a_ref), channel_id=1, source_target_pairs={{1,3},{3,1},{5,7},{7,5},{9,11},{11,9},{13,15},{15,13},{17,19},{19,... | collective-permute-start | bytes 442376 | tf_op jit(solution)/shard_map/ppermute | solution.py:33
  61.9 2.1 %sweep.12 = (f32[512,512]{1,0:T(8,128)S(1)}, f32[64,64]{1,0:T(8,128)S(1)}) custom-call(f32[512,512]{1,0:T(8,128)S(1)} %get-tuple-element.103.h_ref, f32[64,64]{1,0:T(8,128)S(1)} %get-tuple-element.104.inverse_ref), custom_call_target="tpu_custom_call" | custom-call | flops 2000000000 | bytes 100000 | tf_op jit(solution)/shard_map/sweep/pallas_call | solution.py:37
  64.0 1.9 %sweep.13 = (f32[512,512]{1,0:T(8,128)S(1)}, f32[64,64]{1,0:T(8,128)S(1)}) custom-call(f32[512,512]{1,0:T(8,128)S(1)} %get-tuple-element.105.h_ref, f32[64,64]{1,0:T(8,128)S(1)} %get-tuple-element.106.inverse_ref), custom_call_target="tpu_custom_call" | custom-call | flops 2000000000 | bytes 100000 | tf_op jit(solution)/shard_map/sweep/pallas_call | solution.py:37
  66.0 1.3 %collective-permute-start.17 = (s32[144,512]{1,0:T(8,128)S(1)}, s32[144,512]{1,0:T(8,128)S(1)}, u32[]{:S(2)}, u32[]{:S(2)}) collective-permute-start(s32[144,512]{1,0:T(8,128)S(1)} %stack.7.own_ref), channel_id=1, source_target_pairs={{1,0},{3,2},{5,4},{7,6},{9,8},{11,10},{13,12},{15,14},{17,16},{19,... | collective-permute-start | bytes 884744 | tf_op jit(solution)/shard_map/ppermute | solution.py:33
  67.3 2.1 %sweep.14 = (f32[512,512]{1,0:T(8,128)S(1)}, f32[64,64]{1,0:T(8,128)S(1)}) custom-call(f32[512,512]{1,0:T(8,128)S(1)} %get-tuple-element.110.h_ref, f32[64,64]{1,0:T(8,128)S(1)} %get-tuple-element.111.inverse_ref), custom_call_target="tpu_custom_call" | custom-call | flops 2000000000 | bytes 100000 | tf_op jit(solution)/shard_map/sweep/pallas_call | solution.py:37
  69.4 11.3 %collective-permute-done.17.other_ref = s32[144,512]{1,0:T(8,128)S(1)} collective-permute-done((s32[144,512]{1,0:T(8,128)S(1)}, s32[144,512]{1,0:T(8,128)S(1)}, u32[]{:S(2)}, u32[]{:S(2)}) %collective-permute-start.17) | collective-permute-done | bytes 294944 | tf_op jit(solution)/shard_map/ppermute | solution.py:33
  80.8 0.7 sweep.15.minus_ref
  81.5 2.0 %fit.1 = (f32[128,512]{1,0:T(8,128)S(1)}, f32[8,128]{1,0:T(8,128)S(1)}) custom-call(s32[1]{0:T(128)} %bitcast.shard_ref, f32[512,512]{1,0:T(8,128)S(1)} %sweep.15.minus_ref, bf16[512,1024]{1,0:T(8,128)(2,1)S(1)} %get-tuple-element.76.high_ref, bf16[512,1024]{1,0:T(8,128)(2,1)S(1)} %get-tuple-element.77.low_ref, s32[144,512]{1,0:T(8,128)S(1)} %stack.7.own_ref, ...), custom_call_target="tpu_custom_call" | custom-call | flops 1000000000 | bytes 100000 | tf_op jit(solution)/shard_map/fit/pallas_call | solution.py:37
  83.5 1.6 %collective-permute-start.18 = (f32[8,128]{1,0:T(8,128)S(1)}, f32[8,128]{1,0:T(8,128)S(1)}, u32[]{:S(2)}, u32[]{:S(2)}) collective-permute-start(f32[8,128]{1,0:T(8,128)S(1)} %get-tuple-element.119.refs_0_), channel_id=1, source_target_pairs={{0,16},{16,0},{1,17},{17,1},{2,18},{18,2},{3,19},{19,3},{4,20},{20... | collective-permute-start | bytes 12296 | tf_op jit(solution)/shard_map/ppermute | solution.py:28
  85.0 0.8 flip.1
  85.9 1.3 %collective-permute-done.18.refs_1_ = f32[8,128]{1,0:T(8,128)S(1)} collective-permute-done((f32[8,128]{1,0:T(8,128)S(1)}, f32[8,128]{1,0:T(8,128)S(1)}, u32[]{:S(2)}, u32[]{:S(2)}) %collective-permute-start.18) | collective-permute-done | bytes 4128 | tf_op jit(solution)/shard_map/ppermute | solution.py:28
  87.1 0.5 mean.1
  (24 shorter events, 0.4 us)
Async XLA Ops:
  0.6 7.3 %copy-start = (bf16[1,4096,128]{2,1,0:T(8,128)(2,1)S(1)}, bf16[1,4096,128]{2,1,0:T(8,128)(2,1)}, u32[]{:S(2)}) copy-start(bf16[1,4096,128]{2,1,0:T(8,128)(2,1)} %param.7) | copy-start | bytes 3145732
  3.4 1.6 %collective-permute-start = (bf16[768,128]{1,0:T(8,128)(2,1)S(1)}, bf16[768,128]{1,0:T(8,128)(2,1)S(1)}, u32[]{:S(2)}, u32[]{:S(2)}) collective-permute-start(bf16[768,128]{1,0:T(8,128)(2,1)S(1)} %get-tuple-element.62), channel_id=1, source_target_pairs={{0,1},{1,0},{2,3},{3,2},{4,5},{5,4},{6,7},{7,6},{8,9},{9,8},{10,11... | collective-permute-start | bytes 589832 | tf_op jit(solution)/shard_map/ppermute | solution.py:28
  5.0 6.1 %collective-permute-start.1 = (bf16[384,128]{1,0:T(8,128)(2,1)S(1)}, bf16[384,128]{1,0:T(8,128)(2,1)S(1)}, u32[]{:S(2)}, u32[]{:S(2)}) collective-permute-start(bf16[384,128]{1,0:T(8,128)(2,1)S(1)} %get-tuple-element.64), channel_id=1, source_target_pairs={{0,2},{1,3},{2,0},{3,1},{4,6},{5,7},{6,4},{7,5},{8,10},{9,11},{10,... | collective-permute-start | bytes 294920 | tf_op jit(solution)/shard_map/ppermute | solution.py:28
  11.1 7.6 %collective-permute-start.4 = (bf16[384,128]{1,0:T(8,128)(2,1)S(1)}, bf16[384,128]{1,0:T(8,128)(2,1)S(1)}, u32[]{:S(2)}, u32[]{:S(2)}) collective-permute-start(bf16[384,128]{1,0:T(8,128)(2,1)S(1)} %total.2.refs_0_), channel_id=1, source_target_pairs={{0,12},{1,13},{2,14},{3,15},{4,8},{5,9},{6,10},{7,11},{8,4},{9,5},... | collective-permute-start | bytes 294920 | tf_op jit(solution)/shard_map/ppermute | solution.py:28
  15.0 7.7 %collective-permute-start.3 = (bf16[384,128]{1,0:T(8,128)(2,1)S(1)}, bf16[384,128]{1,0:T(8,128)(2,1)S(1)}, u32[]{:S(2)}, u32[]{:S(2)}) collective-permute-start(bf16[384,128]{1,0:T(8,128)(2,1)S(1)} %total.2.refs_0_), channel_id=1, source_target_pairs={{0,8},{1,9},{2,10},{3,11},{4,12},{5,13},{6,14},{7,15},{8,0},{9,1},... | collective-permute-start | bytes 294920 | tf_op jit(solution)/shard_map/ppermute | solution.py:28
  15.0 7.7 %collective-permute-start.2 = (bf16[384,128]{1,0:T(8,128)(2,1)S(1)}, bf16[384,128]{1,0:T(8,128)(2,1)S(1)}, u32[]{:S(2)}, u32[]{:S(2)}) collective-permute-start(bf16[384,128]{1,0:T(8,128)(2,1)S(1)} %total.2.refs_0_), channel_id=1, source_target_pairs={{0,4},{1,5},{2,6},{3,7},{4,0},{5,1},{6,2},{7,3},{8,12},{9,13},{10,... | collective-permute-start | bytes 294920 | tf_op jit(solution)/shard_map/ppermute | solution.py:28
  22.7 4.7 %collective-permute-start.5 = (bf16[384,128]{1,0:T(8,128)(2,1)S(1)}, bf16[384,128]{1,0:T(8,128)(2,1)S(1)}, u32[]{:S(2)}, u32[]{:S(2)}) collective-permute-start(bf16[384,128]{1,0:T(8,128)(2,1)S(1)} %total.3.q_ref.a_ref.near_ref), channel_id=1, source_target_pairs={{0,2},{1,3},{2,0},{3,1},{4,6},{5,7},{6,4},{7,5},{8,10},{9,11},{10,... | collective-permute-start | bytes 294920 | tf_op jit(solution)/shard_map/ppermute | solution.py:28
  27.4 1.9 %collective-permute-start.6 = (bf16[768,128]{1,0:T(8,128)(2,1)S(1)}, bf16[768,128]{1,0:T(8,128)(2,1)S(1)}, u32[]{:S(2)}, u32[]{:S(2)}) collective-permute-start(bf16[768,128]{1,0:T(8,128)(2,1)S(1)} %stack.4), channel_id=1, source_target_pairs={{0,1},{1,0},{2,3},{3,2},{4,5},{5,4},{6,7},{7,6},{8,9},{9,8},{10,11... | collective-permute-start | bytes 589832 | tf_op jit(solution)/shard_map/ppermute | solution.py:28
  31.2 3.7 %collective-permute-start.8 = (s32[72,256]{1,0:T(8,128)S(1)}, s32[72,256]{1,0:T(8,128)S(1)}, u32[]{:S(2)}, u32[]{:S(2)}) collective-permute-start(s32[72,256]{1,0:T(8,128)S(1)} %attention.6.third_ref), channel_id=1, source_target_pairs={{0,1},{2,3},{4,5},{6,7},{8,9},{10,11},{12,13},{14,15},{16,17},{18,... | collective-permute-start | bytes 221192 | tf_op jit(solution)/shard_map/ppermute | solution.py:33
  33.6 2.2 %collective-permute-start.7 = (s32[72,256]{1,0:T(8,128)S(1)}, s32[72,256]{1,0:T(8,128)S(1)}, u32[]{:S(2)}, u32[]{:S(2)}) collective-permute-start(s32[72,256]{1,0:T(8,128)S(1)} %attention.5.second_ref), channel_id=1, source_target_pairs={{0,1},{2,3},{4,5},{6,7},{8,9},{10,11},{12,13},{14,15},{16,17},{18,... | collective-permute-start | bytes 221192 | tf_op jit(solution)/shard_map/ppermute | solution.py:33
  36.0 10.1 %collective-permute-start.11 = (s32[72,512]{1,0:T(8,128)S(1)}, s32[72,512]{1,0:T(8,128)S(1)}, u32[]{:S(2)}, u32[]{:S(2)}) collective-permute-start(s32[72,512]{1,0:T(8,128)S(1)} %far_half.1), channel_id=1, source_target_pairs={{1,3},{3,1},{5,7},{7,5},{9,11},{11,9},{13,15},{15,13},{17,19},{19,... | collective-permute-start | bytes 442376 | tf_op jit(solution)/shard_map/ppermute | solution.py:33
  36.6 9.4 %collective-permute-start.9 = (s32[72,256]{1,0:T(8,128)S(1)}, s32[72,256]{1,0:T(8,128)S(1)}, u32[]{:S(2)}, u32[]{:S(2)}) collective-permute-start(s32[72,256]{1,0:T(8,128)S(1)} %attention.4.first_ref), channel_id=1, source_target_pairs={{0,1},{2,3},{4,5},{6,7},{8,9},{10,11},{12,13},{14,15},{16,17},{18,... | collective-permute-start | bytes 221192 | tf_op jit(solution)/shard_map/ppermute | solution.py:33
  43.2 2.9 %collective-permute-start.10 = (s32[72,256]{1,0:T(8,128)S(1)}, s32[72,256]{1,0:T(8,128)S(1)}, u32[]{:S(2)}, u32[]{:S(2)}) collective-permute-start(s32[72,256]{1,0:T(8,128)S(1)} %attention.7.fourth_ref), channel_id=1, source_target_pairs={{0,1},{2,3},{4,5},{6,7},{8,9},{10,11},{12,13},{14,15},{16,17},{18,... | collective-permute-start | bytes 221192 | tf_op jit(solution)/shard_map/ppermute | solution.py:33
  46.4 2.8 %collective-permute-start.12 = (s32[40,512]{1,0:T(8,128)S(1)}, s32[40,512]{1,0:T(8,128)S(1)}, u32[]{:S(2)}, u32[]{:S(2)}) collective-permute-start(s32[40,512]{1,0:T(8,128)S(1)} %get-tuple-element.83), channel_id=1, source_target_pairs={{1,5},{3,7},{5,1},{7,3},{9,13},{11,15},{13,9},{15,11},{17,21},{19,... | collective-permute-start | bytes 245768 | tf_op jit(solution)/shard_map/ppermute | solution.py:33
  50.9 2.7 %collective-permute-start.13 = (s32[24,512]{1,0:T(8,128)S(1)}, s32[24,512]{1,0:T(8,128)S(1)}, u32[]{:S(2)}, u32[]{:S(2)}) collective-permute-start(s32[24,512]{1,0:T(8,128)S(1)} %get-tuple-element.89), channel_id=1, source_target_pairs={{1,9},{3,11},{5,13},{7,15},{9,1},{11,3},{13,5},{15,7},{17,25},{19,... | collective-permute-start | bytes 147464 | tf_op jit(solution)/shard_map/ppermute | solution.py:33
  53.7 4.6 %collective-permute-start.14 = (f32[32,512]{1,0:T(8,128)S(1)}, f32[32,512]{1,0:T(8,128)S(1)}, u32[]{:S(2)}, u32[]{:S(2)}) collective-permute-start(f32[32,512]{1,0:T(8,128)S(1)} %finish.1.a_ref), channel_id=1, source_target_pairs={{1,9},{3,11},{5,13},{7,15},{9,1},{11,3},{13,5},{15,7},{17,25},{19,... | collective-permute-start | bytes 196616 | tf_op jit(solution)/shard_map/ppermute | solution.py:33
  58.3 2.6 %collective-permute-start.15 = (f32[64,512]{1,0:T(8,128)S(1)}, f32[64,512]{1,0:T(8,128)S(1)}, u32[]{:S(2)}, u32[]{:S(2)}) collective-permute-start(f32[64,512]{1,0:T(8,128)S(1)} %stack.5.a_ref), channel_id=1, source_target_pairs={{1,5},{3,7},{5,1},{7,3},{9,13},{11,15},{13,9},{15,11},{17,21},{19,... | collective-permute-start | bytes 393224 | tf_op jit(solution)/shard_map/ppermute | solution.py:33
  61.0 4.9 %collective-permute-start.16 = (s32[72,512]{1,0:T(8,128)S(1)}, s32[72,512]{1,0:T(8,128)S(1)}, u32[]{:S(2)}, u32[]{:S(2)}) collective-permute-start(s32[72,512]{1,0:T(8,128)S(1)} %pack.1.a_ref), channel_id=1, source_target_pairs={{1,3},{3,1},{5,7},{7,5},{9,11},{11,9},{13,15},{15,13},{17,19},{19,... | collective-permute-start | bytes 442376 | tf_op jit(solution)/shard_map/ppermute | solution.py:33
  66.0 14.8 %collective-permute-start.17 = (s32[144,512]{1,0:T(8,128)S(1)}, s32[144,512]{1,0:T(8,128)S(1)}, u32[]{:S(2)}, u32[]{:S(2)}) collective-permute-start(s32[144,512]{1,0:T(8,128)S(1)} %stack.7.own_ref), channel_id=1, source_target_pairs={{1,0},{3,2},{5,4},{7,6},{9,8},{11,10},{13,12},{15,14},{17,16},{19,... | collective-permute-start | bytes 884744 | tf_op jit(solution)/shard_map/ppermute | solution.py:33
  83.5 3.7 %collective-permute-start.18 = (f32[8,128]{1,0:T(8,128)S(1)}, f32[8,128]{1,0:T(8,128)S(1)}, u32[]{:S(2)}, u32[]{:S(2)}) collective-permute-start(f32[8,128]{1,0:T(8,128)S(1)} %get-tuple-element.119.refs_0_), channel_id=1, source_target_pairs={{0,16},{16,0},{1,17},{17,1},{2,18},{18,2},{3,19},{19,3},{4,20},{20... | collective-permute-start | bytes 12296 | tf_op jit(solution)/shard_map/ppermute | solution.py:28

commit v12 on v9

--- a/solution.py
+++ b/solution.py
@@ -273,62 +273,24 @@
     return out, top, total
 
 
-def merge_kernel(step, shard_ref, *refs):
-    ins, (keep_ref, send_ref, work) = refs[:-3], refs[-3:]
-    out, top, total = merged(*ins)
-    rows = out.shape[0] // 2
-    work[...] = out
-    bit = (shard_ref[0] // step) % 2
-    put_partial(keep_ref, work[aligned(bit, rows), :], top, total)
-    put_partial(send_ref, work[aligned(1 - bit, rows), :], top, total)
-
-
-def finish_kernel(*refs):
-    out, _, total = merged(*refs[:-1])
-    refs[-1][...] = out / total
-
-
-def stack_rows_kernel(step, shard_ref, a_ref, b_ref, out_ref):
-    rows = a_ref.shape[0]
-    bit = (shard_ref[0] // step) % 2
-    out_ref[aligned(bit, rows), :] = a_ref[...]
-    out_ref[aligned(1 - bit, rows), :] = b_ref[...]
-
-
-def pack_kernel(y_ref, out_ref):
-    one = jnp.ones((1, y_ref.shape[1]), F32)
-    out_ref[...] = pack(y_ref[...], one * 0.0, one)
-
-
-def target_rounds(shard, keep, came):
+def merge_kernel(*refs):
+    put_partial(refs[-1], *merged(*refs[:-1]))
+
+
+def target_rounds(keep, came):
     dims, lanes = keep.shape[0] - SUB, keep.shape[1]
-    devices = lax.axis_size("ctx")
+    shape, kind = partial_shape(dims, lanes, True)
     came = yield came
-    steps = [2**i for i in range(2, devices.bit_length() - 1)]
-    rows = dims
-    for step in steps:
-        keep, send = call(
-            functools.partial(merge_kernel, step),
-            (shard, keep, *came),
-            [partial_shape(rows // 2, lanes, packed) for packed in (False, True)],
-            scratch=[pltpu.VMEM((rows, lanes), F32)],
-            name="merge",
-        )
-        came = yield [swap(send, "ctx", step)]
-        rows //= 2
-    (block,) = call(finish_kernel, (keep, *came), [((rows, lanes), F32)], name="finish")
-    for step in reversed(steps):
-        came = yield [swap(block, "ctx", step)]
-        rows *= 2
-        (block,) = call(
-            functools.partial(stack_rows_kernel, step), (shard, block, *came), [((rows, lanes), F32)], name="stack"
-        )
-    shape, kind = partial_shape(dims, lanes, True)
-    (block,) = call(pack_kernel, (block,), [(shape, kind)], name="pack")
-    came = yield [swap(block, "ctx", 2)]
-    (block,) = call(stack_kernel, (block, *came), [((2 * shape[0], lanes), kind)], name="stack")
-    came = yield [swap(block, "ctx", 1)]
-    return block, *came
+    (mine,) = call(merge_kernel, (keep, *came), [(shape, kind)], name="merge")
+    step = 4
+    while step < lax.axis_size("ctx"):
+        came = yield [swap(mine, "ctx", step)]
+        (mine,) = call(merge_kernel, (mine, *came), [(shape, kind)], name="merge")
+        step *= 2
+    came = yield [swap(mine, "ctx", 2)]
+    (both,) = call(stack_kernel, (mine, *came), [((2 * shape[0], lanes), kind)], name="stack")
+    came = yield [swap(both, "ctx", 1)]
+    return both, *came
 
 
 def attend_kernel(score_scale, shard_ref, near_ref, far_ref, other_ref, high_ref, low_ref, c_all):
@@ -489,7 +451,7 @@
 
     attend_to = functools.partial(attention, lanes, score_scale)
     near, far, other, keep, came = spread(shard, queries[0, 0], kept, keys[0], roots, values[0], attend_to)
-    rounds = target_rounds(shard, keep, came)
+    rounds = target_rounds(keep, came)
     came = next(rounds)
     ends = None
 
@@ -514,10 +476,10 @@
     )
     attend = beside(attend)
     (system,) = call(gram_kernel, attend, [system_shape], 4 * 10**9, name="gram")
-    system = beside(system)
     panels = count // PANEL
     block_shape = ((PANEL, PANEL), F32)
     (inverse,) = call(invert_kernel, (system,), [block_shape], 10**9, name="invert")
+    system, inverse = beside((system, inverse))
     for panel in range(panels):
         last = panel == panels - 1
         system, *inverse = call(
@@ -528,7 +490,7 @@
             name="sweep",
         )
         inverse = None if last else inverse[0]
-        if panel in (0, 2, 3, 5, 6):
+        if panel in (2, 4, 6):
             system, inverse = beside((system, inverse))
     while ends is None:
         system = beside(system)

time: 72.5 us -> 66.9 us (0.923)
  waiting for transfers between devices: 18.6 us -> 14.8 us
  starting transfers between devices: 18.8 us -> 17.1 us
    ppermute x17 -> x15, waiting for transfers between devices: 18.6 us -> 14.8 us  [swap(): return lax.ppermute(array, axis, [(i, i ^ step) for i in range(size)])]
    ppermute x17 -> x15, starting transfers between devices: 18.8 us -> 17.1 us  [swap(): return lax.ppermute(array, axis, [(i, i ^ step) for i in range(size)])]
    pallas_call x31 -> x28, Pallas kernels: 33.2 us -> 33.2 us  [call(): pl.pallas_call(kernel, in_specs=specs or [SMEM if x.size == 1 else VMEM f...]
  transfers between devices with their start and end apart: 17 -> 15, of which waited for: 11 -> 8; matrix products, arithmetic and copies ran while one was open for 0% -> 0% of each run, Pallas kernels for 36% -> 41%
where the time goes in v12:
time: 66.9 us; the launch traced here: 66.7 us
  Pallas kernels  33.2 us (50%)
  starting transfers between devices  17.1 us (26%)
  waiting for transfers between devices  14.8 us (22%)
  between operations  1.6 us (2%)
    pallas_call x28, Pallas kernels, call(): pl.pallas_call(kernel, in_specs=specs or [SMEM if x.size == 1 else VMEM f...  33.2 us
    ppermute x15, starting transfers between devices, swap(): return lax.ppermute(array, axis, [(i, i ^ step) for i in range(size)])  17.1 us
    ppermute x15, waiting for transfers between devices, swap(): return lax.ppermute(array, axis, [(i, i ^ step) for i in range(size)])  14.8 us
  transfers between devices with their start and end apart: 15, of which 8 were waited for; matrix products, arithmetic and copies ran while one was open for 0% of the time, Pallas kernels for 41%

profile of v12, /device:TPU:0, one launch (start us, length us, event | category | flops | bytes accessed | tf_op | source)
XLA Modules:
  0.0 66.7 jit_solution(14684363863077968559)
XLA Ops:
  1.4 2.0 %prepare.1 = (bf16[768,128]{1,0:T(8,128)(2,1)S(1)}, bf16[768,128]{1,0:T(8,128)(2,1)S(1)}, bf16[4096,128]{1,0:T(8,128)(2,1)S(1)}) custom-call(s32[1]{0:T(128)} %bitcast.shard_ref, s32[1]{0:T(128)S(6)} %copy.7.root_ref, bf16[1024,128]{1,0:T(8,128)(2,1)} %bitcast.9, s32[1,512]{1,0:T(1,128)} %kept_hbm.1, bf16[4096,128]{1,0:T(8,128)(2,1)} %bitcast.7), custom_call_target="tpu_custom_call" | custom-call | flops 100000 | bytes 100000 | tf_op jit(solution)/shard_map/prepare/pallas_call | solution.py:32
  3.4 0.5 collective-permute-start
  3.9 1.1 %collective-permute-done.b_ref = bf16[768,128]{1,0:T(8,128)(2,1)S(1)} collective-permute-done((bf16[768,128]{1,0:T(8,128)(2,1)S(1)}, bf16[768,128]{1,0:T(8,128)(2,1)S(1)}, u32[]{:S(2)}, u32[]{:S(2)}) %collective-permute-start) | collective-permute-done | bytes 196640 | tf_op jit(solution)/shard_map/ppermute | solution.py:28
  5.0 3.0 %collective-permute-start.1 = (bf16[384,128]{1,0:T(8,128)(2,1)S(1)}, bf16[384,128]{1,0:T(8,128)(2,1)S(1)}, u32[]{:S(2)}, u32[]{:S(2)}) collective-permute-start(bf16[384,128]{1,0:T(8,128)(2,1)S(1)} %get-tuple-element.52), channel_id=1, source_target_pairs={{0,2},{1,3},{2,0},{3,1},{4,6},{5,7},{6,4},{7,5},{8,10},{9,11},{10,... | collective-permute-start | bytes 294920 | tf_op jit(solution)/shard_map/ppermute | solution.py:28
  7.9 0.3 turn.1.vt_ref
  8.3 2.8 %collective-permute-done.1.refs_1_ = bf16[384,128]{1,0:T(8,128)(2,1)S(1)} collective-permute-done((bf16[384,128]{1,0:T(8,128)(2,1)S(1)}, bf16[384,128]{1,0:T(8,128)(2,1)S(1)}, u32[]{:S(2)}, u32[]{:S(2)}) %collective-permute-start.1) | collective-permute-done | bytes 98336 | tf_op jit(solution)/shard_map/ppermute | solution.py:28
  11.1 3.9 %collective-permute-start.4 = (bf16[384,128]{1,0:T(8,128)(2,1)S(1)}, bf16[384,128]{1,0:T(8,128)(2,1)S(1)}, u32[]{:S(2)}, u32[]{:S(2)}) collective-permute-start(bf16[384,128]{1,0:T(8,128)(2,1)S(1)} %total.2.refs_0_), channel_id=1, source_target_pairs={{0,12},{1,13},{2,14},{3,15},{4,8},{5,9},{6,10},{7,11},{8,4},{9,5},... | collective-permute-start | bytes 294920 | tf_op jit(solution)/shard_map/ppermute | solution.py:28
  15.0 0.0 collective-permute-start.3
  15.0 0.6 collective-permute-start.2
  15.6 3.1 %collective-permute-done.4.refs_3_ = bf16[384,128]{1,0:T(8,128)(2,1)S(1)} collective-permute-done((bf16[384,128]{1,0:T(8,128)(2,1)S(1)}, bf16[384,128]{1,0:T(8,128)(2,1)S(1)}, u32[]{:S(2)}, u32[]{:S(2)}) %collective-permute-start.4) | collective-permute-done | bytes 98336 | tf_op jit(solution)/shard_map/ppermute | solution.py:28
  18.7 4.0 %collective-permute-done.3.refs_2_ = bf16[384,128]{1,0:T(8,128)(2,1)S(1)} collective-permute-done((bf16[384,128]{1,0:T(8,128)(2,1)S(1)}, bf16[384,128]{1,0:T(8,128)(2,1)S(1)}, u32[]{:S(2)}, u32[]{:S(2)}) %collective-permute-start.3) | collective-permute-done | bytes 98336 | tf_op jit(solution)/shard_map/ppermute | solution.py:28
  22.7 0.0 collective-permute-done.2.refs_1_
  22.7 1.6 %collective-permute-start.5 = (bf16[384,128]{1,0:T(8,128)(2,1)S(1)}, bf16[384,128]{1,0:T(8,128)(2,1)S(1)}, u32[]{:S(2)}, u32[]{:S(2)}) collective-permute-start(bf16[384,128]{1,0:T(8,128)(2,1)S(1)} %total.3.q_ref.a_ref.near_ref), channel_id=1, source_target_pairs={{0,2},{1,3},{2,0},{3,1},{4,6},{5,7},{6,4},{7,5},{8,10},{9,11},{10,... | collective-permute-start | bytes 294920 | tf_op jit(solution)/shard_map/ppermute | solution.py:28
  24.3 1.8 %attention.4 = s32[72,256]{1,0:T(8,128)S(1)} custom-call(bf16[384,128]{1,0:T(8,128)(2,1)S(1)} %total.3.q_ref.a_ref.near_ref, bf16[4096,128]{1,0:T(8,128)(2,1)S(1)} %get-tuple-element.54.k_ref, bf16[144,4096]{1,0:T(8,128)(2,1)S(1)} %turn.1.vt_ref), custom_call_target="tpu_custom_call" | custom-call | flops 1000000 | bytes 100000 | tf_op jit(solution)/shard_map/attention/pallas_call | solution.py:32
  26.1 1.3 %collective-permute-done.5.b_ref.q_ref.far_ref = bf16[384,128]{1,0:T(8,128)(2,1)S(1)} collective-permute-done((bf16[384,128]{1,0:T(8,128)(2,1)S(1)}, bf16[384,128]{1,0:T(8,128)(2,1)S(1)}, u32[]{:S(2)}, u32[]{:S(2)}) %collective-permute-start.5) | collective-permute-done | bytes 98336 | tf_op jit(solution)/shard_map/ppermute | solution.py:28
  27.4 0.1 collective-permute-start.6
  27.5 0.5 collective-permute-start.7
  28.0 1.8 %attention.5 = s32[72,256]{1,0:T(8,128)S(1)} custom-call(bf16[384,128]{1,0:T(8,128)(2,1)S(1)} %collective-permute-done.5.b_ref.q_ref.far_ref, bf16[4096,128]{1,0:T(8,128)(2,1)S(1)} %get-tuple-element.54.k_ref, bf16[144,4096]{1,0:T(8,128)(2,1)S(1)} %turn.1.vt_ref), custom_call_target="tpu_custom_call" | custom-call | flops 1000000 | bytes 100000 | tf_op jit(solution)/shard_map/attention/pallas_call | solution.py:32
  29.9 0.0 collective-permute-done.6.q_ref.other_ref
  29.9 1.8 %attention.6 = s32[72,256]{1,0:T(8,128)S(1)} custom-call(bf16[768,128]{1,0:T(8,128)(2,1)S(1)} %collective-permute-done.6.q_ref.other_ref, bf16[4096,128]{1,0:T(8,128)(2,1)S(1)} %get-tuple-element.54.k_ref, bf16[144,4096]{1,0:T(8,128)(2,1)S(1)} %turn.1.vt_ref), custom_call_target="tpu_custom_call" | custom-call | flops 1000000 | bytes 100000 | tf_op jit(solution)/shard_map/attention/pallas_call | solution.py:32
  31.7 1.6 %collective-permute-start.9 = (s32[72,256]{1,0:T(8,128)S(1)}, s32[72,256]{1,0:T(8,128)S(1)}, u32[]{:S(2)}, u32[]{:S(2)}) collective-permute-start(s32[72,256]{1,0:T(8,128)S(1)} %attention.6), channel_id=1, source_target_pairs={{0,2},{1,3},{2,0},{3,1},{4,6},{5,7},{6,4},{7,5},{8,10},{9,11},{10,... | collective-permute-start | bytes 221192 | tf_op jit(solution)/shard_map/ppermute | solution.py:28
  33.3 1.8 %attention.7.refs_0_ = f32[136,256]{1,0:T(8,128)S(1)} custom-call(bf16[768,128]{1,0:T(8,128)(2,1)S(1)} %collective-permute-done.6.q_ref.other_ref, bf16[4096,128]{1,0:T(8,128)(2,1)S(1)} %get-tuple-element.54.k_ref, bf16[144,4096]{1,0:T(8,128)(2,1)S(1)} %turn.1.vt_ref), custom_call_target="tpu_custom_call" | custom-call | flops 1000000 | bytes 100000 | tf_op jit(solution)/shard_map/attention/pallas_call | solution.py:32
  35.0 1.5 %attend.1 = (bf16[512,1024]{1,0:T(8,128)(2,1)S(1)}, bf16[512,1024]{1,0:T(8,128)(2,1)S(1)}) custom-call(s32[1]{0:T(128)} %bitcast.shard_ref, bf16[384,128]{1,0:T(8,128)(2,1)S(1)} %total.3.q_ref.a_ref.near_ref, bf16[384,128]{1,0:T(8,128)(2,1)S(1)} %collective-permute-done.5.b_ref.q_ref.far_ref, bf16[768,128]{1,0:T(8,128)(2,1)S(1)} %collective-permute-done.6.q_ref.other_ref), custom_call_target="tpu_custom_call" | custom-call | flops 1000000 | bytes 100000 | tf_op jit(solution)/shard_map/attend/pallas_call | solution.py:32
  36.6 1.2 %collective-permute-done.8.refs_2_ = s32[72,256]{1,0:T(8,128)S(1)} collective-permute-done((s32[72,256]{1,0:T(8,128)S(1)}, s32[72,256]{1,0:T(8,128)S(1)}, u32[]{:S(2)}, u32[]{:S(2)}) %collective-permute-start.8) | collective-permute-done | bytes 73760 | tf_op jit(solution)/shard_map/ppermute | solution.py:28
  37.8 0.2 merge.3.refs_0_
  38.0 0.6 collective-permute-start.10
  38.5 2.0 %gram.1.h_ref = f32[512,512]{1,0:T(8,128)S(1)} custom-call(bf16[512,1024]{1,0:T(8,128)(2,1)S(1)} %get-tuple-element.63.high_ref, bf16[512,1024]{1,0:T(8,128)(2,1)S(1)} %get-tuple-element.64.low_ref), custom_call_target="tpu_custom_call" | custom-call | flops 4000000000 | bytes 100000 | tf_op jit(solution)/shard_map/gram/pallas_call | solution.py:32
  40.5 1.7 %invert.1.inverse_ref = f32[64,64]{1,0:T(8,128)S(1)} custom-call(f32[512,512]{1,0:T(8,128)S(1)} %gram.1.h_ref), custom_call_target="tpu_custom_call" | custom-call | flops 1000000000 | bytes 100000 | tf_op jit(solution)/shard_map/invert/pallas_call | solution.py:32
  42.3 0.1 collective-permute-done.10.refs_1_
  42.4 0.1 merge.4.refs_0_
  42.5 2.5 %collective-permute-start.11 = (s32[72,256]{1,0:T(8,128)S(1)}, s32[72,256]{1,0:T(8,128)S(1)}, u32[]{:S(2)}, u32[]{:S(2)}) collective-permute-start(s32[72,256]{1,0:T(8,128)S(1)} %merge.4.refs_0_), channel_id=1, source_target_pairs={{0,8},{1,9},{2,10},{3,11},{4,12},{5,13},{6,14},{7,15},{8,0},{9,1},... | collective-permute-start | bytes 221192 | tf_op jit(solution)/shard_map/ppermute | solution.py:28
  45.0 2.0 %sweep.8 = (f32[512,512]{1,0:T(8,128)S(1)}, f32[64,64]{1,0:T(8,128)S(1)}) custom-call(f32[512,512]{1,0:T(8,128)S(1)} %gram.1.h_ref, f32[64,64]{1,0:T(8,128)S(1)} %invert.1.inverse_ref), custom_call_target="tpu_custom_call" | custom-call | flops 2000000000 | bytes 100000 | tf_op jit(solution)/shard_map/sweep/pallas_call | solution.py:32
  47.0 1.9 %sweep.9 = (f32[512,512]{1,0:T(8,128)S(1)}, f32[64,64]{1,0:T(8,128)S(1)}) custom-call(f32[512,512]{1,0:T(8,128)S(1)} %get-tuple-element.70.h_ref, f32[64,64]{1,0:T(8,128)S(1)} %get-tuple-element.71.inverse_ref), custom_call_target="tpu_custom_call" | custom-call | flops 2000000000 | bytes 100000 | tf_op jit(solution)/shard_map/sweep/pallas_call | solution.py:32
  48.9 2.0 %sweep.10 = (f32[512,512]{1,0:T(8,128)S(1)}, f32[64,64]{1,0:T(8,128)S(1)}) custom-call(f32[512,512]{1,0:T(8,128)S(1)} %get-tuple-element.72.h_ref, f32[64,64]{1,0:T(8,128)S(1)} %get-tuple-element.73.inverse_ref), custom_call_target="tpu_custom_call" | custom-call | flops 2000000000 | bytes 100000 | tf_op jit(solution)/shard_map/sweep/pallas_call | solution.py:32
  51.0 0.1 merge.5.a_ref
  51.1 0.6 collective-permute-start.12
  51.7 1.9 %sweep.11 = (f32[512,512]{1,0:T(8,128)S(1)}, f32[64,64]{1,0:T(8,128)S(1)}) custom-call(f32[512,512]{1,0:T(8,128)S(1)} %get-tuple-element.77.h_ref, f32[64,64]{1,0:T(8,128)S(1)} %get-tuple-element.78.inverse_ref), custom_call_target="tpu_custom_call" | custom-call | flops 2000000000 | bytes 100000 | tf_op jit(solution)/shard_map/sweep/pallas_call | solution.py:32
  53.6 2.1 %sweep.12 = (f32[512,512]{1,0:T(8,128)S(1)}, f32[64,64]{1,0:T(8,128)S(1)}) custom-call(f32[512,512]{1,0:T(8,128)S(1)} %get-tuple-element.79.h_ref, f32[64,64]{1,0:T(8,128)S(1)} %get-tuple-element.80.inverse_ref), custom_call_target="tpu_custom_call" | custom-call | flops 2000000000 | bytes 100000 | tf_op jit(solution)/shard_map/sweep/pallas_call | solution.py:32
  55.7 0.0 collective-permute-done.12.b_ref
  55.8 0.1 collective-permute-start.13
  55.8 1.9 %sweep.13 = (f32[512,512]{1,0:T(8,128)S(1)}, f32[64,64]{1,0:T(8,128)S(1)}) custom-call(f32[512,512]{1,0:T(8,128)S(1)} %get-tuple-element.84.h_ref, f32[64,64]{1,0:T(8,128)S(1)} %get-tuple-element.85.inverse_ref), custom_call_target="tpu_custom_call" | custom-call | flops 2000000000 | bytes 100000 | tf_op jit(solution)/shard_map/sweep/pallas_call | solution.py:32
  57.8 2.1 %sweep.14 = (f32[512,512]{1,0:T(8,128)S(1)}, f32[64,64]{1,0:T(8,128)S(1)}) custom-call(f32[512,512]{1,0:T(8,128)S(1)} %get-tuple-element.86.h_ref, f32[64,64]{1,0:T(8,128)S(1)} %get-tuple-element.87.inverse_ref), custom_call_target="tpu_custom_call" | custom-call | flops 2000000000 | bytes 100000 | tf_op jit(solution)/shard_map/sweep/pallas_call | solution.py:32
  59.9 0.7 %sweep.15.minus_ref = f32[512,512]{1,0:T(8,128)S(1)} custom-call(f32[512,512]{1,0:T(8,128)S(1)} %get-tuple-element.91.h_ref, f32[64,64]{1,0:T(8,128)S(1)} %get-tuple-element.92.inverse_ref), custom_call_target="tpu_custom_call" | custom-call | flops 2000000000 | bytes 100000 | tf_op jit(solution)/shard_map/sweep/pallas_call | solution.py:32
  60.6 1.9 %fit.1 = (f32[128,512]{1,0:T(8,128)S(1)}, f32[8,128]{1,0:T(8,128)S(1)}) custom-call(s32[1]{0:T(128)} %bitcast.shard_ref, f32[512,512]{1,0:T(8,128)S(1)} %sweep.15.minus_ref, bf16[512,1024]{1,0:T(8,128)(2,1)S(1)} %get-tuple-element.63.high_ref, bf16[512,1024]{1,0:T(8,128)(2,1)S(1)} %get-tuple-element.64.low_ref, s32[144,256]{1,0:T(8,128)S(1)} %stack.3.own_ref, ...), custom_call_target="tpu_custom_call" | custom-call | flops 1000000000 | bytes 100000 | tf_op jit(solution)/shard_map/fit/pallas_call | solution.py:32
  62.6 1.6 %collective-permute-start.14 = (f32[8,128]{1,0:T(8,128)S(1)}, f32[8,128]{1,0:T(8,128)S(1)}, u32[]{:S(2)}, u32[]{:S(2)}) collective-permute-start(f32[8,128]{1,0:T(8,128)S(1)} %get-tuple-element.95.refs_0_), channel_id=1, source_target_pairs={{0,16},{16,0},{1,17},{17,1},{2,18},{18,2},{3,19},{19,3},{4,20},{20... | collective-permute-start | bytes 12296 | tf_op jit(solution)/shard_map/ppermute | solution.py:28
  64.1 0.8 %flip.1 = f32[512,128]{1,0:T(8,128)} custom-call(f32[128,512]{1,0:T(8,128)S(1)} %get-tuple-element.94.x_ref), custom_call_target="tpu_custom_call" | custom-call | flops 1000000 | bytes 100000 | tf_op jit(solution)/shard_map/flip/pallas_call | solution.py:32
  65.0 1.3 %collective-permute-done.14.refs_1_ = f32[8,128]{1,0:T(8,128)S(1)} collective-permute-done((f32[8,128]{1,0:T(8,128)S(1)}, f32[8,128]{1,0:T(8,128)S(1)}, u32[]{:S(2)}, u32[]{:S(2)}) %collective-permute-start.14) | collective-permute-done | bytes 4128 | tf_op jit(solution)/shard_map/ppermute | solution.py:28
  66.2 0.5 mean.1
  (12 shorter events, 0.2 us)
Async XLA Ops:
  0.6 7.3 %copy-start = (bf16[1,4096,128]{2,1,0:T(8,128)(2,1)S(1)}, bf16[1,4096,128]{2,1,0:T(8,128)(2,1)}, u32[]{:S(2)}) copy-start(bf16[1,4096,128]{2,1,0:T(8,128)(2,1)} %param.7) | copy-start | bytes 3145732
  3.4 1.6 %collective-permute-start = (bf16[768,128]{1,0:T(8,128)(2,1)S(1)}, bf16[768,128]{1,0:T(8,128)(2,1)S(1)}, u32[]{:S(2)}, u32[]{:S(2)}) collective-permute-start(bf16[768,128]{1,0:T(8,128)(2,1)S(1)} %get-tuple-element.50), channel_id=1, source_target_pairs={{0,1},{1,0},{2,3},{3,2},{4,5},{5,4},{6,7},{7,6},{8,9},{9,8},{10,11... | collective-permute-start | bytes 589832 | tf_op jit(solution)/shard_map/ppermute | solution.py:28
  5.0 6.0 %collective-permute-start.1 = (bf16[384,128]{1,0:T(8,128)(2,1)S(1)}, bf16[384,128]{1,0:T(8,128)(2,1)S(1)}, u32[]{:S(2)}, u32[]{:S(2)}) collective-permute-start(bf16[384,128]{1,0:T(8,128)(2,1)S(1)} %get-tuple-element.52), channel_id=1, source_target_pairs={{0,2},{1,3},{2,0},{3,1},{4,6},{5,7},{6,4},{7,5},{8,10},{9,11},{10,... | collective-permute-start | bytes 294920 | tf_op jit(solution)/shard_map/ppermute | solution.py:28
  11.1 7.6 %collective-permute-start.4 = (bf16[384,128]{1,0:T(8,128)(2,1)S(1)}, bf16[384,128]{1,0:T(8,128)(2,1)S(1)}, u32[]{:S(2)}, u32[]{:S(2)}) collective-permute-start(bf16[384,128]{1,0:T(8,128)(2,1)S(1)} %total.2.refs_0_), channel_id=1, source_target_pairs={{0,12},{1,13},{2,14},{3,15},{4,8},{5,9},{6,10},{7,11},{8,4},{9,5},... | collective-permute-start | bytes 294920 | tf_op jit(solution)/shard_map/ppermute | solution.py:28
  15.0 7.7 %collective-permute-start.3 = (bf16[384,128]{1,0:T(8,128)(2,1)S(1)}, bf16[384,128]{1,0:T(8,128)(2,1)S(1)}, u32[]{:S(2)}, u32[]{:S(2)}) collective-permute-start(bf16[384,128]{1,0:T(8,128)(2,1)S(1)} %total.2.refs_0_), channel_id=1, source_target_pairs={{0,8},{1,9},{2,10},{3,11},{4,12},{5,13},{6,14},{7,15},{8,0},{9,1},... | collective-permute-start | bytes 294920 | tf_op jit(solution)/shard_map/ppermute | solution.py:28
  15.0 7.7 %collective-permute-start.2 = (bf16[384,128]{1,0:T(8,128)(2,1)S(1)}, bf16[384,128]{1,0:T(8,128)(2,1)S(1)}, u32[]{:S(2)}, u32[]{:S(2)}) collective-permute-start(bf16[384,128]{1,0:T(8,128)(2,1)S(1)} %total.2.refs_0_), channel_id=1, source_target_pairs={{0,4},{1,5},{2,6},{3,7},{4,0},{5,1},{6,2},{7,3},{8,12},{9,13},{10,... | collective-permute-start | bytes 294920 | tf_op jit(solution)/shard_map/ppermute | solution.py:28
  22.7 4.7 %collective-permute-start.5 = (bf16[384,128]{1,0:T(8,128)(2,1)S(1)}, bf16[384,128]{1,0:T(8,128)(2,1)S(1)}, u32[]{:S(2)}, u32[]{:S(2)}) collective-permute-start(bf16[384,128]{1,0:T(8,128)(2,1)S(1)} %total.3.q_ref.a_ref.near_ref), channel_id=1, source_target_pairs={{0,2},{1,3},{2,0},{3,1},{4,6},{5,7},{6,4},{7,5},{8,10},{9,11},{10,... | collective-permute-start | bytes 294920 | tf_op jit(solution)/shard_map/ppermute | solution.py:28
  27.4 2.4 %collective-permute-start.6 = (bf16[768,128]{1,0:T(8,128)(2,1)S(1)}, bf16[768,128]{1,0:T(8,128)(2,1)S(1)}, u32[]{:S(2)}, u32[]{:S(2)}) collective-permute-start(bf16[768,128]{1,0:T(8,128)(2,1)S(1)} %stack.2), channel_id=1, source_target_pairs={{0,1},{1,0},{2,3},{3,2},{4,5},{5,4},{6,7},{7,6},{8,9},{9,8},{10,11... | collective-permute-start | bytes 589832 | tf_op jit(solution)/shard_map/ppermute | solution.py:28
  27.5 9.0 %collective-permute-start.7 = (s32[72,256]{1,0:T(8,128)S(1)}, s32[72,256]{1,0:T(8,128)S(1)}, u32[]{:S(2)}, u32[]{:S(2)}) collective-permute-start(s32[72,256]{1,0:T(8,128)S(1)} %attention.4), channel_id=1, source_target_pairs={{0,1},{1,0},{2,3},{3,2},{4,5},{5,4},{6,7},{7,6},{8,9},{9,8},{10,11... | collective-permute-start | bytes 221192 | tf_op jit(solution)/shard_map/ppermute | solution.py:28
  31.7 4.9 %collective-permute-start.9 = (s32[72,256]{1,0:T(8,128)S(1)}, s32[72,256]{1,0:T(8,128)S(1)}, u32[]{:S(2)}, u32[]{:S(2)}) collective-permute-start(s32[72,256]{1,0:T(8,128)S(1)} %attention.6), channel_id=1, source_target_pairs={{0,2},{1,3},{2,0},{3,1},{4,6},{5,7},{6,4},{7,5},{8,10},{9,11},{10,... | collective-permute-start | bytes 221192 | tf_op jit(solution)/shard_map/ppermute | solution.py:28
  33.3 4.5 %collective-permute-start.8 = (s32[72,256]{1,0:T(8,128)S(1)}, s32[72,256]{1,0:T(8,128)S(1)}, u32[]{:S(2)}, u32[]{:S(2)}) collective-permute-start(s32[72,256]{1,0:T(8,128)S(1)} %attention.5), channel_id=1, source_target_pairs={{0,3},{1,2},{2,1},{3,0},{4,7},{5,6},{6,5},{7,4},{8,11},{9,10},{10,... | collective-permute-start | bytes 221192 | tf_op jit(solution)/shard_map/ppermute | solution.py:28
  38.0 4.4 %collective-permute-start.10 = (s32[72,256]{1,0:T(8,128)S(1)}, s32[72,256]{1,0:T(8,128)S(1)}, u32[]{:S(2)}, u32[]{:S(2)}) collective-permute-start(s32[72,256]{1,0:T(8,128)S(1)} %merge.3.refs_0_), channel_id=1, source_target_pairs={{0,4},{1,5},{2,6},{3,7},{4,0},{5,1},{6,2},{7,3},{8,12},{9,13},{10,... | collective-permute-start | bytes 221192 | tf_op jit(solution)/shard_map/ppermute | solution.py:28
  42.5 8.5 %collective-permute-start.11 = (s32[72,256]{1,0:T(8,128)S(1)}, s32[72,256]{1,0:T(8,128)S(1)}, u32[]{:S(2)}, u32[]{:S(2)}) collective-permute-start(s32[72,256]{1,0:T(8,128)S(1)} %merge.4.refs_0_), channel_id=1, source_target_pairs={{0,8},{1,9},{2,10},{3,11},{4,12},{5,13},{6,14},{7,15},{8,0},{9,1},... | collective-permute-start | bytes 221192 | tf_op jit(solution)/shard_map/ppermute | solution.py:28
  51.1 4.7 %collective-permute-start.12 = (s32[72,256]{1,0:T(8,128)S(1)}, s32[72,256]{1,0:T(8,128)S(1)}, u32[]{:S(2)}, u32[]{:S(2)}) collective-permute-start(s32[72,256]{1,0:T(8,128)S(1)} %merge.5.a_ref), channel_id=1, source_target_pairs={{0,2},{1,3},{2,0},{3,1},{4,6},{5,7},{6,4},{7,5},{8,10},{9,11},{10,... | collective-permute-start | bytes 221192 | tf_op jit(solution)/shard_map/ppermute | solution.py:28
  55.8 4.1 %collective-permute-start.13 = (s32[144,256]{1,0:T(8,128)S(1)}, s32[144,256]{1,0:T(8,128)S(1)}, u32[]{:S(2)}, u32[]{:S(2)}) collective-permute-start(s32[144,256]{1,0:T(8,128)S(1)} %stack.3.own_ref), channel_id=1, source_target_pairs={{0,1},{1,0},{2,3},{3,2},{4,5},{5,4},{6,7},{7,6},{8,9},{9,8},{10,11... | collective-permute-start | bytes 442376 | tf_op jit(solution)/shard_map/ppermute | solution.py:28
  62.6 3.7 %collective-permute-start.14 = (f32[8,128]{1,0:T(8,128)S(1)}, f32[8,128]{1,0:T(8,128)S(1)}, u32[]{:S(2)}, u32[]{:S(2)}) collective-permute-start(f32[8,128]{1,0:T(8,128)S(1)} %get-tuple-element.95.refs_0_), channel_id=1, source_target_pairs={{0,16},{16,0},{1,17},{17,1},{2,18},{18,2},{3,19},{19,3},{4,20},{20... | collective-permute-start | bytes 12296 | tf_op jit(solution)/shard_map/ppermute | solution.py:28

commit v13 on v12

--- a/solution.py
+++ b/solution.py
@@ -293,7 +293,7 @@
     return both, *came
 
 
-def attend_kernel(score_scale, shard_ref, near_ref, far_ref, other_ref, high_ref, low_ref, c_all):
+def attend_kernel(score_scale, shard_ref, near_ref, far_ref, other_ref, high_ref, low_ref, square_ref, c_all):
     part, rows = c_all.shape[0] // 4, high_ref.shape[1] // 4
     tall = part + rows
     pieces = [(near_ref, 0), (other_ref, 0), (far_ref, 0), (other_ref, tall)]
@@ -305,16 +305,29 @@
         weights = jnp.exp(scores - jnp.max(scores, axis=0, keepdims=True))
         weights = weights * (1.0 / jnp.sum(weights, axis=0, keepdims=True))
         high_ref[:, aligned(place, rows)], low_ref[:, aligned(place, rows)] = halves(weights)
-
-
-def gram_kernel(high_ref, low_ref, h_ref):
-    high, low = high_ref[...], low_ref[...]
-    cross = dot(high, low, NT)
-    gram = dot(high, high, NT) + (dot(low, low, NT) + (cross + cross.T))
-    kept = gram.shape[0]
-    diagonal = lax.broadcasted_iota(jnp.int32, gram.shape, 0) == lax.broadcasted_iota(jnp.int32, gram.shape, 1)
-    trace = jnp.sum(jnp.where(diagonal, gram, 0.0))
-    h_ref[...] = gram + jnp.where(diagonal, RIDGE_SHARE * trace / kept, 0.0)
+        square_ref[aligned(place, SUB), :] = jnp.sum((weights * weights).reshape(-1, SUB, rows), axis=0)
+
+
+def gram_kernel(high_ref, low_ref, square_ref, h_ref, inverse_ref):
+    kept = high_ref.shape[0]
+    ridge = RIDGE_SHARE * jnp.sum(square_ref[...]) / kept
+    row = lax.broadcasted_iota(jnp.int32, (128, kept), 0)
+    column = lax.broadcasted_iota(jnp.int32, (128, kept), 1)
+
+    def system(start, rows, columns):
+        at = slice(start, start + rows)
+        left = jnp.concatenate([high_ref[at, :], low_ref[at, :]], axis=0)
+        by_high, by_low = dot(left, high_ref[:columns, :], NT), dot(left, low_ref[:columns, :], NT)
+        gram = by_high[:rows] + (by_high[rows:] + by_low[:rows] + by_low[rows:])
+        return gram + jnp.where(row[:rows, :columns] + start == column[:rows, :columns], ridge, 0.0)
+
+    def piece(start):
+        def fill():
+            h_ref[start : start + 128, :] = system(start, 128, kept)
+
+        return fill
+
+    inverse_ref[...] = inverse_beside(system(0, PANEL, PANEL), [piece(i) for i in range(0, kept, 128)])
 
 
 def invert_block(rows):
@@ -324,35 +337,43 @@
     sub = lax.broadcasted_iota(jnp.int32, (SUB, size), 0)
     spread_lane = lambda array, column: jnp.broadcast_to(array[:, column : column + 1], (SUB, size))
     line = lambda array, row: jnp.broadcast_to(array[row : row + 1, :], (SUB, size))
+    def less(old, left, right):
+        terms = [x * y for x, y in zip(left, right)]
+        while len(terms) > 1:
+            terms = [x + y for x, y in zip(terms[::2], terms[1::2])]
+        return old - terms[0]
+
+    ahead = []
     for k in range(count):
         base = k * SUB
         inside = (lane >= base) & (lane < base + SUB)
-        columns = [spread_lane(rows[k], base + j) for j in range(SUB)]
+        columns = ahead + [spread_lane(rows[k], base + j) for j in range(len(ahead), SUB)]
         work = jnp.where(inside, jnp.where(lane - base == sub, 1.0, 0.0), rows[k])
+        beyond = [spread_lane(rows[k], base + SUB + j) for j in range(2)] if k + 1 < count else []
+        full = columns + [work] + beyond
+        bare = list(full)
         for j in range(0, SUB, 2):
-            first, second = columns[j], columns[j + 1]
-            a, b, c, d = line(first, j), line(second, j), line(first, j + 1), line(second, j + 1)
+            first, second = full[j], full[j + 1]
+            a, b, c, d = line(bare[j], j), line(bare[j + 1], j), line(bare[j], j + 1), line(bare[j + 1], j + 1)
             inverse = 1.0 / (a * d - b * c)
-            at_first, at_second = sub == j, sub == j + 1
-
-            def step(v):
-                upper, lower = line(v, j), line(v, j + 1)
+            for i in range(j + 2, len(full)):
+                upper, lower = line(bare[i], j), line(bare[i], j + 1)
                 new_upper = (d * upper - b * lower) * inverse
                 new_lower = (a * lower - c * upper) * inverse
-                other = v - (first * new_upper + second * new_lower)
-                return jnp.where(at_first, new_upper, jnp.where(at_second, new_lower, other))
-
-            for i in range(j + 2, SUB):
-                columns[i] = step(columns[i])
-            work = step(work)
+                bare[i] = full[i] - (first * new_upper + second * new_lower)
+                full[i] = jnp.where(sub == j, new_upper, jnp.where(sub == j + 1, new_lower, bare[i]))
+        work, beyond = full[SUB], full[SUB + 1 :]
         lines = [line(work, j) for j in range(SUB)]
         updated = list(rows)
         updated[k] = work
         for i in list(range(k + 1, count)) + list(range(k)):
-            terms = [spread_lane(rows[i], base + j) * lines[j] for j in range(SUB)]
-            while len(terms) > 1:
-                terms = [x + y for x, y in zip(terms[::2], terms[1::2])]
-            updated[i] = jnp.where(inside, 0.0, rows[i]) - terms[0]
+            factors = [spread_lane(rows[i], base + j) for j in range(SUB)]
+            if i == k + 1:
+                ahead = [
+                    less(spread_lane(rows[i], base + SUB + j), factors, [line(array, m) for m in range(SUB)])
+                    for j, array in enumerate(beyond)
+                ]
+            updated[i] = less(jnp.where(inside, 0.0, rows[i]), factors, lines)
         rows = updated
         yield
     return jnp.concatenate(rows, axis=0)
@@ -370,10 +391,6 @@
             return stop.value
         if work:
             work.pop(0)()
-
-
-def invert_kernel(h_ref, out_ref):
-    out_ref[...] = inverse_beside(h_ref[:PANEL, :PANEL])
 
 
 def sweep_kernel(panel, h_ref, inverse_ref, out_ref, *next_ref):
@@ -469,17 +486,15 @@
     attend = call(
         functools.partial(attend_kernel, score_scale),
         (shard, near, far, other),
-        [((count, rows), BF16)] * 2,
+        [((count, rows), BF16)] * 2 + [((4 * SUB, lanes), F32)],
         10**6,
         scratch=[pltpu.VMEM((count, dims), BF16)],
         name="attend",
     )
     attend = beside(attend)
-    (system,) = call(gram_kernel, attend, [system_shape], 4 * 10**9, name="gram")
     panels = count // PANEL
     block_shape = ((PANEL, PANEL), F32)
-    (inverse,) = call(invert_kernel, (system,), [block_shape], 10**9, name="invert")
-    system, inverse = beside((system, inverse))
+    system, inverse = call(gram_kernel, attend, [system_shape, block_shape], 4 * 10**9, name="gram")
     for panel in range(panels):
         last = panel == panels - 1
         system, *inverse = call(
@@ -490,14 +505,14 @@
             name="sweep",
         )
         inverse = None if last else inverse[0]
-        if panel in (2, 4, 6):
+        if panel in (0, 2, 4, 6):
             system, inverse = beside((system, inverse))
     while ends is None:
         system = beside(system)
 
     turned_fit, error = call(
         fit_kernel,
-        (shard, system, *attend, *ends),
+        (shard, system, *attend[:2], *ends),
         [((dims, count), F32), ((SUB, 128), F32)],
         10**9,
         scratch=[pltpu.VMEM((dims, rows), F32)],

time: 66.9 us -> 66.6 us (level)
    pallas_call x28 -> x27, Pallas kernels: 33.2 us -> 32.7 us  [call(): pl.pallas_call(kernel, in_specs=specs or [SMEM if x.size == 1 else VMEM f...]
where the time goes in v13:
time: 66.6 us; the launch traced here: 66.5 us
  Pallas kernels  32.7 us (49%)
  starting transfers between devices  17.6 us (26%)
  waiting for transfers between devices  14.6 us (22%)
  between operations  1.6 us (2%)
    pallas_call x27, Pallas kernels, call(): pl.pallas_call(kernel, in_specs=specs or [SMEM if x.size == 1 else VMEM f...  32.7 us
    ppermute x15, starting transfers between devices, swap(): return lax.ppermute(array, axis, [(i, i ^ step) for i in range(size)])  17.6 us
    ppermute x15, waiting for transfers between devices, swap(): return lax.ppermute(array, axis, [(i, i ^ step) for i in range(size)])  14.6 us
  transfers between devices with their start and end apart: 15, of which 8 were waited for; matrix products, arithmetic and copies ran while one was open for 0% of the time, Pallas kernels for 41%

profile of v13, /device:TPU:0, one launch (start us, length us, event | category | flops | bytes accessed | tf_op | source)
XLA Modules:
  0.0 66.5 jit_solution(9230872054942736017)
XLA Ops:
  1.4 2.0 %prepare.1 = (bf16[768,128]{1,0:T(8,128)(2,1)S(1)}, bf16[768,128]{1,0:T(8,128)(2,1)S(1)}, bf16[4096,128]{1,0:T(8,128)(2,1)S(1)}) custom-call(s32[1]{0:T(128)} %bitcast.shard_ref, s32[1]{0:T(128)S(6)} %copy.7.root_ref, bf16[1024,128]{1,0:T(8,128)(2,1)} %bitcast.9, s32[1,512]{1,0:T(1,128)} %kept_hbm.1, bf16[4096,128]{1,0:T(8,128)(2,1)} %bitcast.7), custom_call_target="tpu_custom_call" | custom-call | flops 100000 | bytes 100000 | tf_op jit(solution)/shard_map/prepare/pallas_call | solution.py:32
  3.4 0.5 collective-permute-start
  3.9 1.1 %collective-permute-done.b_ref = bf16[768,128]{1,0:T(8,128)(2,1)S(1)} collective-permute-done((bf16[768,128]{1,0:T(8,128)(2,1)S(1)}, bf16[768,128]{1,0:T(8,128)(2,1)S(1)}, u32[]{:S(2)}, u32[]{:S(2)}) %collective-permute-start) | collective-permute-done | bytes 196640 | tf_op jit(solution)/shard_map/ppermute | solution.py:28
  5.0 3.0 %collective-permute-start.1 = (bf16[384,128]{1,0:T(8,128)(2,1)S(1)}, bf16[384,128]{1,0:T(8,128)(2,1)S(1)}, u32[]{:S(2)}, u32[]{:S(2)}) collective-permute-start(bf16[384,128]{1,0:T(8,128)(2,1)S(1)} %get-tuple-element.56), channel_id=1, source_target_pairs={{0,2},{1,3},{2,0},{3,1},{4,6},{5,7},{6,4},{7,5},{8,10},{9,11},{10,... | collective-permute-start | bytes 294920 | tf_op jit(solution)/shard_map/ppermute | solution.py:28
  7.9 0.3 turn.1.vt_ref
  8.3 2.8 %collective-permute-done.1.refs_1_ = bf16[384,128]{1,0:T(8,128)(2,1)S(1)} collective-permute-done((bf16[384,128]{1,0:T(8,128)(2,1)S(1)}, bf16[384,128]{1,0:T(8,128)(2,1)S(1)}, u32[]{:S(2)}, u32[]{:S(2)}) %collective-permute-start.1) | collective-permute-done | bytes 98336 | tf_op jit(solution)/shard_map/ppermute | solution.py:28
  11.1 3.9 %collective-permute-start.4 = (bf16[384,128]{1,0:T(8,128)(2,1)S(1)}, bf16[384,128]{1,0:T(8,128)(2,1)S(1)}, u32[]{:S(2)}, u32[]{:S(2)}) collective-permute-start(bf16[384,128]{1,0:T(8,128)(2,1)S(1)} %total.2.refs_0_), channel_id=1, source_target_pairs={{0,12},{1,13},{2,14},{3,15},{4,8},{5,9},{6,10},{7,11},{8,4},{9,5},... | collective-permute-start | bytes 294920 | tf_op jit(solution)/shard_map/ppermute | solution.py:28
  15.0 0.0 collective-permute-start.3
  15.0 0.6 collective-permute-start.2
  15.6 3.1 %collective-permute-done.4.refs_3_ = bf16[384,128]{1,0:T(8,128)(2,1)S(1)} collective-permute-done((bf16[384,128]{1,0:T(8,128)(2,1)S(1)}, bf16[384,128]{1,0:T(8,128)(2,1)S(1)}, u32[]{:S(2)}, u32[]{:S(2)}) %collective-permute-start.4) | collective-permute-done | bytes 98336 | tf_op jit(solution)/shard_map/ppermute | solution.py:28
  18.7 4.0 %collective-permute-done.3.refs_2_ = bf16[384,128]{1,0:T(8,128)(2,1)S(1)} collective-permute-done((bf16[384,128]{1,0:T(8,128)(2,1)S(1)}, bf16[384,128]{1,0:T(8,128)(2,1)S(1)}, u32[]{:S(2)}, u32[]{:S(2)}) %collective-permute-start.3) | collective-permute-done | bytes 98336 | tf_op jit(solution)/shard_map/ppermute | solution.py:28
  22.7 0.0 collective-permute-done.2.refs_1_
  22.7 1.6 %collective-permute-start.5 = (bf16[384,128]{1,0:T(8,128)(2,1)S(1)}, bf16[384,128]{1,0:T(8,128)(2,1)S(1)}, u32[]{:S(2)}, u32[]{:S(2)}) collective-permute-start(bf16[384,128]{1,0:T(8,128)(2,1)S(1)} %total.3.q_ref.a_ref.near_ref), channel_id=1, source_target_pairs={{0,2},{1,3},{2,0},{3,1},{4,6},{5,7},{6,4},{7,5},{8,10},{9,11},{10,... | collective-permute-start | bytes 294920 | tf_op jit(solution)/shard_map/ppermute | solution.py:28
  24.3 1.8 %attention.4 = s32[72,256]{1,0:T(8,128)S(1)} custom-call(bf16[384,128]{1,0:T(8,128)(2,1)S(1)} %total.3.q_ref.a_ref.near_ref, bf16[4096,128]{1,0:T(8,128)(2,1)S(1)} %get-tuple-element.58.k_ref, bf16[144,4096]{1,0:T(8,128)(2,1)S(1)} %turn.1.vt_ref), custom_call_target="tpu_custom_call" | custom-call | flops 1000000 | bytes 100000 | tf_op jit(solution)/shard_map/attention/pallas_call | solution.py:32
  26.1 1.3 %collective-permute-done.5.b_ref.q_ref.far_ref = bf16[384,128]{1,0:T(8,128)(2,1)S(1)} collective-permute-done((bf16[384,128]{1,0:T(8,128)(2,1)S(1)}, bf16[384,128]{1,0:T(8,128)(2,1)S(1)}, u32[]{:S(2)}, u32[]{:S(2)}) %collective-permute-start.5) | collective-permute-done | bytes 98336 | tf_op jit(solution)/shard_map/ppermute | solution.py:28
  27.4 0.1 collective-permute-start.6
  27.5 0.5 collective-permute-start.7
  28.0 1.8 %attention.5 = s32[72,256]{1,0:T(8,128)S(1)} custom-call(bf16[384,128]{1,0:T(8,128)(2,1)S(1)} %collective-permute-done.5.b_ref.q_ref.far_ref, bf16[4096,128]{1,0:T(8,128)(2,1)S(1)} %get-tuple-element.58.k_ref, bf16[144,4096]{1,0:T(8,128)(2,1)S(1)} %turn.1.vt_ref), custom_call_target="tpu_custom_call" | custom-call | flops 1000000 | bytes 100000 | tf_op jit(solution)/shard_map/attention/pallas_call | solution.py:32
  29.9 0.0 collective-permute-done.6.q_ref.other_ref
  29.9 1.8 %attention.6 = s32[72,256]{1,0:T(8,128)S(1)} custom-call(bf16[768,128]{1,0:T(8,128)(2,1)S(1)} %collective-permute-done.6.q_ref.other_ref, bf16[4096,128]{1,0:T(8,128)(2,1)S(1)} %get-tuple-element.58.k_ref, bf16[144,4096]{1,0:T(8,128)(2,1)S(1)} %turn.1.vt_ref), custom_call_target="tpu_custom_call" | custom-call | flops 1000000 | bytes 100000 | tf_op jit(solution)/shard_map/attention/pallas_call | solution.py:32
  31.7 1.6 %collective-permute-start.9 = (s32[72,256]{1,0:T(8,128)S(1)}, s32[72,256]{1,0:T(8,128)S(1)}, u32[]{:S(2)}, u32[]{:S(2)}) collective-permute-start(s32[72,256]{1,0:T(8,128)S(1)} %attention.6), channel_id=1, source_target_pairs={{0,2},{1,3},{2,0},{3,1},{4,6},{5,7},{6,4},{7,5},{8,10},{9,11},{10,... | collective-permute-start | bytes 221192 | tf_op jit(solution)/shard_map/ppermute | solution.py:28
  33.3 0.0 collective-permute-start.8
  33.3 1.8 %attention.7.refs_0_ = f32[136,256]{1,0:T(8,128)S(1)} custom-call(bf16[768,128]{1,0:T(8,128)(2,1)S(1)} %collective-permute-done.6.q_ref.other_ref, bf16[4096,128]{1,0:T(8,128)(2,1)S(1)} %get-tuple-element.58.k_ref, bf16[144,4096]{1,0:T(8,128)(2,1)S(1)} %turn.1.vt_ref), custom_call_target="tpu_custom_call" | custom-call | flops 1000000 | bytes 100000 | tf_op jit(solution)/shard_map/attention/pallas_call | solution.py:32
  35.0 1.8 %attend.1 = (bf16[512,1024]{1,0:T(8,128)(2,1)S(1)}, bf16[512,1024]{1,0:T(8,128)(2,1)S(1)}, f32[32,256]{1,0:T(8,128)S(1)}) custom-call(s32[1]{0:T(128)} %bitcast.shard_ref, bf16[384,128]{1,0:T(8,128)(2,1)S(1)} %total.3.q_ref.a_ref.near_ref, bf16[384,128]{1,0:T(8,128)(2,1)S(1)} %collective-permute-done.5.b_ref.q_ref.far_ref, ...), custom_call_target="tpu_custom_call" | custom-call | flops 1000000 | bytes 100000 | tf_op jit(solution)/shard_map/attend/pallas_call | solution.py:32
  36.8 0.0 collective-permute-done.7.refs_1_
  36.8 1.0 %collective-permute-done.8.refs_2_ = s32[72,256]{1,0:T(8,128)S(1)} collective-permute-done((s32[72,256]{1,0:T(8,128)S(1)}, s32[72,256]{1,0:T(8,128)S(1)}, u32[]{:S(2)}, u32[]{:S(2)}) %collective-permute-start.8) | collective-permute-done | bytes 73760 | tf_op jit(solution)/shard_map/ppermute | solution.py:28
  37.8 0.2 merge.3.refs_0_
  38.0 0.6 collective-permute-start.10
  38.5 3.0 %gram.1 = (f32[512,512]{1,0:T(8,128)S(1)}, f32[64,64]{1,0:T(8,128)S(1)}) custom-call(bf16[512,1024]{1,0:T(8,128)(2,1)S(1)} %get-tuple-element.68.high_ref, bf16[512,1024]{1,0:T(8,128)(2,1)S(1)} %get-tuple-element.69.low_ref, f32[32,256]{1,0:T(8,128)S(1)} %get-tuple-element.70.square_ref), custom_call_target="tpu_custom_call" | custom-call | flops 4000000000 | bytes 100000 | tf_op jit(solution)/shard_map/gram/pallas_call | solution.py:32
  41.5 2.0 %sweep.8 = (f32[512,512]{1,0:T(8,128)S(1)}, f32[64,64]{1,0:T(8,128)S(1)}) custom-call(f32[512,512]{1,0:T(8,128)S(1)} %get-tuple-element.71.h_ref, f32[64,64]{1,0:T(8,128)S(1)} %get-tuple-element.72.inverse_ref), custom_call_target="tpu_custom_call" | custom-call | flops 2000000000 | bytes 100000 | tf_op jit(solution)/shard_map/sweep/pallas_call | solution.py:32
  43.6 0.1 merge.4.refs_0_
  43.7 2.6 %collective-permute-start.11 = (s32[72,256]{1,0:T(8,128)S(1)}, s32[72,256]{1,0:T(8,128)S(1)}, u32[]{:S(2)}, u32[]{:S(2)}) collective-permute-start(s32[72,256]{1,0:T(8,128)S(1)} %merge.4.refs_0_), channel_id=1, source_target_pairs={{0,8},{1,9},{2,10},{3,11},{4,12},{5,13},{6,14},{7,15},{8,0},{9,1},... | collective-permute-start | bytes 221192 | tf_op jit(solution)/shard_map/ppermute | solution.py:28
  46.3 1.9 %sweep.9 = (f32[512,512]{1,0:T(8,128)S(1)}, f32[64,64]{1,0:T(8,128)S(1)}) custom-call(f32[512,512]{1,0:T(8,128)S(1)} %get-tuple-element.78.h_ref, f32[64,64]{1,0:T(8,128)S(1)} %get-tuple-element.79.inverse_ref), custom_call_target="tpu_custom_call" | custom-call | flops 2000000000 | bytes 100000 | tf_op jit(solution)/shard_map/sweep/pallas_call | solution.py:32
  48.2 2.0 %sweep.10 = (f32[512,512]{1,0:T(8,128)S(1)}, f32[64,64]{1,0:T(8,128)S(1)}) custom-call(f32[512,512]{1,0:T(8,128)S(1)} %get-tuple-element.80.h_ref, f32[64,64]{1,0:T(8,128)S(1)} %get-tuple-element.81.inverse_ref), custom_call_target="tpu_custom_call" | custom-call | flops 2000000000 | bytes 100000 | tf_op jit(solution)/shard_map/sweep/pallas_call | solution.py:32
  50.2 0.1 collective-permute-done.11.refs_1_
  50.3 0.1 merge.5.a_ref
  50.5 1.0 %collective-permute-start.12 = (s32[72,256]{1,0:T(8,128)S(1)}, s32[72,256]{1,0:T(8,128)S(1)}, u32[]{:S(2)}, u32[]{:S(2)}) collective-permute-start(s32[72,256]{1,0:T(8,128)S(1)} %merge.5.a_ref), channel_id=1, source_target_pairs={{0,2},{1,3},{2,0},{3,1},{4,6},{5,7},{6,4},{7,5},{8,10},{9,11},{10,... | collective-permute-start | bytes 221192 | tf_op jit(solution)/shard_map/ppermute | solution.py:28
  51.4 1.9 %sweep.11 = (f32[512,512]{1,0:T(8,128)S(1)}, f32[64,64]{1,0:T(8,128)S(1)}) custom-call(f32[512,512]{1,0:T(8,128)S(1)} %get-tuple-element.85.h_ref, f32[64,64]{1,0:T(8,128)S(1)} %get-tuple-element.86.inverse_ref), custom_call_target="tpu_custom_call" | custom-call | flops 2000000000 | bytes 100000 | tf_op jit(solution)/shard_map/sweep/pallas_call | solution.py:32
  53.3 2.1 %sweep.12 = (f32[512,512]{1,0:T(8,128)S(1)}, f32[64,64]{1,0:T(8,128)S(1)}) custom-call(f32[512,512]{1,0:T(8,128)S(1)} %get-tuple-element.87.h_ref, f32[64,64]{1,0:T(8,128)S(1)} %get-tuple-element.88.inverse_ref), custom_call_target="tpu_custom_call" | custom-call | flops 2000000000 | bytes 100000 | tf_op jit(solution)/shard_map/sweep/pallas_call | solution.py:32
  55.5 0.1 collective-permute-start.13
  55.6 1.9 %sweep.13 = (f32[512,512]{1,0:T(8,128)S(1)}, f32[64,64]{1,0:T(8,128)S(1)}) custom-call(f32[512,512]{1,0:T(8,128)S(1)} %get-tuple-element.92.h_ref, f32[64,64]{1,0:T(8,128)S(1)} %get-tuple-element.93.inverse_ref), custom_call_target="tpu_custom_call" | custom-call | flops 2000000000 | bytes 100000 | tf_op jit(solution)/shard_map/sweep/pallas_call | solution.py:32
  57.5 2.1 %sweep.14 = (f32[512,512]{1,0:T(8,128)S(1)}, f32[64,64]{1,0:T(8,128)S(1)}) custom-call(f32[512,512]{1,0:T(8,128)S(1)} %get-tuple-element.94.h_ref, f32[64,64]{1,0:T(8,128)S(1)} %get-tuple-element.95.inverse_ref), custom_call_target="tpu_custom_call" | custom-call | flops 2000000000 | bytes 100000 | tf_op jit(solution)/shard_map/sweep/pallas_call | solution.py:32
  59.6 0.7 %sweep.15.minus_ref = f32[512,512]{1,0:T(8,128)S(1)} custom-call(f32[512,512]{1,0:T(8,128)S(1)} %get-tuple-element.99.h_ref, f32[64,64]{1,0:T(8,128)S(1)} %get-tuple-element.100.inverse_ref), custom_call_target="tpu_custom_call" | custom-call | flops 2000000000 | bytes 100000 | tf_op jit(solution)/shard_map/sweep/pallas_call | solution.py:32
  60.4 1.9 %fit.1 = (f32[128,512]{1,0:T(8,128)S(1)}, f32[8,128]{1,0:T(8,128)S(1)}) custom-call(s32[1]{0:T(128)} %bitcast.shard_ref, f32[512,512]{1,0:T(8,128)S(1)} %sweep.15.minus_ref, bf16[512,1024]{1,0:T(8,128)(2,1)S(1)} %get-tuple-element.68.high_ref, bf16[512,1024]{1,0:T(8,128)(2,1)S(1)} %get-tuple-element.69.low_ref, s32[144,256]{1,0:T(8,128)S(1)} %stack.3.own_ref, ...), custom_call_target="tpu_custom_call" | custom-call | flops 1000000000 | bytes 100000 | tf_op jit(solution)/shard_map/fit/pallas_call | solution.py:32
  62.3 1.6 %collective-permute-start.14 = (f32[8,128]{1,0:T(8,128)S(1)}, f32[8,128]{1,0:T(8,128)S(1)}, u32[]{:S(2)}, u32[]{:S(2)}) collective-permute-start(f32[8,128]{1,0:T(8,128)S(1)} %get-tuple-element.103.refs_0_), channel_id=1, source_target_pairs={{0,16},{16,0},{1,17},{17,1},{2,18},{18,2},{3,19},{19,3},{4,20},{20... | collective-permute-start | bytes 12296 | tf_op jit(solution)/shard_map/ppermute | solution.py:28
  63.8 0.8 %flip.1 = f32[512,128]{1,0:T(8,128)} custom-call(f32[128,512]{1,0:T(8,128)S(1)} %get-tuple-element.102.x_ref), custom_call_target="tpu_custom_call" | custom-call | flops 1000000 | bytes 100000 | tf_op jit(solution)/shard_map/flip/pallas_call | solution.py:32
  64.7 1.3 %collective-permute-done.14.refs_1_ = f32[8,128]{1,0:T(8,128)S(1)} collective-permute-done((f32[8,128]{1,0:T(8,128)S(1)}, f32[8,128]{1,0:T(8,128)S(1)}, u32[]{:S(2)}, u32[]{:S(2)}) %collective-permute-start.14) | collective-permute-done | bytes 4128 | tf_op jit(solution)/shard_map/ppermute | solution.py:28
  65.9 0.5 mean.1
  (11 shorter events, 0.2 us)
Async XLA Ops:
  0.6 7.3 %copy-start = (bf16[1,4096,128]{2,1,0:T(8,128)(2,1)S(1)}, bf16[1,4096,128]{2,1,0:T(8,128)(2,1)}, u32[]{:S(2)}) copy-start(bf16[1,4096,128]{2,1,0:T(8,128)(2,1)} %param.7) | copy-start | bytes 3145732
  3.4 1.6 %collective-permute-start = (bf16[768,128]{1,0:T(8,128)(2,1)S(1)}, bf16[768,128]{1,0:T(8,128)(2,1)S(1)}, u32[]{:S(2)}, u32[]{:S(2)}) collective-permute-start(bf16[768,128]{1,0:T(8,128)(2,1)S(1)} %get-tuple-element.54), channel_id=1, source_target_pairs={{0,1},{1,0},{2,3},{3,2},{4,5},{5,4},{6,7},{7,6},{8,9},{9,8},{10,11... | collective-permute-start | bytes 589832 | tf_op jit(solution)/shard_map/ppermute | solution.py:28
  5.0 6.1 %collective-permute-start.1 = (bf16[384,128]{1,0:T(8,128)(2,1)S(1)}, bf16[384,128]{1,0:T(8,128)(2,1)S(1)}, u32[]{:S(2)}, u32[]{:S(2)}) collective-permute-start(bf16[384,128]{1,0:T(8,128)(2,1)S(1)} %get-tuple-element.56), channel_id=1, source_target_pairs={{0,2},{1,3},{2,0},{3,1},{4,6},{5,7},{6,4},{7,5},{8,10},{9,11},{10,... | collective-permute-start | bytes 294920 | tf_op jit(solution)/shard_map/ppermute | solution.py:28
  11.1 7.6 %collective-permute-start.4 = (bf16[384,128]{1,0:T(8,128)(2,1)S(1)}, bf16[384,128]{1,0:T(8,128)(2,1)S(1)}, u32[]{:S(2)}, u32[]{:S(2)}) collective-permute-start(bf16[384,128]{1,0:T(8,128)(2,1)S(1)} %total.2.refs_0_), channel_id=1, source_target_pairs={{0,12},{1,13},{2,14},{3,15},{4,8},{5,9},{6,10},{7,11},{8,4},{9,5},... | collective-permute-start | bytes 294920 | tf_op jit(solution)/shard_map/ppermute | solution.py:28
  15.0 7.7 %collective-permute-start.3 = (bf16[384,128]{1,0:T(8,128)(2,1)S(1)}, bf16[384,128]{1,0:T(8,128)(2,1)S(1)}, u32[]{:S(2)}, u32[]{:S(2)}) collective-permute-start(bf16[384,128]{1,0:T(8,128)(2,1)S(1)} %total.2.refs_0_), channel_id=1, source_target_pairs={{0,8},{1,9},{2,10},{3,11},{4,12},{5,13},{6,14},{7,15},{8,0},{9,1},... | collective-permute-start | bytes 294920 | tf_op jit(solution)/shard_map/ppermute | solution.py:28
  15.0 7.7 %collective-permute-start.2 = (bf16[384,128]{1,0:T(8,128)(2,1)S(1)}, bf16[384,128]{1,0:T(8,128)(2,1)S(1)}, u32[]{:S(2)}, u32[]{:S(2)}) collective-permute-start(bf16[384,128]{1,0:T(8,128)(2,1)S(1)} %total.2.refs_0_), channel_id=1, source_target_pairs={{0,4},{1,5},{2,6},{3,7},{4,0},{5,1},{6,2},{7,3},{8,12},{9,13},{10,... | collective-permute-start | bytes 294920 | tf_op jit(solution)/shard_map/ppermute | solution.py:28
  22.7 4.7 %collective-permute-start.5 = (bf16[384,128]{1,0:T(8,128)(2,1)S(1)}, bf16[384,128]{1,0:T(8,128)(2,1)S(1)}, u32[]{:S(2)}, u32[]{:S(2)}) collective-permute-start(bf16[384,128]{1,0:T(8,128)(2,1)S(1)} %total.3.q_ref.a_ref.near_ref), channel_id=1, source_target_pairs={{0,2},{1,3},{2,0},{3,1},{4,6},{5,7},{6,4},{7,5},{8,10},{9,11},{10,... | collective-permute-start | bytes 294920 | tf_op jit(solution)/shard_map/ppermute | solution.py:28
  27.4 2.4 %collective-permute-start.6 = (bf16[768,128]{1,0:T(8,128)(2,1)S(1)}, bf16[768,128]{1,0:T(8,128)(2,1)S(1)}, u32[]{:S(2)}, u32[]{:S(2)}) collective-permute-start(bf16[768,128]{1,0:T(8,128)(2,1)S(1)} %stack.2), channel_id=1, source_target_pairs={{0,1},{1,0},{2,3},{3,2},{4,5},{5,4},{6,7},{7,6},{8,9},{9,8},{10,11... | collective-permute-start | bytes 589832 | tf_op jit(solution)/shard_map/ppermute | solution.py:28
  27.5 9.3 %collective-permute-start.7 = (s32[72,256]{1,0:T(8,128)S(1)}, s32[72,256]{1,0:T(8,128)S(1)}, u32[]{:S(2)}, u32[]{:S(2)}) collective-permute-start(s32[72,256]{1,0:T(8,128)S(1)} %attention.4), channel_id=1, source_target_pairs={{0,1},{1,0},{2,3},{3,2},{4,5},{5,4},{6,7},{7,6},{8,9},{9,8},{10,11... | collective-permute-start | bytes 221192 | tf_op jit(solution)/shard_map/ppermute | solution.py:28
  31.7 5.1 %collective-permute-start.9 = (s32[72,256]{1,0:T(8,128)S(1)}, s32[72,256]{1,0:T(8,128)S(1)}, u32[]{:S(2)}, u32[]{:S(2)}) collective-permute-start(s32[72,256]{1,0:T(8,128)S(1)} %attention.6), channel_id=1, source_target_pairs={{0,2},{1,3},{2,0},{3,1},{4,6},{5,7},{6,4},{7,5},{8,10},{9,11},{10,... | collective-permute-start | bytes 221192 | tf_op jit(solution)/shard_map/ppermute | solution.py:28
  33.3 4.5 %collective-permute-start.8 = (s32[72,256]{1,0:T(8,128)S(1)}, s32[72,256]{1,0:T(8,128)S(1)}, u32[]{:S(2)}, u32[]{:S(2)}) collective-permute-start(s32[72,256]{1,0:T(8,128)S(1)} %attention.5), channel_id=1, source_target_pairs={{0,3},{1,2},{2,1},{3,0},{4,7},{5,6},{6,5},{7,4},{8,11},{9,10},{10,... | collective-permute-start | bytes 221192 | tf_op jit(solution)/shard_map/ppermute | solution.py:28
  38.0 5.6 %collective-permute-start.10 = (s32[72,256]{1,0:T(8,128)S(1)}, s32[72,256]{1,0:T(8,128)S(1)}, u32[]{:S(2)}, u32[]{:S(2)}) collective-permute-start(s32[72,256]{1,0:T(8,128)S(1)} %merge.3.refs_0_), channel_id=1, source_target_pairs={{0,4},{1,5},{2,6},{3,7},{4,0},{5,1},{6,2},{7,3},{8,12},{9,13},{10,... | collective-permute-start | bytes 221192 | tf_op jit(solution)/shard_map/ppermute | solution.py:28
  43.7 6.7 %collective-permute-start.11 = (s32[72,256]{1,0:T(8,128)S(1)}, s32[72,256]{1,0:T(8,128)S(1)}, u32[]{:S(2)}, u32[]{:S(2)}) collective-permute-start(s32[72,256]{1,0:T(8,128)S(1)} %merge.4.refs_0_), channel_id=1, source_target_pairs={{0,8},{1,9},{2,10},{3,11},{4,12},{5,13},{6,14},{7,15},{8,0},{9,1},... | collective-permute-start | bytes 221192 | tf_op jit(solution)/shard_map/ppermute | solution.py:28
  50.5 5.0 %collective-permute-start.12 = (s32[72,256]{1,0:T(8,128)S(1)}, s32[72,256]{1,0:T(8,128)S(1)}, u32[]{:S(2)}, u32[]{:S(2)}) collective-permute-start(s32[72,256]{1,0:T(8,128)S(1)} %merge.5.a_ref), channel_id=1, source_target_pairs={{0,2},{1,3},{2,0},{3,1},{4,6},{5,7},{6,4},{7,5},{8,10},{9,11},{10,... | collective-permute-start | bytes 221192 | tf_op jit(solution)/shard_map/ppermute | solution.py:28
  55.5 4.1 %collective-permute-start.13 = (s32[144,256]{1,0:T(8,128)S(1)}, s32[144,256]{1,0:T(8,128)S(1)}, u32[]{:S(2)}, u32[]{:S(2)}) collective-permute-start(s32[144,256]{1,0:T(8,128)S(1)} %stack.3.own_ref), channel_id=1, source_target_pairs={{0,1},{1,0},{2,3},{3,2},{4,5},{5,4},{6,7},{7,6},{8,9},{9,8},{10,11... | collective-permute-start | bytes 442376 | tf_op jit(solution)/shard_map/ppermute | solution.py:28
  62.3 3.7 %collective-permute-start.14 = (f32[8,128]{1,0:T(8,128)S(1)}, f32[8,128]{1,0:T(8,128)S(1)}, u32[]{:S(2)}, u32[]{:S(2)}) collective-permute-start(f32[8,128]{1,0:T(8,128)S(1)} %get-tuple-element.103.refs_0_), channel_id=1, source_target_pairs={{0,16},{16,0},{1,17},{17,1},{2,18},{18,2},{3,19},{19,3},{4,20},{20... | collective-permute-start | bytes 12296 | tf_op jit(solution)/shard_map/ppermute | solution.py:28

commit v14 on v13

--- a/solution.py
+++ b/solution.py
@@ -1,4 +1,5 @@
 import functools
+import itertools
 import math
 
 import jax
@@ -212,10 +213,7 @@
     second = attend_to(far, keys, turned)
     other, second = lax.optimization_barrier((other, second))
     came.append(swap(second, "ctx", 3))
-    third = attend_to(other, keys, turned, start=quarter[0])
-    came.append(swap(third, "ctx", 2))
-    other, third = lax.optimization_barrier((other, third))
-    return near, far, other, attend_to(other, keys, turned, packed=False), came
+    return near, far, other, keys, turned, came
 
 
 def turn_kernel(v_ref, vt_ref):
@@ -224,33 +222,34 @@
     vt_ref[dims:, :] = jnp.ones((vt_ref.shape[0] - dims, v_ref.shape[0]), BF16)
 
 
-def attention_kernel(start, block, score_scale, q_ref, k_ref, vt_ref, out_ref):
+def attention_pieces(start, block, score_scale, q_ref, k_ref, vt_ref, out_ref):
     dims = k_ref.shape[1]
+    slab = k_ref.shape[0]
     lanes = out_ref.shape[1]
     factor = score_scale * math.log2(math.e)
-    queries = q_ref[start : start + lanes, :]
-    scores = lambda b: dot(k_ref[b : b + block, :], queries, NT)
-    slab = k_ref.shape[0]
-    ahead = scores(0)
-    for b in range(0, slab, block):
-        s = ahead
+    state = {}
+
+    def scores(b):
+        return dot(k_ref[b : b + block, :], q_ref[start : start + lanes, :], NT)
+
+    def step(b):
+        s = state["ahead"] if b else scores(0)
         if b + block < slab:
-            ahead = scores(b + block)
+            state["ahead"] = scores(b + block)
         top = jnp.max(s, axis=0, keepdims=True)
         e = jnp.exp2((s - top) * factor).astype(BF16)
         out = dot(vt_ref[:, b : b + block], e, NN)
-        top = top * factor
-        total = out[dims : dims + 1, :]
-        out = out[:dims, :]
-        if b:
-            joint = jnp.maximum(old_top, top)
-            old_scale = jnp.exp2(old_top - joint)
-            new_scale = jnp.exp2(top - joint)
-            out = old_out * old_scale + out * new_scale
-            total = old_total * old_scale + total * new_scale
-            top = joint
-        old_out, old_top, old_total = out, top, total
-    put_partial(out_ref, out, top, total)
+        part = out[:dims, :], top * factor, out[dims : dims + 1, :]
+        state["part"] = join(state["part"], part) if b else part
+        if b + block >= slab:
+            put_partial(out_ref, *state["part"])
+
+    return [functools.partial(step, b) for b in range(0, slab, block)]
+
+
+def attention_kernel(start, block, score_scale, *refs):
+    for step in attention_pieces(start, block, score_scale, *refs):
+        step()
 
 
 def attention(lanes, score_scale, piece, keys, turned, start=0, packed=True):
@@ -264,13 +263,16 @@
     )[0]
 
 
-def merged(*refs):
-    parts = [partial_of(ref) for ref in refs]
+def join(*parts):
     top = functools.reduce(jnp.maximum, [part[1] for part in parts])
     scales = [jnp.exp2(part[1] - top) for part in parts]
     total = sum(part[2] * scale for part, scale in zip(parts, scales))
     out = sum(part[0] * scale for part, scale in zip(parts, scales))
     return out, top, total
+
+
+def merged(*refs):
+    return join(*[partial_of(ref) for ref in refs])
 
 
 def merge_kernel(*refs):
@@ -308,7 +310,7 @@
         square_ref[aligned(place, SUB), :] = jnp.sum((weights * weights).reshape(-1, SUB, rows), axis=0)
 
 
-def gram_kernel(high_ref, low_ref, square_ref, h_ref, inverse_ref):
+def gram_kernel(start, block, score_scale, high_ref, low_ref, square_ref, q_ref, k_ref, vt_ref, h_ref, inverse_ref, part_ref):
     kept = high_ref.shape[0]
     ridge = RIDGE_SHARE * jnp.sum(square_ref[...]) / kept
     row = lax.broadcasted_iota(jnp.int32, (128, kept), 0)
@@ -327,7 +329,9 @@
 
         return fill
 
-    inverse_ref[...] = inverse_beside(system(0, PANEL, PANEL), [piece(i) for i in range(0, kept, 128)])
+    steps = attention_pieces(start, block, score_scale, q_ref, k_ref, vt_ref, part_ref)
+    rows_of = [piece(i) for i in range(0, kept, 128)]
+    inverse_ref[...] = inverse_beside(system(0, PANEL, PANEL), alternate(steps, rows_of))
 
 
 def invert_block(rows):
@@ -393,7 +397,11 @@
             work.pop(0)()
 
 
-def sweep_kernel(panel, h_ref, inverse_ref, out_ref, *next_ref):
+def alternate(*lists):
+    return [x for group in itertools.zip_longest(*lists) for x in group if x is not None]
+
+
+def sweep_kernel(panel, h_ref, inverse_ref, out_ref, *next_ref, steps=()):
     size = h_ref.shape[0]
     at = slice(panel * PANEL, (panel + 1) * PANEL)
     wide = slice(panel * PANEL // 128 * 128, panel * PANEL // 128 * 128 + 128)
@@ -420,7 +428,7 @@
 
         return piece
 
-    work = [rows_update(i) for i in range(0, size, 128)]
+    work = alternate(steps, [rows_update(i) for i in range(0, size, 128)])
     if next_ref:
         after = slice(at.stop, at.stop + PANEL)
         block = h_ref[after, after] - product(
@@ -430,6 +438,11 @@
     else:
         for piece in work:
             piece()
+
+
+def first_sweep_kernel(start, block, score_scale, h_ref, inverse_ref, q_ref, k_ref, vt_ref, out_ref, next_ref, part_ref):
+    steps = attention_pieces(start, block, score_scale, q_ref, k_ref, vt_ref, part_ref)
+    sweep_kernel(0, h_ref, inverse_ref, out_ref, next_ref, steps=steps)
 
 
 def fit_kernel(shard_ref, minus_ref, high_ref, low_ref, own_ref, other_ref, x_ref, err_ref, yt):
@@ -467,10 +480,8 @@
     shard = lax.axis_index("ctx").astype(jnp.int32).reshape(1)
 
     attend_to = functools.partial(attention, lanes, score_scale)
-    near, far, other, keep, came = spread(shard, queries[0, 0], kept, keys[0], roots, values[0], attend_to)
-    rounds = target_rounds(keep, came)
-    came = next(rounds)
-    ends = None
+    near, far, other, own_keys, turned, sent = spread(shard, queries[0, 0], kept, keys[0], roots, values[0], attend_to)
+    came = ends = rounds = None
 
     def beside(arrays):
         nonlocal came, ends
@@ -491,11 +502,29 @@
         scratch=[pltpu.VMEM((count, dims), BF16)],
         name="attend",
     )
-    attend = beside(attend)
     panels = count // PANEL
     block_shape = ((PANEL, PANEL), F32)
-    system, inverse = call(gram_kernel, attend, [system_shape, block_shape], 4 * 10**9, name="gram")
-    for panel in range(panels):
+    tall = near.shape[0]
+    quarter = lambda kernel, s: functools.partial(kernel, s // 2 * tall, min(KBLK, slab), score_scale)
+    system, inverse, third = call(
+        quarter(gram_kernel, 3),
+        (*attend, other, own_keys, turned),
+        [system_shape, block_shape, partial_shape(dims, lanes, True)],
+        4 * 10**9,
+        name="gram",
+    )
+    sent.append(swap(third, "ctx", 2))
+    system, inverse, keep = call(
+        quarter(first_sweep_kernel, 1),
+        (system, inverse, other, own_keys, turned),
+        [system_shape, block_shape, partial_shape(dims, lanes, False)],
+        2 * 10**9,
+        name="first_sweep",
+    )
+    rounds = target_rounds(keep, sent)
+    came = next(rounds)
+    system, inverse = beside((system, inverse))
+    for panel in range(1, panels):
         last = panel == panels - 1
         system, *inverse = call(
             functools.partial(sweep_kernel, panel),
@@ -505,7 +534,7 @@
             name="sweep",
         )
         inverse = None if last else inverse[0]
-        if panel in (0, 2, 4, 6):
+        if panel in (1, 3, 5, 6):
             system, inverse = beside((system, inverse))
     while ends is None:
         system = beside(system)

time: 66.6 us -> 66.7 us (level)
  waiting for transfers between devices: 14.6 us -> 17.6 us
  starting transfers between devices: 17.6 us -> 15.9 us
  Pallas kernels: 32.7 us -> 31.4 us
    ppermute x15, waiting for transfers between devices: 14.6 us -> 17.6 us  [swap(): return lax.ppermute(array, axis, [(i, i ^ step) for i in range(size)])]
    ppermute x15, starting transfers between devices: 17.6 us -> 15.9 us  [swap(): return lax.ppermute(array, axis, [(i, i ^ step) for i in range(size)])]
    pallas_call x27 -> x25, Pallas kernels: 32.7 us -> 31.4 us  [call(): pl.pallas_call(kernel, in_specs=specs or [SMEM if x.size == 1 else VMEM f...]
  transfers between devices with their start and end apart: 15 -> 15, of which waited for: 8 -> 9; matrix products, arithmetic and copies ran while one was open for 0% -> 0% of each run, Pallas kernels for 41% -> 39%
where the time goes in v14:
time: 66.7 us; the launch traced here: 66.5 us
  Pallas kernels  31.4 us (47%)
  waiting for transfers between devices  17.6 us (26%)
  starting transfers between devices  15.9 us (24%)
  between operations  1.57 us (2%)
    pallas_call x25, Pallas kernels, call(): pl.pallas_call(kernel, in_specs=specs or [SMEM if x.size == 1 else VMEM f...  31.4 us
    ppermute x15, waiting for transfers between devices, swap(): return lax.ppermute(array, axis, [(i, i ^ step) for i in range(size)])  17.6 us
    ppermute x15, starting transfers between devices, swap(): return lax.ppermute(array, axis, [(i, i ^ step) for i in range(size)])  15.9 us
  transfers between devices with their start and end apart: 15, of which 9 were waited for; matrix products, arithmetic and copies ran while one was open for 0% of the time, Pallas kernels for 39%

profile of v14, /device:TPU:0, one launch (start us, length us, event | category | flops | bytes accessed | tf_op | source)
XLA Modules:
  0.0 66.5 jit_solution(14670422038083157319)
XLA Ops:
  1.4 2.0 %prepare.1 = (bf16[768,128]{1,0:T(8,128)(2,1)S(1)}, bf16[768,128]{1,0:T(8,128)(2,1)S(1)}, bf16[4096,128]{1,0:T(8,128)(2,1)S(1)}) custom-call(s32[1]{0:T(128)} %bitcast.shard_ref, s32[1]{0:T(128)S(6)} %copy.7.root_ref, bf16[1024,128]{1,0:T(8,128)(2,1)} %bitcast.9, s32[1,512]{1,0:T(1,128)} %kept_hbm.1, bf16[4096,128]{1,0:T(8,128)(2,1)} %bitcast.7), custom_call_target="tpu_custom_call" | custom-call | flops 100000 | bytes 100000 | tf_op jit(solution)/shard_map/prepare/pallas_call | solution.py:33
  3.4 0.5 collective-permute-start
  3.9 1.1 %collective-permute-done.b_ref = bf16[768,128]{1,0:T(8,128)(2,1)S(1)} collective-permute-done((bf16[768,128]{1,0:T(8,128)(2,1)S(1)}, bf16[768,128]{1,0:T(8,128)(2,1)S(1)}, u32[]{:S(2)}, u32[]{:S(2)}) %collective-permute-start) | collective-permute-done | bytes 196640 | tf_op jit(solution)/shard_map/ppermute | solution.py:29
  5.0 3.0 %collective-permute-start.1 = (bf16[384,128]{1,0:T(8,128)(2,1)S(1)}, bf16[384,128]{1,0:T(8,128)(2,1)S(1)}, u32[]{:S(2)}, u32[]{:S(2)}) collective-permute-start(bf16[384,128]{1,0:T(8,128)(2,1)S(1)} %get-tuple-element.56), channel_id=1, source_target_pairs={{0,2},{1,3},{2,0},{3,1},{4,6},{5,7},{6,4},{7,5},{8,10},{9,11},{10,... | collective-permute-start | bytes 294920 | tf_op jit(solution)/shard_map/ppermute | solution.py:29
  8.0 0.3 turn.1.refs_2_.vt_ref
  8.3 2.8 %collective-permute-done.1.refs_1_ = bf16[384,128]{1,0:T(8,128)(2,1)S(1)} collective-permute-done((bf16[384,128]{1,0:T(8,128)(2,1)S(1)}, bf16[384,128]{1,0:T(8,128)(2,1)S(1)}, u32[]{:S(2)}, u32[]{:S(2)}) %collective-permute-start.1) | collective-permute-done | bytes 98336 | tf_op jit(solution)/shard_map/ppermute | solution.py:29
  11.1 3.9 %collective-permute-start.4 = (bf16[384,128]{1,0:T(8,128)(2,1)S(1)}, bf16[384,128]{1,0:T(8,128)(2,1)S(1)}, u32[]{:S(2)}, u32[]{:S(2)}) collective-permute-start(bf16[384,128]{1,0:T(8,128)(2,1)S(1)} %total.2.refs_0_), channel_id=1, source_target_pairs={{0,12},{1,13},{2,14},{3,15},{4,8},{5,9},{6,10},{7,11},{8,4},{9,5},... | collective-permute-start | bytes 294920 | tf_op jit(solution)/shard_map/ppermute | solution.py:29
  15.0 0.0 collective-permute-start.3
  15.0 0.6 collective-permute-start.2
  15.6 3.1 %collective-permute-done.4.refs_3_ = bf16[384,128]{1,0:T(8,128)(2,1)S(1)} collective-permute-done((bf16[384,128]{1,0:T(8,128)(2,1)S(1)}, bf16[384,128]{1,0:T(8,128)(2,1)S(1)}, u32[]{:S(2)}, u32[]{:S(2)}) %collective-permute-start.4) | collective-permute-done | bytes 98336 | tf_op jit(solution)/shard_map/ppermute | solution.py:29
  18.7 4.0 %collective-permute-done.3.refs_2_ = bf16[384,128]{1,0:T(8,128)(2,1)S(1)} collective-permute-done((bf16[384,128]{1,0:T(8,128)(2,1)S(1)}, bf16[384,128]{1,0:T(8,128)(2,1)S(1)}, u32[]{:S(2)}, u32[]{:S(2)}) %collective-permute-start.3) | collective-permute-done | bytes 98336 | tf_op jit(solution)/shard_map/ppermute | solution.py:29
  22.7 0.0 collective-permute-done.2.refs_1_
  22.8 1.6 %collective-permute-start.5 = (bf16[384,128]{1,0:T(8,128)(2,1)S(1)}, bf16[384,128]{1,0:T(8,128)(2,1)S(1)}, u32[]{:S(2)}, u32[]{:S(2)}) collective-permute-start(bf16[384,128]{1,0:T(8,128)(2,1)S(1)} %total.3.refs_0_.a_ref.near_ref), channel_id=1, source_target_pairs={{0,2},{1,3},{2,0},{3,1},{4,6},{5,7},{6,4},{7,5},{8,10},{9,11},{10,... | collective-permute-start | bytes 294920 | tf_op jit(solution)/shard_map/ppermute | solution.py:29
  24.4 1.8 %attention.2 = s32[72,256]{1,0:T(8,128)S(1)} custom-call(bf16[384,128]{1,0:T(8,128)(2,1)S(1)} %total.3.refs_0_.a_ref.near_ref, bf16[4096,128]{1,0:T(8,128)(2,1)S(1)} %get-tuple-element.58.refs_1_.k_ref, bf16[144,4096]{1,0:T(8,128)(2,1)S(1)} %turn.1.refs_2_.vt_ref), custom_call_target="tpu_custom_call" | custom-call | flops 1000000 | bytes 100000 | tf_op jit(solution)/shard_map/attention/pallas_call | solution.py:33
  26.2 1.3 %collective-permute-done.5.b_ref.refs_0_.far_ref = bf16[384,128]{1,0:T(8,128)(2,1)S(1)} collective-permute-done((bf16[384,128]{1,0:T(8,128)(2,1)S(1)}, bf16[384,128]{1,0:T(8,128)(2,1)S(1)}, u32[]{:S(2)}, u32[]{:S(2)}) %collective-permute-start.5) | collective-permute-done | bytes 98336 | tf_op jit(solution)/shard_map/ppermute | solution.py:29
  27.5 0.1 collective-permute-start.6
  27.5 0.5 collective-permute-start.7
  28.0 1.8 %attention.3 = s32[72,256]{1,0:T(8,128)S(1)} custom-call(bf16[384,128]{1,0:T(8,128)(2,1)S(1)} %collective-permute-done.5.b_ref.refs_0_.far_ref, bf16[4096,128]{1,0:T(8,128)(2,1)S(1)} %get-tuple-element.58.refs_1_.k_ref, bf16[144,4096]{1,0:T(8,128)(2,1)S(1)} %turn.1.refs_2_.vt_ref), custom_call_target="tpu_custom_call" | custom-call | flops 1000000 | bytes 100000 | tf_op jit(solution)/shard_map/attention/pallas_call | solution.py:33
  29.9 0.0 collective-permute-done.6.other_ref.q_ref
  29.9 1.3 %collective-permute-start.8 = (s32[72,256]{1,0:T(8,128)S(1)}, s32[72,256]{1,0:T(8,128)S(1)}, u32[]{:S(2)}, u32[]{:S(2)}) collective-permute-start(s32[72,256]{1,0:T(8,128)S(1)} %attention.3), channel_id=1, source_target_pairs={{0,3},{1,2},{2,1},{3,0},{4,7},{5,6},{6,5},{7,4},{8,11},{9,10},{10,... | collective-permute-start | bytes 221192 | tf_op jit(solution)/shard_map/ppermute | solution.py:29
  31.1 1.7 %attend.1 = (bf16[512,1024]{1,0:T(8,128)(2,1)S(1)}, bf16[512,1024]{1,0:T(8,128)(2,1)S(1)}, f32[32,256]{1,0:T(8,128)S(1)}) custom-call(s32[1]{0:T(128)} %bitcast.shard_ref, bf16[384,128]{1,0:T(8,128)(2,1)S(1)} %total.3.refs_0_.a_ref.near_ref, bf16[384,128]{1,0:T(8,128)(2,1)S(1)} %collective-permute-done.5.b_ref.refs_0_.far_ref, ...), custom_call_target="tpu_custom_call" | custom-call | flops 1000000 | bytes 100000 | tf_op jit(solution)/shard_map/attend/pallas_call | solution.py:33
  32.9 4.4 %gram.1 = (f32[512,512]{1,0:T(8,128)S(1)}, f32[64,64]{1,0:T(8,128)S(1)}, s32[72,256]{1,0:T(8,128)S(1)}) custom-call(bf16[512,1024]{1,0:T(8,128)(2,1)S(1)} %get-tuple-element.62.high_ref, bf16[512,1024]{1,0:T(8,128)(2,1)S(1)} %get-tuple-element.63.low_ref, f32[32,256]{1,0:T(8,128)S(1)} %get-tuple-element.64.square_ref, ...), custom_call_target="tpu_custom_call" | custom-call | flops 4000000000 | bytes 100000 | tf_op jit(solution)/shard_map/gram/pallas_call | solution.py:33
  37.2 0.6 collective-permute-start.9
  37.8 2.9 %first_sweep.1 = (f32[512,512]{1,0:T(8,128)S(1)}, f32[64,64]{1,0:T(8,128)S(1)}, f32[136,256]{1,0:T(8,128)S(1)}) custom-call(f32[512,512]{1,0:T(8,128)S(1)} %get-tuple-element.65.h_ref, f32[64,64]{1,0:T(8,128)S(1)} %get-tuple-element.66.inverse_ref, bf16[768,128]{1,0:T(8,128)(2,1)S(1)} %collective-permute-done.6.other_ref.q_ref, ...), custom_call_target="tpu_custom_call" | custom-call | flops 2000000000 | bytes 100000 | tf_op jit(solution)/shard_map/first_sweep/pallas_call | solution.py:33
  40.7 0.0 collective-permute-done.7.refs_1_
  40.8 0.0 collective-permute-done.8.refs_2_
  40.8 1.2 %collective-permute-done.9.refs_3_ = s32[72,256]{1,0:T(8,128)S(1)} collective-permute-done((s32[72,256]{1,0:T(8,128)S(1)}, s32[72,256]{1,0:T(8,128)S(1)}, u32[]{:S(2)}, u32[]{:S(2)}) %collective-permute-start.9) | collective-permute-done | bytes 73760 | tf_op jit(solution)/shard_map/ppermute | solution.py:29
  41.9 0.2 merge.3.refs_0_
  42.1 0.6 collective-permute-start.10
  42.7 1.9 %sweep.7 = (f32[512,512]{1,0:T(8,128)S(1)}, f32[64,64]{1,0:T(8,128)S(1)}) custom-call(f32[512,512]{1,0:T(8,128)S(1)} %get-tuple-element.72.h_ref, f32[64,64]{1,0:T(8,128)S(1)} %get-tuple-element.73.inverse_ref), custom_call_target="tpu_custom_call" | custom-call | flops 2000000000 | bytes 100000 | tf_op jit(solution)/shard_map/sweep/pallas_call | solution.py:33
  44.5 2.0 %collective-permute-done.10.refs_1_ = s32[72,256]{1,0:T(8,128)S(1)} collective-permute-done((s32[72,256]{1,0:T(8,128)S(1)}, s32[72,256]{1,0:T(8,128)S(1)}, u32[]{:S(2)}, u32[]{:S(2)}) %collective-permute-start.10) | collective-permute-done | bytes 73760 | tf_op jit(solution)/shard_map/ppermute | solution.py:29
  46.5 0.1 merge.4.refs_0_
  46.6 1.1 %collective-permute-start.11 = (s32[72,256]{1,0:T(8,128)S(1)}, s32[72,256]{1,0:T(8,128)S(1)}, u32[]{:S(2)}, u32[]{:S(2)}) collective-permute-start(s32[72,256]{1,0:T(8,128)S(1)} %merge.4.refs_0_), channel_id=1, source_target_pairs={{0,8},{1,9},{2,10},{3,11},{4,12},{5,13},{6,14},{7,15},{8,0},{9,1},... | collective-permute-start | bytes 221192 | tf_op jit(solution)/shard_map/ppermute | solution.py:29
  47.7 2.0 %sweep.8 = (f32[512,512]{1,0:T(8,128)S(1)}, f32[64,64]{1,0:T(8,128)S(1)}) custom-call(f32[512,512]{1,0:T(8,128)S(1)} %get-tuple-element.80.h_ref, f32[64,64]{1,0:T(8,128)S(1)} %get-tuple-element.81.inverse_ref), custom_call_target="tpu_custom_call" | custom-call | flops 2000000000 | bytes 100000 | tf_op jit(solution)/shard_map/sweep/pallas_call | solution.py:33
  49.7 1.9 %sweep.9 = (f32[512,512]{1,0:T(8,128)S(1)}, f32[64,64]{1,0:T(8,128)S(1)}) custom-call(f32[512,512]{1,0:T(8,128)S(1)} %get-tuple-element.82.h_ref, f32[64,64]{1,0:T(8,128)S(1)} %get-tuple-element.83.inverse_ref), custom_call_target="tpu_custom_call" | custom-call | flops 2000000000 | bytes 100000 | tf_op jit(solution)/shard_map/sweep/pallas_call | solution.py:33
  51.6 1.0 %collective-permute-done.11.refs_1_ = s32[72,256]{1,0:T(8,128)S(1)} collective-permute-done((s32[72,256]{1,0:T(8,128)S(1)}, s32[72,256]{1,0:T(8,128)S(1)}, u32[]{:S(2)}, u32[]{:S(2)}) %collective-permute-start.11) | collective-permute-done | bytes 73760 | tf_op jit(solution)/shard_map/ppermute | solution.py:29
  52.7 0.1 merge.5.a_ref
  52.8 0.6 collective-permute-start.12
  53.4 2.1 %sweep.10 = (f32[512,512]{1,0:T(8,128)S(1)}, f32[64,64]{1,0:T(8,128)S(1)}) custom-call(f32[512,512]{1,0:T(8,128)S(1)} %get-tuple-element.87.h_ref, f32[64,64]{1,0:T(8,128)S(1)} %get-tuple-element.88.inverse_ref), custom_call_target="tpu_custom_call" | custom-call | flops 2000000000 | bytes 100000 | tf_op jit(solution)/shard_map/sweep/pallas_call | solution.py:33
  55.5 1.9 %sweep.11 = (f32[512,512]{1,0:T(8,128)S(1)}, f32[64,64]{1,0:T(8,128)S(1)}) custom-call(f32[512,512]{1,0:T(8,128)S(1)} %get-tuple-element.89.h_ref, f32[64,64]{1,0:T(8,128)S(1)} %get-tuple-element.90.inverse_ref), custom_call_target="tpu_custom_call" | custom-call | flops 2000000000 | bytes 100000 | tf_op jit(solution)/shard_map/sweep/pallas_call | solution.py:33
  57.4 0.1 collective-permute-start.13
  57.5 2.1 %sweep.12 = (f32[512,512]{1,0:T(8,128)S(1)}, f32[64,64]{1,0:T(8,128)S(1)}) custom-call(f32[512,512]{1,0:T(8,128)S(1)} %get-tuple-element.94.h_ref, f32[64,64]{1,0:T(8,128)S(1)} %get-tuple-element.95.inverse_ref), custom_call_target="tpu_custom_call" | custom-call | flops 2000000000 | bytes 100000 | tf_op jit(solution)/shard_map/sweep/pallas_call | solution.py:33
  59.7 0.7 %sweep.13.minus_ref = f32[512,512]{1,0:T(8,128)S(1)} custom-call(f32[512,512]{1,0:T(8,128)S(1)} %get-tuple-element.99.h_ref, f32[64,64]{1,0:T(8,128)S(1)} %get-tuple-element.100.inverse_ref), custom_call_target="tpu_custom_call" | custom-call | flops 2000000000 | bytes 100000 | tf_op jit(solution)/shard_map/sweep/pallas_call | solution.py:33
  60.4 1.9 %fit.1 = (f32[128,512]{1,0:T(8,128)S(1)}, f32[8,128]{1,0:T(8,128)S(1)}) custom-call(s32[1]{0:T(128)} %bitcast.shard_ref, f32[512,512]{1,0:T(8,128)S(1)} %sweep.13.minus_ref, bf16[512,1024]{1,0:T(8,128)(2,1)S(1)} %get-tuple-element.62.high_ref, bf16[512,1024]{1,0:T(8,128)(2,1)S(1)} %get-tuple-element.63.low_ref, s32[144,256]{1,0:T(8,128)S(1)} %stack.3.own_ref, ...), custom_call_target="tpu_custom_call" | custom-call | flops 1000000000 | bytes 100000 | tf_op jit(solution)/shard_map/fit/pallas_call | solution.py:33
  62.3 1.6 %collective-permute-start.14 = (f32[8,128]{1,0:T(8,128)S(1)}, f32[8,128]{1,0:T(8,128)S(1)}, u32[]{:S(2)}, u32[]{:S(2)}) collective-permute-start(f32[8,128]{1,0:T(8,128)S(1)} %get-tuple-element.103.refs_0_), channel_id=1, source_target_pairs={{0,16},{16,0},{1,17},{17,1},{2,18},{18,2},{3,19},{19,3},{4,20},{20... | collective-permute-start | bytes 12296 | tf_op jit(solution)/shard_map/ppermute | solution.py:29
  63.9 0.8 %flip.1 = f32[512,128]{1,0:T(8,128)} custom-call(f32[128,512]{1,0:T(8,128)S(1)} %get-tuple-element.102.x_ref), custom_call_target="tpu_custom_call" | custom-call | flops 1000000 | bytes 100000 | tf_op jit(solution)/shard_map/flip/pallas_call | solution.py:33
  64.7 1.3 %collective-permute-done.14.refs_1_ = f32[8,128]{1,0:T(8,128)S(1)} collective-permute-done((f32[8,128]{1,0:T(8,128)S(1)}, f32[8,128]{1,0:T(8,128)S(1)}, u32[]{:S(2)}, u32[]{:S(2)}) %collective-permute-start.14) | collective-permute-done | bytes 4128 | tf_op jit(solution)/shard_map/ppermute | solution.py:29
  66.0 0.5 mean.1
  (9 shorter events, 0.1 us)
Async XLA Ops:
  0.6 7.3 %copy-start = (bf16[1,4096,128]{2,1,0:T(8,128)(2,1)S(1)}, bf16[1,4096,128]{2,1,0:T(8,128)(2,1)}, u32[]{:S(2)}) copy-start(bf16[1,4096,128]{2,1,0:T(8,128)(2,1)} %param.7) | copy-start | bytes 3145732
  3.4 1.6 %collective-permute-start = (bf16[768,128]{1,0:T(8,128)(2,1)S(1)}, bf16[768,128]{1,0:T(8,128)(2,1)S(1)}, u32[]{:S(2)}, u32[]{:S(2)}) collective-permute-start(bf16[768,128]{1,0:T(8,128)(2,1)S(1)} %get-tuple-element.54), channel_id=1, source_target_pairs={{0,1},{1,0},{2,3},{3,2},{4,5},{5,4},{6,7},{7,6},{8,9},{9,8},{10,11... | collective-permute-start | bytes 589832 | tf_op jit(solution)/shard_map/ppermute | solution.py:29
  5.0 6.0 %collective-permute-start.1 = (bf16[384,128]{1,0:T(8,128)(2,1)S(1)}, bf16[384,128]{1,0:T(8,128)(2,1)S(1)}, u32[]{:S(2)}, u32[]{:S(2)}) collective-permute-start(bf16[384,128]{1,0:T(8,128)(2,1)S(1)} %get-tuple-element.56), channel_id=1, source_target_pairs={{0,2},{1,3},{2,0},{3,1},{4,6},{5,7},{6,4},{7,5},{8,10},{9,11},{10,... | collective-permute-start | bytes 294920 | tf_op jit(solution)/shard_map/ppermute | solution.py:29
  11.1 7.6 %collective-permute-start.4 = (bf16[384,128]{1,0:T(8,128)(2,1)S(1)}, bf16[384,128]{1,0:T(8,128)(2,1)S(1)}, u32[]{:S(2)}, u32[]{:S(2)}) collective-permute-start(bf16[384,128]{1,0:T(8,128)(2,1)S(1)} %total.2.refs_0_), channel_id=1, source_target_pairs={{0,12},{1,13},{2,14},{3,15},{4,8},{5,9},{6,10},{7,11},{8,4},{9,5},... | collective-permute-start | bytes 294920 | tf_op jit(solution)/shard_map/ppermute | solution.py:29
  15.0 7.7 %collective-permute-start.3 = (bf16[384,128]{1,0:T(8,128)(2,1)S(1)}, bf16[384,128]{1,0:T(8,128)(2,1)S(1)}, u32[]{:S(2)}, u32[]{:S(2)}) collective-permute-start(bf16[384,128]{1,0:T(8,128)(2,1)S(1)} %total.2.refs_0_), channel_id=1, source_target_pairs={{0,8},{1,9},{2,10},{3,11},{4,12},{5,13},{6,14},{7,15},{8,0},{9,1},... | collective-permute-start | bytes 294920 | tf_op jit(solution)/shard_map/ppermute | solution.py:29
  15.0 7.7 %collective-permute-start.2 = (bf16[384,128]{1,0:T(8,128)(2,1)S(1)}, bf16[384,128]{1,0:T(8,128)(2,1)S(1)}, u32[]{:S(2)}, u32[]{:S(2)}) collective-permute-start(bf16[384,128]{1,0:T(8,128)(2,1)S(1)} %total.2.refs_0_), channel_id=1, source_target_pairs={{0,4},{1,5},{2,6},{3,7},{4,0},{5,1},{6,2},{7,3},{8,12},{9,13},{10,... | collective-permute-start | bytes 294920 | tf_op jit(solution)/shard_map/ppermute | solution.py:29
  22.8 4.7 %collective-permute-start.5 = (bf16[384,128]{1,0:T(8,128)(2,1)S(1)}, bf16[384,128]{1,0:T(8,128)(2,1)S(1)}, u32[]{:S(2)}, u32[]{:S(2)}) collective-permute-start(bf16[384,128]{1,0:T(8,128)(2,1)S(1)} %total.3.refs_0_.a_ref.near_ref), channel_id=1, source_target_pairs={{0,2},{1,3},{2,0},{3,1},{4,6},{5,7},{6,4},{7,5},{8,10},{9,11},{10,... | collective-permute-start | bytes 294920 | tf_op jit(solution)/shard_map/ppermute | solution.py:29
  27.5 2.4 %collective-permute-start.6 = (bf16[768,128]{1,0:T(8,128)(2,1)S(1)}, bf16[768,128]{1,0:T(8,128)(2,1)S(1)}, u32[]{:S(2)}, u32[]{:S(2)}) collective-permute-start(bf16[768,128]{1,0:T(8,128)(2,1)S(1)} %stack.2), channel_id=1, source_target_pairs={{0,1},{1,0},{2,3},{3,2},{4,5},{5,4},{6,7},{7,6},{8,9},{9,8},{10,11... | collective-permute-start | bytes 589832 | tf_op jit(solution)/shard_map/ppermute | solution.py:29
  27.5 13.2 %collective-permute-start.7 = (s32[72,256]{1,0:T(8,128)S(1)}, s32[72,256]{1,0:T(8,128)S(1)}, u32[]{:S(2)}, u32[]{:S(2)}) collective-permute-start(s32[72,256]{1,0:T(8,128)S(1)} %attention.2), channel_id=1, source_target_pairs={{0,1},{1,0},{2,3},{3,2},{4,5},{5,4},{6,7},{7,6},{8,9},{9,8},{10,11... | collective-permute-start | bytes 221192 | tf_op jit(solution)/shard_map/ppermute | solution.py:29
  29.9 10.9 %collective-permute-start.8 = (s32[72,256]{1,0:T(8,128)S(1)}, s32[72,256]{1,0:T(8,128)S(1)}, u32[]{:S(2)}, u32[]{:S(2)}) collective-permute-start(s32[72,256]{1,0:T(8,128)S(1)} %attention.3), channel_id=1, source_target_pairs={{0,3},{1,2},{2,1},{3,0},{4,7},{5,6},{6,5},{7,4},{8,11},{9,10},{10,... | collective-permute-start | bytes 221192 | tf_op jit(solution)/shard_map/ppermute | solution.py:29
  37.2 4.7 %collective-permute-start.9 = (s32[72,256]{1,0:T(8,128)S(1)}, s32[72,256]{1,0:T(8,128)S(1)}, u32[]{:S(2)}, u32[]{:S(2)}) collective-permute-start(s32[72,256]{1,0:T(8,128)S(1)} %get-tuple-element.71), channel_id=1, source_target_pairs={{0,2},{1,3},{2,0},{3,1},{4,6},{5,7},{6,4},{7,5},{8,10},{9,11},{10,... | collective-permute-start | bytes 221192 | tf_op jit(solution)/shard_map/ppermute | solution.py:29
  42.1 4.4 %collective-permute-start.10 = (s32[72,256]{1,0:T(8,128)S(1)}, s32[72,256]{1,0:T(8,128)S(1)}, u32[]{:S(2)}, u32[]{:S(2)}) collective-permute-start(s32[72,256]{1,0:T(8,128)S(1)} %merge.3.refs_0_), channel_id=1, source_target_pairs={{0,4},{1,5},{2,6},{3,7},{4,0},{5,1},{6,2},{7,3},{8,12},{9,13},{10,... | collective-permute-start | bytes 221192 | tf_op jit(solution)/shard_map/ppermute | solution.py:29
  46.6 6.1 %collective-permute-start.11 = (s32[72,256]{1,0:T(8,128)S(1)}, s32[72,256]{1,0:T(8,128)S(1)}, u32[]{:S(2)}, u32[]{:S(2)}) collective-permute-start(s32[72,256]{1,0:T(8,128)S(1)} %merge.4.refs_0_), channel_id=1, source_target_pairs={{0,8},{1,9},{2,10},{3,11},{4,12},{5,13},{6,14},{7,15},{8,0},{9,1},... | collective-permute-start | bytes 221192 | tf_op jit(solution)/shard_map/ppermute | solution.py:29
  52.8 4.6 %collective-permute-start.12 = (s32[72,256]{1,0:T(8,128)S(1)}, s32[72,256]{1,0:T(8,128)S(1)}, u32[]{:S(2)}, u32[]{:S(2)}) collective-permute-start(s32[72,256]{1,0:T(8,128)S(1)} %merge.5.a_ref), channel_id=1, source_target_pairs={{0,2},{1,3},{2,0},{3,1},{4,6},{5,7},{6,4},{7,5},{8,10},{9,11},{10,... | collective-permute-start | bytes 221192 | tf_op jit(solution)/shard_map/ppermute | solution.py:29
  57.4 2.2 %collective-permute-start.13 = (s32[144,256]{1,0:T(8,128)S(1)}, s32[144,256]{1,0:T(8,128)S(1)}, u32[]{:S(2)}, u32[]{:S(2)}) collective-permute-start(s32[144,256]{1,0:T(8,128)S(1)} %stack.3.own_ref), channel_id=1, source_target_pairs={{0,1},{1,0},{2,3},{3,2},{4,5},{5,4},{6,7},{7,6},{8,9},{9,8},{10,11... | collective-permute-start | bytes 442376 | tf_op jit(solution)/shard_map/ppermute | solution.py:29
  62.3 3.7 %collective-permute-start.14 = (f32[8,128]{1,0:T(8,128)S(1)}, f32[8,128]{1,0:T(8,128)S(1)}, u32[]{:S(2)}, u32[]{:S(2)}) collective-permute-start(f32[8,128]{1,0:T(8,128)S(1)} %get-tuple-element.103.refs_0_), channel_id=1, source_target_pairs={{0,16},{16,0},{1,17},{17,1},{2,18},{18,2},{3,19},{19,3},{4,20},{20... | collective-permute-start | bytes 12296 | tf_op jit(solution)/shard_map/ppermute | solution.py:29

commit v15 on v13

--- a/solution.py
+++ b/solution.py
@@ -231,7 +231,7 @@
     queries = q_ref[start : start + lanes, :]
     scores = lambda b: dot(k_ref[b : b + block, :], queries, NT)
     slab = k_ref.shape[0]
-    ahead = scores(0)
+    ahead, parts = scores(0), []
     for b in range(0, slab, block):
         s = ahead
         if b + block < slab:
@@ -239,18 +239,8 @@
         top = jnp.max(s, axis=0, keepdims=True)
         e = jnp.exp2((s - top) * factor).astype(BF16)
         out = dot(vt_ref[:, b : b + block], e, NN)
-        top = top * factor
-        total = out[dims : dims + 1, :]
-        out = out[:dims, :]
-        if b:
-            joint = jnp.maximum(old_top, top)
-            old_scale = jnp.exp2(old_top - joint)
-            new_scale = jnp.exp2(top - joint)
-            out = old_out * old_scale + out * new_scale
-            total = old_total * old_scale + total * new_scale
-            top = joint
-        old_out, old_top, old_total = out, top, total
-    put_partial(out_ref, out, top, total)
+        parts.append((out[:dims, :], top * factor, out[dims : dims + 1, :]))
+    put_partial(out_ref, *join(*parts))
 
 
 def attention(lanes, score_scale, piece, keys, turned, start=0, packed=True):
@@ -264,13 +254,16 @@
     )[0]
 
 
-def merged(*refs):
-    parts = [partial_of(ref) for ref in refs]
+def join(*parts):
     top = functools.reduce(jnp.maximum, [part[1] for part in parts])
     scales = [jnp.exp2(part[1] - top) for part in parts]
     total = sum(part[2] * scale for part, scale in zip(parts, scales))
     out = sum(part[0] * scale for part, scale in zip(parts, scales))
     return out, top, total
+
+
+def merged(*refs):
+    return join(*[partial_of(ref) for ref in refs])
 
 
 def merge_kernel(*refs):
@@ -301,8 +294,8 @@
     for place, (ref, at) in zip(places, pieces):
         c_all[aligned(place, part), :] = ref[at + rows : at + tall, :]
     for place, (ref, at) in zip(places, pieces):
-        scores = lax.dot_general(c_all[...], ref[at : at + rows, :], NT, preferred_element_type=F32) * score_scale
-        weights = jnp.exp(scores - jnp.max(scores, axis=0, keepdims=True))
+        scores = dot(c_all[...], ref[at : at + rows, :], NT)
+        weights = jnp.exp2((scores - jnp.max(scores, axis=0, keepdims=True)) * (score_scale * math.log2(math.e)))
         weights = weights * (1.0 / jnp.sum(weights, axis=0, keepdims=True))
         high_ref[:, aligned(place, rows)], low_ref[:, aligned(place, rows)] = halves(weights)
         square_ref[aligned(place, SUB), :] = jnp.sum((weights * weights).reshape(-1, SUB, rows), axis=0)
@@ -393,16 +386,26 @@
             work.pop(0)()
 
 
-def sweep_kernel(panel, h_ref, inverse_ref, out_ref, *next_ref):
+def sweep_kernel(panel, h_ref, inverse_ref, out_ref, next_ref):
     size = h_ref.shape[0]
     at = slice(panel * PANEL, (panel + 1) * PANEL)
-    wide = slice(panel * PANEL // 128 * 128, panel * PANEL // 128 * 128 + 128)
+    after = slice(at.stop, at.stop + PANEL)
+    wide, after_wide = (slice(x.start // 128 * 128, x.start // 128 * 128 + 128) for x in (at, after))
     offset = at.start - wide.start
     inverse = inverse_ref[...]
-    turned = product(halves(inverse), halves(h_ref[at, :]), NN)
-    padded = jnp.concatenate(
-        [turned if i == offset else jnp.zeros_like(turned) for i in range(0, 128, PANEL)], axis=0
-    )
+    split_inverse = halves(inverse)
+    blank = jnp.zeros((PANEL, 1), F32)
+
+    def pad(array):
+        zeros = jnp.broadcast_to(blank, array.shape)
+        return jnp.concatenate([array if i == offset else zeros for i in range(0, 128, PANEL)], axis=0)
+
+    near = pad(product(split_inverse, halves(h_ref[at, after_wide]), NN))
+    block = h_ref[after, after_wide] - product(halves(h_ref[after, wide]), halves(near), NN)
+    block = block[:, after.start - after_wide.start :][:, :PANEL]
+
+    turned = product(split_inverse, halves(h_ref[at, :]), NN)
+    padded = pad(turned)
     split = halves(padded)
     columns = padded.T
     lane = lax.broadcasted_iota(jnp.int32, (128, 128), 1)
@@ -420,19 +423,10 @@
 
         return piece
 
-    work = [rows_update(i) for i in range(0, size, 128)]
-    if next_ref:
-        after = slice(at.stop, at.stop + PANEL)
-        block = h_ref[after, after] - product(
-            halves(h_ref[after, wide]), tuple(x[:, after] for x in split), NN
-        )
-        next_ref[0][...] = inverse_beside(block, work)
-    else:
-        for piece in work:
-            piece()
-
-
-def fit_kernel(shard_ref, minus_ref, high_ref, low_ref, own_ref, other_ref, x_ref, err_ref, yt):
+    next_ref[...] = inverse_beside(block, [rows_update(i) for i in range(0, size, 128)])
+
+
+def fit_kernel(shard_ref, swept_ref, inverse_ref, high_ref, low_ref, own_ref, other_ref, x_ref, err_ref, yt):
     rows, lanes = own_ref.shape[0] // 2, own_ref.shape[1]
     place = shard_ref[0] % 4
     for s, ref in ((1, own_ref), (3, own_ref), (0, other_ref), (2, other_ref)):
@@ -441,7 +435,12 @@
     target = yt[...]
     attend = high_ref[...], low_ref[...]
     cross = product(halves(target), attend, NT)
-    fitted = -product(halves(cross), halves(minus_ref[...]), NN)
+    size = swept_ref.shape[0]
+    last = slice(size - PANEL, size)
+    first = product(halves(jnp.concatenate([cross[:, : last.start], jnp.zeros_like(cross[:, last])], axis=1)), halves(swept_ref[...]), NN)
+    rest = product(halves(cross[:, last] - first[:, last]), halves(inverse_ref[...]), NN)
+    others = first + product(halves(rest), halves(swept_ref[last, :]), NN)
+    fitted = jnp.concatenate([-others[:, : last.start], rest], axis=1)
     x_ref[...] = fitted
     misfit = product(halves(fitted), attend, NN) - target
     error = jnp.sum(misfit * misfit) / jnp.sum(target * target)
@@ -495,16 +494,14 @@
     panels = count // PANEL
     block_shape = ((PANEL, PANEL), F32)
     system, inverse = call(gram_kernel, attend, [system_shape, block_shape], 4 * 10**9, name="gram")
-    for panel in range(panels):
-        last = panel == panels - 1
-        system, *inverse = call(
+    for panel in range(panels - 1):
+        system, inverse = call(
             functools.partial(sweep_kernel, panel),
             (system, inverse),
-            [system_shape] if last else [system_shape, block_shape],
+            [system_shape, block_shape],
             2 * 10**9,
             name="sweep",
         )
-        inverse = None if last else inverse[0]
         if panel in (0, 2, 4, 6):
             system, inverse = beside((system, inverse))
     while ends is None:
@@ -512,7 +509,7 @@
 
     turned_fit, error = call(
         fit_kernel,
-        (shard, system, *attend[:2], *ends),
+        (shard, system, inverse, *attend[:2], *ends),
         [((dims, count), F32), ((SUB, 128), F32)],
         10**9,
         scratch=[pltpu.VMEM((dims, rows), F32)],

time: 66.6 us -> 66 us (level)
  Pallas kernels: 32.7 us -> 31.9 us
    pallas_call x27 -> x26, Pallas kernels: 32.7 us -> 31.9 us  [call(): pl.pallas_call(kernel, in_specs=specs or [SMEM if x.size == 1 else VMEM f...]
  transfers between devices with their start and end apart: 15 -> 15, of which waited for: 8 -> 8; matrix products, arithmetic and copies ran while one was open for 0% -> 0% of each run, Pallas kernels for 41% -> 40%
where the time goes in v15:
time: 66 us; the launch traced here: 65.8 us
  Pallas kernels  31.9 us (48%)
  starting transfers between devices  17.5 us (27%)
  waiting for transfers between devices  14.8 us (22%)
  between operations  1.59 us (2%)
    pallas_call x26, Pallas kernels, call(): pl.pallas_call(kernel, in_specs=specs or [SMEM if x.size == 1 else VMEM f...  31.9 us
    ppermute x15, starting transfers between devices, swap(): return lax.ppermute(array, axis, [(i, i ^ step) for i in range(size)])  17.5 us
    ppermute x15, waiting for transfers between devices, swap(): return lax.ppermute(array, axis, [(i, i ^ step) for i in range(size)])  14.8 us
  transfers between devices with their start and end apart: 15, of which 8 were waited for; matrix products, arithmetic and copies ran while one was open for 0% of the time, Pallas kernels for 40%

profile of v15, /device:TPU:0, one launch (start us, length us, event | category | flops | bytes accessed | tf_op | source)
XLA Modules:
  0.0 65.8 jit_solution(8706783933794518102)
XLA Ops:
  1.4 2.0 %prepare.1 = (bf16[768,128]{1,0:T(8,128)(2,1)S(1)}, bf16[768,128]{1,0:T(8,128)(2,1)S(1)}, bf16[4096,128]{1,0:T(8,128)(2,1)S(1)}) custom-call(s32[1]{0:T(128)} %bitcast.shard_ref, s32[1]{0:T(128)S(6)} %copy.7.root_ref, bf16[1024,128]{1,0:T(8,128)(2,1)} %bitcast.9, s32[1,512]{1,0:T(1,128)} %kept_hbm.1, bf16[4096,128]{1,0:T(8,128)(2,1)} %bitcast.7), custom_call_target="tpu_custom_call" | custom-call | flops 100000 | bytes 100000 | tf_op jit(solution)/shard_map/prepare/pallas_call | solution.py:32
  3.4 0.5 collective-permute-start
  3.9 1.1 %collective-permute-done.b_ref = bf16[768,128]{1,0:T(8,128)(2,1)S(1)} collective-permute-done((bf16[768,128]{1,0:T(8,128)(2,1)S(1)}, bf16[768,128]{1,0:T(8,128)(2,1)S(1)}, u32[]{:S(2)}, u32[]{:S(2)}) %collective-permute-start) | collective-permute-done | bytes 196640 | tf_op jit(solution)/shard_map/ppermute | solution.py:28
  5.0 3.0 %collective-permute-start.1 = (bf16[384,128]{1,0:T(8,128)(2,1)S(1)}, bf16[384,128]{1,0:T(8,128)(2,1)S(1)}, u32[]{:S(2)}, u32[]{:S(2)}) collective-permute-start(bf16[384,128]{1,0:T(8,128)(2,1)S(1)} %get-tuple-element.56), channel_id=1, source_target_pairs={{0,2},{1,3},{2,0},{3,1},{4,6},{5,7},{6,4},{7,5},{8,10},{9,11},{10,... | collective-permute-start | bytes 294920 | tf_op jit(solution)/shard_map/ppermute | solution.py:28
  7.9 0.3 turn.1.vt_ref
  8.3 2.8 %collective-permute-done.1.refs_1_ = bf16[384,128]{1,0:T(8,128)(2,1)S(1)} collective-permute-done((bf16[384,128]{1,0:T(8,128)(2,1)S(1)}, bf16[384,128]{1,0:T(8,128)(2,1)S(1)}, u32[]{:S(2)}, u32[]{:S(2)}) %collective-permute-start.1) | collective-permute-done | bytes 98336 | tf_op jit(solution)/shard_map/ppermute | solution.py:28
  11.1 3.9 %collective-permute-start.4 = (bf16[384,128]{1,0:T(8,128)(2,1)S(1)}, bf16[384,128]{1,0:T(8,128)(2,1)S(1)}, u32[]{:S(2)}, u32[]{:S(2)}) collective-permute-start(bf16[384,128]{1,0:T(8,128)(2,1)S(1)} %total.2.refs_0_), channel_id=1, source_target_pairs={{0,12},{1,13},{2,14},{3,15},{4,8},{5,9},{6,10},{7,11},{8,4},{9,5},... | collective-permute-start | bytes 294920 | tf_op jit(solution)/shard_map/ppermute | solution.py:28
  15.0 0.0 collective-permute-start.3
  15.0 0.6 collective-permute-start.2
  15.6 3.1 %collective-permute-done.4.refs_3_ = bf16[384,128]{1,0:T(8,128)(2,1)S(1)} collective-permute-done((bf16[384,128]{1,0:T(8,128)(2,1)S(1)}, bf16[384,128]{1,0:T(8,128)(2,1)S(1)}, u32[]{:S(2)}, u32[]{:S(2)}) %collective-permute-start.4) | collective-permute-done | bytes 98336 | tf_op jit(solution)/shard_map/ppermute | solution.py:28
  18.7 4.0 %collective-permute-done.3.refs_2_ = bf16[384,128]{1,0:T(8,128)(2,1)S(1)} collective-permute-done((bf16[384,128]{1,0:T(8,128)(2,1)S(1)}, bf16[384,128]{1,0:T(8,128)(2,1)S(1)}, u32[]{:S(2)}, u32[]{:S(2)}) %collective-permute-start.3) | collective-permute-done | bytes 98336 | tf_op jit(solution)/shard_map/ppermute | solution.py:28
  22.7 0.0 collective-permute-done.2.refs_1_
  22.7 1.6 %collective-permute-start.5 = (bf16[384,128]{1,0:T(8,128)(2,1)S(1)}, bf16[384,128]{1,0:T(8,128)(2,1)S(1)}, u32[]{:S(2)}, u32[]{:S(2)}) collective-permute-start(bf16[384,128]{1,0:T(8,128)(2,1)S(1)} %total.3.q_ref.a_ref.near_ref), channel_id=1, source_target_pairs={{0,2},{1,3},{2,0},{3,1},{4,6},{5,7},{6,4},{7,5},{8,10},{9,11},{10,... | collective-permute-start | bytes 294920 | tf_op jit(solution)/shard_map/ppermute | solution.py:28
  24.3 1.8 %attention.4 = s32[72,256]{1,0:T(8,128)S(1)} custom-call(bf16[384,128]{1,0:T(8,128)(2,1)S(1)} %total.3.q_ref.a_ref.near_ref, bf16[4096,128]{1,0:T(8,128)(2,1)S(1)} %get-tuple-element.58.k_ref, bf16[144,4096]{1,0:T(8,128)(2,1)S(1)} %turn.1.vt_ref), custom_call_target="tpu_custom_call" | custom-call | flops 1000000 | bytes 100000 | tf_op jit(solution)/shard_map/attention/pallas_call | solution.py:32
  26.2 1.3 %collective-permute-done.5.b_ref.q_ref.far_ref = bf16[384,128]{1,0:T(8,128)(2,1)S(1)} collective-permute-done((bf16[384,128]{1,0:T(8,128)(2,1)S(1)}, bf16[384,128]{1,0:T(8,128)(2,1)S(1)}, u32[]{:S(2)}, u32[]{:S(2)}) %collective-permute-start.5) | collective-permute-done | bytes 98336 | tf_op jit(solution)/shard_map/ppermute | solution.py:28
  27.4 0.1 collective-permute-start.6
  27.5 0.5 collective-permute-start.7
  28.0 1.8 %attention.5 = s32[72,256]{1,0:T(8,128)S(1)} custom-call(bf16[384,128]{1,0:T(8,128)(2,1)S(1)} %collective-permute-done.5.b_ref.q_ref.far_ref, bf16[4096,128]{1,0:T(8,128)(2,1)S(1)} %get-tuple-element.58.k_ref, bf16[144,4096]{1,0:T(8,128)(2,1)S(1)} %turn.1.vt_ref), custom_call_target="tpu_custom_call" | custom-call | flops 1000000 | bytes 100000 | tf_op jit(solution)/shard_map/attention/pallas_call | solution.py:32
  29.9 0.0 collective-permute-done.6.q_ref.other_ref
  29.9 1.8 %attention.6 = s32[72,256]{1,0:T(8,128)S(1)} custom-call(bf16[768,128]{1,0:T(8,128)(2,1)S(1)} %collective-permute-done.6.q_ref.other_ref, bf16[4096,128]{1,0:T(8,128)(2,1)S(1)} %get-tuple-element.58.k_ref, bf16[144,4096]{1,0:T(8,128)(2,1)S(1)} %turn.1.vt_ref), custom_call_target="tpu_custom_call" | custom-call | flops 1000000 | bytes 100000 | tf_op jit(solution)/shard_map/attention/pallas_call | solution.py:32
  31.7 1.6 %collective-permute-start.9 = (s32[72,256]{1,0:T(8,128)S(1)}, s32[72,256]{1,0:T(8,128)S(1)}, u32[]{:S(2)}, u32[]{:S(2)}) collective-permute-start(s32[72,256]{1,0:T(8,128)S(1)} %attention.6), channel_id=1, source_target_pairs={{0,2},{1,3},{2,0},{3,1},{4,6},{5,7},{6,4},{7,5},{8,10},{9,11},{10,... | collective-permute-start | bytes 221192 | tf_op jit(solution)/shard_map/ppermute | solution.py:28
  33.3 0.0 collective-permute-start.8
  33.3 1.8 %attention.7.refs_0_ = f32[136,256]{1,0:T(8,128)S(1)} custom-call(bf16[768,128]{1,0:T(8,128)(2,1)S(1)} %collective-permute-done.6.q_ref.other_ref, bf16[4096,128]{1,0:T(8,128)(2,1)S(1)} %get-tuple-element.58.k_ref, bf16[144,4096]{1,0:T(8,128)(2,1)S(1)} %turn.1.vt_ref), custom_call_target="tpu_custom_call" | custom-call | flops 1000000 | bytes 100000 | tf_op jit(solution)/shard_map/attention/pallas_call | solution.py:32
  35.1 1.7 %attend.1 = (bf16[512,1024]{1,0:T(8,128)(2,1)S(1)}, bf16[512,1024]{1,0:T(8,128)(2,1)S(1)}, f32[32,256]{1,0:T(8,128)S(1)}) custom-call(s32[1]{0:T(128)} %bitcast.shard_ref, bf16[384,128]{1,0:T(8,128)(2,1)S(1)} %total.3.q_ref.a_ref.near_ref, bf16[384,128]{1,0:T(8,128)(2,1)S(1)} %collective-permute-done.5.b_ref.q_ref.far_ref, ...), custom_call_target="tpu_custom_call" | custom-call | flops 1000000 | bytes 100000 | tf_op jit(solution)/shard_map/attend/pallas_call | solution.py:32
  36.8 0.0 collective-permute-done.7.refs_1_
  36.8 1.1 %collective-permute-done.8.refs_2_ = s32[72,256]{1,0:T(8,128)S(1)} collective-permute-done((s32[72,256]{1,0:T(8,128)S(1)}, s32[72,256]{1,0:T(8,128)S(1)}, u32[]{:S(2)}, u32[]{:S(2)}) %collective-permute-start.8) | collective-permute-done | bytes 73760 | tf_op jit(solution)/shard_map/ppermute | solution.py:28
  37.9 0.2 merge.3.refs_0_
  38.0 0.6 collective-permute-start.10
  38.6 3.0 %gram.1 = (f32[512,512]{1,0:T(8,128)S(1)}, f32[64,64]{1,0:T(8,128)S(1)}) custom-call(bf16[512,1024]{1,0:T(8,128)(2,1)S(1)} %get-tuple-element.68.high_ref, bf16[512,1024]{1,0:T(8,128)(2,1)S(1)} %get-tuple-element.69.low_ref, f32[32,256]{1,0:T(8,128)S(1)} %get-tuple-element.70.square_ref), custom_call_target="tpu_custom_call" | custom-call | flops 4000000000 | bytes 100000 | tf_op jit(solution)/shard_map/gram/pallas_call | solution.py:32
  41.6 2.0 %sweep.7 = (f32[512,512]{1,0:T(8,128)S(1)}, f32[64,64]{1,0:T(8,128)S(1)}) custom-call(f32[512,512]{1,0:T(8,128)S(1)} %get-tuple-element.71.h_ref, f32[64,64]{1,0:T(8,128)S(1)} %get-tuple-element.72.inverse_ref), custom_call_target="tpu_custom_call" | custom-call | flops 2000000000 | bytes 100000 | tf_op jit(solution)/shard_map/sweep/pallas_call | solution.py:32
  43.6 0.1 merge.4.refs_0_
  43.7 2.6 %collective-permute-start.11 = (s32[72,256]{1,0:T(8,128)S(1)}, s32[72,256]{1,0:T(8,128)S(1)}, u32[]{:S(2)}, u32[]{:S(2)}) collective-permute-start(s32[72,256]{1,0:T(8,128)S(1)} %merge.4.refs_0_), channel_id=1, source_target_pairs={{0,8},{1,9},{2,10},{3,11},{4,12},{5,13},{6,14},{7,15},{8,0},{9,1},... | collective-permute-start | bytes 221192 | tf_op jit(solution)/shard_map/ppermute | solution.py:28
  46.3 1.9 %sweep.8 = (f32[512,512]{1,0:T(8,128)S(1)}, f32[64,64]{1,0:T(8,128)S(1)}) custom-call(f32[512,512]{1,0:T(8,128)S(1)} %get-tuple-element.78.h_ref, f32[64,64]{1,0:T(8,128)S(1)} %get-tuple-element.79.inverse_ref), custom_call_target="tpu_custom_call" | custom-call | flops 2000000000 | bytes 100000 | tf_op jit(solution)/shard_map/sweep/pallas_call | solution.py:32
  48.1 2.0 %sweep.9 = (f32[512,512]{1,0:T(8,128)S(1)}, f32[64,64]{1,0:T(8,128)S(1)}) custom-call(f32[512,512]{1,0:T(8,128)S(1)} %get-tuple-element.80.h_ref, f32[64,64]{1,0:T(8,128)S(1)} %get-tuple-element.81.inverse_ref), custom_call_target="tpu_custom_call" | custom-call | flops 2000000000 | bytes 100000 | tf_op jit(solution)/shard_map/sweep/pallas_call | solution.py:32
  50.1 0.2 collective-permute-done.11.refs_1_
  50.3 0.1 merge.5.a_ref
  50.4 1.0 %collective-permute-start.12 = (s32[72,256]{1,0:T(8,128)S(1)}, s32[72,256]{1,0:T(8,128)S(1)}, u32[]{:S(2)}, u32[]{:S(2)}) collective-permute-start(s32[72,256]{1,0:T(8,128)S(1)} %merge.5.a_ref), channel_id=1, source_target_pairs={{0,2},{1,3},{2,0},{3,1},{4,6},{5,7},{6,4},{7,5},{8,10},{9,11},{10,... | collective-permute-start | bytes 221192 | tf_op jit(solution)/shard_map/ppermute | solution.py:28
  51.4 1.9 %sweep.10 = (f32[512,512]{1,0:T(8,128)S(1)}, f32[64,64]{1,0:T(8,128)S(1)}) custom-call(f32[512,512]{1,0:T(8,128)S(1)} %get-tuple-element.85.h_ref, f32[64,64]{1,0:T(8,128)S(1)} %get-tuple-element.86.inverse_ref), custom_call_target="tpu_custom_call" | custom-call | flops 2000000000 | bytes 100000 | tf_op jit(solution)/shard_map/sweep/pallas_call | solution.py:32
  53.3 2.0 %sweep.11 = (f32[512,512]{1,0:T(8,128)S(1)}, f32[64,64]{1,0:T(8,128)S(1)}) custom-call(f32[512,512]{1,0:T(8,128)S(1)} %get-tuple-element.87.h_ref, f32[64,64]{1,0:T(8,128)S(1)} %get-tuple-element.88.inverse_ref), custom_call_target="tpu_custom_call" | custom-call | flops 2000000000 | bytes 100000 | tf_op jit(solution)/shard_map/sweep/pallas_call | solution.py:32
  55.3 0.0 collective-permute-done.12.b_ref
  55.3 0.1 collective-permute-start.13
  55.4 1.9 %sweep.12 = (f32[512,512]{1,0:T(8,128)S(1)}, f32[64,64]{1,0:T(8,128)S(1)}) custom-call(f32[512,512]{1,0:T(8,128)S(1)} %get-tuple-element.92.h_ref, f32[64,64]{1,0:T(8,128)S(1)} %get-tuple-element.93.inverse_ref), custom_call_target="tpu_custom_call" | custom-call | flops 2000000000 | bytes 100000 | tf_op jit(solution)/shard_map/sweep/pallas_call | solution.py:32
  57.3 2.0 %sweep.13 = (f32[512,512]{1,0:T(8,128)S(1)}, f32[64,64]{1,0:T(8,128)S(1)}) custom-call(f32[512,512]{1,0:T(8,128)S(1)} %get-tuple-element.94.h_ref, f32[64,64]{1,0:T(8,128)S(1)} %get-tuple-element.95.inverse_ref), custom_call_target="tpu_custom_call" | custom-call | flops 2000000000 | bytes 100000 | tf_op jit(solution)/shard_map/sweep/pallas_call | solution.py:32
  59.3 2.3 %fit.1 = (f32[128,512]{1,0:T(8,128)S(1)}, f32[8,128]{1,0:T(8,128)S(1)}) custom-call(s32[1]{0:T(128)} %bitcast.shard_ref, f32[512,512]{1,0:T(8,128)S(1)} %get-tuple-element.99.swept_ref, f32[64,64]{1,0:T(8,128)S(1)} %get-tuple-element.100.inverse_ref, bf16[512,1024]{1,0:T(8,128)(2,1)S(1)} %get-tuple-element.68.high_ref, ...), custom_call_target="tpu_custom_call" | custom-call | flops 1000000000 | bytes 100000 | tf_op jit(solution)/shard_map/fit/pallas_call | solution.py:32
  61.6 1.6 %collective-permute-start.14 = (f32[8,128]{1,0:T(8,128)S(1)}, f32[8,128]{1,0:T(8,128)S(1)}, u32[]{:S(2)}, u32[]{:S(2)}) collective-permute-start(f32[8,128]{1,0:T(8,128)S(1)} %get-tuple-element.103.refs_0_), channel_id=1, source_target_pairs={{0,16},{16,0},{1,17},{17,1},{2,18},{18,2},{3,19},{19,3},{4,20},{20... | collective-permute-start | bytes 12296 | tf_op jit(solution)/shard_map/ppermute | solution.py:28
  63.1 0.8 %flip.1 = f32[512,128]{1,0:T(8,128)} custom-call(f32[128,512]{1,0:T(8,128)S(1)} %get-tuple-element.102.x_ref), custom_call_target="tpu_custom_call" | custom-call | flops 1000000 | bytes 100000 | tf_op jit(solution)/shard_map/flip/pallas_call | solution.py:32
  64.0 1.3 %collective-permute-done.14.refs_1_ = f32[8,128]{1,0:T(8,128)S(1)} collective-permute-done((f32[8,128]{1,0:T(8,128)S(1)}, f32[8,128]{1,0:T(8,128)S(1)}, u32[]{:S(2)}, u32[]{:S(2)}) %collective-permute-start.14) | collective-permute-done | bytes 4128 | tf_op jit(solution)/shard_map/ppermute | solution.py:28
  65.3 0.5 mean.1
  (10 shorter events, 0.1 us)
Async XLA Ops:
  0.6 7.3 %copy-start = (bf16[1,4096,128]{2,1,0:T(8,128)(2,1)S(1)}, bf16[1,4096,128]{2,1,0:T(8,128)(2,1)}, u32[]{:S(2)}) copy-start(bf16[1,4096,128]{2,1,0:T(8,128)(2,1)} %param.7) | copy-start | bytes 3145732
  3.4 1.6 %collective-permute-start = (bf16[768,128]{1,0:T(8,128)(2,1)S(1)}, bf16[768,128]{1,0:T(8,128)(2,1)S(1)}, u32[]{:S(2)}, u32[]{:S(2)}) collective-permute-start(bf16[768,128]{1,0:T(8,128)(2,1)S(1)} %get-tuple-element.54), channel_id=1, source_target_pairs={{0,1},{1,0},{2,3},{3,2},{4,5},{5,4},{6,7},{7,6},{8,9},{9,8},{10,11... | collective-permute-start | bytes 589832 | tf_op jit(solution)/shard_map/ppermute | solution.py:28
  5.0 6.0 %collective-permute-start.1 = (bf16[384,128]{1,0:T(8,128)(2,1)S(1)}, bf16[384,128]{1,0:T(8,128)(2,1)S(1)}, u32[]{:S(2)}, u32[]{:S(2)}) collective-permute-start(bf16[384,128]{1,0:T(8,128)(2,1)S(1)} %get-tuple-element.56), channel_id=1, source_target_pairs={{0,2},{1,3},{2,0},{3,1},{4,6},{5,7},{6,4},{7,5},{8,10},{9,11},{10,... | collective-permute-start | bytes 294920 | tf_op jit(solution)/shard_map/ppermute | solution.py:28
  11.1 7.6 %collective-permute-start.4 = (bf16[384,128]{1,0:T(8,128)(2,1)S(1)}, bf16[384,128]{1,0:T(8,128)(2,1)S(1)}, u32[]{:S(2)}, u32[]{:S(2)}) collective-permute-start(bf16[384,128]{1,0:T(8,128)(2,1)S(1)} %total.2.refs_0_), channel_id=1, source_target_pairs={{0,12},{1,13},{2,14},{3,15},{4,8},{5,9},{6,10},{7,11},{8,4},{9,5},... | collective-permute-start | bytes 294920 | tf_op jit(solution)/shard_map/ppermute | solution.py:28
  15.0 7.7 %collective-permute-start.3 = (bf16[384,128]{1,0:T(8,128)(2,1)S(1)}, bf16[384,128]{1,0:T(8,128)(2,1)S(1)}, u32[]{:S(2)}, u32[]{:S(2)}) collective-permute-start(bf16[384,128]{1,0:T(8,128)(2,1)S(1)} %total.2.refs_0_), channel_id=1, source_target_pairs={{0,8},{1,9},{2,10},{3,11},{4,12},{5,13},{6,14},{7,15},{8,0},{9,1},... | collective-permute-start | bytes 294920 | tf_op jit(solution)/shard_map/ppermute | solution.py:28
  15.0 7.7 %collective-permute-start.2 = (bf16[384,128]{1,0:T(8,128)(2,1)S(1)}, bf16[384,128]{1,0:T(8,128)(2,1)S(1)}, u32[]{:S(2)}, u32[]{:S(2)}) collective-permute-start(bf16[384,128]{1,0:T(8,128)(2,1)S(1)} %total.2.refs_0_), channel_id=1, source_target_pairs={{0,4},{1,5},{2,6},{3,7},{4,0},{5,1},{6,2},{7,3},{8,12},{9,13},{10,... | collective-permute-start | bytes 294920 | tf_op jit(solution)/shard_map/ppermute | solution.py:28
  22.7 4.7 %collective-permute-start.5 = (bf16[384,128]{1,0:T(8,128)(2,1)S(1)}, bf16[384,128]{1,0:T(8,128)(2,1)S(1)}, u32[]{:S(2)}, u32[]{:S(2)}) collective-permute-start(bf16[384,128]{1,0:T(8,128)(2,1)S(1)} %total.3.q_ref.a_ref.near_ref), channel_id=1, source_target_pairs={{0,2},{1,3},{2,0},{3,1},{4,6},{5,7},{6,4},{7,5},{8,10},{9,11},{10,... | collective-permute-start | bytes 294920 | tf_op jit(solution)/shard_map/ppermute | solution.py:28
  27.4 2.4 %collective-permute-start.6 = (bf16[768,128]{1,0:T(8,128)(2,1)S(1)}, bf16[768,128]{1,0:T(8,128)(2,1)S(1)}, u32[]{:S(2)}, u32[]{:S(2)}) collective-permute-start(bf16[768,128]{1,0:T(8,128)(2,1)S(1)} %stack.2), channel_id=1, source_target_pairs={{0,1},{1,0},{2,3},{3,2},{4,5},{5,4},{6,7},{7,6},{8,9},{9,8},{10,11... | collective-permute-start | bytes 589832 | tf_op jit(solution)/shard_map/ppermute | solution.py:28
  27.5 9.2 %collective-permute-start.7 = (s32[72,256]{1,0:T(8,128)S(1)}, s32[72,256]{1,0:T(8,128)S(1)}, u32[]{:S(2)}, u32[]{:S(2)}) collective-permute-start(s32[72,256]{1,0:T(8,128)S(1)} %attention.4), channel_id=1, source_target_pairs={{0,1},{1,0},{2,3},{3,2},{4,5},{5,4},{6,7},{7,6},{8,9},{9,8},{10,11... | collective-permute-start | bytes 221192 | tf_op jit(solution)/shard_map/ppermute | solution.py:28
  31.7 5.0 %collective-permute-start.9 = (s32[72,256]{1,0:T(8,128)S(1)}, s32[72,256]{1,0:T(8,128)S(1)}, u32[]{:S(2)}, u32[]{:S(2)}) collective-permute-start(s32[72,256]{1,0:T(8,128)S(1)} %attention.6), channel_id=1, source_target_pairs={{0,2},{1,3},{2,0},{3,1},{4,6},{5,7},{6,4},{7,5},{8,10},{9,11},{10,... | collective-permute-start | bytes 221192 | tf_op jit(solution)/shard_map/ppermute | solution.py:28
  33.3 4.5 %collective-permute-start.8 = (s32[72,256]{1,0:T(8,128)S(1)}, s32[72,256]{1,0:T(8,128)S(1)}, u32[]{:S(2)}, u32[]{:S(2)}) collective-permute-start(s32[72,256]{1,0:T(8,128)S(1)} %attention.5), channel_id=1, source_target_pairs={{0,3},{1,2},{2,1},{3,0},{4,7},{5,6},{6,5},{7,4},{8,11},{9,10},{10,... | collective-permute-start | bytes 221192 | tf_op jit(solution)/shard_map/ppermute | solution.py:28
  38.0 5.5 %collective-permute-start.10 = (s32[72,256]{1,0:T(8,128)S(1)}, s32[72,256]{1,0:T(8,128)S(1)}, u32[]{:S(2)}, u32[]{:S(2)}) collective-permute-start(s32[72,256]{1,0:T(8,128)S(1)} %merge.3.refs_0_), channel_id=1, source_target_pairs={{0,4},{1,5},{2,6},{3,7},{4,0},{5,1},{6,2},{7,3},{8,12},{9,13},{10,... | collective-permute-start | bytes 221192 | tf_op jit(solution)/shard_map/ppermute | solution.py:28
  43.7 6.7 %collective-permute-start.11 = (s32[72,256]{1,0:T(8,128)S(1)}, s32[72,256]{1,0:T(8,128)S(1)}, u32[]{:S(2)}, u32[]{:S(2)}) collective-permute-start(s32[72,256]{1,0:T(8,128)S(1)} %merge.4.refs_0_), channel_id=1, source_target_pairs={{0,8},{1,9},{2,10},{3,11},{4,12},{5,13},{6,14},{7,15},{8,0},{9,1},... | collective-permute-start | bytes 221192 | tf_op jit(solution)/shard_map/ppermute | solution.py:28
  50.4 4.8 %collective-permute-start.12 = (s32[72,256]{1,0:T(8,128)S(1)}, s32[72,256]{1,0:T(8,128)S(1)}, u32[]{:S(2)}, u32[]{:S(2)}) collective-permute-start(s32[72,256]{1,0:T(8,128)S(1)} %merge.5.a_ref), channel_id=1, source_target_pairs={{0,2},{1,3},{2,0},{3,1},{4,6},{5,7},{6,4},{7,5},{8,10},{9,11},{10,... | collective-permute-start | bytes 221192 | tf_op jit(solution)/shard_map/ppermute | solution.py:28
  55.3 3.9 %collective-permute-start.13 = (s32[144,256]{1,0:T(8,128)S(1)}, s32[144,256]{1,0:T(8,128)S(1)}, u32[]{:S(2)}, u32[]{:S(2)}) collective-permute-start(s32[144,256]{1,0:T(8,128)S(1)} %stack.3.own_ref), channel_id=1, source_target_pairs={{0,1},{1,0},{2,3},{3,2},{4,5},{5,4},{6,7},{7,6},{8,9},{9,8},{10,11... | collective-permute-start | bytes 442376 | tf_op jit(solution)/shard_map/ppermute | solution.py:28
  61.6 3.7 %collective-permute-start.14 = (f32[8,128]{1,0:T(8,128)S(1)}, f32[8,128]{1,0:T(8,128)S(1)}, u32[]{:S(2)}, u32[]{:S(2)}) collective-permute-start(f32[8,128]{1,0:T(8,128)S(1)} %get-tuple-element.103.refs_0_), channel_id=1, source_target_pairs={{0,16},{16,0},{1,17},{17,1},{2,18},{18,2},{3,19},{19,3},{4,20},{20... | collective-permute-start | bytes 12296 | tf_op jit(solution)/shard_map/ppermute | solution.py:28

commit v16 on v15

--- a/solution.py
+++ b/solution.py
@@ -118,7 +118,7 @@
         part = pl.ds(i * chunk, chunk)
         loads.append(pltpu.make_async_copy(k_hbm.at[part], k_ref.at[part], sems.at[i]))
     loads.append(pltpu.make_async_copy(q_hbm, q_ref, sems.at[steps + 1]))
-    for load in loads:
+    for load in [loads[0], loads[-1]] + loads[1:-1]:
         load.start()
     base = shard_ref[0] * slab
     loads[0].wait()
@@ -131,6 +131,14 @@
     spot = pl.ds(pl.multiple_of(start * 16, 16), window)
     mine = spots[spot, :]
     column = lax.broadcasted_iota(jnp.int32, (window, 128), 1).astype(F32)
+    share, part = q_ref.shape[0] // 4, kept // 4
+    tall = share + part
+    is_root = shard_ref[0] == root_ref[0]
+    targets = [((keep_ref, send_ref)[s % 2], s // 2 * tall, (shard_ref[0] % 4) ^ s) for s in range(4)]
+    loads[-1].wait()
+    for out, at, place in targets:
+        q = q_ref[aligned(place, share), :]
+        out[at : at + share, :] = jnp.where(is_root, q, jnp.zeros_like(q))
     rows = jnp.zeros((window, dims), F32)
     for i in range(steps):
         onehot = jnp.concatenate(
@@ -141,15 +149,7 @@
         rows += lax.dot_general(onehot, k_ref[i * chunk : (i + 1) * chunk, :], NN, preferred_element_type=F32)
     picked[...] = jnp.zeros_like(picked)
     picked[spot, :] = rows.astype(BF16)
-    loads[-1].wait()
-    share, part = q_ref.shape[0] // 4, kept // 4
-    is_root = shard_ref[0] == root_ref[0]
-    tall = share + part
-    for s in range(4):
-        out, at = (keep_ref, send_ref)[s % 2], s // 2 * tall
-        place = (shard_ref[0] % 4) ^ s
-        q = q_ref[aligned(place, share), :]
-        out[at : at + share, :] = jnp.where(is_root, q, jnp.zeros_like(q))
+    for out, at, place in targets:
         out[at + share : at + tall, :] = picked[aligned(place, part), :]
 
 
@@ -386,7 +386,7 @@
             work.pop(0)()
 
 
-def sweep_kernel(panel, h_ref, inverse_ref, out_ref, next_ref):
+def sweep_kernel(panel, h_ref, inverse_ref, out_ref, next_ref, beside=()):
     size = h_ref.shape[0]
     at = slice(panel * PANEL, (panel + 1) * PANEL)
     after = slice(at.stop, at.stop + PANEL)
@@ -423,18 +423,26 @@
 
         return piece
 
-    next_ref[...] = inverse_beside(block, [rows_update(i) for i in range(0, size, 128)])
-
-
-def fit_kernel(shard_ref, swept_ref, inverse_ref, high_ref, low_ref, own_ref, other_ref, x_ref, err_ref, yt):
-    rows, lanes = own_ref.shape[0] // 2, own_ref.shape[1]
-    place = shard_ref[0] % 4
-    for s, ref in ((1, own_ref), (3, own_ref), (0, other_ref), (2, other_ref)):
-        half = s // 2
-        yt[:, aligned(place ^ s, lanes)] = means(ref[half * rows : (half + 1) * rows, :])
-    target = yt[...]
+    next_ref[...] = inverse_beside(block, [rows_update(i) for i in range(0, size, 128)] + list(beside))
+
+
+def last_sweep_kernel(panel, shard_ref, h_ref, inverse_ref, high_ref, low_ref, own_ref, other_ref, out_ref, next_ref, yt_ref, cross_ref):
+    def target():
+        rows, lanes = own_ref.shape[0] // 2, own_ref.shape[1]
+        place = shard_ref[0] % 4
+        for s, ref in ((1, own_ref), (3, own_ref), (0, other_ref), (2, other_ref)):
+            half = s // 2
+            yt_ref[:, aligned(place ^ s, lanes)] = means(ref[half * rows : (half + 1) * rows, :])
+
+    def cross():
+        cross_ref[...] = product(halves(yt_ref[...]), (high_ref[...], low_ref[...]), NT)
+
+    sweep_kernel(panel, h_ref, inverse_ref, out_ref, next_ref, (target, cross))
+
+
+def fit_kernel(swept_ref, inverse_ref, high_ref, low_ref, yt_ref, cross_ref, x_ref, err_ref):
+    target, cross = yt_ref[...], cross_ref[...]
     attend = high_ref[...], low_ref[...]
-    cross = product(halves(target), attend, NT)
     size = swept_ref.shape[0]
     last = slice(size - PANEL, size)
     first = product(halves(jnp.concatenate([cross[:, : last.start], jnp.zeros_like(cross[:, last])], axis=1)), halves(swept_ref[...]), NN)
@@ -494,7 +502,7 @@
     panels = count // PANEL
     block_shape = ((PANEL, PANEL), F32)
     system, inverse = call(gram_kernel, attend, [system_shape, block_shape], 4 * 10**9, name="gram")
-    for panel in range(panels - 1):
+    for panel in range(panels - 2):
         system, inverse = call(
             functools.partial(sweep_kernel, panel),
             (system, inverse),
@@ -502,17 +510,22 @@
             2 * 10**9,
             name="sweep",
         )
-        if panel in (0, 2, 4, 6):
+        if panel in (0, 2, 4, 5):
             system, inverse = beside((system, inverse))
     while ends is None:
         system = beside(system)
-
+    system, inverse, target, cross = call(
+        functools.partial(last_sweep_kernel, panels - 2),
+        (shard, system, inverse, *attend[:2], *ends),
+        [system_shape, block_shape, ((dims, rows), F32), ((dims, count), F32)],
+        2 * 10**9,
+        name="last_sweep",
+    )
     turned_fit, error = call(
         fit_kernel,
-        (shard, system, inverse, *attend[:2], *ends),
+        (system, inverse, *attend[:2], target, cross),
         [((dims, count), F32), ((SUB, 128), F32)],
         10**9,
-        scratch=[pltpu.VMEM((dims, rows), F32)],
         name="fit",
     )
     heads = lax.axis_size("head")

time: 66 us -> 65.5 us (level)
  transfers between devices with their start and end apart: 15 -> 15, of which waited for: 8 -> 8; matrix products, arithmetic and copies ran while one was open for 0% -> 0% of each run, Pallas kernels for 40% -> 38%
where the time goes in v16:
time: 65.5 us; the launch traced here: 65.3 us
  Pallas kernels  31.4 us (48%)
  starting transfers between devices  17.5 us (27%)
  waiting for transfers between devices  14.8 us (23%)
  between operations  1.59 us (2%)
    pallas_call x26, Pallas kernels, call(): pl.pallas_call(kernel, in_specs=specs or [SMEM if x.size == 1 else VMEM f...  31.4 us
    ppermute x15, starting transfers between devices, swap(): return lax.ppermute(array, axis, [(i, i ^ step) for i in range(size)])  17.5 us
    ppermute x15, waiting for transfers between devices, swap(): return lax.ppermute(array, axis, [(i, i ^ step) for i in range(size)])  14.8 us
  transfers between devices with their start and end apart: 15, of which 8 were waited for; matrix products, arithmetic and copies ran while one was open for 0% of the time, Pallas kernels for 38%

profile of v16, /device:TPU:0, one launch (start us, length us, event | category | flops | bytes accessed | tf_op | source)
XLA Modules:
  0.0 65.3 jit_solution(6308856630464253528)
XLA Ops:
  1.4 2.0 %prepare.1 = (bf16[768,128]{1,0:T(8,128)(2,1)S(1)}, bf16[768,128]{1,0:T(8,128)(2,1)S(1)}, bf16[4096,128]{1,0:T(8,128)(2,1)S(1)}) custom-call(s32[1]{0:T(128)} %bitcast.shard_ref, s32[1]{0:T(128)S(6)} %copy.7.root_ref, bf16[1024,128]{1,0:T(8,128)(2,1)} %bitcast.9, s32[1,512]{1,0:T(1,128)} %kept_hbm.1, bf16[4096,128]{1,0:T(8,128)(2,1)} %bitcast.7), custom_call_target="tpu_custom_call" | custom-call | flops 100000 | bytes 100000 | tf_op jit(solution)/shard_map/prepare/pallas_call | solution.py:32
  3.4 0.5 collective-permute-start
  3.9 1.1 %collective-permute-done.b_ref = bf16[768,128]{1,0:T(8,128)(2,1)S(1)} collective-permute-done((bf16[768,128]{1,0:T(8,128)(2,1)S(1)}, bf16[768,128]{1,0:T(8,128)(2,1)S(1)}, u32[]{:S(2)}, u32[]{:S(2)}) %collective-permute-start) | collective-permute-done | bytes 196640 | tf_op jit(solution)/shard_map/ppermute | solution.py:28
  5.0 2.9 %collective-permute-start.1 = (bf16[384,128]{1,0:T(8,128)(2,1)S(1)}, bf16[384,128]{1,0:T(8,128)(2,1)S(1)}, u32[]{:S(2)}, u32[]{:S(2)}) collective-permute-start(bf16[384,128]{1,0:T(8,128)(2,1)S(1)} %get-tuple-element.58), channel_id=1, source_target_pairs={{0,2},{1,3},{2,0},{3,1},{4,6},{5,7},{6,4},{7,5},{8,10},{9,11},{10,... | collective-permute-start | bytes 294920 | tf_op jit(solution)/shard_map/ppermute | solution.py:28
  8.0 0.3 turn.1.vt_ref
  8.3 2.8 %collective-permute-done.1.refs_1_ = bf16[384,128]{1,0:T(8,128)(2,1)S(1)} collective-permute-done((bf16[384,128]{1,0:T(8,128)(2,1)S(1)}, bf16[384,128]{1,0:T(8,128)(2,1)S(1)}, u32[]{:S(2)}, u32[]{:S(2)}) %collective-permute-start.1) | collective-permute-done | bytes 98336 | tf_op jit(solution)/shard_map/ppermute | solution.py:28
  11.1 3.9 %collective-permute-start.4 = (bf16[384,128]{1,0:T(8,128)(2,1)S(1)}, bf16[384,128]{1,0:T(8,128)(2,1)S(1)}, u32[]{:S(2)}, u32[]{:S(2)}) collective-permute-start(bf16[384,128]{1,0:T(8,128)(2,1)S(1)} %total.2.refs_0_), channel_id=1, source_target_pairs={{0,12},{1,13},{2,14},{3,15},{4,8},{5,9},{6,10},{7,11},{8,4},{9,5},... | collective-permute-start | bytes 294920 | tf_op jit(solution)/shard_map/ppermute | solution.py:28
  15.0 0.0 collective-permute-start.3
  15.0 0.6 collective-permute-start.2
  15.6 3.1 %collective-permute-done.4.refs_3_ = bf16[384,128]{1,0:T(8,128)(2,1)S(1)} collective-permute-done((bf16[384,128]{1,0:T(8,128)(2,1)S(1)}, bf16[384,128]{1,0:T(8,128)(2,1)S(1)}, u32[]{:S(2)}, u32[]{:S(2)}) %collective-permute-start.4) | collective-permute-done | bytes 98336 | tf_op jit(solution)/shard_map/ppermute | solution.py:28
  18.7 4.0 %collective-permute-done.3.refs_2_ = bf16[384,128]{1,0:T(8,128)(2,1)S(1)} collective-permute-done((bf16[384,128]{1,0:T(8,128)(2,1)S(1)}, bf16[384,128]{1,0:T(8,128)(2,1)S(1)}, u32[]{:S(2)}, u32[]{:S(2)}) %collective-permute-start.3) | collective-permute-done | bytes 98336 | tf_op jit(solution)/shard_map/ppermute | solution.py:28
  22.8 0.0 collective-permute-done.2.refs_1_
  22.8 1.6 %collective-permute-start.5 = (bf16[384,128]{1,0:T(8,128)(2,1)S(1)}, bf16[384,128]{1,0:T(8,128)(2,1)S(1)}, u32[]{:S(2)}, u32[]{:S(2)}) collective-permute-start(bf16[384,128]{1,0:T(8,128)(2,1)S(1)} %total.3.q_ref.a_ref.near_ref), channel_id=1, source_target_pairs={{0,2},{1,3},{2,0},{3,1},{4,6},{5,7},{6,4},{7,5},{8,10},{9,11},{10,... | collective-permute-start | bytes 294920 | tf_op jit(solution)/shard_map/ppermute | solution.py:28
  24.4 1.8 %attention.4 = s32[72,256]{1,0:T(8,128)S(1)} custom-call(bf16[384,128]{1,0:T(8,128)(2,1)S(1)} %total.3.q_ref.a_ref.near_ref, bf16[4096,128]{1,0:T(8,128)(2,1)S(1)} %get-tuple-element.60.k_ref, bf16[144,4096]{1,0:T(8,128)(2,1)S(1)} %turn.1.vt_ref), custom_call_target="tpu_custom_call" | custom-call | flops 1000000 | bytes 100000 | tf_op jit(solution)/shard_map/attention/pallas_call | solution.py:32
  26.2 1.3 %collective-permute-done.5.b_ref.q_ref.far_ref = bf16[384,128]{1,0:T(8,128)(2,1)S(1)} collective-permute-done((bf16[384,128]{1,0:T(8,128)(2,1)S(1)}, bf16[384,128]{1,0:T(8,128)(2,1)S(1)}, u32[]{:S(2)}, u32[]{:S(2)}) %collective-permute-start.5) | collective-permute-done | bytes 98336 | tf_op jit(solution)/shard_map/ppermute | solution.py:28
  27.5 0.1 collective-permute-start.6
  27.6 0.5 collective-permute-start.7
  28.1 1.8 %attention.5 = s32[72,256]{1,0:T(8,128)S(1)} custom-call(bf16[384,128]{1,0:T(8,128)(2,1)S(1)} %collective-permute-done.5.b_ref.q_ref.far_ref, bf16[4096,128]{1,0:T(8,128)(2,1)S(1)} %get-tuple-element.60.k_ref, bf16[144,4096]{1,0:T(8,128)(2,1)S(1)} %turn.1.vt_ref), custom_call_target="tpu_custom_call" | custom-call | flops 1000000 | bytes 100000 | tf_op jit(solution)/shard_map/attention/pallas_call | solution.py:32
  29.9 0.0 collective-permute-done.6.q_ref.other_ref
  29.9 1.8 %attention.6 = s32[72,256]{1,0:T(8,128)S(1)} custom-call(bf16[768,128]{1,0:T(8,128)(2,1)S(1)} %collective-permute-done.6.q_ref.other_ref, bf16[4096,128]{1,0:T(8,128)(2,1)S(1)} %get-tuple-element.60.k_ref, bf16[144,4096]{1,0:T(8,128)(2,1)S(1)} %turn.1.vt_ref), custom_call_target="tpu_custom_call" | custom-call | flops 1000000 | bytes 100000 | tf_op jit(solution)/shard_map/attention/pallas_call | solution.py:32
  31.8 1.6 %collective-permute-start.9 = (s32[72,256]{1,0:T(8,128)S(1)}, s32[72,256]{1,0:T(8,128)S(1)}, u32[]{:S(2)}, u32[]{:S(2)}) collective-permute-start(s32[72,256]{1,0:T(8,128)S(1)} %attention.6), channel_id=1, source_target_pairs={{0,2},{1,3},{2,0},{3,1},{4,6},{5,7},{6,4},{7,5},{8,10},{9,11},{10,... | collective-permute-start | bytes 221192 | tf_op jit(solution)/shard_map/ppermute | solution.py:28
  33.4 0.0 collective-permute-start.8
  33.4 1.8 %attention.7.refs_0_ = f32[136,256]{1,0:T(8,128)S(1)} custom-call(bf16[768,128]{1,0:T(8,128)(2,1)S(1)} %collective-permute-done.6.q_ref.other_ref, bf16[4096,128]{1,0:T(8,128)(2,1)S(1)} %get-tuple-element.60.k_ref, bf16[144,4096]{1,0:T(8,128)(2,1)S(1)} %turn.1.vt_ref), custom_call_target="tpu_custom_call" | custom-call | flops 1000000 | bytes 100000 | tf_op jit(solution)/shard_map/attention/pallas_call | solution.py:32
  35.2 1.7 %attend.1 = (bf16[512,1024]{1,0:T(8,128)(2,1)S(1)}, bf16[512,1024]{1,0:T(8,128)(2,1)S(1)}, f32[32,256]{1,0:T(8,128)S(1)}) custom-call(s32[1]{0:T(128)} %bitcast.shard_ref, bf16[384,128]{1,0:T(8,128)(2,1)S(1)} %total.3.q_ref.a_ref.near_ref, bf16[384,128]{1,0:T(8,128)(2,1)S(1)} %collective-permute-done.5.b_ref.q_ref.far_ref, ...), custom_call_target="tpu_custom_call" | custom-call | flops 1000000 | bytes 100000 | tf_op jit(solution)/shard_map/attend/pallas_call | solution.py:32
  36.8 0.0 collective-permute-done.9.refs_3_
  36.8 1.1 %collective-permute-done.8.refs_2_ = s32[72,256]{1,0:T(8,128)S(1)} collective-permute-done((s32[72,256]{1,0:T(8,128)S(1)}, s32[72,256]{1,0:T(8,128)S(1)}, u32[]{:S(2)}, u32[]{:S(2)}) %collective-permute-start.8) | collective-permute-done | bytes 73760 | tf_op jit(solution)/shard_map/ppermute | solution.py:28
  37.9 0.2 merge.3.refs_0_
  38.1 0.6 collective-permute-start.10
  38.6 3.1 %gram.1 = (f32[512,512]{1,0:T(8,128)S(1)}, f32[64,64]{1,0:T(8,128)S(1)}) custom-call(bf16[512,1024]{1,0:T(8,128)(2,1)S(1)} %get-tuple-element.70.high_ref, bf16[512,1024]{1,0:T(8,128)(2,1)S(1)} %get-tuple-element.71.low_ref, f32[32,256]{1,0:T(8,128)S(1)} %get-tuple-element.72.square_ref), custom_call_target="tpu_custom_call" | custom-call | flops 4000000000 | bytes 100000 | tf_op jit(solution)/shard_map/gram/pallas_call | solution.py:32
  41.7 2.0 %sweep.6 = (f32[512,512]{1,0:T(8,128)S(1)}, f32[64,64]{1,0:T(8,128)S(1)}) custom-call(f32[512,512]{1,0:T(8,128)S(1)} %get-tuple-element.73.h_ref, f32[64,64]{1,0:T(8,128)S(1)} %get-tuple-element.74.inverse_ref), custom_call_target="tpu_custom_call" | custom-call | flops 2000000000 | bytes 100000 | tf_op jit(solution)/shard_map/sweep/pallas_call | solution.py:32
  43.7 0.1 merge.4.refs_0_
  43.8 2.6 %collective-permute-start.11 = (s32[72,256]{1,0:T(8,128)S(1)}, s32[72,256]{1,0:T(8,128)S(1)}, u32[]{:S(2)}, u32[]{:S(2)}) collective-permute-start(s32[72,256]{1,0:T(8,128)S(1)} %merge.4.refs_0_), channel_id=1, source_target_pairs={{0,8},{1,9},{2,10},{3,11},{4,12},{5,13},{6,14},{7,15},{8,0},{9,1},... | collective-permute-start | bytes 221192 | tf_op jit(solution)/shard_map/ppermute | solution.py:28
  46.4 1.9 %sweep.7 = (f32[512,512]{1,0:T(8,128)S(1)}, f32[64,64]{1,0:T(8,128)S(1)}) custom-call(f32[512,512]{1,0:T(8,128)S(1)} %get-tuple-element.80.h_ref, f32[64,64]{1,0:T(8,128)S(1)} %get-tuple-element.81.inverse_ref), custom_call_target="tpu_custom_call" | custom-call | flops 2000000000 | bytes 100000 | tf_op jit(solution)/shard_map/sweep/pallas_call | solution.py:32
  48.3 1.9 %sweep.8 = (f32[512,512]{1,0:T(8,128)S(1)}, f32[64,64]{1,0:T(8,128)S(1)}) custom-call(f32[512,512]{1,0:T(8,128)S(1)} %get-tuple-element.82.h_ref, f32[64,64]{1,0:T(8,128)S(1)} %get-tuple-element.83.inverse_ref), custom_call_target="tpu_custom_call" | custom-call | flops 2000000000 | bytes 100000 | tf_op jit(solution)/shard_map/sweep/pallas_call | solution.py:32
  50.2 0.3 collective-permute-done.11.refs_1_
  50.5 0.1 merge.5.a_ref
  50.6 0.9 %collective-permute-start.12 = (s32[72,256]{1,0:T(8,128)S(1)}, s32[72,256]{1,0:T(8,128)S(1)}, u32[]{:S(2)}, u32[]{:S(2)}) collective-permute-start(s32[72,256]{1,0:T(8,128)S(1)} %merge.5.a_ref), channel_id=1, source_target_pairs={{0,2},{1,3},{2,0},{3,1},{4,6},{5,7},{6,4},{7,5},{8,10},{9,11},{10,... | collective-permute-start | bytes 221192 | tf_op jit(solution)/shard_map/ppermute | solution.py:28
  51.5 1.9 %sweep.9 = (f32[512,512]{1,0:T(8,128)S(1)}, f32[64,64]{1,0:T(8,128)S(1)}) custom-call(f32[512,512]{1,0:T(8,128)S(1)} %get-tuple-element.87.h_ref, f32[64,64]{1,0:T(8,128)S(1)} %get-tuple-element.88.inverse_ref), custom_call_target="tpu_custom_call" | custom-call | flops 2000000000 | bytes 100000 | tf_op jit(solution)/shard_map/sweep/pallas_call | solution.py:32
  53.4 2.0 %sweep.10 = (f32[512,512]{1,0:T(8,128)S(1)}, f32[64,64]{1,0:T(8,128)S(1)}) custom-call(f32[512,512]{1,0:T(8,128)S(1)} %get-tuple-element.89.h_ref, f32[64,64]{1,0:T(8,128)S(1)} %get-tuple-element.90.inverse_ref), custom_call_target="tpu_custom_call" | custom-call | flops 2000000000 | bytes 100000 | tf_op jit(solution)/shard_map/sweep/pallas_call | solution.py:32
  55.4 0.1 collective-permute-start.13
  55.5 1.9 %sweep.11 = (f32[512,512]{1,0:T(8,128)S(1)}, f32[64,64]{1,0:T(8,128)S(1)}) custom-call(f32[512,512]{1,0:T(8,128)S(1)} %get-tuple-element.94.h_ref, f32[64,64]{1,0:T(8,128)S(1)} %get-tuple-element.95.inverse_ref), custom_call_target="tpu_custom_call" | custom-call | flops 2000000000 | bytes 100000 | tf_op jit(solution)/shard_map/sweep/pallas_call | solution.py:32
  57.4 0.0 collective-permute-done.13.other_ref
  57.4 2.1 %last_sweep.1 = (f32[512,512]{1,0:T(8,128)S(1)}, f32[64,64]{1,0:T(8,128)S(1)}, f32[128,1024]{1,0:T(8,128)S(1)}, f32[128,512]{1,0:T(8,128)S(1)}) custom-call(s32[1]{0:T(128)} %bitcast.shard_ref, f32[512,512]{1,0:T(8,128)S(1)} %get-tuple-element.99.h_ref, f32[64,64]{1,0:T(8,128)S(1)} %get-tuple-element.100.inverse_ref, ...), custom_call_target="tpu_custom_call" | custom-call | flops 2000000000 | bytes 100000 | tf_op jit(solution)/shard_map/last_sweep/pallas_call | solution.py:32
  59.5 1.6 %fit.1 = (f32[128,512]{1,0:T(8,128)S(1)}, f32[8,128]{1,0:T(8,128)S(1)}) custom-call(f32[512,512]{1,0:T(8,128)S(1)} %get-tuple-element.102.swept_ref, f32[64,64]{1,0:T(8,128)S(1)} %get-tuple-element.103.inverse_ref, bf16[512,1024]{1,0:T(8,128)(2,1)S(1)} %get-tuple-element.70.high_ref, bf16[512,1024]{1,0:T(8,128)(2,1)S(1)} %get-tuple-element.71.low_ref, ...), custom_call_target="tpu_custom_call" | custom-call | flops 1000000000 | bytes 100000 | tf_op jit(solution)/shard_map/fit/pallas_call | solution.py:32
  61.1 1.6 %collective-permute-start.14 = (f32[8,128]{1,0:T(8,128)S(1)}, f32[8,128]{1,0:T(8,128)S(1)}, u32[]{:S(2)}, u32[]{:S(2)}) collective-permute-start(f32[8,128]{1,0:T(8,128)S(1)} %get-tuple-element.107.refs_0_), channel_id=1, source_target_pairs={{0,16},{16,0},{1,17},{17,1},{2,18},{18,2},{3,19},{19,3},{4,20},{20... | collective-permute-start | bytes 12296 | tf_op jit(solution)/shard_map/ppermute | solution.py:28
  62.7 0.8 %flip.1 = f32[512,128]{1,0:T(8,128)} custom-call(f32[128,512]{1,0:T(8,128)S(1)} %get-tuple-element.106.x_ref), custom_call_target="tpu_custom_call" | custom-call | flops 1000000 | bytes 100000 | tf_op jit(solution)/shard_map/flip/pallas_call | solution.py:32
  63.6 1.3 %collective-permute-done.14.refs_1_ = f32[8,128]{1,0:T(8,128)S(1)} collective-permute-done((f32[8,128]{1,0:T(8,128)S(1)}, f32[8,128]{1,0:T(8,128)S(1)}, u32[]{:S(2)}, u32[]{:S(2)}) %collective-permute-start.14) | collective-permute-done | bytes 4128 | tf_op jit(solution)/shard_map/ppermute | solution.py:28
  64.8 0.5 mean.1
  (10 shorter events, 0.1 us)
Async XLA Ops:
  0.6 7.4 %copy-start = (bf16[1,4096,128]{2,1,0:T(8,128)(2,1)S(1)}, bf16[1,4096,128]{2,1,0:T(8,128)(2,1)}, u32[]{:S(2)}) copy-start(bf16[1,4096,128]{2,1,0:T(8,128)(2,1)} %param.7) | copy-start | bytes 3145732
  3.4 1.6 %collective-permute-start = (bf16[768,128]{1,0:T(8,128)(2,1)S(1)}, bf16[768,128]{1,0:T(8,128)(2,1)S(1)}, u32[]{:S(2)}, u32[]{:S(2)}) collective-permute-start(bf16[768,128]{1,0:T(8,128)(2,1)S(1)} %get-tuple-element.56), channel_id=1, source_target_pairs={{0,1},{1,0},{2,3},{3,2},{4,5},{5,4},{6,7},{7,6},{8,9},{9,8},{10,11... | collective-permute-start | bytes 589832 | tf_op jit(solution)/shard_map/ppermute | solution.py:28
  5.0 6.0 %collective-permute-start.1 = (bf16[384,128]{1,0:T(8,128)(2,1)S(1)}, bf16[384,128]{1,0:T(8,128)(2,1)S(1)}, u32[]{:S(2)}, u32[]{:S(2)}) collective-permute-start(bf16[384,128]{1,0:T(8,128)(2,1)S(1)} %get-tuple-element.58), channel_id=1, source_target_pairs={{0,2},{1,3},{2,0},{3,1},{4,6},{5,7},{6,4},{7,5},{8,10},{9,11},{10,... | collective-permute-start | bytes 294920 | tf_op jit(solution)/shard_map/ppermute | solution.py:28
  11.1 7.6 %collective-permute-start.4 = (bf16[384,128]{1,0:T(8,128)(2,1)S(1)}, bf16[384,128]{1,0:T(8,128)(2,1)S(1)}, u32[]{:S(2)}, u32[]{:S(2)}) collective-permute-start(bf16[384,128]{1,0:T(8,128)(2,1)S(1)} %total.2.refs_0_), channel_id=1, source_target_pairs={{0,12},{1,13},{2,14},{3,15},{4,8},{5,9},{6,10},{7,11},{8,4},{9,5},... | collective-permute-start | bytes 294920 | tf_op jit(solution)/shard_map/ppermute | solution.py:28
  15.0 7.7 %collective-permute-start.3 = (bf16[384,128]{1,0:T(8,128)(2,1)S(1)}, bf16[384,128]{1,0:T(8,128)(2,1)S(1)}, u32[]{:S(2)}, u32[]{:S(2)}) collective-permute-start(bf16[384,128]{1,0:T(8,128)(2,1)S(1)} %total.2.refs_0_), channel_id=1, source_target_pairs={{0,8},{1,9},{2,10},{3,11},{4,12},{5,13},{6,14},{7,15},{8,0},{9,1},... | collective-permute-start | bytes 294920 | tf_op jit(solution)/shard_map/ppermute | solution.py:28
  15.0 7.7 %collective-permute-start.2 = (bf16[384,128]{1,0:T(8,128)(2,1)S(1)}, bf16[384,128]{1,0:T(8,128)(2,1)S(1)}, u32[]{:S(2)}, u32[]{:S(2)}) collective-permute-start(bf16[384,128]{1,0:T(8,128)(2,1)S(1)} %total.2.refs_0_), channel_id=1, source_target_pairs={{0,4},{1,5},{2,6},{3,7},{4,0},{5,1},{6,2},{7,3},{8,12},{9,13},{10,... | collective-permute-start | bytes 294920 | tf_op jit(solution)/shard_map/ppermute | solution.py:28
  22.8 4.7 %collective-permute-start.5 = (bf16[384,128]{1,0:T(8,128)(2,1)S(1)}, bf16[384,128]{1,0:T(8,128)(2,1)S(1)}, u32[]{:S(2)}, u32[]{:S(2)}) collective-permute-start(bf16[384,128]{1,0:T(8,128)(2,1)S(1)} %total.3.q_ref.a_ref.near_ref), channel_id=1, source_target_pairs={{0,2},{1,3},{2,0},{3,1},{4,6},{5,7},{6,4},{7,5},{8,10},{9,11},{10,... | collective-permute-start | bytes 294920 | tf_op jit(solution)/shard_map/ppermute | solution.py:28
  27.5 2.4 %collective-permute-start.6 = (bf16[768,128]{1,0:T(8,128)(2,1)S(1)}, bf16[768,128]{1,0:T(8,128)(2,1)S(1)}, u32[]{:S(2)}, u32[]{:S(2)}) collective-permute-start(bf16[768,128]{1,0:T(8,128)(2,1)S(1)} %stack.2), channel_id=1, source_target_pairs={{0,1},{1,0},{2,3},{3,2},{4,5},{5,4},{6,7},{7,6},{8,9},{9,8},{10,11... | collective-permute-start | bytes 589832 | tf_op jit(solution)/shard_map/ppermute | solution.py:28
  27.6 9.2 %collective-permute-start.7 = (s32[72,256]{1,0:T(8,128)S(1)}, s32[72,256]{1,0:T(8,128)S(1)}, u32[]{:S(2)}, u32[]{:S(2)}) collective-permute-start(s32[72,256]{1,0:T(8,128)S(1)} %attention.4), channel_id=1, source_target_pairs={{0,1},{1,0},{2,3},{3,2},{4,5},{5,4},{6,7},{7,6},{8,9},{9,8},{10,11... | collective-permute-start | bytes 221192 | tf_op jit(solution)/shard_map/ppermute | solution.py:28
  31.8 5.0 %collective-permute-start.9 = (s32[72,256]{1,0:T(8,128)S(1)}, s32[72,256]{1,0:T(8,128)S(1)}, u32[]{:S(2)}, u32[]{:S(2)}) collective-permute-start(s32[72,256]{1,0:T(8,128)S(1)} %attention.6), channel_id=1, source_target_pairs={{0,2},{1,3},{2,0},{3,1},{4,6},{5,7},{6,4},{7,5},{8,10},{9,11},{10,... | collective-permute-start | bytes 221192 | tf_op jit(solution)/shard_map/ppermute | solution.py:28
  33.4 4.6 %collective-permute-start.8 = (s32[72,256]{1,0:T(8,128)S(1)}, s32[72,256]{1,0:T(8,128)S(1)}, u32[]{:S(2)}, u32[]{:S(2)}) collective-permute-start(s32[72,256]{1,0:T(8,128)S(1)} %attention.5), channel_id=1, source_target_pairs={{0,3},{1,2},{2,1},{3,0},{4,7},{5,6},{6,5},{7,4},{8,11},{9,10},{10,... | collective-permute-start | bytes 221192 | tf_op jit(solution)/shard_map/ppermute | solution.py:28
  38.1 5.6 %collective-permute-start.10 = (s32[72,256]{1,0:T(8,128)S(1)}, s32[72,256]{1,0:T(8,128)S(1)}, u32[]{:S(2)}, u32[]{:S(2)}) collective-permute-start(s32[72,256]{1,0:T(8,128)S(1)} %merge.3.refs_0_), channel_id=1, source_target_pairs={{0,4},{1,5},{2,6},{3,7},{4,0},{5,1},{6,2},{7,3},{8,12},{9,13},{10,... | collective-permute-start | bytes 221192 | tf_op jit(solution)/shard_map/ppermute | solution.py:28
  43.8 6.7 %collective-permute-start.11 = (s32[72,256]{1,0:T(8,128)S(1)}, s32[72,256]{1,0:T(8,128)S(1)}, u32[]{:S(2)}, u32[]{:S(2)}) collective-permute-start(s32[72,256]{1,0:T(8,128)S(1)} %merge.4.refs_0_), channel_id=1, source_target_pairs={{0,8},{1,9},{2,10},{3,11},{4,12},{5,13},{6,14},{7,15},{8,0},{9,1},... | collective-permute-start | bytes 221192 | tf_op jit(solution)/shard_map/ppermute | solution.py:28
  50.6 4.8 %collective-permute-start.12 = (s32[72,256]{1,0:T(8,128)S(1)}, s32[72,256]{1,0:T(8,128)S(1)}, u32[]{:S(2)}, u32[]{:S(2)}) collective-permute-start(s32[72,256]{1,0:T(8,128)S(1)} %merge.5.a_ref), channel_id=1, source_target_pairs={{0,2},{1,3},{2,0},{3,1},{4,6},{5,7},{6,4},{7,5},{8,10},{9,11},{10,... | collective-permute-start | bytes 221192 | tf_op jit(solution)/shard_map/ppermute | solution.py:28
  55.4 2.0 %collective-permute-start.13 = (s32[144,256]{1,0:T(8,128)S(1)}, s32[144,256]{1,0:T(8,128)S(1)}, u32[]{:S(2)}, u32[]{:S(2)}) collective-permute-start(s32[144,256]{1,0:T(8,128)S(1)} %stack.3.own_ref), channel_id=1, source_target_pairs={{0,1},{1,0},{2,3},{3,2},{4,5},{5,4},{6,7},{7,6},{8,9},{9,8},{10,11... | collective-permute-start | bytes 442376 | tf_op jit(solution)/shard_map/ppermute | solution.py:28
  61.1 3.7 %collective-permute-start.14 = (f32[8,128]{1,0:T(8,128)S(1)}, f32[8,128]{1,0:T(8,128)S(1)}, u32[]{:S(2)}, u32[]{:S(2)}) collective-permute-start(f32[8,128]{1,0:T(8,128)S(1)} %get-tuple-element.107.refs_0_), channel_id=1, source_target_pairs={{0,16},{16,0},{1,17},{17,1},{2,18},{18,2},{3,19},{19,3},{4,20},{20... | collective-permute-start | bytes 12296 | tf_op jit(solution)/shard_map/ppermute | solution.py:28

commit v17 on v16

--- a/solution.py
+++ b/solution.py
@@ -336,14 +336,12 @@
             terms = [x + y for x, y in zip(terms[::2], terms[1::2])]
         return old - terms[0]
 
-    ahead = []
     for k in range(count):
         base = k * SUB
         inside = (lane >= base) & (lane < base + SUB)
-        columns = ahead + [spread_lane(rows[k], base + j) for j in range(len(ahead), SUB)]
+        columns = [spread_lane(rows[k], base + j) for j in range(SUB)]
         work = jnp.where(inside, jnp.where(lane - base == sub, 1.0, 0.0), rows[k])
-        beyond = [spread_lane(rows[k], base + SUB + j) for j in range(2)] if k + 1 < count else []
-        full = columns + [work] + beyond
+        full = columns + [work]
         bare = list(full)
         for j in range(0, SUB, 2):
             first, second = full[j], full[j + 1]
@@ -355,17 +353,12 @@
                 new_lower = (a * lower - c * upper) * inverse
                 bare[i] = full[i] - (first * new_upper + second * new_lower)
                 full[i] = jnp.where(sub == j, new_upper, jnp.where(sub == j + 1, new_lower, bare[i]))
-        work, beyond = full[SUB], full[SUB + 1 :]
+        work = full[SUB]
         lines = [line(work, j) for j in range(SUB)]
         updated = list(rows)
         updated[k] = work
         for i in list(range(k + 1, count)) + list(range(k)):
             factors = [spread_lane(rows[i], base + j) for j in range(SUB)]
-            if i == k + 1:
-                ahead = [
-                    less(spread_lane(rows[i], base + SUB + j), factors, [line(array, m) for m in range(SUB)])
-                    for j, array in enumerate(beyond)
-                ]
             updated[i] = less(jnp.where(inside, 0.0, rows[i]), factors, lines)
         rows = updated
         yield

time: 65.5 us -> 65.4 us (level)
  no operation moved by 1% of the time
where the time goes in v17:
time: 65.4 us; the launch traced here: 65.2 us
  Pallas kernels  31.2 us (48%)
  starting transfers between devices  17.5 us (27%)
  waiting for transfers between devices  14.8 us (23%)
  between operations  1.6 us (2%)
    pallas_call x26, Pallas kernels, call(): pl.pallas_call(kernel, in_specs=specs or [SMEM if x.size == 1 else VMEM f...  31.2 us
    ppermute x15, starting transfers between devices, swap(): return lax.ppermute(array, axis, [(i, i ^ step) for i in range(size)])  17.5 us
    ppermute x15, waiting for transfers between devices, swap(): return lax.ppermute(array, axis, [(i, i ^ step) for i in range(size)])  14.8 us
  transfers between devices with their start and end apart: 15, of which 8 were waited for; matrix products, arithmetic and copies ran while one was open for 0% of the time, Pallas kernels for 38%

profile of v17, /device:TPU:0, one launch (start us, length us, event | category | flops | bytes accessed | tf_op | source)
XLA Modules:
  0.0 65.2 jit_solution(3783131260584610144)
XLA Ops:
  1.4 2.0 %prepare.1 = (bf16[768,128]{1,0:T(8,128)(2,1)S(1)}, bf16[768,128]{1,0:T(8,128)(2,1)S(1)}, bf16[4096,128]{1,0:T(8,128)(2,1)S(1)}) custom-call(s32[1]{0:T(128)} %bitcast.shard_ref, s32[1]{0:T(128)S(6)} %copy.7.root_ref, bf16[1024,128]{1,0:T(8,128)(2,1)} %bitcast.9, s32[1,512]{1,0:T(1,128)} %kept_hbm.1, bf16[4096,128]{1,0:T(8,128)(2,1)} %bitcast.7), custom_call_target="tpu_custom_call" | custom-call | flops 100000 | bytes 100000 | tf_op jit(solution)/shard_map/prepare/pallas_call | solution.py:32
  3.4 0.5 collective-permute-start
  3.9 1.1 %collective-permute-done.b_ref = bf16[768,128]{1,0:T(8,128)(2,1)S(1)} collective-permute-done((bf16[768,128]{1,0:T(8,128)(2,1)S(1)}, bf16[768,128]{1,0:T(8,128)(2,1)S(1)}, u32[]{:S(2)}, u32[]{:S(2)}) %collective-permute-start) | collective-permute-done | bytes 196640 | tf_op jit(solution)/shard_map/ppermute | solution.py:28
  5.0 2.9 %collective-permute-start.1 = (bf16[384,128]{1,0:T(8,128)(2,1)S(1)}, bf16[384,128]{1,0:T(8,128)(2,1)S(1)}, u32[]{:S(2)}, u32[]{:S(2)}) collective-permute-start(bf16[384,128]{1,0:T(8,128)(2,1)S(1)} %get-tuple-element.58), channel_id=1, source_target_pairs={{0,2},{1,3},{2,0},{3,1},{4,6},{5,7},{6,4},{7,5},{8,10},{9,11},{10,... | collective-permute-start | bytes 294920 | tf_op jit(solution)/shard_map/ppermute | solution.py:28
  8.0 0.3 turn.1.vt_ref
  8.3 2.8 %collective-permute-done.1.refs_1_ = bf16[384,128]{1,0:T(8,128)(2,1)S(1)} collective-permute-done((bf16[384,128]{1,0:T(8,128)(2,1)S(1)}, bf16[384,128]{1,0:T(8,128)(2,1)S(1)}, u32[]{:S(2)}, u32[]{:S(2)}) %collective-permute-start.1) | collective-permute-done | bytes 98336 | tf_op jit(solution)/shard_map/ppermute | solution.py:28
  11.1 3.9 %collective-permute-start.4 = (bf16[384,128]{1,0:T(8,128)(2,1)S(1)}, bf16[384,128]{1,0:T(8,128)(2,1)S(1)}, u32[]{:S(2)}, u32[]{:S(2)}) collective-permute-start(bf16[384,128]{1,0:T(8,128)(2,1)S(1)} %total.2.refs_0_), channel_id=1, source_target_pairs={{0,12},{1,13},{2,14},{3,15},{4,8},{5,9},{6,10},{7,11},{8,4},{9,5},... | collective-permute-start | bytes 294920 | tf_op jit(solution)/shard_map/ppermute | solution.py:28
  15.0 0.0 collective-permute-start.3
  15.0 0.6 collective-permute-start.2
  15.6 3.1 %collective-permute-done.4.refs_3_ = bf16[384,128]{1,0:T(8,128)(2,1)S(1)} collective-permute-done((bf16[384,128]{1,0:T(8,128)(2,1)S(1)}, bf16[384,128]{1,0:T(8,128)(2,1)S(1)}, u32[]{:S(2)}, u32[]{:S(2)}) %collective-permute-start.4) | collective-permute-done | bytes 98336 | tf_op jit(solution)/shard_map/ppermute | solution.py:28
  18.7 4.0 %collective-permute-done.3.refs_2_ = bf16[384,128]{1,0:T(8,128)(2,1)S(1)} collective-permute-done((bf16[384,128]{1,0:T(8,128)(2,1)S(1)}, bf16[384,128]{1,0:T(8,128)(2,1)S(1)}, u32[]{:S(2)}, u32[]{:S(2)}) %collective-permute-start.3) | collective-permute-done | bytes 98336 | tf_op jit(solution)/shard_map/ppermute | solution.py:28
  22.8 1.6 %collective-permute-start.5 = (bf16[384,128]{1,0:T(8,128)(2,1)S(1)}, bf16[384,128]{1,0:T(8,128)(2,1)S(1)}, u32[]{:S(2)}, u32[]{:S(2)}) collective-permute-start(bf16[384,128]{1,0:T(8,128)(2,1)S(1)} %total.3.q_ref.a_ref.near_ref), channel_id=1, source_target_pairs={{0,2},{1,3},{2,0},{3,1},{4,6},{5,7},{6,4},{7,5},{8,10},{9,11},{10,... | collective-permute-start | bytes 294920 | tf_op jit(solution)/shard_map/ppermute | solution.py:28
  24.4 1.8 %attention.4 = s32[72,256]{1,0:T(8,128)S(1)} custom-call(bf16[384,128]{1,0:T(8,128)(2,1)S(1)} %total.3.q_ref.a_ref.near_ref, bf16[4096,128]{1,0:T(8,128)(2,1)S(1)} %get-tuple-element.60.k_ref, bf16[144,4096]{1,0:T(8,128)(2,1)S(1)} %turn.1.vt_ref), custom_call_target="tpu_custom_call" | custom-call | flops 1000000 | bytes 100000 | tf_op jit(solution)/shard_map/attention/pallas_call | solution.py:32
  26.2 1.3 %collective-permute-done.5.b_ref.q_ref.far_ref = bf16[384,128]{1,0:T(8,128)(2,1)S(1)} collective-permute-done((bf16[384,128]{1,0:T(8,128)(2,1)S(1)}, bf16[384,128]{1,0:T(8,128)(2,1)S(1)}, u32[]{:S(2)}, u32[]{:S(2)}) %collective-permute-start.5) | collective-permute-done | bytes 98336 | tf_op jit(solution)/shard_map/ppermute | solution.py:28
  27.5 0.1 collective-permute-start.6
  27.6 0.5 collective-permute-start.7
  28.1 1.8 %attention.5 = s32[72,256]{1,0:T(8,128)S(1)} custom-call(bf16[384,128]{1,0:T(8,128)(2,1)S(1)} %collective-permute-done.5.b_ref.q_ref.far_ref, bf16[4096,128]{1,0:T(8,128)(2,1)S(1)} %get-tuple-element.60.k_ref, bf16[144,4096]{1,0:T(8,128)(2,1)S(1)} %turn.1.vt_ref), custom_call_target="tpu_custom_call" | custom-call | flops 1000000 | bytes 100000 | tf_op jit(solution)/shard_map/attention/pallas_call | solution.py:32
  29.9 0.0 collective-permute-done.6.q_ref.other_ref
  29.9 1.8 %attention.6 = s32[72,256]{1,0:T(8,128)S(1)} custom-call(bf16[768,128]{1,0:T(8,128)(2,1)S(1)} %collective-permute-done.6.q_ref.other_ref, bf16[4096,128]{1,0:T(8,128)(2,1)S(1)} %get-tuple-element.60.k_ref, bf16[144,4096]{1,0:T(8,128)(2,1)S(1)} %turn.1.vt_ref), custom_call_target="tpu_custom_call" | custom-call | flops 1000000 | bytes 100000 | tf_op jit(solution)/shard_map/attention/pallas_call | solution.py:32
  31.8 1.6 %collective-permute-start.9 = (s32[72,256]{1,0:T(8,128)S(1)}, s32[72,256]{1,0:T(8,128)S(1)}, u32[]{:S(2)}, u32[]{:S(2)}) collective-permute-start(s32[72,256]{1,0:T(8,128)S(1)} %attention.6), channel_id=1, source_target_pairs={{0,2},{1,3},{2,0},{3,1},{4,6},{5,7},{6,4},{7,5},{8,10},{9,11},{10,... | collective-permute-start | bytes 221192 | tf_op jit(solution)/shard_map/ppermute | solution.py:28
  33.4 1.8 %attention.7.refs_0_ = f32[136,256]{1,0:T(8,128)S(1)} custom-call(bf16[768,128]{1,0:T(8,128)(2,1)S(1)} %collective-permute-done.6.q_ref.other_ref, bf16[4096,128]{1,0:T(8,128)(2,1)S(1)} %get-tuple-element.60.k_ref, bf16[144,4096]{1,0:T(8,128)(2,1)S(1)} %turn.1.vt_ref), custom_call_target="tpu_custom_call" | custom-call | flops 1000000 | bytes 100000 | tf_op jit(solution)/shard_map/attention/pallas_call | solution.py:32
  35.2 1.7 %attend.1 = (bf16[512,1024]{1,0:T(8,128)(2,1)S(1)}, bf16[512,1024]{1,0:T(8,128)(2,1)S(1)}, f32[32,256]{1,0:T(8,128)S(1)}) custom-call(s32[1]{0:T(128)} %bitcast.shard_ref, bf16[384,128]{1,0:T(8,128)(2,1)S(1)} %total.3.q_ref.a_ref.near_ref, bf16[384,128]{1,0:T(8,128)(2,1)S(1)} %collective-permute-done.5.b_ref.q_ref.far_ref, ...), custom_call_target="tpu_custom_call" | custom-call | flops 1000000 | bytes 100000 | tf_op jit(solution)/shard_map/attend/pallas_call | solution.py:32
  36.8 0.0 collective-permute-done.7.refs_1_
  36.8 1.1 %collective-permute-done.8.refs_2_ = s32[72,256]{1,0:T(8,128)S(1)} collective-permute-done((s32[72,256]{1,0:T(8,128)S(1)}, s32[72,256]{1,0:T(8,128)S(1)}, u32[]{:S(2)}, u32[]{:S(2)}) %collective-permute-start.8) | collective-permute-done | bytes 73760 | tf_op jit(solution)/shard_map/ppermute | solution.py:28
  37.9 0.2 merge.3.refs_0_
  38.1 0.6 collective-permute-start.10
  38.6 2.9 %gram.1 = (f32[512,512]{1,0:T(8,128)S(1)}, f32[64,64]{1,0:T(8,128)S(1)}) custom-call(bf16[512,1024]{1,0:T(8,128)(2,1)S(1)} %get-tuple-element.70.high_ref, bf16[512,1024]{1,0:T(8,128)(2,1)S(1)} %get-tuple-element.71.low_ref, f32[32,256]{1,0:T(8,128)S(1)} %get-tuple-element.72.square_ref), custom_call_target="tpu_custom_call" | custom-call | flops 4000000000 | bytes 100000 | tf_op jit(solution)/shard_map/gram/pallas_call | solution.py:32
  41.6 1.9 %sweep.6 = (f32[512,512]{1,0:T(8,128)S(1)}, f32[64,64]{1,0:T(8,128)S(1)}) custom-call(f32[512,512]{1,0:T(8,128)S(1)} %get-tuple-element.73.h_ref, f32[64,64]{1,0:T(8,128)S(1)} %get-tuple-element.74.inverse_ref), custom_call_target="tpu_custom_call" | custom-call | flops 2000000000 | bytes 100000 | tf_op jit(solution)/shard_map/sweep/pallas_call | solution.py:32
  43.5 0.0 collective-permute-done.10.refs_1_
  43.5 0.1 merge.4.refs_0_
  43.6 2.6 %collective-permute-start.11 = (s32[72,256]{1,0:T(8,128)S(1)}, s32[72,256]{1,0:T(8,128)S(1)}, u32[]{:S(2)}, u32[]{:S(2)}) collective-permute-start(s32[72,256]{1,0:T(8,128)S(1)} %merge.4.refs_0_), channel_id=1, source_target_pairs={{0,8},{1,9},{2,10},{3,11},{4,12},{5,13},{6,14},{7,15},{8,0},{9,1},... | collective-permute-start | bytes 221192 | tf_op jit(solution)/shard_map/ppermute | solution.py:28
  46.3 1.9 %sweep.7 = (f32[512,512]{1,0:T(8,128)S(1)}, f32[64,64]{1,0:T(8,128)S(1)}) custom-call(f32[512,512]{1,0:T(8,128)S(1)} %get-tuple-element.80.h_ref, f32[64,64]{1,0:T(8,128)S(1)} %get-tuple-element.81.inverse_ref), custom_call_target="tpu_custom_call" | custom-call | flops 2000000000 | bytes 100000 | tf_op jit(solution)/shard_map/sweep/pallas_call | solution.py:32
  48.2 1.9 %sweep.8 = (f32[512,512]{1,0:T(8,128)S(1)}, f32[64,64]{1,0:T(8,128)S(1)}) custom-call(f32[512,512]{1,0:T(8,128)S(1)} %get-tuple-element.82.h_ref, f32[64,64]{1,0:T(8,128)S(1)} %get-tuple-element.83.inverse_ref), custom_call_target="tpu_custom_call" | custom-call | flops 2000000000 | bytes 100000 | tf_op jit(solution)/shard_map/sweep/pallas_call | solution.py:32
  50.1 0.3 collective-permute-done.11.refs_1_
  50.4 0.1 merge.5.a_ref
  50.5 0.9 %collective-permute-start.12 = (s32[72,256]{1,0:T(8,128)S(1)}, s32[72,256]{1,0:T(8,128)S(1)}, u32[]{:S(2)}, u32[]{:S(2)}) collective-permute-start(s32[72,256]{1,0:T(8,128)S(1)} %merge.5.a_ref), channel_id=1, source_target_pairs={{0,2},{1,3},{2,0},{3,1},{4,6},{5,7},{6,4},{7,5},{8,10},{9,11},{10,... | collective-permute-start | bytes 221192 | tf_op jit(solution)/shard_map/ppermute | solution.py:28
  51.4 1.9 %sweep.9 = (f32[512,512]{1,0:T(8,128)S(1)}, f32[64,64]{1,0:T(8,128)S(1)}) custom-call(f32[512,512]{1,0:T(8,128)S(1)} %get-tuple-element.87.h_ref, f32[64,64]{1,0:T(8,128)S(1)} %get-tuple-element.88.inverse_ref), custom_call_target="tpu_custom_call" | custom-call | flops 2000000000 | bytes 100000 | tf_op jit(solution)/shard_map/sweep/pallas_call | solution.py:32
  53.3 1.9 %sweep.10 = (f32[512,512]{1,0:T(8,128)S(1)}, f32[64,64]{1,0:T(8,128)S(1)}) custom-call(f32[512,512]{1,0:T(8,128)S(1)} %get-tuple-element.89.h_ref, f32[64,64]{1,0:T(8,128)S(1)} %get-tuple-element.90.inverse_ref), custom_call_target="tpu_custom_call" | custom-call | flops 2000000000 | bytes 100000 | tf_op jit(solution)/shard_map/sweep/pallas_call | solution.py:32
  55.2 0.0 collective-permute-done.12.b_ref
  55.3 0.1 collective-permute-start.13
  55.3 1.9 %sweep.11 = (f32[512,512]{1,0:T(8,128)S(1)}, f32[64,64]{1,0:T(8,128)S(1)}) custom-call(f32[512,512]{1,0:T(8,128)S(1)} %get-tuple-element.94.h_ref, f32[64,64]{1,0:T(8,128)S(1)} %get-tuple-element.95.inverse_ref), custom_call_target="tpu_custom_call" | custom-call | flops 2000000000 | bytes 100000 | tf_op jit(solution)/shard_map/sweep/pallas_call | solution.py:32
  57.2 0.0 collective-permute-done.13.other_ref
  57.2 2.1 %last_sweep.1 = (f32[512,512]{1,0:T(8,128)S(1)}, f32[64,64]{1,0:T(8,128)S(1)}, f32[128,1024]{1,0:T(8,128)S(1)}, f32[128,512]{1,0:T(8,128)S(1)}) custom-call(s32[1]{0:T(128)} %bitcast.shard_ref, f32[512,512]{1,0:T(8,128)S(1)} %get-tuple-element.99.h_ref, f32[64,64]{1,0:T(8,128)S(1)} %get-tuple-element.100.inverse_ref, ...), custom_call_target="tpu_custom_call" | custom-call | flops 2000000000 | bytes 100000 | tf_op jit(solution)/shard_map/last_sweep/pallas_call | solution.py:32
  59.4 1.6 %fit.1 = (f32[128,512]{1,0:T(8,128)S(1)}, f32[8,128]{1,0:T(8,128)S(1)}) custom-call(f32[512,512]{1,0:T(8,128)S(1)} %get-tuple-element.102.swept_ref, f32[64,64]{1,0:T(8,128)S(1)} %get-tuple-element.103.inverse_ref, bf16[512,1024]{1,0:T(8,128)(2,1)S(1)} %get-tuple-element.70.high_ref, bf16[512,1024]{1,0:T(8,128)(2,1)S(1)} %get-tuple-element.71.low_ref, ...), custom_call_target="tpu_custom_call" | custom-call | flops 1000000000 | bytes 100000 | tf_op jit(solution)/shard_map/fit/pallas_call | solution.py:32
  61.0 1.6 %collective-permute-start.14 = (f32[8,128]{1,0:T(8,128)S(1)}, f32[8,128]{1,0:T(8,128)S(1)}, u32[]{:S(2)}, u32[]{:S(2)}) collective-permute-start(f32[8,128]{1,0:T(8,128)S(1)} %get-tuple-element.107.refs_0_), channel_id=1, source_target_pairs={{0,16},{16,0},{1,17},{17,1},{2,18},{18,2},{3,19},{19,3},{4,20},{20... | collective-permute-start | bytes 12296 | tf_op jit(solution)/shard_map/ppermute | solution.py:28
  62.6 0.8 %flip.1 = f32[512,128]{1,0:T(8,128)} custom-call(f32[128,512]{1,0:T(8,128)S(1)} %get-tuple-element.106.x_ref), custom_call_target="tpu_custom_call" | custom-call | flops 1000000 | bytes 100000 | tf_op jit(solution)/shard_map/flip/pallas_call | solution.py:32
  63.4 1.3 %collective-permute-done.14.refs_1_ = f32[8,128]{1,0:T(8,128)S(1)} collective-permute-done((f32[8,128]{1,0:T(8,128)S(1)}, f32[8,128]{1,0:T(8,128)S(1)}, u32[]{:S(2)}, u32[]{:S(2)}) %collective-permute-start.14) | collective-permute-done | bytes 4128 | tf_op jit(solution)/shard_map/ppermute | solution.py:28
  64.7 0.5 mean.1
  (10 shorter events, 0.1 us)
Async XLA Ops:
  0.6 7.4 %copy-start = (bf16[1,4096,128]{2,1,0:T(8,128)(2,1)S(1)}, bf16[1,4096,128]{2,1,0:T(8,128)(2,1)}, u32[]{:S(2)}) copy-start(bf16[1,4096,128]{2,1,0:T(8,128)(2,1)} %param.7) | copy-start | bytes 3145732
  3.4 1.6 %collective-permute-start = (bf16[768,128]{1,0:T(8,128)(2,1)S(1)}, bf16[768,128]{1,0:T(8,128)(2,1)S(1)}, u32[]{:S(2)}, u32[]{:S(2)}) collective-permute-start(bf16[768,128]{1,0:T(8,128)(2,1)S(1)} %get-tuple-element.56), channel_id=1, source_target_pairs={{0,1},{1,0},{2,3},{3,2},{4,5},{5,4},{6,7},{7,6},{8,9},{9,8},{10,11... | collective-permute-start | bytes 589832 | tf_op jit(solution)/shard_map/ppermute | solution.py:28
  5.0 6.0 %collective-permute-start.1 = (bf16[384,128]{1,0:T(8,128)(2,1)S(1)}, bf16[384,128]{1,0:T(8,128)(2,1)S(1)}, u32[]{:S(2)}, u32[]{:S(2)}) collective-permute-start(bf16[384,128]{1,0:T(8,128)(2,1)S(1)} %get-tuple-element.58), channel_id=1, source_target_pairs={{0,2},{1,3},{2,0},{3,1},{4,6},{5,7},{6,4},{7,5},{8,10},{9,11},{10,... | collective-permute-start | bytes 294920 | tf_op jit(solution)/shard_map/ppermute | solution.py:28
  11.1 7.6 %collective-permute-start.4 = (bf16[384,128]{1,0:T(8,128)(2,1)S(1)}, bf16[384,128]{1,0:T(8,128)(2,1)S(1)}, u32[]{:S(2)}, u32[]{:S(2)}) collective-permute-start(bf16[384,128]{1,0:T(8,128)(2,1)S(1)} %total.2.refs_0_), channel_id=1, source_target_pairs={{0,12},{1,13},{2,14},{3,15},{4,8},{5,9},{6,10},{7,11},{8,4},{9,5},... | collective-permute-start | bytes 294920 | tf_op jit(solution)/shard_map/ppermute | solution.py:28
  15.0 7.7 %collective-permute-start.3 = (bf16[384,128]{1,0:T(8,128)(2,1)S(1)}, bf16[384,128]{1,0:T(8,128)(2,1)S(1)}, u32[]{:S(2)}, u32[]{:S(2)}) collective-permute-start(bf16[384,128]{1,0:T(8,128)(2,1)S(1)} %total.2.refs_0_), channel_id=1, source_target_pairs={{0,8},{1,9},{2,10},{3,11},{4,12},{5,13},{6,14},{7,15},{8,0},{9,1},... | collective-permute-start | bytes 294920 | tf_op jit(solution)/shard_map/ppermute | solution.py:28
  15.0 7.7 %collective-permute-start.2 = (bf16[384,128]{1,0:T(8,128)(2,1)S(1)}, bf16[384,128]{1,0:T(8,128)(2,1)S(1)}, u32[]{:S(2)}, u32[]{:S(2)}) collective-permute-start(bf16[384,128]{1,0:T(8,128)(2,1)S(1)} %total.2.refs_0_), channel_id=1, source_target_pairs={{0,4},{1,5},{2,6},{3,7},{4,0},{5,1},{6,2},{7,3},{8,12},{9,13},{10,... | collective-permute-start | bytes 294920 | tf_op jit(solution)/shard_map/ppermute | solution.py:28
  22.8 4.7 %collective-permute-start.5 = (bf16[384,128]{1,0:T(8,128)(2,1)S(1)}, bf16[384,128]{1,0:T(8,128)(2,1)S(1)}, u32[]{:S(2)}, u32[]{:S(2)}) collective-permute-start(bf16[384,128]{1,0:T(8,128)(2,1)S(1)} %total.3.q_ref.a_ref.near_ref), channel_id=1, source_target_pairs={{0,2},{1,3},{2,0},{3,1},{4,6},{5,7},{6,4},{7,5},{8,10},{9,11},{10,... | collective-permute-start | bytes 294920 | tf_op jit(solution)/shard_map/ppermute | solution.py:28
  27.5 2.4 %collective-permute-start.6 = (bf16[768,128]{1,0:T(8,128)(2,1)S(1)}, bf16[768,128]{1,0:T(8,128)(2,1)S(1)}, u32[]{:S(2)}, u32[]{:S(2)}) collective-permute-start(bf16[768,128]{1,0:T(8,128)(2,1)S(1)} %stack.2), channel_id=1, source_target_pairs={{0,1},{1,0},{2,3},{3,2},{4,5},{5,4},{6,7},{7,6},{8,9},{9,8},{10,11... | collective-permute-start | bytes 589832 | tf_op jit(solution)/shard_map/ppermute | solution.py:28
  27.6 9.2 %collective-permute-start.7 = (s32[72,256]{1,0:T(8,128)S(1)}, s32[72,256]{1,0:T(8,128)S(1)}, u32[]{:S(2)}, u32[]{:S(2)}) collective-permute-start(s32[72,256]{1,0:T(8,128)S(1)} %attention.4), channel_id=1, source_target_pairs={{0,1},{1,0},{2,3},{3,2},{4,5},{5,4},{6,7},{7,6},{8,9},{9,8},{10,11... | collective-permute-start | bytes 221192 | tf_op jit(solution)/shard_map/ppermute | solution.py:28
  31.8 5.1 %collective-permute-start.9 = (s32[72,256]{1,0:T(8,128)S(1)}, s32[72,256]{1,0:T(8,128)S(1)}, u32[]{:S(2)}, u32[]{:S(2)}) collective-permute-start(s32[72,256]{1,0:T(8,128)S(1)} %attention.6), channel_id=1, source_target_pairs={{0,2},{1,3},{2,0},{3,1},{4,6},{5,7},{6,4},{7,5},{8,10},{9,11},{10,... | collective-permute-start | bytes 221192 | tf_op jit(solution)/shard_map/ppermute | solution.py:28
  33.4 4.5 %collective-permute-start.8 = (s32[72,256]{1,0:T(8,128)S(1)}, s32[72,256]{1,0:T(8,128)S(1)}, u32[]{:S(2)}, u32[]{:S(2)}) collective-permute-start(s32[72,256]{1,0:T(8,128)S(1)} %attention.5), channel_id=1, source_target_pairs={{0,3},{1,2},{2,1},{3,0},{4,7},{5,6},{6,5},{7,4},{8,11},{9,10},{10,... | collective-permute-start | bytes 221192 | tf_op jit(solution)/shard_map/ppermute | solution.py:28
  38.1 5.5 %collective-permute-start.10 = (s32[72,256]{1,0:T(8,128)S(1)}, s32[72,256]{1,0:T(8,128)S(1)}, u32[]{:S(2)}, u32[]{:S(2)}) collective-permute-start(s32[72,256]{1,0:T(8,128)S(1)} %merge.3.refs_0_), channel_id=1, source_target_pairs={{0,4},{1,5},{2,6},{3,7},{4,0},{5,1},{6,2},{7,3},{8,12},{9,13},{10,... | collective-permute-start | bytes 221192 | tf_op jit(solution)/shard_map/ppermute | solution.py:28
  43.6 6.7 %collective-permute-start.11 = (s32[72,256]{1,0:T(8,128)S(1)}, s32[72,256]{1,0:T(8,128)S(1)}, u32[]{:S(2)}, u32[]{:S(2)}) collective-permute-start(s32[72,256]{1,0:T(8,128)S(1)} %merge.4.refs_0_), channel_id=1, source_target_pairs={{0,8},{1,9},{2,10},{3,11},{4,12},{5,13},{6,14},{7,15},{8,0},{9,1},... | collective-permute-start | bytes 221192 | tf_op jit(solution)/shard_map/ppermute | solution.py:28
  50.5 4.8 %collective-permute-start.12 = (s32[72,256]{1,0:T(8,128)S(1)}, s32[72,256]{1,0:T(8,128)S(1)}, u32[]{:S(2)}, u32[]{:S(2)}) collective-permute-start(s32[72,256]{1,0:T(8,128)S(1)} %merge.5.a_ref), channel_id=1, source_target_pairs={{0,2},{1,3},{2,0},{3,1},{4,6},{5,7},{6,4},{7,5},{8,10},{9,11},{10,... | collective-permute-start | bytes 221192 | tf_op jit(solution)/shard_map/ppermute | solution.py:28
  55.3 2.0 %collective-permute-start.13 = (s32[144,256]{1,0:T(8,128)S(1)}, s32[144,256]{1,0:T(8,128)S(1)}, u32[]{:S(2)}, u32[]{:S(2)}) collective-permute-start(s32[144,256]{1,0:T(8,128)S(1)} %stack.3.own_ref), channel_id=1, source_target_pairs={{0,1},{1,0},{2,3},{3,2},{4,5},{5,4},{6,7},{7,6},{8,9},{9,8},{10,11... | collective-permute-start | bytes 442376 | tf_op jit(solution)/shard_map/ppermute | solution.py:28
  61.0 3.7 %collective-permute-start.14 = (f32[8,128]{1,0:T(8,128)S(1)}, f32[8,128]{1,0:T(8,128)S(1)}, u32[]{:S(2)}, u32[]{:S(2)}) collective-permute-start(f32[8,128]{1,0:T(8,128)S(1)} %get-tuple-element.107.refs_0_), channel_id=1, source_target_pairs={{0,16},{16,0},{1,17},{17,1},{2,18},{18,2},{3,19},{19,3},{4,20},{20... | collective-permute-start | bytes 12296 | tf_op jit(solution)/shard_map/ppermute | solution.py:28

commit v18 on v17

--- a/solution.py
+++ b/solution.py
@@ -416,7 +416,7 @@
 
         return piece
 
-    next_ref[...] = inverse_beside(block, [rows_update(i) for i in range(0, size, 128)] + list(beside))
+    next_ref[...] = inverse_beside(block, list(beside) + [rows_update(i) for i in range(0, size, 128)])
 
 
 def last_sweep_kernel(panel, shard_ref, h_ref, inverse_ref, high_ref, low_ref, own_ref, other_ref, out_ref, next_ref, yt_ref, cross_ref):

time: 65.4 us -> 65.2 us (level)
  no operation moved by 1% of the time
where the time goes in v18:
time: 65.2 us; the launch traced here: 65.1 us
  Pallas kernels  31.1 us (48%)
  starting transfers between devices  17.6 us (27%)
  waiting for transfers between devices  14.8 us (23%)
  between operations  1.6 us (2%)
    pallas_call x26, Pallas kernels, call(): pl.pallas_call(kernel, in_specs=specs or [SMEM if x.size == 1 else VMEM f...  31.1 us
    ppermute x15, starting transfers between devices, swap(): return lax.ppermute(array, axis, [(i, i ^ step) for i in range(size)])  17.6 us
    ppermute x15, waiting for transfers between devices, swap(): return lax.ppermute(array, axis, [(i, i ^ step) for i in range(size)])  14.8 us
  transfers between devices with their start and end apart: 15, of which 8 were waited for; matrix products, arithmetic and copies ran while one was open for 0% of the time, Pallas kernels for 38%

profile of v18, /device:TPU:0, one launch (start us, length us, event | category | flops | bytes accessed | tf_op | source)
XLA Modules:
  0.0 65.1 jit_solution(862426329542087860)
XLA Ops:
  1.4 2.0 %prepare.1 = (bf16[768,128]{1,0:T(8,128)(2,1)S(1)}, bf16[768,128]{1,0:T(8,128)(2,1)S(1)}, bf16[4096,128]{1,0:T(8,128)(2,1)S(1)}) custom-call(s32[1]{0:T(128)} %bitcast.shard_ref, s32[1]{0:T(128)S(6)} %copy.7.root_ref, bf16[1024,128]{1,0:T(8,128)(2,1)} %bitcast.9, s32[1,512]{1,0:T(1,128)} %kept_hbm.1, bf16[4096,128]{1,0:T(8,128)(2,1)} %bitcast.7), custom_call_target="tpu_custom_call" | custom-call | flops 100000 | bytes 100000 | tf_op jit(solution)/shard_map/prepare/pallas_call | solution.py:32
  3.4 0.5 collective-permute-start
  3.9 1.1 %collective-permute-done.b_ref = bf16[768,128]{1,0:T(8,128)(2,1)S(1)} collective-permute-done((bf16[768,128]{1,0:T(8,128)(2,1)S(1)}, bf16[768,128]{1,0:T(8,128)(2,1)S(1)}, u32[]{:S(2)}, u32[]{:S(2)}) %collective-permute-start) | collective-permute-done | bytes 196640 | tf_op jit(solution)/shard_map/ppermute | solution.py:28
  5.0 2.9 %collective-permute-start.1 = (bf16[384,128]{1,0:T(8,128)(2,1)S(1)}, bf16[384,128]{1,0:T(8,128)(2,1)S(1)}, u32[]{:S(2)}, u32[]{:S(2)}) collective-permute-start(bf16[384,128]{1,0:T(8,128)(2,1)S(1)} %get-tuple-element.58), channel_id=1, source_target_pairs={{0,2},{1,3},{2,0},{3,1},{4,6},{5,7},{6,4},{7,5},{8,10},{9,11},{10,... | collective-permute-start | bytes 294920 | tf_op jit(solution)/shard_map/ppermute | solution.py:28
  8.0 0.3 turn.1.vt_ref
  8.3 2.8 %collective-permute-done.1.refs_1_ = bf16[384,128]{1,0:T(8,128)(2,1)S(1)} collective-permute-done((bf16[384,128]{1,0:T(8,128)(2,1)S(1)}, bf16[384,128]{1,0:T(8,128)(2,1)S(1)}, u32[]{:S(2)}, u32[]{:S(2)}) %collective-permute-start.1) | collective-permute-done | bytes 98336 | tf_op jit(solution)/shard_map/ppermute | solution.py:28
  11.1 3.9 %collective-permute-start.4 = (bf16[384,128]{1,0:T(8,128)(2,1)S(1)}, bf16[384,128]{1,0:T(8,128)(2,1)S(1)}, u32[]{:S(2)}, u32[]{:S(2)}) collective-permute-start(bf16[384,128]{1,0:T(8,128)(2,1)S(1)} %total.2.refs_0_), channel_id=1, source_target_pairs={{0,12},{1,13},{2,14},{3,15},{4,8},{5,9},{6,10},{7,11},{8,4},{9,5},... | collective-permute-start | bytes 294920 | tf_op jit(solution)/shard_map/ppermute | solution.py:28
  15.0 0.0 collective-permute-start.3
  15.0 0.6 collective-permute-start.2
  15.6 3.1 %collective-permute-done.4.refs_3_ = bf16[384,128]{1,0:T(8,128)(2,1)S(1)} collective-permute-done((bf16[384,128]{1,0:T(8,128)(2,1)S(1)}, bf16[384,128]{1,0:T(8,128)(2,1)S(1)}, u32[]{:S(2)}, u32[]{:S(2)}) %collective-permute-start.4) | collective-permute-done | bytes 98336 | tf_op jit(solution)/shard_map/ppermute | solution.py:28
  18.7 4.0 %collective-permute-done.3.refs_2_ = bf16[384,128]{1,0:T(8,128)(2,1)S(1)} collective-permute-done((bf16[384,128]{1,0:T(8,128)(2,1)S(1)}, bf16[384,128]{1,0:T(8,128)(2,1)S(1)}, u32[]{:S(2)}, u32[]{:S(2)}) %collective-permute-start.3) | collective-permute-done | bytes 98336 | tf_op jit(solution)/shard_map/ppermute | solution.py:28
  22.8 0.0 collective-permute-done.2.refs_1_
  22.8 1.6 %collective-permute-start.5 = (bf16[384,128]{1,0:T(8,128)(2,1)S(1)}, bf16[384,128]{1,0:T(8,128)(2,1)S(1)}, u32[]{:S(2)}, u32[]{:S(2)}) collective-permute-start(bf16[384,128]{1,0:T(8,128)(2,1)S(1)} %total.3.q_ref.a_ref.near_ref), channel_id=1, source_target_pairs={{0,2},{1,3},{2,0},{3,1},{4,6},{5,7},{6,4},{7,5},{8,10},{9,11},{10,... | collective-permute-start | bytes 294920 | tf_op jit(solution)/shard_map/ppermute | solution.py:28
  24.4 1.8 %attention.4 = s32[72,256]{1,0:T(8,128)S(1)} custom-call(bf16[384,128]{1,0:T(8,128)(2,1)S(1)} %total.3.q_ref.a_ref.near_ref, bf16[4096,128]{1,0:T(8,128)(2,1)S(1)} %get-tuple-element.60.k_ref, bf16[144,4096]{1,0:T(8,128)(2,1)S(1)} %turn.1.vt_ref), custom_call_target="tpu_custom_call" | custom-call | flops 1000000 | bytes 100000 | tf_op jit(solution)/shard_map/attention/pallas_call | solution.py:32
  26.2 1.3 %collective-permute-done.5.b_ref.q_ref.far_ref = bf16[384,128]{1,0:T(8,128)(2,1)S(1)} collective-permute-done((bf16[384,128]{1,0:T(8,128)(2,1)S(1)}, bf16[384,128]{1,0:T(8,128)(2,1)S(1)}, u32[]{:S(2)}, u32[]{:S(2)}) %collective-permute-start.5) | collective-permute-done | bytes 98336 | tf_op jit(solution)/shard_map/ppermute | solution.py:28
  27.5 0.1 collective-permute-start.6
  27.6 0.5 collective-permute-start.7
  28.1 1.8 %attention.5 = s32[72,256]{1,0:T(8,128)S(1)} custom-call(bf16[384,128]{1,0:T(8,128)(2,1)S(1)} %collective-permute-done.5.b_ref.q_ref.far_ref, bf16[4096,128]{1,0:T(8,128)(2,1)S(1)} %get-tuple-element.60.k_ref, bf16[144,4096]{1,0:T(8,128)(2,1)S(1)} %turn.1.vt_ref), custom_call_target="tpu_custom_call" | custom-call | flops 1000000 | bytes 100000 | tf_op jit(solution)/shard_map/attention/pallas_call | solution.py:32
  29.9 1.8 %attention.6 = s32[72,256]{1,0:T(8,128)S(1)} custom-call(bf16[768,128]{1,0:T(8,128)(2,1)S(1)} %collective-permute-done.6.q_ref.other_ref, bf16[4096,128]{1,0:T(8,128)(2,1)S(1)} %get-tuple-element.60.k_ref, bf16[144,4096]{1,0:T(8,128)(2,1)S(1)} %turn.1.vt_ref), custom_call_target="tpu_custom_call" | custom-call | flops 1000000 | bytes 100000 | tf_op jit(solution)/shard_map/attention/pallas_call | solution.py:32
  31.8 1.6 %collective-permute-start.9 = (s32[72,256]{1,0:T(8,128)S(1)}, s32[72,256]{1,0:T(8,128)S(1)}, u32[]{:S(2)}, u32[]{:S(2)}) collective-permute-start(s32[72,256]{1,0:T(8,128)S(1)} %attention.6), channel_id=1, source_target_pairs={{0,2},{1,3},{2,0},{3,1},{4,6},{5,7},{6,4},{7,5},{8,10},{9,11},{10,... | collective-permute-start | bytes 221192 | tf_op jit(solution)/shard_map/ppermute | solution.py:28
  33.4 1.8 %attention.7.refs_0_ = f32[136,256]{1,0:T(8,128)S(1)} custom-call(bf16[768,128]{1,0:T(8,128)(2,1)S(1)} %collective-permute-done.6.q_ref.other_ref, bf16[4096,128]{1,0:T(8,128)(2,1)S(1)} %get-tuple-element.60.k_ref, bf16[144,4096]{1,0:T(8,128)(2,1)S(1)} %turn.1.vt_ref), custom_call_target="tpu_custom_call" | custom-call | flops 1000000 | bytes 100000 | tf_op jit(solution)/shard_map/attention/pallas_call | solution.py:32
  35.2 1.7 %attend.1 = (bf16[512,1024]{1,0:T(8,128)(2,1)S(1)}, bf16[512,1024]{1,0:T(8,128)(2,1)S(1)}, f32[32,256]{1,0:T(8,128)S(1)}) custom-call(s32[1]{0:T(128)} %bitcast.shard_ref, bf16[384,128]{1,0:T(8,128)(2,1)S(1)} %total.3.q_ref.a_ref.near_ref, bf16[384,128]{1,0:T(8,128)(2,1)S(1)} %collective-permute-done.5.b_ref.q_ref.far_ref, ...), custom_call_target="tpu_custom_call" | custom-call | flops 1000000 | bytes 100000 | tf_op jit(solution)/shard_map/attend/pallas_call | solution.py:32
  36.8 0.0 collective-permute-done.7.refs_1_
  36.8 1.1 %collective-permute-done.8.refs_2_ = s32[72,256]{1,0:T(8,128)S(1)} collective-permute-done((s32[72,256]{1,0:T(8,128)S(1)}, s32[72,256]{1,0:T(8,128)S(1)}, u32[]{:S(2)}, u32[]{:S(2)}) %collective-permute-start.8) | collective-permute-done | bytes 73760 | tf_op jit(solution)/shard_map/ppermute | solution.py:28
  37.9 0.2 merge.3.refs_0_
  38.1 0.6 collective-permute-start.10
  38.6 2.9 %gram.1 = (f32[512,512]{1,0:T(8,128)S(1)}, f32[64,64]{1,0:T(8,128)S(1)}) custom-call(bf16[512,1024]{1,0:T(8,128)(2,1)S(1)} %get-tuple-element.70.high_ref, bf16[512,1024]{1,0:T(8,128)(2,1)S(1)} %get-tuple-element.71.low_ref, f32[32,256]{1,0:T(8,128)S(1)} %get-tuple-element.72.square_ref), custom_call_target="tpu_custom_call" | custom-call | flops 4000000000 | bytes 100000 | tf_op jit(solution)/shard_map/gram/pallas_call | solution.py:32
  41.6 1.9 %sweep.6 = (f32[512,512]{1,0:T(8,128)S(1)}, f32[64,64]{1,0:T(8,128)S(1)}) custom-call(f32[512,512]{1,0:T(8,128)S(1)} %get-tuple-element.73.h_ref, f32[64,64]{1,0:T(8,128)S(1)} %get-tuple-element.74.inverse_ref), custom_call_target="tpu_custom_call" | custom-call | flops 2000000000 | bytes 100000 | tf_op jit(solution)/shard_map/sweep/pallas_call | solution.py:32
  43.5 0.0 collective-permute-done.10.refs_1_
  43.5 0.1 merge.4.refs_0_
  43.6 2.6 %collective-permute-start.11 = (s32[72,256]{1,0:T(8,128)S(1)}, s32[72,256]{1,0:T(8,128)S(1)}, u32[]{:S(2)}, u32[]{:S(2)}) collective-permute-start(s32[72,256]{1,0:T(8,128)S(1)} %merge.4.refs_0_), channel_id=1, source_target_pairs={{0,8},{1,9},{2,10},{3,11},{4,12},{5,13},{6,14},{7,15},{8,0},{9,1},... | collective-permute-start | bytes 221192 | tf_op jit(solution)/shard_map/ppermute | solution.py:28
  46.3 1.9 %sweep.7 = (f32[512,512]{1,0:T(8,128)S(1)}, f32[64,64]{1,0:T(8,128)S(1)}) custom-call(f32[512,512]{1,0:T(8,128)S(1)} %get-tuple-element.80.h_ref, f32[64,64]{1,0:T(8,128)S(1)} %get-tuple-element.81.inverse_ref), custom_call_target="tpu_custom_call" | custom-call | flops 2000000000 | bytes 100000 | tf_op jit(solution)/shard_map/sweep/pallas_call | solution.py:32
  48.2 1.9 %sweep.8 = (f32[512,512]{1,0:T(8,128)S(1)}, f32[64,64]{1,0:T(8,128)S(1)}) custom-call(f32[512,512]{1,0:T(8,128)S(1)} %get-tuple-element.82.h_ref, f32[64,64]{1,0:T(8,128)S(1)} %get-tuple-element.83.inverse_ref), custom_call_target="tpu_custom_call" | custom-call | flops 2000000000 | bytes 100000 | tf_op jit(solution)/shard_map/sweep/pallas_call | solution.py:32
  50.1 0.2 collective-permute-done.11.refs_1_
  50.3 0.1 merge.5.a_ref
  50.4 1.0 %collective-permute-start.12 = (s32[72,256]{1,0:T(8,128)S(1)}, s32[72,256]{1,0:T(8,128)S(1)}, u32[]{:S(2)}, u32[]{:S(2)}) collective-permute-start(s32[72,256]{1,0:T(8,128)S(1)} %merge.5.a_ref), channel_id=1, source_target_pairs={{0,2},{1,3},{2,0},{3,1},{4,6},{5,7},{6,4},{7,5},{8,10},{9,11},{10,... | collective-permute-start | bytes 221192 | tf_op jit(solution)/shard_map/ppermute | solution.py:28
  51.4 1.9 %sweep.9 = (f32[512,512]{1,0:T(8,128)S(1)}, f32[64,64]{1,0:T(8,128)S(1)}) custom-call(f32[512,512]{1,0:T(8,128)S(1)} %get-tuple-element.87.h_ref, f32[64,64]{1,0:T(8,128)S(1)} %get-tuple-element.88.inverse_ref), custom_call_target="tpu_custom_call" | custom-call | flops 2000000000 | bytes 100000 | tf_op jit(solution)/shard_map/sweep/pallas_call | solution.py:32
  53.3 1.9 %sweep.10 = (f32[512,512]{1,0:T(8,128)S(1)}, f32[64,64]{1,0:T(8,128)S(1)}) custom-call(f32[512,512]{1,0:T(8,128)S(1)} %get-tuple-element.89.h_ref, f32[64,64]{1,0:T(8,128)S(1)} %get-tuple-element.90.inverse_ref), custom_call_target="tpu_custom_call" | custom-call | flops 2000000000 | bytes 100000 | tf_op jit(solution)/shard_map/sweep/pallas_call | solution.py:32
  55.2 0.0 collective-permute-done.12.b_ref
  55.3 0.1 collective-permute-start.13
  55.3 1.9 %sweep.11 = (f32[512,512]{1,0:T(8,128)S(1)}, f32[64,64]{1,0:T(8,128)S(1)}) custom-call(f32[512,512]{1,0:T(8,128)S(1)} %get-tuple-element.94.h_ref, f32[64,64]{1,0:T(8,128)S(1)} %get-tuple-element.95.inverse_ref), custom_call_target="tpu_custom_call" | custom-call | flops 2000000000 | bytes 100000 | tf_op jit(solution)/shard_map/sweep/pallas_call | solution.py:32
  57.2 0.0 collective-permute-done.13.other_ref
  57.2 2.0 %last_sweep.1 = (f32[512,512]{1,0:T(8,128)S(1)}, f32[64,64]{1,0:T(8,128)S(1)}, f32[128,1024]{1,0:T(8,128)S(1)}, f32[128,512]{1,0:T(8,128)S(1)}) custom-call(s32[1]{0:T(128)} %bitcast.shard_ref, f32[512,512]{1,0:T(8,128)S(1)} %get-tuple-element.99.h_ref, f32[64,64]{1,0:T(8,128)S(1)} %get-tuple-element.100.inverse_ref, ...), custom_call_target="tpu_custom_call" | custom-call | flops 2000000000 | bytes 100000 | tf_op jit(solution)/shard_map/last_sweep/pallas_call | solution.py:32
  59.3 1.6 %fit.1 = (f32[128,512]{1,0:T(8,128)S(1)}, f32[8,128]{1,0:T(8,128)S(1)}) custom-call(f32[512,512]{1,0:T(8,128)S(1)} %get-tuple-element.102.swept_ref, f32[64,64]{1,0:T(8,128)S(1)} %get-tuple-element.103.inverse_ref, bf16[512,1024]{1,0:T(8,128)(2,1)S(1)} %get-tuple-element.70.high_ref, bf16[512,1024]{1,0:T(8,128)(2,1)S(1)} %get-tuple-element.71.low_ref, ...), custom_call_target="tpu_custom_call" | custom-call | flops 1000000000 | bytes 100000 | tf_op jit(solution)/shard_map/fit/pallas_call | solution.py:32
  60.9 1.6 %collective-permute-start.14 = (f32[8,128]{1,0:T(8,128)S(1)}, f32[8,128]{1,0:T(8,128)S(1)}, u32[]{:S(2)}, u32[]{:S(2)}) collective-permute-start(f32[8,128]{1,0:T(8,128)S(1)} %get-tuple-element.107.refs_0_), channel_id=1, source_target_pairs={{0,16},{16,0},{1,17},{17,1},{2,18},{18,2},{3,19},{19,3},{4,20},{20... | collective-permute-start | bytes 12296 | tf_op jit(solution)/shard_map/ppermute | solution.py:28
  62.4 0.8 %flip.1 = f32[512,128]{1,0:T(8,128)} custom-call(f32[128,512]{1,0:T(8,128)S(1)} %get-tuple-element.106.x_ref), custom_call_target="tpu_custom_call" | custom-call | flops 1000000 | bytes 100000 | tf_op jit(solution)/shard_map/flip/pallas_call | solution.py:32
  63.3 1.3 %collective-permute-done.14.refs_1_ = f32[8,128]{1,0:T(8,128)S(1)} collective-permute-done((f32[8,128]{1,0:T(8,128)S(1)}, f32[8,128]{1,0:T(8,128)S(1)}, u32[]{:S(2)}, u32[]{:S(2)}) %collective-permute-start.14) | collective-permute-done | bytes 4128 | tf_op jit(solution)/shard_map/ppermute | solution.py:28
  64.5 0.5 mean.1
  (10 shorter events, 0.1 us)
Async XLA Ops:
  0.6 7.4 %copy-start = (bf16[1,4096,128]{2,1,0:T(8,128)(2,1)S(1)}, bf16[1,4096,128]{2,1,0:T(8,128)(2,1)}, u32[]{:S(2)}) copy-start(bf16[1,4096,128]{2,1,0:T(8,128)(2,1)} %param.7) | copy-start | bytes 3145732
  3.4 1.6 %collective-permute-start = (bf16[768,128]{1,0:T(8,128)(2,1)S(1)}, bf16[768,128]{1,0:T(8,128)(2,1)S(1)}, u32[]{:S(2)}, u32[]{:S(2)}) collective-permute-start(bf16[768,128]{1,0:T(8,128)(2,1)S(1)} %get-tuple-element.56), channel_id=1, source_target_pairs={{0,1},{1,0},{2,3},{3,2},{4,5},{5,4},{6,7},{7,6},{8,9},{9,8},{10,11... | collective-permute-start | bytes 589832 | tf_op jit(solution)/shard_map/ppermute | solution.py:28
  5.0 6.0 %collective-permute-start.1 = (bf16[384,128]{1,0:T(8,128)(2,1)S(1)}, bf16[384,128]{1,0:T(8,128)(2,1)S(1)}, u32[]{:S(2)}, u32[]{:S(2)}) collective-permute-start(bf16[384,128]{1,0:T(8,128)(2,1)S(1)} %get-tuple-element.58), channel_id=1, source_target_pairs={{0,2},{1,3},{2,0},{3,1},{4,6},{5,7},{6,4},{7,5},{8,10},{9,11},{10,... | collective-permute-start | bytes 294920 | tf_op jit(solution)/shard_map/ppermute | solution.py:28
  11.1 7.6 %collective-permute-start.4 = (bf16[384,128]{1,0:T(8,128)(2,1)S(1)}, bf16[384,128]{1,0:T(8,128)(2,1)S(1)}, u32[]{:S(2)}, u32[]{:S(2)}) collective-permute-start(bf16[384,128]{1,0:T(8,128)(2,1)S(1)} %total.2.refs_0_), channel_id=1, source_target_pairs={{0,12},{1,13},{2,14},{3,15},{4,8},{5,9},{6,10},{7,11},{8,4},{9,5},... | collective-permute-start | bytes 294920 | tf_op jit(solution)/shard_map/ppermute | solution.py:28
  15.0 7.7 %collective-permute-start.3 = (bf16[384,128]{1,0:T(8,128)(2,1)S(1)}, bf16[384,128]{1,0:T(8,128)(2,1)S(1)}, u32[]{:S(2)}, u32[]{:S(2)}) collective-permute-start(bf16[384,128]{1,0:T(8,128)(2,1)S(1)} %total.2.refs_0_), channel_id=1, source_target_pairs={{0,8},{1,9},{2,10},{3,11},{4,12},{5,13},{6,14},{7,15},{8,0},{9,1},... | collective-permute-start | bytes 294920 | tf_op jit(solution)/shard_map/ppermute | solution.py:28
  15.0 7.7 %collective-permute-start.2 = (bf16[384,128]{1,0:T(8,128)(2,1)S(1)}, bf16[384,128]{1,0:T(8,128)(2,1)S(1)}, u32[]{:S(2)}, u32[]{:S(2)}) collective-permute-start(bf16[384,128]{1,0:T(8,128)(2,1)S(1)} %total.2.refs_0_), channel_id=1, source_target_pairs={{0,4},{1,5},{2,6},{3,7},{4,0},{5,1},{6,2},{7,3},{8,12},{9,13},{10,... | collective-permute-start | bytes 294920 | tf_op jit(solution)/shard_map/ppermute | solution.py:28
  22.8 4.7 %collective-permute-start.5 = (bf16[384,128]{1,0:T(8,128)(2,1)S(1)}, bf16[384,128]{1,0:T(8,128)(2,1)S(1)}, u32[]{:S(2)}, u32[]{:S(2)}) collective-permute-start(bf16[384,128]{1,0:T(8,128)(2,1)S(1)} %total.3.q_ref.a_ref.near_ref), channel_id=1, source_target_pairs={{0,2},{1,3},{2,0},{3,1},{4,6},{5,7},{6,4},{7,5},{8,10},{9,11},{10,... | collective-permute-start | bytes 294920 | tf_op jit(solution)/shard_map/ppermute | solution.py:28
  27.5 2.4 %collective-permute-start.6 = (bf16[768,128]{1,0:T(8,128)(2,1)S(1)}, bf16[768,128]{1,0:T(8,128)(2,1)S(1)}, u32[]{:S(2)}, u32[]{:S(2)}) collective-permute-start(bf16[768,128]{1,0:T(8,128)(2,1)S(1)} %stack.2), channel_id=1, source_target_pairs={{0,1},{1,0},{2,3},{3,2},{4,5},{5,4},{6,7},{7,6},{8,9},{9,8},{10,11... | collective-permute-start | bytes 589832 | tf_op jit(solution)/shard_map/ppermute | solution.py:28
  27.6 9.2 %collective-permute-start.7 = (s32[72,256]{1,0:T(8,128)S(1)}, s32[72,256]{1,0:T(8,128)S(1)}, u32[]{:S(2)}, u32[]{:S(2)}) collective-permute-start(s32[72,256]{1,0:T(8,128)S(1)} %attention.4), channel_id=1, source_target_pairs={{0,1},{1,0},{2,3},{3,2},{4,5},{5,4},{6,7},{7,6},{8,9},{9,8},{10,11... | collective-permute-start | bytes 221192 | tf_op jit(solution)/shard_map/ppermute | solution.py:28
  31.8 5.1 %collective-permute-start.9 = (s32[72,256]{1,0:T(8,128)S(1)}, s32[72,256]{1,0:T(8,128)S(1)}, u32[]{:S(2)}, u32[]{:S(2)}) collective-permute-start(s32[72,256]{1,0:T(8,128)S(1)} %attention.6), channel_id=1, source_target_pairs={{0,2},{1,3},{2,0},{3,1},{4,6},{5,7},{6,4},{7,5},{8,10},{9,11},{10,... | collective-permute-start | bytes 221192 | tf_op jit(solution)/shard_map/ppermute | solution.py:28
  33.4 4.5 %collective-permute-start.8 = (s32[72,256]{1,0:T(8,128)S(1)}, s32[72,256]{1,0:T(8,128)S(1)}, u32[]{:S(2)}, u32[]{:S(2)}) collective-permute-start(s32[72,256]{1,0:T(8,128)S(1)} %attention.5), channel_id=1, source_target_pairs={{0,3},{1,2},{2,1},{3,0},{4,7},{5,6},{6,5},{7,4},{8,11},{9,10},{10,... | collective-permute-start | bytes 221192 | tf_op jit(solution)/shard_map/ppermute | solution.py:28
  38.1 5.5 %collective-permute-start.10 = (s32[72,256]{1,0:T(8,128)S(1)}, s32[72,256]{1,0:T(8,128)S(1)}, u32[]{:S(2)}, u32[]{:S(2)}) collective-permute-start(s32[72,256]{1,0:T(8,128)S(1)} %merge.3.refs_0_), channel_id=1, source_target_pairs={{0,4},{1,5},{2,6},{3,7},{4,0},{5,1},{6,2},{7,3},{8,12},{9,13},{10,... | collective-permute-start | bytes 221192 | tf_op jit(solution)/shard_map/ppermute | solution.py:28
  43.6 6.7 %collective-permute-start.11 = (s32[72,256]{1,0:T(8,128)S(1)}, s32[72,256]{1,0:T(8,128)S(1)}, u32[]{:S(2)}, u32[]{:S(2)}) collective-permute-start(s32[72,256]{1,0:T(8,128)S(1)} %merge.4.refs_0_), channel_id=1, source_target_pairs={{0,8},{1,9},{2,10},{3,11},{4,12},{5,13},{6,14},{7,15},{8,0},{9,1},... | collective-permute-start | bytes 221192 | tf_op jit(solution)/shard_map/ppermute | solution.py:28
  50.4 4.8 %collective-permute-start.12 = (s32[72,256]{1,0:T(8,128)S(1)}, s32[72,256]{1,0:T(8,128)S(1)}, u32[]{:S(2)}, u32[]{:S(2)}) collective-permute-start(s32[72,256]{1,0:T(8,128)S(1)} %merge.5.a_ref), channel_id=1, source_target_pairs={{0,2},{1,3},{2,0},{3,1},{4,6},{5,7},{6,4},{7,5},{8,10},{9,11},{10,... | collective-permute-start | bytes 221192 | tf_op jit(solution)/shard_map/ppermute | solution.py:28
  55.3 2.0 %collective-permute-start.13 = (s32[144,256]{1,0:T(8,128)S(1)}, s32[144,256]{1,0:T(8,128)S(1)}, u32[]{:S(2)}, u32[]{:S(2)}) collective-permute-start(s32[144,256]{1,0:T(8,128)S(1)} %stack.3.own_ref), channel_id=1, source_target_pairs={{0,1},{1,0},{2,3},{3,2},{4,5},{5,4},{6,7},{7,6},{8,9},{9,8},{10,11... | collective-permute-start | bytes 442376 | tf_op jit(solution)/shard_map/ppermute | solution.py:28
  60.9 3.7 %collective-permute-start.14 = (f32[8,128]{1,0:T(8,128)S(1)}, f32[8,128]{1,0:T(8,128)S(1)}, u32[]{:S(2)}, u32[]{:S(2)}) collective-permute-start(f32[8,128]{1,0:T(8,128)S(1)} %get-tuple-element.107.refs_0_), channel_id=1, source_target_pairs={{0,16},{16,0},{1,17},{17,1},{2,18},{18,2},{3,19},{19,3},{4,20},{20... | collective-permute-start | bytes 12296 | tf_op jit(solution)/shard_map/ppermute | solution.py:28
